TPU v7x, 512 devices: a whole 4x8x8 slice. The times are simulated.
512 devices in a mesh: row: 16 (over y, core), col: 32 (over x, z).
Axes of the slice: x: 4, y: 8, z: 8, core: 2. Of those that a mesh axis runs over, the one named last changes fastest.
Arguments:
- tokens: bfloat16 [2304, 8192], P('col', 'row'), may hold values from -6 to 6
- out_grad: bfloat16 [2304, 8192], P('col', 'row'), may hold values from -6 to 6
- gate_pre: bfloat16 [2304, 12288], P('row', 'col'), may hold values from -8 to 8
- up_pre: bfloat16 [2304, 12288], P('row', 'col'), may hold values from -6 to 6
- w_gate: bfloat16 [8192, 12288], P('row', 'col'), may hold values from -0.0625 to 0.0625
- w_up: bfloat16 [8192, 12288], P('row', 'col'), may hold values from -0.0625 to 0.0625
- w_down: bfloat16 [12288, 8192], P('col', 'row'), may hold values from -0.0546875 to 0.0546875
Outputs:
- token_grad: bfloat16 [2304, 8192], P('col', 'row')
- gate_wgrad: bfloat16 [8192, 12288], P('row', 'col')
- up_wgrad: bfloat16 [8192, 12288], P('row', 'col')
- down_wgrad: bfloat16 [12288, 8192], P('col', 'row')
All inputs are finite; a program needn't handle non-finite values.
Results may differ from a plain program's by a relative error of at most 0.035.
Values may be sent and summed in bfloat16 or wider, within the bound.
No kernel may reach another device: no remote copies, remote signals or barrier semaphores. Data moves between devices by JAX's collectives and lax.ppermute only.
A program may use at most 64 MiB of HBM per device.

v0:
```python
import jax
import jax.numpy as jnp
from jax import lax
from jax.sharding import PartitionSpec as P


def contract_last(left_side, right_side):
    return lax.dot_general(
        left_side, right_side, (((1,), (1,)), ((), ())), preferred_element_type=jnp.float32
    )


def contract_first(left_side, right_side):
    return lax.dot_general(
        left_side, right_side, (((0,), (0,)), ((), ())), preferred_element_type=jnp.float32
    )


def swiglu_grads(hidden_grad, gate_pre, up_pre):
    gate_float = gate_pre.astype(jnp.float32)
    up_float = up_pre.astype(jnp.float32)
    sigmoid_gate = jax.nn.sigmoid(gate_float)
    swish_gate = gate_float * sigmoid_gate
    gate_grad = (
        hidden_grad * up_float * sigmoid_gate * (1.0 + gate_float * (1.0 - sigmoid_gate))
    ).astype(jnp.bfloat16)
    up_grad = (hidden_grad * swish_gate).astype(jnp.bfloat16)
    hidden = (swish_gate * up_float).astype(jnp.bfloat16)
    return (gate_grad, up_grad, hidden)


def local(tokens, out_grad, gate_pre, up_pre, w_gate, w_up, w_down):
    token_rows, grad_rows = (
        lax.all_gather(tokens, "col", axis=0, tiled=True),
        lax.all_gather(out_grad, "col", axis=0, tiled=True),
    )
    total_rows = grad_rows.shape[0]
    hidden_grad = lax.psum_scatter(
        contract_last(grad_rows, w_down).astype(jnp.bfloat16),
        "row",
        scatter_dimension=0,
        tiled=True,
    ).astype(jnp.float32)
    gate_share, up_share, hidden_share = swiglu_grads(hidden_grad, gate_pre, up_pre)
    gate_grad, up_grad, hidden = (
        lax.all_gather(gate_share, "row", axis=0, tiled=True),
        lax.all_gather(up_share, "row", axis=0, tiled=True),
        lax.all_gather(hidden_share, "row", axis=0, tiled=True),
    )
    token_grad = lax.psum_scatter(
        (contract_last(gate_grad, w_gate) + contract_last(up_grad, w_up)).astype(jnp.bfloat16),
        "col",
        scatter_dimension=0,
        tiled=True,
    )
    grad_scale = total_rows ** (-0.5)
    gate_wgrad = (contract_first(token_rows, gate_grad) * grad_scale).astype(jnp.bfloat16)
    up_wgrad = (contract_first(token_rows, up_grad) * grad_scale).astype(jnp.bfloat16)
    down_wgrad = (contract_first(hidden, grad_rows) * grad_scale).astype(jnp.bfloat16)
    return (token_grad, gate_wgrad, up_wgrad, down_wgrad)


def solution(mesh):
    return jax.shard_map(
        local,
        mesh=mesh,
        in_specs=(
            P("col", "row"),
            P("col", "row"),
            P("row", "col"),
            P("row", "col"),
            P("row", "col"),
            P("row", "col"),
            P("col", "row"),
        ),
        out_specs=(P("col", "row"), P("row", "col"), P("row", "col"), P("col", "row")),
        check_vma=False,
    )
```

profile of v0, /device:TPU:6, one launch (start us, length us, event | category | flops | bytes accessed | tf_op | source)
XLA Modules:
  0.0 612.5 jit_solution(11523516848758164644)
XLA Ops:
  7.2 0.0 copy-start
  7.2 0.0 all-gather.6.cloned.1.call-start
  7.2 0.7 all-gather.6.cloned.1.call-update
  7.9 0.0 copy-start.3
  7.9 0.0 copy-start.4
  7.9 0.0 reduce-scatter.3.cloned.1.call-start
  8.0 91.3 %all-gather.6.cloned.1.call-done = bf16[2304,512]{1,0:T(8,128)(2,1)} async-done(((bf16[72,512]{1,0:T(8,128)(2,1)}), bf16[2304,512]{1,0:T(8,128)(2,1)}) %all-gather.6.cloned.1.call-update) | async-done | bytes 2359312 | tf_op jit(solution)/shard_map/all_gather | solution.py:35
  99.3 4.4 convolution_convert_fusion
  103.6 0.0 reduce-scatter.3.cloned.1.call-update
  103.6 0.0 all-gather.8.cloned.1.call-start
  103.7 59.0 %reduce-scatter.3.cloned.1.call-done = bf16[144,384]{1,0:T(8,128)(2,1)} async-done(((bf16[2304,384]{1,0:T(8,128)(2,1)}), bf16[144,384]{1,0:T(8,128)(2,1)}) %reduce-scatter.3.cloned.1.call-update) | async-done | bytes 110608 | tf_op jit(solution)/shard_map/reduce_scatter | solution.py:38
  162.7 0.0 copy-done.3
  162.7 0.0 copy-done.4
  162.7 1.7 fusion.10
  164.5 0.0 all-gather.8.cloned.1.call-update
  164.5 0.0 all-gather.10.cloned.1.call-start
  164.5 0.5 all-gather.10.cloned.1.call-update
  165.1 0.0 all-gather.12.cloned.1.call-start
  165.1 0.5 all-gather.12.cloned.1.call-update
  165.7 0.0 all-gather.14.cloned.1.call-start
  165.7 0.5 all-gather.14.cloned.1.call-update
  166.2 0.0 copy-start.2
  166.2 0.0 reduce-scatter.5.cloned.1.call-start
  166.3 39.9 %all-gather.8.cloned.1.call-done = bf16[2304,384]{1,0:T(8,128)(2,1)} async-done(((bf16[144,384]{1,0:T(8,128)(2,1)}), bf16[2304,384]{1,0:T(8,128)(2,1)}) %all-gather.8.cloned.1.call-update) | async-done | bytes 1769488 | tf_op jit(solution)/shard_map/all_gather | solution.py:46
  206.2 0.0 copy-done
  206.2 5.0 fusion.15
  211.3 38.3 %all-gather.10.cloned.1.call-done = bf16[2304,384]{1,0:T(8,128)(2,1)} async-done(((bf16[144,384]{1,0:T(8,128)(2,1)}), bf16[2304,384]{1,0:T(8,128)(2,1)}) %all-gather.10.cloned.1.call-update) | async-done | bytes 1769488 | tf_op jit(solution)/shard_map/all_gather | solution.py:47
  249.6 0.0 copy-done.2
  249.6 5.7 fusion
  255.3 0.0 copy-start.1
  255.3 0.0 reduce-scatter.5.cloned.1.call-update
  255.3 80.1 %all-gather.12.cloned.1.call-done = bf16[2304,512]{1,0:T(8,128)(2,1)} async-done(((bf16[72,512]{1,0:T(8,128)(2,1)}), bf16[2304,512]{1,0:T(8,128)(2,1)}) %all-gather.12.cloned.1.call-update) | async-done | bytes 2359312 | tf_op jit(solution)/shard_map/all_gather | solution.py:34
  335.4 0.0 copy-done.1
  335.4 2.8 fusion.5
  338.2 0.9 copy.11
  339.1 0.0 copy-start.5
  339.1 3.5 fusion.4
  342.6 0.9 copy.12
  343.5 34.2 %all-gather.14.cloned.1.call-done = bf16[2304,384]{1,0:T(8,128)(2,1)} async-done(((bf16[144,384]{1,0:T(8,128)(2,1)}), bf16[2304,384]{1,0:T(8,128)(2,1)}) %all-gather.14.cloned.1.call-update) | async-done | bytes 1769488 | tf_op jit(solution)/shard_map/all_gather | solution.py:48
  377.7 0.0 copy-done.5
  377.7 3.3 fusion.3
  381.0 224.6 %reduce-scatter.5.cloned.1.call-done = bf16[72,512]{1,0:T(8,128)(2,1)} async-done(((bf16[2304,512]{1,0:T(8,128)(2,1)}), bf16[72,512]{1,0:T(8,128)(2,1)}) %reduce-scatter.5.cloned.1.call-update) | async-done | bytes 73744 | tf_op jit(solution)/shard_map/reduce_scatter | solution.py:50
Async XLA Ops:
  7.2 199.1 %copy-start = (bf16[512,384]{1,0:T(8,128)(2,1)S(1)}, bf16[512,384]{1,0:T(8,128)(2,1)}, u32[]{:S(2)}) copy-start(bf16[512,384]{1,0:T(8,128)(2,1)} %param.11) | copy-start | bytes 1179652
  7.2 92.1 %all-gather.6.cloned.1.call-start = ((), (), s32[]{:S(2)}) async-start(), calls=%async_computation.2 | async-start | bytes 2433024 | tf_op jit(solution)/shard_map/all_gather | solution.py:35
  7.9 154.8 %copy-start.3 = (bf16[144,384]{1,0:T(8,128)(2,1)S(1)}, bf16[144,384]{1,0:T(8,128)(2,1)}, u32[]{:S(2)}) copy-start(bf16[144,384]{1,0:T(8,128)(2,1)} %param.10) | copy-start | bytes 331780
  7.9 154.8 %copy-start.4 = (bf16[144,384]{1,0:T(8,128)(2,1)S(1)}, bf16[144,384]{1,0:T(8,128)(2,1)}, u32[]{:S(2)}) copy-start(bf16[144,384]{1,0:T(8,128)(2,1)} %param.9) | copy-start | bytes 331780
  7.9 154.8 %reduce-scatter.3.cloned.1.call-start = ((), (), s32[]{:S(2)}) async-start(), calls=%async_computation.3 | async-start | bytes 1880064 | tf_op jit(solution)/shard_map/reduce_scatter | solution.py:38
  103.6 102.6 %all-gather.8.cloned.1.call-start = ((), (), s32[]{:S(2)}) async-start(), calls=%async_computation.4 | async-start | bytes 1880064 | tf_op jit(solution)/shard_map/all_gather | solution.py:46
  164.5 85.1 %all-gather.10.cloned.1.call-start = ((), (), s32[]{:S(2)}) async-start(), calls=%async_computation.5 | async-start | bytes 1880064 | tf_op jit(solution)/shard_map/all_gather | solution.py:47
  165.1 170.3 %all-gather.12.cloned.1.call-start = ((), (), s32[]{:S(2)}) async-start(), calls=%async_computation.7 | async-start | bytes 2433024 | tf_op jit(solution)/shard_map/all_gather | solution.py:34
  165.7 212.0 %all-gather.14.cloned.1.call-start = ((), (), s32[]{:S(2)}) async-start(), calls=%async_computation.8 | async-start | bytes 1880064 | tf_op jit(solution)/shard_map/all_gather | solution.py:48
  166.2 83.3 %copy-start.2 = (bf16[512,384]{1,0:T(8,128)(2,1)S(1)}, bf16[512,384]{1,0:T(8,128)(2,1)}, u32[]{:S(2)}) copy-start(bf16[512,384]{1,0:T(8,128)(2,1)} %param.12) | copy-start | bytes 1179652
  166.2 439.4 %reduce-scatter.5.cloned.1.call-start = ((), (), s32[]{:S(2)}) async-start(), calls=%async_computation.6 | async-start | bytes 2433024 | tf_op jit(solution)/shard_map/reduce_scatter | solution.py:50
  255.3 80.1 %copy-start.1 = (bf16[2304,384]{1,0:T(8,128)(2,1)S(1)}, bf16[2304,384]{1,0:T(8,128)(2,1)}, u32[]{:S(2)}) copy-start(bf16[2304,384]{1,0:T(8,128)(2,1)} %all-gather.8.cloned.1.call-done) | copy-start | bytes 5308420
  339.1 38.6 %copy-start.5 = (bf16[2304,512]{1,0:T(8,128)(2,1)S(1)}, bf16[2304,512]{1,0:T(8,128)(2,1)}, u32[]{:S(2)}) copy-start(bf16[2304,512]{1,0:T(8,128)(2,1)} %all-gather.6.cloned.1.call-done) | copy-start | bytes 7077892
Sparse Core Ops, SparseCore 0:
  11.2 88.0 all-gather.5
  103.8 58.9 reduce-scatter.2
  165.6 40.5 all-gather.7
  209.0 40.5 all-gather.9
  253.1 82.3 all-gather.11
  338.2 39.4 all-gather.13
  383.3 222.2 reduce-scatter.4
where the time goes:
time: 614 us; the launch traced here: 613 us
  waiting for transfers between devices  570 us (93%)
  matrix products  24.6 us (4%)
  between operations  14.2 us (2%)
    reduce_scatter x1, waiting for transfers between devices, local(): lax.psum_scatter((contract_last(gate_grad, w_gate) + contract_last(up_gra...  225 us
    all_gather x1, waiting for transfers between devices, local(): lax.all_gather(out_grad, 'col', axis=0, tiled=True)  91.3 us
    all_gather x1, waiting for transfers between devices, local(): lax.all_gather(tokens, 'col', axis=0, tiled=True)  80.1 us
    reduce_scatter x1, waiting for transfers between devices, local(): lax.psum_scatter(contract_last(grad_rows, w_down).astype(jnp.bfloat16), '...  59 us
    all_gather x1, waiting for transfers between devices, local(): lax.all_gather(gate_share, 'row', axis=0, tiled=True)  39.9 us
    all_gather x1, waiting for transfers between devices, local(): lax.all_gather(up_share, 'row', axis=0, tiled=True)  38.3 us
    all_gather x1, waiting for transfers between devices, local(): lax.all_gather(hidden_share, 'row', axis=0, tiled=True)  34.2 us
    dot_general x3, matrix products, contract_last(): lax.dot_general(left_side, right_side, (((1,), (1,)), ((), ())), preferre...  15.1 us
  transfers between devices with their start and end apart: 7, of which 7 were waited for; matrix products, arithmetic and copies ran while one was open for 4% of the time, Pallas kernels for 0%

commit v1 on v0

--- a/solution.py
+++ b/solution.py
@@ -2,6 +2,9 @@
 import jax.numpy as jnp
 from jax import lax
 from jax.sharding import PartitionSpec as P
+
+N_CORE = 2
+N_Z = 8
 
 
 def contract_last(left_side, right_side):
@@ -29,30 +32,71 @@
     return (gate_grad, up_grad, hidden)
 
 
-def local(tokens, out_grad, gate_pre, up_pre, w_gate, w_up, w_down):
-    token_rows, grad_rows = (
-        lax.all_gather(tokens, "col", axis=0, tiled=True),
-        lax.all_gather(out_grad, "col", axis=0, tiled=True),
+def exchange(pieces, axis, groups):
+    return lax.all_to_all(pieces, axis, 0, 0, tiled=True, axis_index_groups=groups)
+
+
+def spread(block, size, axis, groups):
+    return exchange(jnp.broadcast_to(block[None], (size,) + block.shape), axis, groups)
+
+
+def local(n_row, n_col, tokens, out_grad, gate_pre, up_pre, w_gate, w_up, w_down):
+    n_y, n_x = n_row // N_CORE, n_col // N_Z
+    z_groups = [[x * N_Z + z for z in range(N_Z)] for x in range(n_x)]
+    x_groups = [[x * N_Z + z for x in range(n_x)] for z in range(N_Z)]
+    y_groups = [[y * N_CORE + c for y in range(n_y)] for c in range(N_CORE)]
+    core_swap = [(r, r ^ 1) for r in range(n_row)]
+    core = lax.rem(lax.axis_index("row"), N_CORE)
+    x_here = lax.div(lax.axis_index("col"), N_Z)
+    units = gate_pre.shape[1]
+    features = tokens.shape[1]
+    rows = gate_pre.shape[0]
+
+    saved = lax.all_gather(
+        jnp.concatenate([gate_pre, up_pre], axis=1), "row", axis=0, tiled=True
     )
-    total_rows = grad_rows.shape[0]
-    hidden_grad = lax.psum_scatter(
-        contract_last(grad_rows, w_down).astype(jnp.bfloat16),
-        "row",
-        scatter_dimension=0,
-        tiled=True,
-    ).astype(jnp.float32)
-    gate_share, up_share, hidden_share = swiglu_grads(hidden_grad, gate_pre, up_pre)
-    gate_grad, up_grad, hidden = (
-        lax.all_gather(gate_share, "row", axis=0, tiled=True),
-        lax.all_gather(up_share, "row", axis=0, tiled=True),
-        lax.all_gather(hidden_share, "row", axis=0, tiled=True),
+    total_rows = saved.shape[0]
+    grad_z = spread(out_grad, N_Z, "col", z_groups)
+    grad_rows = spread(
+        grad_z.reshape(-1, features), n_x, "col", x_groups
+    ).reshape(total_rows, features)
+
+    part = contract_last(grad_rows, w_down).astype(jnp.bfloat16)
+    part = part.reshape(n_y, N_CORE, rows, units)
+    keep = lax.dynamic_index_in_dim(part, core, 1, keepdims=False)
+    give = lax.dynamic_index_in_dim(part, 1 - core, 1, keepdims=False)
+    got = lax.ppermute(give, "row", core_swap)
+    pair = (keep.astype(jnp.float32) + got.astype(jnp.float32)).astype(jnp.bfloat16)
+    terms = exchange(pair, "row", y_groups)
+    share = jnp.sum(terms.astype(jnp.float32), axis=0).astype(jnp.bfloat16)
+
+    own = spread(share, n_y, "row", y_groups)
+    tokens, saved = lax.optimization_barrier((tokens, saved))
+    token_rows = lax.all_gather(tokens, "col", axis=0, tiled=True)
+    other = lax.ppermute(own, "row", core_swap)
+    hidden_grad = jnp.where(
+        core == 0, jnp.stack([own, other], axis=1), jnp.stack([other, own], axis=1)
+    ).reshape(total_rows, units)
+    gate_grad, up_grad, hidden = swiglu_grads(
+        hidden_grad.astype(jnp.float32), saved[:, :units], saved[:, units:]
     )
-    token_grad = lax.psum_scatter(
-        (contract_last(gate_grad, w_gate) + contract_last(up_grad, w_up)).astype(jnp.bfloat16),
-        "col",
-        scatter_dimension=0,
-        tiled=True,
+    part_in = (contract_last(gate_grad, w_gate) + contract_last(up_grad, w_up)).astype(
+        jnp.bfloat16
     )
+    part_in = part_in.reshape(n_x, -1, features)
+    total = lax.dynamic_index_in_dim(part_in, x_here, 0, keepdims=False).astype(jnp.float32)
+    for step in range(1, n_x):
+        moves = [
+            (x * N_Z + z, (x + step) % n_x * N_Z + z) for x in range(n_x) for z in range(N_Z)
+        ]
+        piece = lax.dynamic_index_in_dim(
+            part_in, lax.rem(x_here + step, n_x), 0, keepdims=False
+        )
+        total = total + lax.ppermute(piece, "col", moves).astype(jnp.float32)
+    total = total.astype(jnp.bfloat16).reshape(N_Z, -1, features)
+    token_terms = exchange(total, "col", z_groups)
+    token_grad = jnp.sum(token_terms.astype(jnp.float32), axis=0).astype(jnp.bfloat16)
+
     grad_scale = total_rows ** (-0.5)
     gate_wgrad = (contract_first(token_rows, gate_grad) * grad_scale).astype(jnp.bfloat16)
     up_wgrad = (contract_first(token_rows, up_grad) * grad_scale).astype(jnp.bfloat16)
@@ -61,8 +105,13 @@
 
 
 def solution(mesh):
+    n_row, n_col = mesh.shape["row"], mesh.shape["col"]
+
+    def device_program(*arrays):
+        return local(n_row, n_col, *arrays)
+
     return jax.shard_map(
-        local,
+        device_program,
         mesh=mesh,
         in_specs=(
             P("col", "row"),

time: 614 us -> 239 us (0.39)
  waiting for transfers between devices: 570 us -> 83 us
  blocking collectives: 0 us -> 88.1 us
  starting transfers between devices: 0.27 us -> 22.2 us
  matrix products: 24.6 us -> 15.8 us
    reduce_scatter x2 -> x0, waiting for transfers between devices: 284 us -> none  [the longest x1 225 us: local(): lax.psum_scatter((contract_last(gate_grad, w_gate) + contract_last(up_gra...]
    all_gather x5 -> x2, waiting for transfers between devices: 284 us -> 10.4 us  [the longest x1 10.4 us: local(): token_rows = lax.all_gather(tokens, 'col', axis=0, tiled=True)]
    all_to_all x0 -> x3, blocking collectives: none -> 88.1 us  [exchange(): lax.all_to_all(pieces, axis, 0, 0, tiled=True, axis_index_groups=groups)]
    all_to_all x0 -> x2, waiting for transfers between devices: none -> 42.2 us  [exchange(): lax.all_to_all(pieces, axis, 0, 0, tiled=True, axis_index_groups=groups)]
    ppermute x0 -> x5, waiting for transfers between devices: none -> 30.4 us  [the longest x3 25.6 us: local(): total = total + lax.ppermute(piece, 'col', moves).astype(jnp.float32)]
    ppermute x0 -> x5, starting transfers between devices: none -> 13.7 us  [the longest x3 9.84 us: local(): total = total + lax.ppermute(piece, 'col', moves).astype(jnp.float32)]
    dot_general x3, matrix products: 15.1 us -> 4.35 us  [contract_last(): lax.dot_general(left_side, right_side, (((1,), (1,)), ((), ())), preferre...]
    all_to_all x0 -> x2, starting transfers between devices: none -> 8.44 us  [exchange(): lax.all_to_all(pieces, axis, 0, 0, tiled=True, axis_index_groups=groups)]
  transfers between devices with their start and end apart: 7 -> 9, of which waited for: 7 -> 7; matrix products, arithmetic and copies ran while one was open for 4% -> 8% of each run, Pallas kernels for 0% -> 0%
where the time goes in v1:
time: 239 us; the launch traced here: 238 us
  blocking collectives  88.1 us (37%)
  waiting for transfers between devices  83 us (35%)
  starting transfers between devices  22.2 us (9%)
  matrix products  15.8 us (7%)
  between operations  14.3 us (6%)
  other arithmetic  7.74 us (3%)
  local copies, waits for them, and re-layouts  6.63 us (3%)
    all_to_all x3, blocking collectives, exchange(): lax.all_to_all(pieces, axis, 0, 0, tiled=True, axis_index_groups=groups)  88.1 us
    all_to_all x2, waiting for transfers between devices, exchange(): lax.all_to_all(pieces, axis, 0, 0, tiled=True, axis_index_groups=groups)  42.2 us
    ppermute x3, waiting for transfers between devices, local(): total = total + lax.ppermute(piece, 'col', moves).astype(jnp.float32)  25.6 us
    dot_general x3, matrix products, contract_first(): lax.dot_general(left_side, right_side, (((0,), (0,)), ((), ())), preferre...  11.5 us
    all_gather x1, waiting for transfers between devices, local(): token_rows = lax.all_gather(tokens, 'col', axis=0, tiled=True)  10.4 us
    ppermute x3, starting transfers between devices, local(): total = total + lax.ppermute(piece, 'col', moves).astype(jnp.float32)  9.84 us
    all_to_all x2, starting transfers between devices, exchange(): lax.all_to_all(pieces, axis, 0, 0, tiled=True, axis_index_groups=groups)  8.44 us
  transfers between devices with their start and end apart: 9, of which 7 were waited for; matrix products, arithmetic and copies ran while one was open for 8% of the time, Pallas kernels for 0%

profile of v1, /device:TPU:6, one launch (start us, length us, event | category | flops | bytes accessed | tf_op | source)
XLA Modules:
  0.0 237.7 jit_solution(16974930826978360705)
XLA Ops:
  7.2 0.0 copy-start
  7.2 1.0 broadcast_in_dim.8
  8.2 29.0 %all_to_all.25 = bf16[8,72,512]{2,1,0:T(8,128)(2,1)S(1)} all-to-all(bf16[8,72,512]{2,1,0:T(8,128)(2,1)S(1)} %broadcast_in_dim.8), channel_id=1, replica_groups={{0,1,2,3,4,5,6,7},{8,9,10,11,12,13,14,15},{16,17,18,19,20,21,22,23},{24..., dimensions={0} | all-to-all | bytes 1179648 | tf_op jit(solution)/shard_map/all_to_all | solution.py:36
  37.2 1.6 broadcast_in_dim.10
  38.8 4.9 %all-to-all-start.1 = ((bf16[4,576,512]{2,1,0:T(8,128)(2,1)}), bf16[4,576,512]{2,1,0:T(8,128)(2,1)S(1)}, u32[]{:S(2)}, u32[]{:S(2)}) async-start(bf16[4,576,512]{2,1,0:T(8,128)(2,1)} %broadcast_in_dim.10), calls=%async_computation.1 | async-start | bytes 4718592 | tf_op jit(solution)/shard_map/all_to_all | solution.py:36
  43.7 0.0 all-gather.3.cloned.1.call-start
  43.7 0.0 copy-done.8
  43.7 0.7 pad_maximum_fusion
  44.4 0.0 all-gather.3.cloned.1.call-update
  44.4 0.0 all-gather.5.cloned.1.call-start
  44.5 24.5 %all-to-all-done.1 = bf16[4,576,512]{2,1,0:T(8,128)(2,1)S(1)} async-done(((bf16[4,576,512]{2,1,0:T(8,128)(2,1)}), bf16[4,576,512]{2,1,0:T(8,128)(2,1)S(1)}, u32[]{:S(2)}, u32[]{:S(2)}) %all-to-all-start.1) | async-done | bytes 2359328 | tf_op jit(solution)/shard_map/all_to_all | solution.py:36
  69.0 1.4 convolution_convert_fusion
  70.4 1.2 copy-done.6
  71.7 0.1 dynamic-slice_bitcast_fusion
  71.8 1.9 collective-permute-start
  73.7 2.5 %collective-permute-done = bf16[8,144,384]{2,1,0:T(8,128)(2,1)S(1)} collective-permute-done((bf16[8,144,384]{2,1,0:T(8,128)(2,1)S(1)}, bf16[8,144,384]{2,1,0:T(8,128)(2,1)S(1)}, u32[]{:S(2)}, u32[]{:S(2)}) %collective-permute-start) | collective-permute-done | bytes 884768 | tf_op jit(solution)/shard_map/ppermute | solution.py:68
  76.2 1.4 fusion.12
  77.6 32.3 %all_to_all.26 = bf16[8,144,384]{2,1,0:T(8,128)(2,1)S(1)} all-to-all(bf16[8,144,384]{2,1,0:T(8,128)(2,1)S(1)} %fusion.12), channel_id=1, replica_groups={{0,64,128,192,256,320,384,448},{32,96,160,224,288,352,416,480},{1,65,12..., dimensions={0} | all-to-all | bytes 1769472 | tf_op jit(solution)/shard_map/all_to_all | solution.py:36
  109.9 0.1 reduce_sum.24
  110.0 0.1 broadcast_in_dim.22
  110.1 26.8 %all_to_all.27 = bf16[8,144,384]{2,1,0:T(8,128)(2,1)S(1)} all-to-all(bf16[8,144,384]{2,1,0:T(8,128)(2,1)S(1)} %broadcast_in_dim.22), channel_id=1, replica_groups={{0,64,128,192,256,320,384,448},{32,96,160,224,288,352,416,480},{1,65,12..., dimensions={0} | all-to-all | bytes 1769472 | tf_op jit(solution)/shard_map/all_to_all | solution.py:36
  136.9 1.9 collective-permute-start.1
  138.8 0.0 all-gather.3.cloned.1.call-done
  138.8 0.0 all-gather.5.cloned.1.call-update
  138.9 2.3 collective-permute-done.1
  141.2 0.2 maximum_select_fusion
  141.4 2.0 fusion.5
  143.5 0.0 copy-start.7
  143.5 1.4 fusion.26
  144.9 0.0 copy-done.1
  144.9 0.0 copy-done.7
  144.9 1.5 fusion
  146.4 1.5 copy-done.2
  147.9 1.1 dynamic-slice_bitcast_fusion.3
  149.1 4.0 %collective-permute-start.2 = (bf16[576,512]{1,0:T(8,128)(2,1)}, bf16[576,512]{1,0:T(8,128)(2,1)S(1)}, u32[]{:S(2)}, u32[]{:S(2)}) collective-permute-start(bf16[576,512]{1,0:T(8,128)(2,1)} %get-tuple-element.10), channel_id=1, source_target_pairs={{0,8},{1,9},{2,10},{3,11},{4,12},{5,13},{6,14},{7,15},{8,16},{9,17... | collective-permute-start | bytes 1769480 | tf_op jit(solution)/shard_map/ppermute | solution.py:95
  153.1 1.9 collective-permute-start.4
  155.0 3.9 %collective-permute-start.3 = (bf16[576,512]{1,0:T(8,128)(2,1)S(1)}, bf16[576,512]{1,0:T(8,128)(2,1)}, u32[]{:S(2)}, u32[]{:S(2)}) collective-permute-start(bf16[576,512]{1,0:T(8,128)(2,1)S(1)} %get-tuple-element.12), channel_id=1, source_target_pairs={{0,16},{1,17},{2,18},{3,19},{4,20},{5,21},{6,22},{7,23},{8,24},{9,... | collective-permute-start | bytes 1769480 | tf_op jit(solution)/shard_map/ppermute | solution.py:95
  158.9 20.5 %collective-permute-done.2 = bf16[576,512]{1,0:T(8,128)(2,1)S(1)} collective-permute-done((bf16[576,512]{1,0:T(8,128)(2,1)}, bf16[576,512]{1,0:T(8,128)(2,1)S(1)}, u32[]{:S(2)}, u32[]{:S(2)}) %collective-permute-start.2) | collective-permute-done | bytes 589856 | tf_op jit(solution)/shard_map/ppermute | solution.py:95
  179.4 5.1 %collective-permute-done.4 = bf16[576,512]{1,0:T(8,128)(2,1)} collective-permute-done((bf16[576,512]{1,0:T(8,128)(2,1)}, bf16[576,512]{1,0:T(8,128)(2,1)}, u32[]{:S(2)}, u32[]{:S(2)}) %collective-permute-start.4) | collective-permute-done | bytes 589856 | tf_op jit(solution)/shard_map/ppermute | solution.py:95
  184.5 0.0 collective-permute-done.3
  184.5 2.5 %fusion.24 = bf16[576,512]{1,0:T(8,128)(2,1)} fusion(bf16[576,512]{1,0:T(8,128)(2,1)} %collective-permute-done.4, bf16[576,512]{1,0:T(8,128)(2,1)} %collective-permute-done.3, bf16[576,512]{1,0:T(8,128)(2,1)S(1)} %collective-permute-done.2, bf16[4,576,512]{2,1,0:T(8,128)(2,1)} %bitcast.37, s32[]{:T(128)S(6)} %select_n.34), kind=kLoop, calls=%fused_computation.32 | loop fusion | flops 2359296 | bytes 2949124 | tf_op jit(solution)/shard_map/convert_element_type | solution.py:96
  187.1 3.5 %all-to-all-start.4 = ((bf16[8,72,512]{2,1,0:T(8,128)(2,1)}), bf16[8,72,512]{2,1,0:T(8,128)(2,1)S(1)}, u32[]{:S(2)}, u32[]{:S(2)}) async-start(bf16[8,72,512]{2,1,0:T(8,128)(2,1)} %bitcast.14), calls=%async_computation.4 | async-start | bytes 1179648 | tf_op jit(solution)/shard_map/all_to_all | solution.py:36
  190.6 4.8 %fusion.19 = bf16[384,512]{1,0:T(8,128)(2,1)} fusion(bf16[2304,512]{1,0:T(8,128)(2,1)} %bitcast.40, bf16[2304,768]{1,0:T(8,128)(2,1)} %all-gather.3.cloned.1.call-done), kind=kOutput, calls=%fused_computation.28 | convolution fusion | flops 913440768 | bytes 6291456 | tf_op jit(solution)/shard_map/dot_general | solution.py:17
  195.5 17.6 %all-to-all-done.4 = bf16[8,72,512]{2,1,0:T(8,128)(2,1)S(1)} async-done(((bf16[8,72,512]{2,1,0:T(8,128)(2,1)}), bf16[8,72,512]{2,1,0:T(8,128)(2,1)S(1)}, u32[]{:S(2)}, u32[]{:S(2)}) %all-to-all-start.4) | async-done | bytes 589856 | tf_op jit(solution)/shard_map/all_to_all | solution.py:36
  213.1 0.7 reduce_sum.25
  213.8 10.4 %all-gather.5.cloned.1.call-done = bf16[2304,512]{1,0:T(8,128)(2,1)} async-done(((bf16[72,512]{1,0:T(8,128)(2,1)}), bf16[2304,512]{1,0:T(8,128)(2,1)}) %all-gather.5.cloned.1.call-update) | async-done | bytes 2359312 | tf_op jit(solution)/shard_map/all_gather | solution.py:75
  224.2 4.5 %fusion.18 = bf16[512,384]{1,0:T(8,128)(2,1)} fusion(bf16[2304,512]{1,0:T(8,128)(2,1)} %all-gather.5.cloned.1.call-done, bf16[2304,384]{1,0:T(8,128)(2,1)} %copy-done.1), kind=kOutput, calls=%fused_computation.27 | convolution fusion | flops 906362880 | bytes 4521984 | tf_op jit(solution)/shard_map/dot_general | solution.py:17
  228.7 2.2 fusion.17
  (15 shorter events, 0.0 us)
Async XLA Ops:
  7.2 136.3 %copy-start = (bf16[512,384]{1,0:T(8,128)(2,1)S(1)}, bf16[512,384]{1,0:T(8,128)(2,1)}, u32[]{:S(2)}) copy-start(bf16[512,384]{1,0:T(8,128)(2,1)} %param.11) | copy-start | bytes 1179652
  38.8 4.9 %copy-start.8 = (bf16[144,384]{1,0:T(8,128)(2,1)S(1)}, bf16[144,384]{1,0:T(8,128)(2,1)}, u32[]{:S(2)}) copy-start(bf16[144,384]{1,0:T(8,128)(2,1)} %param.10) | copy-start | bytes 331780
  38.8 4.9 %copy-start.9 = (bf16[144,384]{1,0:T(8,128)(2,1)S(1)}, bf16[144,384]{1,0:T(8,128)(2,1)}, u32[]{:S(2)}) copy-start(bf16[144,384]{1,0:T(8,128)(2,1)} %param.9) | copy-start | bytes 331780
  38.8 30.2 %copy-start.10 = (bf16[384,512]{1,0:T(8,128)(2,1)S(1)}, bf16[384,512]{1,0:T(8,128)(2,1)}, u32[]{:S(2)}) copy-start(bf16[384,512]{1,0:T(8,128)(2,1)} %param.13) | copy-start | bytes 1179652
  38.8 30.2 %all-to-all-start.1 = ((bf16[4,576,512]{2,1,0:T(8,128)(2,1)}), bf16[4,576,512]{2,1,0:T(8,128)(2,1)S(1)}, u32[]{:S(2)}, u32[]{:S(2)}) async-start(bf16[4,576,512]{2,1,0:T(8,128)(2,1)} %broadcast_in_dim.10), calls=%async_computation.1 | async-start | bytes 4718592 | tf_op jit(solution)/shard_map/all_to_all | solution.py:36
  43.7 95.1 %all-gather.3.cloned.1.call-start = ((), (), s32[]{:S(2)}) async-start(), calls=%async_computation.5 | async-start | bytes 3760128 | tf_op jit(solution)/shard_map/all_gather | solution.py:55
  44.4 179.8 %all-gather.5.cloned.1.call-start = ((), (), s32[]{:S(2)}) async-start(), calls=%async_computation.6 | async-start | bytes 2433024 | tf_op jit(solution)/shard_map/all_gather | solution.py:75
  69.0 1.4 copy-start.5
  70.4 1.3 copy-start.6
  71.8 4.4 %collective-permute-start = (bf16[8,144,384]{2,1,0:T(8,128)(2,1)S(1)}, bf16[8,144,384]{2,1,0:T(8,128)(2,1)S(1)}, u32[]{:S(2)}, u32[]{:S(2)}) collective-permute-start(bf16[8,144,384]{2,1,0:T(8,128)(2,1)S(1)} %dynamic-slice_bitcast_fusion), channel_id=1, source_target_pairs={{0,32},{32,0},{64,96},{96,64},{128,160},{160,128},{192,224},{224,1... | collective-permute-start | bytes 2654216 | tf_op jit(solution)/shard_map/ppermute | solution.py:68
  136.9 4.3 %collective-permute-start.1 = (bf16[8,144,384]{2,1,0:T(8,128)(2,1)S(1)}, bf16[8,144,384]{2,1,0:T(8,128)(2,1)S(1)}, u32[]{:S(2)}, u32[]{:S(2)}) collective-permute-start(bf16[8,144,384]{2,1,0:T(8,128)(2,1)S(1)} %all_to_all.27), channel_id=1, source_target_pairs={{0,32},{32,0},{64,96},{96,64},{128,160},{160,128},{192,224},{224,1... | collective-permute-start | bytes 2654216 | tf_op jit(solution)/shard_map/ppermute | solution.py:76
  138.9 2.5 %copy-start.4 = (bf16[2304,768]{1,0:T(8,128)(2,1)S(1)}, bf16[2304,768]{1,0:T(8,128)(2,1)}, u32[]{:S(2)}) copy-start(bf16[2304,768]{1,0:T(8,128)(2,1)} %all-gather.3.cloned.1.call-done) | copy-start | bytes 10616836
  143.4 1.5 copy-start.1
  143.5 1.5 copy-start.7
  146.4 1.5 copy-start.2
  149.1 30.4 %collective-permute-start.2 = (bf16[576,512]{1,0:T(8,128)(2,1)}, bf16[576,512]{1,0:T(8,128)(2,1)S(1)}, u32[]{:S(2)}, u32[]{:S(2)}) collective-permute-start(bf16[576,512]{1,0:T(8,128)(2,1)} %get-tuple-element.10), channel_id=1, source_target_pairs={{0,8},{1,9},{2,10},{3,11},{4,12},{5,13},{6,14},{7,15},{8,16},{9,17... | collective-permute-start | bytes 1769480 | tf_op jit(solution)/shard_map/ppermute | solution.py:95
  153.1 31.5 %collective-permute-start.4 = (bf16[576,512]{1,0:T(8,128)(2,1)}, bf16[576,512]{1,0:T(8,128)(2,1)}, u32[]{:S(2)}, u32[]{:S(2)}) collective-permute-start(bf16[576,512]{1,0:T(8,128)(2,1)} %get-tuple-element.11), channel_id=1, source_target_pairs={{0,24},{1,25},{2,26},{3,27},{4,28},{5,29},{6,30},{7,31},{8,0},{9,1... | collective-permute-start | bytes 1769480 | tf_op jit(solution)/shard_map/ppermute | solution.py:95
  155.0 29.6 %collective-permute-start.3 = (bf16[576,512]{1,0:T(8,128)(2,1)S(1)}, bf16[576,512]{1,0:T(8,128)(2,1)}, u32[]{:S(2)}, u32[]{:S(2)}) collective-permute-start(bf16[576,512]{1,0:T(8,128)(2,1)S(1)} %get-tuple-element.12), channel_id=1, source_target_pairs={{0,16},{1,17},{2,18},{3,19},{4,20},{5,21},{6,22},{7,23},{8,24},{9,... | collective-permute-start | bytes 1769480 | tf_op jit(solution)/shard_map/ppermute | solution.py:95
  187.1 26.0 %all-to-all-start.4 = ((bf16[8,72,512]{2,1,0:T(8,128)(2,1)}), bf16[8,72,512]{2,1,0:T(8,128)(2,1)S(1)}, u32[]{:S(2)}, u32[]{:S(2)}) async-start(bf16[8,72,512]{2,1,0:T(8,128)(2,1)} %bitcast.14), calls=%async_computation.4 | async-start | bytes 1179648 | tf_op jit(solution)/shard_map/all_to_all | solution.py:36
  224.2 4.5 %copy-start.3 = (bf16[2304,512]{1,0:T(8,128)(2,1)S(1)}, bf16[2304,512]{1,0:T(8,128)(2,1)}, u32[]{:S(2)}) copy-start(bf16[2304,512]{1,0:T(8,128)(2,1)} %all-gather.5.cloned.1.call-done) | copy-start | bytes 7077892
Sparse Core Ops, SparseCore 0:
  47.2 40.1 all-gather.2
  139.0 85.1 all-gather.4

commit v2 on v1

--- a/solution.py
+++ b/solution.py
@@ -71,7 +71,6 @@
     share = jnp.sum(terms.astype(jnp.float32), axis=0).astype(jnp.bfloat16)
 
     own = spread(share, n_y, "row", y_groups)
-    tokens, saved = lax.optimization_barrier((tokens, saved))
     token_rows = lax.all_gather(tokens, "col", axis=0, tiled=True)
     other = lax.ppermute(own, "row", core_swap)
     hidden_grad = jnp.where(

time: 239 us -> 237 us (level)
  waiting for transfers between devices: 83 us -> 77.2 us
  other arithmetic: 7.74 us -> 10.7 us
    all_to_all x2, waiting for transfers between devices: 42.2 us -> 24.5 us  [exchange(): lax.all_to_all(pieces, axis, 0, 0, tiled=True, axis_index_groups=groups)]
    all_gather x1, waiting for transfers between devices: 10.4 us -> 22.2 us  [local(): token_rows = lax.all_gather(tokens, 'col', axis=0, tiled=True)]
  transfers between devices with their start and end apart: 9 -> 9, of which waited for: 7 -> 6; matrix products, arithmetic and copies ran while one was open for 8% -> 12% of each run, Pallas kernels for 0% -> 0%
where the time goes in v2:
time: 237 us; the launch traced here: 236 us
  blocking collectives  87.9 us (37%)
  waiting for transfers between devices  77.2 us (33%)
  starting transfers between devices  22.2 us (9%)
  matrix products  15.1 us (6%)
  between operations  14.3 us (6%)
  other arithmetic  10.7 us (5%)
  local copies, waits for them, and re-layouts  8.42 us (4%)
    all_to_all x3, blocking collectives, exchange(): lax.all_to_all(pieces, axis, 0, 0, tiled=True, axis_index_groups=groups)  87.9 us
    ppermute x3, waiting for transfers between devices, local(): total = total + lax.ppermute(piece, 'col', moves).astype(jnp.float32)  25.5 us
    all_to_all x2, waiting for transfers between devices, exchange(): lax.all_to_all(pieces, axis, 0, 0, tiled=True, axis_index_groups=groups)  24.5 us
    all_gather x1, waiting for transfers between devices, local(): token_rows = lax.all_gather(tokens, 'col', axis=0, tiled=True)  22.2 us
    dot_general x3, matrix products, contract_first(): lax.dot_general(left_side, right_side, (((0,), (0,)), ((), ())), preferre...  10.8 us
    ppermute x3, starting transfers between devices, local(): total = total + lax.ppermute(piece, 'col', moves).astype(jnp.float32)  9.84 us
    all_to_all x2, starting transfers between devices, exchange(): lax.all_to_all(pieces, axis, 0, 0, tiled=True, axis_index_groups=groups)  8.44 us
  transfers between devices with their start and end apart: 9, of which 6 were waited for; matrix products, arithmetic and copies ran while one was open for 12% of the time, Pallas kernels for 0%

profile of v2, /device:TPU:6, one launch (start us, length us, event | category | flops | bytes accessed | tf_op | source)
XLA Modules:
  0.0 235.7 jit_solution(15735262077055678324)
XLA Ops:
  7.2 0.0 copy-start
  7.2 1.0 broadcast_in_dim.8
  8.2 29.0 %all_to_all.25 = bf16[8,72,512]{2,1,0:T(8,128)(2,1)S(1)} all-to-all(bf16[8,72,512]{2,1,0:T(8,128)(2,1)S(1)} %broadcast_in_dim.8), channel_id=1, replica_groups={{0,1,2,3,4,5,6,7},{8,9,10,11,12,13,14,15},{16,17,18,19,20,21,22,23},{24..., dimensions={0} | all-to-all | bytes 1179648 | tf_op jit(solution)/shard_map/all_to_all | solution.py:36
  37.2 1.6 broadcast_in_dim.10
  38.8 4.9 %all-to-all-start.1 = ((bf16[4,576,512]{2,1,0:T(8,128)(2,1)}), bf16[4,576,512]{2,1,0:T(8,128)(2,1)S(1)}, u32[]{:S(2)}, u32[]{:S(2)}) async-start(bf16[4,576,512]{2,1,0:T(8,128)(2,1)} %broadcast_in_dim.10), calls=%async_computation.1 | async-start | bytes 4718592 | tf_op jit(solution)/shard_map/all_to_all | solution.py:36
  43.7 0.7 pad_maximum_fusion
  44.4 0.0 all-gather.3.cloned.1.call-update
  44.4 0.0 all-gather.5.cloned.1.call-start
  44.5 24.5 %all-to-all-done.1 = bf16[4,576,512]{2,1,0:T(8,128)(2,1)S(1)} async-done(((bf16[4,576,512]{2,1,0:T(8,128)(2,1)}), bf16[4,576,512]{2,1,0:T(8,128)(2,1)S(1)}, u32[]{:S(2)}, u32[]{:S(2)}) %all-to-all-start.1) | async-done | bytes 2359328 | tf_op jit(solution)/shard_map/all_to_all | solution.py:36
  69.0 1.4 convolution_convert_fusion
  70.4 1.2 copy-done.4
  71.6 0.1 dynamic-slice_bitcast_fusion
  71.7 1.9 collective-permute-start
  73.7 2.6 %collective-permute-done = bf16[8,144,384]{2,1,0:T(8,128)(2,1)S(1)} collective-permute-done((bf16[8,144,384]{2,1,0:T(8,128)(2,1)S(1)}, bf16[8,144,384]{2,1,0:T(8,128)(2,1)S(1)}, u32[]{:S(2)}, u32[]{:S(2)}) %collective-permute-start) | collective-permute-done | bytes 884768 | tf_op jit(solution)/shard_map/ppermute | solution.py:68
  76.3 1.4 fusion.12
  77.7 32.2 %all_to_all.26 = bf16[8,144,384]{2,1,0:T(8,128)(2,1)S(1)} all-to-all(bf16[8,144,384]{2,1,0:T(8,128)(2,1)S(1)} %fusion.12), channel_id=1, replica_groups={{0,64,128,192,256,320,384,448},{32,96,160,224,288,352,416,480},{1,65,12..., dimensions={0} | all-to-all | bytes 1769472 | tf_op jit(solution)/shard_map/all_to_all | solution.py:36
  109.9 0.1 reduce_sum.24
  110.0 0.1 broadcast_in_dim.22
  110.1 26.8 %all_to_all.27 = bf16[8,144,384]{2,1,0:T(8,128)(2,1)S(1)} all-to-all(bf16[8,144,384]{2,1,0:T(8,128)(2,1)S(1)} %broadcast_in_dim.22), channel_id=1, replica_groups={{0,64,128,192,256,320,384,448},{32,96,160,224,288,352,416,480},{1,65,12..., dimensions={0} | all-to-all | bytes 1769472 | tf_op jit(solution)/shard_map/all_to_all | solution.py:36
  136.8 1.9 collective-permute-start.1
  138.7 0.0 all-gather.5.cloned.1.call-update
  138.8 2.3 collective-permute-done.1
  141.1 1.5 maximum_select_fusion
  142.6 3.7 %fusion.5 = (bf16[2304,384]{1,0:T(8,128)(2,1)S(1)}, bf16[2304,384]{1,0:T(8,128)(2,1)S(1)}) fusion(bf16[8,2,144,384]{3,2,1,0:T(8,128)(2,1)} %maximum_select_fusion, bf16[2304,768]{1,0:T(8,128)(2,1)} %all-gather.3.cloned.1.call-done), kind=kLoop, calls=%fused_computation.13 | loop fusion | flops 14155776 | bytes 8847360 | tf_op jit(solution)/shard_map/convert_element_type | solution.py:30
  146.3 0.0 copy-start.2
  146.3 0.0 copy-done
  146.3 0.0 copy-start.5
  146.3 1.4 fusion.28
  147.8 0.0 copy-done.2
  147.8 1.5 fusion
  149.3 1.5 copy-done.1
  150.8 1.2 dynamic-slice_bitcast_fusion.3
  151.9 4.0 %collective-permute-start.2 = (bf16[576,512]{1,0:T(8,128)(2,1)}, bf16[576,512]{1,0:T(8,128)(2,1)S(1)}, u32[]{:S(2)}, u32[]{:S(2)}) collective-permute-start(bf16[576,512]{1,0:T(8,128)(2,1)} %get-tuple-element.10), channel_id=1, source_target_pairs={{0,8},{1,9},{2,10},{3,11},{4,12},{5,13},{6,14},{7,15},{8,16},{9,17... | collective-permute-start | bytes 1769480 | tf_op jit(solution)/shard_map/ppermute | solution.py:94
  156.0 1.9 collective-permute-start.4
  157.9 3.9 %collective-permute-start.3 = (bf16[576,512]{1,0:T(8,128)(2,1)S(1)}, bf16[576,512]{1,0:T(8,128)(2,1)}, u32[]{:S(2)}, u32[]{:S(2)}) collective-permute-start(bf16[576,512]{1,0:T(8,128)(2,1)S(1)} %get-tuple-element.12), channel_id=1, source_target_pairs={{0,16},{1,17},{2,18},{3,19},{4,20},{5,21},{6,22},{7,23},{8,24},{9,... | collective-permute-start | bytes 1769480 | tf_op jit(solution)/shard_map/ppermute | solution.py:94
  161.8 20.4 %collective-permute-done.2 = bf16[576,512]{1,0:T(8,128)(2,1)S(1)} collective-permute-done((bf16[576,512]{1,0:T(8,128)(2,1)}, bf16[576,512]{1,0:T(8,128)(2,1)S(1)}, u32[]{:S(2)}, u32[]{:S(2)}) %collective-permute-start.2) | collective-permute-done | bytes 589856 | tf_op jit(solution)/shard_map/ppermute | solution.py:94
  182.2 5.1 %collective-permute-done.4 = bf16[576,512]{1,0:T(8,128)(2,1)} collective-permute-done((bf16[576,512]{1,0:T(8,128)(2,1)}, bf16[576,512]{1,0:T(8,128)(2,1)}, u32[]{:S(2)}, u32[]{:S(2)}) %collective-permute-start.4) | collective-permute-done | bytes 589856 | tf_op jit(solution)/shard_map/ppermute | solution.py:94
  187.3 0.0 collective-permute-done.3
  187.3 2.6 %fusion.26 = bf16[576,512]{1,0:T(8,128)(2,1)} fusion(bf16[576,512]{1,0:T(8,128)(2,1)} %collective-permute-done.4, bf16[576,512]{1,0:T(8,128)(2,1)} %collective-permute-done.3, bf16[576,512]{1,0:T(8,128)(2,1)S(1)} %collective-permute-done.2, bf16[4,576,512]{2,1,0:T(8,128)(2,1)} %bitcast.41, s32[]{:T(128)S(6)} %select_n.34), kind=kLoop, calls=%fused_computation.34 | loop fusion | flops 2359296 | bytes 2949124 | tf_op jit(solution)/shard_map/convert_element_type | solution.py:95
  189.8 3.5 %all-to-all-start.4 = ((bf16[8,72,512]{2,1,0:T(8,128)(2,1)}), bf16[8,72,512]{2,1,0:T(8,128)(2,1)S(1)}, u32[]{:S(2)}, u32[]{:S(2)}) async-start(bf16[8,72,512]{2,1,0:T(8,128)(2,1)} %bitcast.14), calls=%async_computation.4 | async-start | bytes 1179648 | tf_op jit(solution)/shard_map/all_to_all | solution.py:36
  193.4 4.7 %fusion.19 = bf16[384,512]{1,0:T(8,128)(2,1)} fusion(bf16[2304,512]{1,0:T(8,128)(2,1)} %bitcast.44, bf16[2304,768]{1,0:T(8,128)(2,1)} %all-gather.3.cloned.1.call-done), kind=kOutput, calls=%fused_computation.28 | convolution fusion | flops 913440768 | bytes 6291456 | tf_op jit(solution)/shard_map/dot_general | solution.py:17
  198.1 22.2 %all-gather.5.cloned.1.call-done = bf16[2304,512]{1,0:T(8,128)(2,1)} async-done(((bf16[72,512]{1,0:T(8,128)(2,1)}), bf16[2304,512]{1,0:T(8,128)(2,1)}) %all-gather.5.cloned.1.call-update) | async-done | bytes 2359312 | tf_op jit(solution)/shard_map/all_gather | solution.py:74
  220.3 2.8 %fusion.23 = bf16[512,384]{0,1:T(8,128)(2,1)S(1)} fusion(bf16[2304,384]{1,0:T(8,128)(2,1)S(1)} %get-tuple-element.9, bf16[2304,512]{1,0:T(8,128)(2,1)} %all-gather.5.cloned.1.call-done), kind=kOutput, calls=%fused_computation.30 | convolution fusion | flops 906362880 | bytes 4521984 | tf_op jit(solution)/shard_map/dot_general | solution.py:17
  223.0 0.9 copy.11
  224.0 3.3 %fusion.22 = bf16[512,384]{0,1:T(8,128)(2,1)S(1)} fusion(bf16[2304,384]{1,0:T(8,128)(2,1)} %copy-done.2, bf16[2304,512]{1,0:T(8,128)(2,1)} %all-gather.5.cloned.1.call-done), kind=kOutput, calls=%fused_computation.29 | convolution fusion | flops 906362880 | bytes 4521984 | tf_op jit(solution)/shard_map/dot_general | solution.py:17
  227.3 0.9 copy.12
  228.2 0.0 all-to-all-done.4
  228.2 0.7 reduce_sum.25
  (13 shorter events, 0.0 us)
Async XLA Ops:
  7.2 139.1 %copy-start = (bf16[512,384]{1,0:T(8,128)(2,1)S(1)}, bf16[512,384]{1,0:T(8,128)(2,1)}, u32[]{:S(2)}) copy-start(bf16[512,384]{1,0:T(8,128)(2,1)} %param.11) | copy-start | bytes 1179652
  38.8 4.9 %copy-start.6 = (bf16[144,384]{1,0:T(8,128)(2,1)S(1)}, bf16[144,384]{1,0:T(8,128)(2,1)}, u32[]{:S(2)}) copy-start(bf16[144,384]{1,0:T(8,128)(2,1)} %param.10) | copy-start | bytes 331780
  38.8 4.9 %copy-start.7 = (bf16[144,384]{1,0:T(8,128)(2,1)S(1)}, bf16[144,384]{1,0:T(8,128)(2,1)}, u32[]{:S(2)}) copy-start(bf16[144,384]{1,0:T(8,128)(2,1)} %param.9) | copy-start | bytes 331780
  38.8 30.2 %copy-start.8 = (bf16[384,512]{1,0:T(8,128)(2,1)S(1)}, bf16[384,512]{1,0:T(8,128)(2,1)}, u32[]{:S(2)}) copy-start(bf16[384,512]{1,0:T(8,128)(2,1)} %param.13) | copy-start | bytes 1179652
  38.8 30.2 %all-to-all-start.1 = ((bf16[4,576,512]{2,1,0:T(8,128)(2,1)}), bf16[4,576,512]{2,1,0:T(8,128)(2,1)S(1)}, u32[]{:S(2)}, u32[]{:S(2)}) async-start(bf16[4,576,512]{2,1,0:T(8,128)(2,1)} %broadcast_in_dim.10), calls=%async_computation.1 | async-start | bytes 4718592 | tf_op jit(solution)/shard_map/all_to_all | solution.py:36
  43.7 99.0 %all-gather.3.cloned.1.call-start = ((), (), s32[]{:S(2)}) async-start(), calls=%async_computation.5 | async-start | bytes 3760128 | tf_op jit(solution)/shard_map/all_gather | solution.py:55
  44.4 175.9 %all-gather.5.cloned.1.call-start = ((), (), s32[]{:S(2)}) async-start(), calls=%async_computation.6 | async-start | bytes 2433024 | tf_op jit(solution)/shard_map/all_gather | solution.py:74
  69.0 1.4 copy-start.3
  70.4 1.2 copy-start.4
  71.7 4.6 %collective-permute-start = (bf16[8,144,384]{2,1,0:T(8,128)(2,1)S(1)}, bf16[8,144,384]{2,1,0:T(8,128)(2,1)S(1)}, u32[]{:S(2)}, u32[]{:S(2)}) collective-permute-start(bf16[8,144,384]{2,1,0:T(8,128)(2,1)S(1)} %dynamic-slice_bitcast_fusion), channel_id=1, source_target_pairs={{0,32},{32,0},{64,96},{96,64},{128,160},{160,128},{192,224},{224,1... | collective-permute-start | bytes 2654216 | tf_op jit(solution)/shard_map/ppermute | solution.py:68
  136.8 4.3 %collective-permute-start.1 = (bf16[8,144,384]{2,1,0:T(8,128)(2,1)S(1)}, bf16[8,144,384]{2,1,0:T(8,128)(2,1)S(1)}, u32[]{:S(2)}, u32[]{:S(2)}) collective-permute-start(bf16[8,144,384]{2,1,0:T(8,128)(2,1)S(1)} %all_to_all.27), channel_id=1, source_target_pairs={{0,32},{32,0},{64,96},{96,64},{128,160},{160,128},{192,224},{224,1... | collective-permute-start | bytes 2654216 | tf_op jit(solution)/shard_map/ppermute | solution.py:75
  146.3 1.5 copy-start.2
  146.3 1.5 copy-start.5
  149.3 1.5 copy-start.1
  151.9 30.2 %collective-permute-start.2 = (bf16[576,512]{1,0:T(8,128)(2,1)}, bf16[576,512]{1,0:T(8,128)(2,1)S(1)}, u32[]{:S(2)}, u32[]{:S(2)}) collective-permute-start(bf16[576,512]{1,0:T(8,128)(2,1)} %get-tuple-element.10), channel_id=1, source_target_pairs={{0,8},{1,9},{2,10},{3,11},{4,12},{5,13},{6,14},{7,15},{8,16},{9,17... | collective-permute-start | bytes 1769480 | tf_op jit(solution)/shard_map/ppermute | solution.py:94
  156.0 31.3 %collective-permute-start.4 = (bf16[576,512]{1,0:T(8,128)(2,1)}, bf16[576,512]{1,0:T(8,128)(2,1)}, u32[]{:S(2)}, u32[]{:S(2)}) collective-permute-start(bf16[576,512]{1,0:T(8,128)(2,1)} %get-tuple-element.11), channel_id=1, source_target_pairs={{0,24},{1,25},{2,26},{3,27},{4,28},{5,29},{6,30},{7,31},{8,0},{9,1... | collective-permute-start | bytes 1769480 | tf_op jit(solution)/shard_map/ppermute | solution.py:94
  157.9 29.4 %collective-permute-start.3 = (bf16[576,512]{1,0:T(8,128)(2,1)S(1)}, bf16[576,512]{1,0:T(8,128)(2,1)}, u32[]{:S(2)}, u32[]{:S(2)}) collective-permute-start(bf16[576,512]{1,0:T(8,128)(2,1)S(1)} %get-tuple-element.12), channel_id=1, source_target_pairs={{0,16},{1,17},{2,18},{3,19},{4,20},{5,21},{6,22},{7,23},{8,24},{9,... | collective-permute-start | bytes 1769480 | tf_op jit(solution)/shard_map/ppermute | solution.py:94
  189.8 38.4 %all-to-all-start.4 = ((bf16[8,72,512]{2,1,0:T(8,128)(2,1)}), bf16[8,72,512]{2,1,0:T(8,128)(2,1)S(1)}, u32[]{:S(2)}, u32[]{:S(2)}) async-start(bf16[8,72,512]{2,1,0:T(8,128)(2,1)} %bitcast.14), calls=%async_computation.4 | async-start | bytes 1179648 | tf_op jit(solution)/shard_map/all_to_all | solution.py:36
Sparse Core Ops, SparseCore 0:
  47.2 40.1 all-gather.2
  138.9 81.3 all-gather.4

commit v3 on v2

v3 whole, which is shorter than its diff:
```python
import jax
import jax.numpy as jnp
from jax import lax
from jax.sharding import PartitionSpec as P

N_CORE = 2
N_Z = 8


def contract_last(left_side, right_side):
    return lax.dot_general(
        left_side, right_side, (((1,), (1,)), ((), ())), preferred_element_type=jnp.float32
    )


def contract_first(left_side, right_side):
    return lax.dot_general(
        left_side, right_side, (((0,), (0,)), ((), ())), preferred_element_type=jnp.float32
    )


def swiglu_inputs(hidden_grad, gate_pre, up_pre):
    gate_float = gate_pre.astype(jnp.float32)
    up_float = up_pre.astype(jnp.float32)
    grad_float = hidden_grad.astype(jnp.float32)
    sigmoid_gate = jax.nn.sigmoid(gate_float)
    swish_gate = gate_float * sigmoid_gate
    gate_grad = (
        grad_float * up_float * sigmoid_gate * (1.0 + gate_float * (1.0 - sigmoid_gate))
    ).astype(jnp.bfloat16)
    up_grad = (grad_float * swish_gate).astype(jnp.bfloat16)
    hidden = (swish_gate * up_float).astype(jnp.bfloat16)
    return (gate_grad, up_grad, hidden)


def exchange(pieces, axis, groups):
    return lax.all_to_all(pieces, axis, 0, 0, tiled=True, axis_index_groups=groups)


def spread(block, size, axis, groups):
    return exchange(jnp.broadcast_to(block[None], (size,) + block.shape), axis, groups)


def pick(stacked, index, axis=0):
    return lax.dynamic_index_in_dim(stacked, index, axis, keepdims=False)


def local(n_row, n_col, tokens, out_grad, gate_pre, up_pre, w_gate, w_up, w_down):
    n_y, n_x = n_row // N_CORE, n_col // N_Z
    z_groups = [[x * N_Z + z for z in range(N_Z)] for x in range(n_x)]
    x_groups = [[x * N_Z + z for x in range(n_x)] for z in range(N_Z)]
    y_groups = [[y * N_CORE + c for y in range(n_y)] for c in range(N_CORE)]
    core_swap = [(r, r ^ 1) for r in range(n_row)]
    row_here, col_here = lax.axis_index("row"), lax.axis_index("col")
    core, y_here = lax.rem(row_here, N_CORE), lax.div(row_here, N_CORE)
    x_here = lax.div(col_here, N_Z)
    rows, units = gate_pre.shape
    block, features = out_grad.shape
    half = 2 * units
    group_rows = N_Z * block

    def x_shift(step):
        return [
            (x * N_Z + z, (x + step) % n_x * N_Z + z) for x in range(n_x) for z in range(N_Z)
        ]

    def to_group(turn):
        pairs = []
        for r in range(n_row):
            for x in range(n_x):
                piece = (turn + x) % 2
                new_row = (2 * (r % n_x) + piece) * N_CORE + x // 2
                for z in range(N_Z):
                    pairs.append((r * n_col + x * N_Z + z, new_row * n_col + r // n_x * N_Z + z))
        return pairs

    def to_shard(turn):
        pairs = []
        for y in range(n_y):
            for c in range(N_CORE):
                slot = (turn + y) % 2
                for x in range(n_x):
                    for z in range(N_Z):
                        source = (y * N_CORE + c) * n_col + x * N_Z + z
                        new_row = n_x * x + y // 2
                        pairs.append((source, new_row * n_col + (2 * c + slot) * N_Z + z))
        return pairs

    down_all = lax.all_gather(
        w_down, "col", axis=0, tiled=True, axis_index_groups=x_groups
    ).reshape(N_CORE, half, features)

    saved_pieces = jnp.concatenate([gate_pre, up_pre], axis=1).reshape(2, block, half)
    moved = [
        lax.ppermute(
            pick(saved_pieces, lax.rem(x_here + turn, 2)), ("row", "col"), to_group(turn)
        )
        for turn in range(2)
    ]
    y_even = lax.rem(y_here, 2) == 0
    first = jnp.where(y_even, moved[0], moved[1])
    second = jnp.where(y_even, moved[1], moved[0])
    saved_share = jnp.concatenate(
        [first[:, :units], second[:, :units], first[:, units:], second[:, units:]], axis=1
    )
    saved = lax.all_gather(saved_share, "row", axis=0, tiled=True).reshape(
        n_y, N_CORE, block, 2 * half
    )

    both = spread(jnp.concatenate([out_grad, tokens], axis=1), N_Z, "col", z_groups).reshape(
        group_rows, 2 * features
    )
    grad_rows = both[:, :features]

    w_both = jnp.concatenate([w_gate, w_up], axis=1)
    w_stack = jnp.stack(
        [w_both] + [lax.ppermute(w_both, "col", x_shift(step)) for step in range(1, n_x)]
    )
    w_order = [
        pick(w_stack, lax.rem(x_here - 2 * core - place + 2 * n_x, n_x)) for place in range(n_x)
    ]

    def w_half(side, which):
        pieces = w_order[2 * side : 2 * side + 2]
        return jnp.concatenate(
            [piece[:, which * units : (which + 1) * units] for piece in pieces], axis=1
        )

    give = contract_last(grad_rows, pick(down_all, 1 - core)).astype(jnp.bfloat16)
    got = lax.ppermute(give, "row", core_swap)
    keep = contract_last(grad_rows, pick(down_all, core)).astype(jnp.bfloat16)
    pair = (keep.astype(jnp.float32) + got.astype(jnp.float32)).astype(jnp.bfloat16)
    terms = exchange(pair.reshape(n_y, block, half), "row", y_groups)
    share = jnp.sum(terms.astype(jnp.float32), axis=0).astype(jnp.bfloat16)

    sent = [
        lax.ppermute(
            jnp.where(lax.rem(y_here + turn, 2) == 0, share[:, :units], share[:, units:]),
            ("row", "col"),
            to_shard(turn),
        )
        for turn in range(2)
    ]
    x_even = lax.rem(x_here, 2) == 0
    shard_grad = jnp.concatenate(
        [jnp.where(x_even, sent[0], sent[1]), jnp.where(x_even, sent[1], sent[0])], axis=0
    )
    unit_arrays = lax.all_gather(
        jnp.concatenate(swiglu_inputs(shard_grad, gate_pre, up_pre), axis=1),
        "row",
        axis=0,
        tiled=True,
    )
    total_rows = unit_arrays.shape[0]

    own = spread(share, n_y, "row", y_groups)
    other = lax.ppermute(own, "row", core_swap)
    part_in = 0.0
    for side, hidden_grad in enumerate((own, other)):
        side_saved = pick(saved, lax.rem(core + side, 2), 1)
        gate_grad, up_grad, _ = swiglu_inputs(
            hidden_grad, side_saved[..., :half], side_saved[..., half:]
        )
        part_in = part_in + contract_last(gate_grad.reshape(group_rows, half), w_half(side, 0))
        part_in = part_in + contract_last(up_grad.reshape(group_rows, half), w_half(side, 1))
    token_terms = exchange(
        part_in.astype(jnp.bfloat16).reshape(N_Z, block, features), "col", z_groups
    )
    token_grad = jnp.sum(token_terms.astype(jnp.float32), axis=0).astype(jnp.bfloat16)

    all_rows = jnp.zeros((n_x,) + both.shape, both.dtype)
    for step in range(n_x):
        piece = lax.ppermute(both, "col", x_shift(step)) if step else both
        all_rows = lax.dynamic_update_index_in_dim(
            all_rows, piece, lax.rem(x_here - step + n_x, n_x), 0
        )
    all_rows = all_rows.reshape(total_rows, 2 * features)
    grad_scale = total_rows ** (-0.5)
    gate_wgrad, up_wgrad = (
        (
            contract_first(all_rows[:, features:], unit_arrays[:, k * units : (k + 1) * units])
            * grad_scale
        ).astype(jnp.bfloat16)
        for k in range(2)
    )
    down_wgrad = (
        contract_first(unit_arrays[:, 2 * units :], all_rows[:, :features]) * grad_scale
    ).astype(jnp.bfloat16)
    return (token_grad, gate_wgrad, up_wgrad, down_wgrad)


def solution(mesh):
    n_row, n_col = mesh.shape["row"], mesh.shape["col"]

    def device_program(*arrays):
        return local(n_row, n_col, *arrays)

    return jax.shard_map(
        device_program,
        mesh=mesh,
        in_specs=(
            P("col", "row"),
            P("col", "row"),
            P("row", "col"),
            P("row", "col"),
            P("row", "col"),
            P("row", "col"),
            P("col", "row"),
        ),
        out_specs=(P("col", "row"), P("row", "col"), P("row", "col"), P("col", "row")),
        check_vma=False,
    )
```

time: 237 us -> 254 us (1.072)
  blocking collectives: 87.9 us -> 0 us
  waiting for transfers between devices: 77.2 us -> 123 us
  starting transfers between devices: 22.2 us -> 66.7 us
  local copies, waits for them, and re-layouts: 8.42 us -> 18.5 us
  matrix products: 15.1 us -> 21 us
    all_to_all x3 -> x0, blocking collectives: 87.9 us -> none  [exchange(): lax.all_to_all(pieces, axis, 0, 0, tiled=True, axis_index_groups=groups)]
    ppermute x3 -> x10, waiting for transfers between devices: 25.5 us -> 60.8 us  [the longest x3 24 us: local(): lax.ppermute(w_both, 'col', x_shift(step))]
    all_to_all x2 -> x4, waiting for transfers between devices: 24.5 us -> 58.3 us  [exchange(): lax.all_to_all(pieces, axis, 0, 0, tiled=True, axis_index_groups=groups)]
    ppermute x3 -> x10, starting transfers between devices: 9.84 us -> 32.5 us  [the longest x3 9.26 us: local(): piece = lax.ppermute(both, 'col', x_shift(step)) if step else both]
    all_gather x2 -> x3, waiting for transfers between devices: 22.2 us -> 0.02 us  [the longest x1 0.02 us: local(): lax.all_gather(saved_share, 'row', axis=0, tiled=True)]
    all_to_all x2 -> x4, starting transfers between devices: 8.44 us -> 30.2 us  [exchange(): lax.all_to_all(pieces, axis, 0, 0, tiled=True, axis_index_groups=groups)]
    dynamic_update_slice x0 -> x4, local copies, waits for them, and re-layouts: none -> 8.37 us  [local(): lax.dynamic_update_index_in_dim(all_rows, piece, lax.rem(x_here - step +...]
    dot_general x3 -> x6, matrix products: 4.34 us -> 9.12 us  [contract_last(): lax.dot_general(left_side, right_side, (((1,), (1,)), ((), ())), preferre...]
  transfers between devices with their start and end apart: 9 -> 19, of which waited for: 6 -> 11; matrix products, arithmetic and copies ran while one was open for 12% -> 14% of each run, Pallas kernels for 0% -> 0%
where the time goes in v3:
time: 254 us; the launch traced here: 251 us
  waiting for transfers between devices  123 us (48%)
  starting transfers between devices  66.7 us (26%)
  matrix products  21 us (8%)
  local copies, waits for them, and re-layouts  18.5 us (7%)
  between operations  14.2 us (6%)
  other arithmetic  8.48 us (3%)
    all_to_all x4, waiting for transfers between devices, exchange(): lax.all_to_all(pieces, axis, 0, 0, tiled=True, axis_index_groups=groups)  58.3 us
    all_to_all x4, starting transfers between devices, exchange(): lax.all_to_all(pieces, axis, 0, 0, tiled=True, axis_index_groups=groups)  30.2 us
    ppermute x3, waiting for transfers between devices, local(): lax.ppermute(w_both, 'col', x_shift(step))  24 us
    ppermute x3, waiting for transfers between devices, local(): piece = lax.ppermute(both, 'col', x_shift(step)) if step else both  23.3 us
    dot_general x3, matrix products, contract_first(): lax.dot_general(left_side, right_side, (((0,), (0,)), ((), ())), preferre...  11.9 us
    ppermute x3, starting transfers between devices, local(): piece = lax.ppermute(both, 'col', x_shift(step)) if step else both  9.26 us
    dot_general x6, matrix products, contract_last(): lax.dot_general(left_side, right_side, (((1,), (1,)), ((), ())), preferre...  9.12 us
    ppermute x2, waiting for transfers between devices, local(): lax.ppermute(pick(saved_pieces, lax.rem(x_here + turn, 2)), ('row', 'col'...  8.74 us
  transfers between devices with their start and end apart: 19, of which 11 were waited for; matrix products, arithmetic and copies ran while one was open for 14% of the time, Pallas kernels for 0%

profile of v3, /device:TPU:6, one launch (start us, length us, event | category | flops | bytes accessed | tf_op | source)
XLA Modules:
  0.0 251.4 jit_solution(9341753665843895745)
XLA Ops:
  8.0 1.0 pad_maximum_fusion.2
  9.0 2.8 %collective-permute-start.1 = (bf16[72,768]{1,0:T(8,128)(2,1)S(1)}, bf16[72,768]{1,0:T(8,128)(2,1)S(1)}, u32[]{:S(2)}, u32[]{:S(2)}) collective-permute-start(bf16[72,768]{1,0:T(8,128)(2,1)S(1)} %get-tuple-element.27), channel_id=1, source_target_pairs={{0,0},{1,1},{2,2},{3,3},{4,4},{5,5},{6,6},{7,7},{8,64},{9,65},{10,... | collective-permute-start | bytes 331784 | tf_op jit(solution)/shard_map/ppermute | solution.py:95
  11.9 3.8 %collective-permute-start.2 = (bf16[72,768]{1,0:T(8,128)(2,1)S(1)}, bf16[72,768]{1,0:T(8,128)(2,1)S(1)}, u32[]{:S(2)}, u32[]{:S(2)}) collective-permute-start(bf16[72,768]{1,0:T(8,128)(2,1)S(1)} %get-tuple-element.28), channel_id=1, source_target_pairs={{0,64},{1,65},{2,66},{3,67},{4,68},{5,69},{6,70},{7,71},{8,0},{9,1... | collective-permute-start | bytes 331784 | tf_op jit(solution)/shard_map/ppermute | solution.py:95
  15.6 4.2 %collective-permute-done.1 = bf16[72,768]{1,0:T(8,128)(2,1)S(1)} collective-permute-done((bf16[72,768]{1,0:T(8,128)(2,1)S(1)}, bf16[72,768]{1,0:T(8,128)(2,1)S(1)}, u32[]{:S(2)}, u32[]{:S(2)}) %collective-permute-start.1) | collective-permute-done | bytes 110624 | tf_op jit(solution)/shard_map/ppermute | solution.py:95
  19.9 4.5 %collective-permute-done.2 = bf16[72,768]{1,0:T(8,128)(2,1)S(1)} collective-permute-done((bf16[72,768]{1,0:T(8,128)(2,1)S(1)}, bf16[72,768]{1,0:T(8,128)(2,1)S(1)}, u32[]{:S(2)}, u32[]{:S(2)}) %collective-permute-start.2) | collective-permute-done | bytes 110624 | tf_op jit(solution)/shard_map/ppermute | solution.py:95
  25.2 1.2 broadcast_in_dim.28
  26.4 10.3 %all-to-all-start = ((bf16[8,72,1024]{2,1,0:T(8,128)(2,1)}), bf16[8,72,1024]{2,1,0:T(8,128)(2,1)S(1)}, u32[]{:S(2)}, u32[]{:S(2)}) async-start(bf16[8,72,1024]{2,1,0:T(8,128)(2,1)} %broadcast_in_dim.28), calls=%async_computation | async-start | bytes 2359296 | tf_op jit(solution)/shard_map/all_to_all | solution.py:37
  36.7 31.9 %all-to-all-done = bf16[8,72,1024]{2,1,0:T(8,128)(2,1)S(1)} async-done(((bf16[8,72,1024]{2,1,0:T(8,128)(2,1)}), bf16[8,72,1024]{2,1,0:T(8,128)(2,1)S(1)}, u32[]{:S(2)}, u32[]{:S(2)}) %all-to-all-start) | async-done | bytes 1179680 | tf_op jit(solution)/shard_map/all_to_all | solution.py:37
  68.6 2.9 %convolution_convert_fusion = bf16[576,768]{1,0:T(8,128)(2,1)} fusion(bf16[2,768,512]{2,1,0:T(8,128)(2,1)} %bitcast.63, s32[]{:T(128)S(6)} %select_n.84, bf16[576,1024]{1,0:T(8,128)(2,1)S(1)} %bitcast.50), kind=kOutput, calls=%fused_computation.39 | convolution fusion | flops 453427200 | bytes 2260996 | tf_op jit(solution)/shard_map/dot_general | solution.py:11
  71.5 1.9 collective-permute-start
  73.4 2.7 %collective-permute-done = bf16[576,768]{1,0:T(8,128)(2,1)} collective-permute-done((bf16[576,768]{1,0:T(8,128)(2,1)}, bf16[576,768]{1,0:T(8,128)(2,1)}, u32[]{:S(2)}, u32[]{:S(2)}) %collective-permute-start) | collective-permute-done | bytes 884768 | tf_op jit(solution)/shard_map/ppermute | solution.py:130
  76.1 2.8 %add_convert_fusion = bf16[576,768]{1,0:T(8,128)(2,1)} fusion(bf16[576,768]{1,0:T(8,128)(2,1)} %collective-permute-done, bf16[2,768,512]{2,1,0:T(8,128)(2,1)S(1)} %bitcast.64, s32[]{:T(128)S(6)} %select_n.83, bf16[576,1024]{1,0:T(8,128)(2,1)S(1)} %bitcast.51), kind=kOutput, calls=%fused_computation.38 | convolution fusion | flops 455196672 | bytes 3145732 | tf_op jit(solution)/shard_map/dot_general | solution.py:11
  78.9 4.4 %all-to-all-start.1 = ((bf16[8,72,768]{2,1,0:T(8,128)(2,1)}), bf16[8,72,768]{2,1,0:T(8,128)(2,1)S(1)}, u32[]{:S(2)}, u32[]{:S(2)}) async-start(bf16[8,72,768]{2,1,0:T(8,128)(2,1)} %bitcast.4), calls=%async_computation.1 | async-start | bytes 1769472 | tf_op jit(solution)/shard_map/all_to_all | solution.py:37
  83.4 26.3 %all-to-all-done.1 = bf16[8,72,768]{2,1,0:T(8,128)(2,1)S(1)} async-done(((bf16[8,72,768]{2,1,0:T(8,128)(2,1)}), bf16[8,72,768]{2,1,0:T(8,128)(2,1)S(1)}, u32[]{:S(2)}, u32[]{:S(2)}) %all-to-all-start.1) | async-done | bytes 884768 | tf_op jit(solution)/shard_map/all_to_all | solution.py:37
  109.9 6.2 %collective-permute-start.10 = (bf16[72,384]{1,0:T(8,128)(2,1)S(1)}, bf16[72,384]{1,0:T(8,128)(2,1)S(1)}, u32[]{:S(2)}, u32[]{:S(2)}) collective-permute-start(bf16[72,384]{1,0:T(8,128)(2,1)S(1)} %get-tuple-element.31), channel_id=1, source_target_pairs={{0,0},{1,1},{2,2},{3,3},{4,4},{5,5},{6,6},{7,7},{8,128},{9,129},{1... | collective-permute-start | bytes 165896 | tf_op jit(solution)/shard_map/ppermute | solution.py:137
  116.1 1.9 collective-permute-start.11
  118.0 4.7 %collective-permute-done.11 = bf16[72,384]{1,0:T(8,128)(2,1)S(1)} collective-permute-done((bf16[72,384]{1,0:T(8,128)(2,1)S(1)}, bf16[72,384]{1,0:T(8,128)(2,1)S(1)}, u32[]{:S(2)}, u32[]{:S(2)}) %collective-permute-start.11) | collective-permute-done | bytes 55328 | tf_op jit(solution)/shard_map/ppermute | solution.py:137
  123.0 0.8 pad_maximum_fusion.1
  123.9 1.9 collective-permute-start.3
  125.8 4.6 %collective-permute-start.4 = (bf16[512,768]{1,0:T(8,128)(2,1)S(1)}, bf16[512,768]{1,0:T(8,128)(2,1)}, u32[]{:S(2)}, u32[]{:S(2)}) collective-permute-start(bf16[512,768]{1,0:T(8,128)(2,1)S(1)} %constant_dynamic-update-slice_fusion), channel_id=1, source_target_pairs={{0,16},{1,17},{2,18},{3,19},{4,20},{5,21},{6,22},{7,23},{8,24},{9,... | collective-permute-start | bytes 2359304 | tf_op jit(solution)/shard_map/ppermute | solution.py:117
  130.5 1.9 collective-permute-start.5
  132.4 1.0 broadcast_in_dim.29
  133.4 9.2 %all-to-all-start.2 = ((bf16[8,72,768]{2,1,0:T(8,128)(2,1)}), bf16[8,72,768]{2,1,0:T(8,128)(2,1)S(1)}, u32[]{:S(2)}, u32[]{:S(2)}) async-start(bf16[8,72,768]{2,1,0:T(8,128)(2,1)} %broadcast_in_dim.29), calls=%async_computation.2 | async-start | bytes 1769472 | tf_op jit(solution)/shard_map/all_to_all | solution.py:37
  142.6 3.6 %collective-permute-done.3 = bf16[512,768]{1,0:T(8,128)(2,1)} collective-permute-done((bf16[512,768]{1,0:T(8,128)(2,1)S(1)}, bf16[512,768]{1,0:T(8,128)(2,1)}, u32[]{:S(2)}, u32[]{:S(2)}) %collective-permute-start.3) | collective-permute-done | bytes 786464 | tf_op jit(solution)/shard_map/ppermute | solution.py:117
  146.2 3.5 %collective-permute-done.4 = bf16[512,768]{1,0:T(8,128)(2,1)} collective-permute-done((bf16[512,768]{1,0:T(8,128)(2,1)S(1)}, bf16[512,768]{1,0:T(8,128)(2,1)}, u32[]{:S(2)}, u32[]{:S(2)}) %collective-permute-start.4) | collective-permute-done | bytes 786464 | tf_op jit(solution)/shard_map/ppermute | solution.py:117
  149.7 16.9 %collective-permute-done.5 = bf16[512,768]{1,0:T(8,128)(2,1)} collective-permute-done((bf16[512,768]{1,0:T(8,128)(2,1)S(1)}, bf16[512,768]{1,0:T(8,128)(2,1)}, u32[]{:S(2)}, u32[]{:S(2)}) %collective-permute-start.5) | collective-permute-done | bytes 786464 | tf_op jit(solution)/shard_map/ppermute | solution.py:117
  166.6 1.8 pad_maximum_fusion
  168.7 1.1 fusion.94
  169.7 1.0 fusion.92
  170.7 2.4 collective-permute-start.7
  173.2 4.2 %collective-permute-start.8 = (bf16[576,1024]{1,0:T(8,128)(2,1)S(1)}, bf16[576,1024]{1,0:T(8,128)(2,1)}, u32[]{:S(2)}, u32[]{:S(2)}) collective-permute-start(bf16[576,1024]{1,0:T(8,128)(2,1)S(1)} %bitcast.53), channel_id=1, source_target_pairs={{0,16},{1,17},{2,18},{3,19},{4,20},{5,21},{6,22},{7,23},{8,24},{9,... | collective-permute-start | bytes 3538952 | tf_op jit(solution)/shard_map/ppermute | solution.py:173
  177.3 2.7 %collective-permute-start.9 = (bf16[576,1024]{1,0:T(8,128)(2,1)S(1)}, bf16[576,1024]{1,0:T(8,128)(2,1)}, u32[]{:S(2)}, u32[]{:S(2)}) collective-permute-start(bf16[576,1024]{1,0:T(8,128)(2,1)S(1)} %bitcast.54), channel_id=1, source_target_pairs={{0,24},{1,25},{2,26},{3,27},{4,28},{5,29},{6,30},{7,31},{8,0},{9,1... | collective-permute-start | bytes 3538952 | tf_op jit(solution)/shard_map/ppermute | solution.py:173
  180.0 1.9 collective-permute-start.6
  182.0 2.3 dynamic-slice_bitcast_fusion.1
  184.3 1.0 fusion.9
  187.0 2.2 fusion.12
  189.9 1.5 fusion.26
  191.4 6.3 %all-to-all-start.3 = ((bf16[8,72,512]{2,1,0:T(8,128)(2,1)}), bf16[8,72,512]{2,1,0:T(8,128)(2,1)S(1)}, u32[]{:S(2)}, u32[]{:S(2)}) async-start(bf16[8,72,512]{2,1,0:T(8,128)(2,1)} %bitcast.23), calls=%async_computation.3 | async-start | bytes 1179648 | tf_op jit(solution)/shard_map/all_to_all | solution.py:37
  197.7 2.8 %broadcast_in_dim.30 = bf16[4,576,1024]{2,1,0:T(8,128)(2,1)} broadcast(bf16[]{:T(256)} %constant.111.clone.1), dimensions={} | broadcast | bytes 4718594 | tf_op jit(solution)/shard_map/broadcast_in_dim | solution.py:171
  200.5 1.1 bitcast_dynamic-update-slice_fusion.3
  201.6 2.4 bitcast_dynamic-update-slice_fusion.2
  204.1 1.5 collective-permute-done.8
  205.6 2.4 bitcast_dynamic-update-slice_fusion.1
  208.0 21.9 %collective-permute-done.9 = bf16[576,1024]{1,0:T(8,128)(2,1)} collective-permute-done((bf16[576,1024]{1,0:T(8,128)(2,1)S(1)}, bf16[576,1024]{1,0:T(8,128)(2,1)}, u32[]{:S(2)}, u32[]{:S(2)}) %collective-permute-start.9) | collective-permute-done | bytes 1179680 | tf_op jit(solution)/shard_map/ppermute | solution.py:173
  229.8 2.4 bitcast_dynamic-update-slice_fusion
  233.0 4.2 %fusion.42 = bf16[384,512]{1,0:T(8,128)(2,1)} fusion(bf16[2304,1024]{1,0:T(8,128)(2,1)} %bitcast.28, bf16[2304,1152]{1,0:T(8,128)(2,1)} %all-gather.8.cloned.1.call-done), kind=kOutput, calls=%fused_computation.48 | convolution fusion | flops 906362880 | bytes 4521984 | tf_op jit(solution)/shard_map/dot_general | solution.py:17
  237.2 3.8 %fusion.47 = bf16[512,384]{1,0:T(8,128)(2,1)} fusion(bf16[2304,1152]{1,0:T(8,128)(2,1)S(1)} %copy-done.11, bf16[2304,1024]{1,0:T(8,128)(2,1)} %bitcast.28), kind=kOutput, calls=%fused_computation.49 | convolution fusion | flops 906362880 | bytes 4521984 | tf_op jit(solution)/shard_map/dot_general | solution.py:17
  241.0 3.8 %fusion.52 = bf16[512,384]{1,0:T(8,128)(2,1)} fusion(bf16[2304,1152]{1,0:T(8,128)(2,1)S(1)} %copy-done.11, bf16[2304,1024]{1,0:T(8,128)(2,1)} %bitcast.28), kind=kOutput, calls=%fused_computation.50 | convolution fusion | flops 906362880 | bytes 4521984 | tf_op jit(solution)/shard_map/dot_general | solution.py:17
  (56 shorter events, 5.4 us)
Async XLA Ops:
  7.2 18.0 %copy-start.9 = (bf16[72,512]{1,0:T(8,128)(2,1)S(1)}, bf16[72,512]{1,0:T(8,128)(2,1)}, u32[]{:S(2)}) copy-start(bf16[72,512]{1,0:T(8,128)(2,1)} %param.7) | copy-start | bytes 221188
  7.2 18.0 %copy-start.10 = (bf16[72,512]{1,0:T(8,128)(2,1)S(1)}, bf16[72,512]{1,0:T(8,128)(2,1)}, u32[]{:S(2)}) copy-start(bf16[72,512]{1,0:T(8,128)(2,1)} %param.8) | copy-start | bytes 221188
  7.2 61.4 %all-gather.4.cloned.1.call-start = ((), (), s32[]{:S(2)}) async-start(), calls=%async_computation.4 | async-start | bytes 1966080 | tf_op jit(solution)/shard_map/all_gather | solution.py:89
  7.9 174.1 %all-gather.6.cloned.1.call-start = ((), (), s32[]{:S(2)}) async-start(), calls=%async_computation.5 | async-start | bytes 3760128 | tf_op jit(solution)/shard_map/all_gather | solution.py:106
  9.0 10.9 %collective-permute-start.1 = (bf16[72,768]{1,0:T(8,128)(2,1)S(1)}, bf16[72,768]{1,0:T(8,128)(2,1)S(1)}, u32[]{:S(2)}, u32[]{:S(2)}) collective-permute-start(bf16[72,768]{1,0:T(8,128)(2,1)S(1)} %get-tuple-element.27), channel_id=1, source_target_pairs={{0,0},{1,1},{2,2},{3,3},{4,4},{5,5},{6,6},{7,7},{8,64},{9,65},{10,... | collective-permute-start | bytes 331784 | tf_op jit(solution)/shard_map/ppermute | solution.py:95
  11.9 12.5 %collective-permute-start.2 = (bf16[72,768]{1,0:T(8,128)(2,1)S(1)}, bf16[72,768]{1,0:T(8,128)(2,1)S(1)}, u32[]{:S(2)}, u32[]{:S(2)}) collective-permute-start(bf16[72,768]{1,0:T(8,128)(2,1)S(1)} %get-tuple-element.28), channel_id=1, source_target_pairs={{0,64},{1,65},{2,66},{3,67},{4,68},{5,69},{6,70},{7,71},{8,0},{9,1... | collective-permute-start | bytes 331784 | tf_op jit(solution)/shard_map/ppermute | solution.py:95
  26.4 42.2 %all-to-all-start = ((bf16[8,72,1024]{2,1,0:T(8,128)(2,1)}), bf16[8,72,1024]{2,1,0:T(8,128)(2,1)S(1)}, u32[]{:S(2)}, u32[]{:S(2)}) async-start(bf16[8,72,1024]{2,1,0:T(8,128)(2,1)} %broadcast_in_dim.28), calls=%async_computation | async-start | bytes 2359296 | tf_op jit(solution)/shard_map/all_to_all | solution.py:37
  68.6 7.5 %copy-start.12 = (bf16[1536,512]{1,0:T(8,128)(2,1)S(1)}, bf16[1536,512]{1,0:T(8,128)(2,1)}, u32[]{:S(2)}) copy-start(bf16[1536,512]{1,0:T(8,128)(2,1)} %all-gather.4.cloned.1.call-done) | copy-start | bytes 4718596
  71.5 4.7 %collective-permute-start = (bf16[576,768]{1,0:T(8,128)(2,1)}, bf16[576,768]{1,0:T(8,128)(2,1)}, u32[]{:S(2)}, u32[]{:S(2)}) collective-permute-start(bf16[576,768]{1,0:T(8,128)(2,1)} %convolution_convert_fusion), channel_id=1, source_target_pairs={{0,32},{32,0},{64,96},{96,64},{128,160},{160,128},{192,224},{224,1... | collective-permute-start | bytes 2654216 | tf_op jit(solution)/shard_map/ppermute | solution.py:130
  78.9 43.9 %copy-start.1 = (bf16[144,384]{1,0:T(8,128)(2,1)S(1)}, bf16[144,384]{1,0:T(8,128)(2,1)}, u32[]{:S(2)}) copy-start(bf16[144,384]{1,0:T(8,128)(2,1)} %param.10) | copy-start | bytes 331780
  78.9 43.9 %copy-start.2 = (bf16[144,384]{1,0:T(8,128)(2,1)S(1)}, bf16[144,384]{1,0:T(8,128)(2,1)}, u32[]{:S(2)}) copy-start(bf16[144,384]{1,0:T(8,128)(2,1)} %param.9) | copy-start | bytes 331780
  78.9 30.8 %all-to-all-start.1 = ((bf16[8,72,768]{2,1,0:T(8,128)(2,1)}), bf16[8,72,768]{2,1,0:T(8,128)(2,1)S(1)}, u32[]{:S(2)}, u32[]{:S(2)}) async-start(bf16[8,72,768]{2,1,0:T(8,128)(2,1)} %bitcast.4), calls=%async_computation.1 | async-start | bytes 1769472 | tf_op jit(solution)/shard_map/all_to_all | solution.py:37
  83.3 40.5 %copy-start.7 = (bf16[512,384]{1,0:T(8,128)(2,1)S(1)}, bf16[512,384]{1,0:T(8,128)(2,1)}, u32[]{:S(2)}) copy-start(bf16[512,384]{1,0:T(8,128)(2,1)} %param.11) | copy-start | bytes 1179652
  83.3 149.6 %all-gather.8.cloned.1.call-start = ((), (), s32[]{:S(2)}) async-start(), calls=%async_computation.6 | async-start | bytes 5640192 | tf_op jit(solution)/shard_map/all_gather | solution.py:148
  83.4 40.5 %copy-start.8 = (bf16[512,384]{1,0:T(8,128)(2,1)S(1)}, bf16[512,384]{1,0:T(8,128)(2,1)}, u32[]{:S(2)}) copy-start(bf16[512,384]{1,0:T(8,128)(2,1)} %param.12) | copy-start | bytes 1179652
  109.9 8.1 %collective-permute-start.10 = (bf16[72,384]{1,0:T(8,128)(2,1)S(1)}, bf16[72,384]{1,0:T(8,128)(2,1)S(1)}, u32[]{:S(2)}, u32[]{:S(2)}) collective-permute-start(bf16[72,384]{1,0:T(8,128)(2,1)S(1)} %get-tuple-element.31), channel_id=1, source_target_pairs={{0,0},{1,1},{2,2},{3,3},{4,4},{5,5},{6,6},{7,7},{8,128},{9,129},{1... | collective-permute-start | bytes 165896 | tf_op jit(solution)/shard_map/ppermute | solution.py:137
  116.1 6.7 %collective-permute-start.11 = (bf16[72,384]{1,0:T(8,128)(2,1)S(1)}, bf16[72,384]{1,0:T(8,128)(2,1)S(1)}, u32[]{:S(2)}, u32[]{:S(2)}) collective-permute-start(bf16[72,384]{1,0:T(8,128)(2,1)S(1)} %get-tuple-element.32), channel_id=1, source_target_pairs={{0,8},{1,9},{2,10},{3,11},{4,12},{5,13},{6,14},{7,15},{8,136},{9,1... | collective-permute-start | bytes 165896 | tf_op jit(solution)/shard_map/ppermute | solution.py:137
  123.9 22.3 %collective-permute-start.3 = (bf16[512,768]{1,0:T(8,128)(2,1)S(1)}, bf16[512,768]{1,0:T(8,128)(2,1)}, u32[]{:S(2)}, u32[]{:S(2)}) collective-permute-start(bf16[512,768]{1,0:T(8,128)(2,1)S(1)} %constant_dynamic-update-slice_fusion), channel_id=1, source_target_pairs={{0,8},{1,9},{2,10},{3,11},{4,12},{5,13},{6,14},{7,15},{8,16},{9,17... | collective-permute-start | bytes 2359304 | tf_op jit(solution)/shard_map/ppermute | solution.py:117
  125.8 23.9 %collective-permute-start.4 = (bf16[512,768]{1,0:T(8,128)(2,1)S(1)}, bf16[512,768]{1,0:T(8,128)(2,1)}, u32[]{:S(2)}, u32[]{:S(2)}) collective-permute-start(bf16[512,768]{1,0:T(8,128)(2,1)S(1)} %constant_dynamic-update-slice_fusion), channel_id=1, source_target_pairs={{0,16},{1,17},{2,18},{3,19},{4,20},{5,21},{6,22},{7,23},{8,24},{9,... | collective-permute-start | bytes 2359304 | tf_op jit(solution)/shard_map/ppermute | solution.py:117
  130.5 36.1 %collective-permute-start.5 = (bf16[512,768]{1,0:T(8,128)(2,1)S(1)}, bf16[512,768]{1,0:T(8,128)(2,1)}, u32[]{:S(2)}, u32[]{:S(2)}) collective-permute-start(bf16[512,768]{1,0:T(8,128)(2,1)S(1)} %constant_dynamic-update-slice_fusion), channel_id=1, source_target_pairs={{0,24},{1,25},{2,26},{3,27},{4,28},{5,29},{6,30},{7,31},{8,0},{9,1... | collective-permute-start | bytes 2359304 | tf_op jit(solution)/shard_map/ppermute | solution.py:117
  133.4 46.6 %all-to-all-start.2 = ((bf16[8,72,768]{2,1,0:T(8,128)(2,1)}), bf16[8,72,768]{2,1,0:T(8,128)(2,1)S(1)}, u32[]{:S(2)}, u32[]{:S(2)}) async-start(bf16[8,72,768]{2,1,0:T(8,128)(2,1)} %broadcast_in_dim.29), calls=%async_computation.2 | async-start | bytes 1769472 | tf_op jit(solution)/shard_map/all_to_all | solution.py:37
  170.7 30.9 %collective-permute-start.7 = (bf16[576,1024]{1,0:T(8,128)(2,1)S(1)}, bf16[576,1024]{1,0:T(8,128)(2,1)}, u32[]{:S(2)}, u32[]{:S(2)}) collective-permute-start(bf16[576,1024]{1,0:T(8,128)(2,1)S(1)} %bitcast.52), channel_id=1, source_target_pairs={{0,8},{1,9},{2,10},{3,11},{4,12},{5,13},{6,14},{7,15},{8,16},{9,17... | collective-permute-start | bytes 3538952 | tf_op jit(solution)/shard_map/ppermute | solution.py:173
  173.2 32.4 %collective-permute-start.8 = (bf16[576,1024]{1,0:T(8,128)(2,1)S(1)}, bf16[576,1024]{1,0:T(8,128)(2,1)}, u32[]{:S(2)}, u32[]{:S(2)}) collective-permute-start(bf16[576,1024]{1,0:T(8,128)(2,1)S(1)} %bitcast.53), channel_id=1, source_target_pairs={{0,16},{1,17},{2,18},{3,19},{4,20},{5,21},{6,22},{7,23},{8,24},{9,... | collective-permute-start | bytes 3538952 | tf_op jit(solution)/shard_map/ppermute | solution.py:173
  177.3 52.5 %collective-permute-start.9 = (bf16[576,1024]{1,0:T(8,128)(2,1)S(1)}, bf16[576,1024]{1,0:T(8,128)(2,1)}, u32[]{:S(2)}, u32[]{:S(2)}) collective-permute-start(bf16[576,1024]{1,0:T(8,128)(2,1)S(1)} %bitcast.54), channel_id=1, source_target_pairs={{0,24},{1,25},{2,26},{3,27},{4,28},{5,29},{6,30},{7,31},{8,0},{9,1... | collective-permute-start | bytes 3538952 | tf_op jit(solution)/shard_map/ppermute | solution.py:173
  180.0 7.0 %collective-permute-start.6 = (bf16[8,72,768]{2,1,0:T(8,128)(2,1)S(1)}, bf16[8,72,768]{2,1,0:T(8,128)(2,1)}, u32[]{:S(2)}, u32[]{:S(2)}) collective-permute-start(bf16[8,72,768]{2,1,0:T(8,128)(2,1)S(1)} %all-to-all-done.2), channel_id=1, source_target_pairs={{0,32},{32,0},{64,96},{96,64},{128,160},{160,128},{192,224},{224,1... | collective-permute-start | bytes 2654216 | tf_op jit(solution)/shard_map/ppermute | solution.py:157
  184.3 1.0 copy-start.5
  184.3 1.1 copy-start.6
  185.3 1.0 copy-start
  187.0 2.2 copy-start.3
  187.0 2.2 copy-start.4
  191.4 40.8 %all-to-all-start.3 = ((bf16[8,72,512]{2,1,0:T(8,128)(2,1)}), bf16[8,72,512]{2,1,0:T(8,128)(2,1)S(1)}, u32[]{:S(2)}, u32[]{:S(2)}) async-start(bf16[8,72,512]{2,1,0:T(8,128)(2,1)} %bitcast.23), calls=%async_computation.3 | async-start | bytes 1179648 | tf_op jit(solution)/shard_map/all_to_all | solution.py:37
  233.0 4.2 %copy-start.11 = (bf16[2304,1152]{1,0:T(8,128)(2,1)S(1)}, bf16[2304,1152]{1,0:T(8,128)(2,1)}, u32[]{:S(2)}) copy-start(bf16[2304,1152]{1,0:T(8,128)(2,1)} %all-gather.8.cloned.1.call-done) | copy-start | bytes 15925252
Sparse Core Ops, SparseCore 0:
  10.1 35.3 all-gather.3
  47.7 51.5 all-gather.5
  123.9 63.2 all-gather.7

commit v4 on v3

v4 whole, which is shorter than its diff:
```python
import jax
import jax.numpy as jnp
from jax import lax
from jax.sharding import PartitionSpec as P

N_CORE = 2
N_Z = 8


def contract_last(left_side, right_side):
    return lax.dot_general(
        left_side, right_side, (((1,), (1,)), ((), ())), preferred_element_type=jnp.float32
    )


def contract_first(left_side, right_side):
    return lax.dot_general(
        left_side, right_side, (((0,), (0,)), ((), ())), preferred_element_type=jnp.float32
    )


def swiglu_grads(hidden_grad, gate_pre, up_pre):
    gate_float = gate_pre.astype(jnp.float32)
    up_float = up_pre.astype(jnp.float32)
    grad_float = hidden_grad.astype(jnp.float32)
    sigmoid_gate = jax.nn.sigmoid(gate_float)
    gate_grad = grad_float * up_float * sigmoid_gate * (1.0 + gate_float * (1.0 - sigmoid_gate))
    up_grad = grad_float * (gate_float * sigmoid_gate)
    return gate_grad.astype(jnp.bfloat16), up_grad.astype(jnp.bfloat16)


def swiglu_hidden(gate_pre, up_pre):
    gate_float = gate_pre.astype(jnp.float32)
    swish_gate = gate_float * jax.nn.sigmoid(gate_float)
    return (swish_gate * up_pre.astype(jnp.float32)).astype(jnp.bfloat16)


def exchange(pieces, axis, groups):
    return lax.all_to_all(pieces, axis, 0, 0, tiled=True, axis_index_groups=groups)


def spread(block, size, axis, groups):
    return exchange(jnp.broadcast_to(block[None], (size,) + block.shape), axis, groups)


def pick(stacked, index, axis=0):
    return lax.dynamic_index_in_dim(stacked, index, axis, keepdims=False)


def local(n_row, n_col, tokens, out_grad, gate_pre, up_pre, w_gate, w_up, w_down):
    n_y, n_x = n_row // N_CORE, n_col // N_Z
    z_groups = [[x * N_Z + z for z in range(N_Z)] for x in range(n_x)]
    x_groups = [[x * N_Z + z for x in range(n_x)] for z in range(N_Z)]
    y_groups = [[y * N_CORE + c for y in range(n_y)] for c in range(N_CORE)]
    core_swap = [(r, r ^ 1) for r in range(n_row)]
    row_here, col_here = lax.axis_index("row"), lax.axis_index("col")
    core, y_here = lax.rem(row_here, N_CORE), lax.div(row_here, N_CORE)
    x_here = lax.div(col_here, N_Z)
    rows, units = gate_pre.shape
    block, features = out_grad.shape
    half = 2 * units
    group_rows = N_Z * block

    def x_shift(step):
        return [
            (x * N_Z + z, (x + step) % n_x * N_Z + z) for x in range(n_x) for z in range(N_Z)
        ]

    def to_group(turn):
        pairs = []
        for r in range(n_row):
            for x in range(n_x):
                piece = (turn + x) % 2
                new_row = (2 * (r % n_x) + piece) * N_CORE + x // 2
                for z in range(N_Z):
                    pairs.append((r * n_col + x * N_Z + z, new_row * n_col + r // n_x * N_Z + z))
        return pairs

    down_all = lax.all_gather(
        w_down, "col", axis=0, tiled=True, axis_index_groups=x_groups
    ).reshape(N_CORE, half, features)

    grad_rows = spread(out_grad, N_Z, "col", z_groups).reshape(group_rows, features)
    tokens, grad_rows = lax.optimization_barrier((tokens, grad_rows))
    token_rows = spread(tokens, N_Z, "col", z_groups).reshape(group_rows, features)

    saved_pieces = jnp.concatenate([gate_pre, up_pre], axis=1).reshape(2, block, half)
    moved = [
        lax.ppermute(
            pick(saved_pieces, lax.rem(x_here + turn, 2)), ("row", "col"), to_group(turn)
        )
        for turn in range(2)
    ]
    y_even = lax.rem(y_here, 2) == 0
    first = jnp.where(y_even, moved[0], moved[1])
    second = jnp.where(y_even, moved[1], moved[0])
    saved_share = jnp.concatenate(
        [first[:, :units], second[:, :units], first[:, units:], second[:, units:]], axis=1
    )
    saved = lax.all_gather(saved_share, "row", axis=0, tiled=True).reshape(
        n_y, N_CORE, block, 2 * half
    )

    w_both = jnp.concatenate([w_gate, w_up], axis=1)
    w_both, down_all = lax.optimization_barrier((w_both, down_all))
    w_left = lax.ppermute(w_both, "col", x_shift(1))
    w_right = lax.ppermute(w_both, "col", x_shift(n_x - 1))
    w_far = lax.ppermute(w_left, "col", x_shift(1))

    give = contract_last(grad_rows, pick(down_all, 1 - core)).astype(jnp.bfloat16)
    got = lax.ppermute(give, "row", core_swap)
    keep = contract_last(grad_rows, pick(down_all, core)).astype(jnp.bfloat16)
    pair = (keep.astype(jnp.float32) + got.astype(jnp.float32)).astype(jnp.bfloat16)
    pair, token_rows = lax.optimization_barrier((pair, token_rows))
    terms = exchange(pair.reshape(n_y, block, half), "row", y_groups)
    share = jnp.sum(terms.astype(jnp.float32), axis=0).astype(jnp.bfloat16)
    own = spread(share, n_y, "row", y_groups)

    grad_scale = (rows * n_row) ** (-0.5)

    def side_saved(side):
        return saved[:, side, :, :half], saved[:, side, :, half:]

    down_part = []
    for side in range(2):
        hidden = swiglu_hidden(*side_saved(side)).reshape(group_rows, half)
        down_part.append(contract_first(hidden, grad_rows).astype(jnp.bfloat16))
    down_part = jnp.concatenate(down_part, axis=0)
    own, _ = lax.optimization_barrier((own, down_part))
    down_sum = lax.psum_scatter(
        down_part,
        "col",
        scatter_dimension=0,
        tiled=True,
        axis_index_groups=x_groups,
    )
    down_wgrad = (down_sum.astype(jnp.float32) * grad_scale).astype(jnp.bfloat16)

    own, w_left, w_right, w_far = lax.optimization_barrier((own, w_left, w_right, w_far))
    w_stack = jnp.stack([w_both, w_left, w_far, w_right])
    w_order = [pick(w_stack, lax.rem(x_here - place + n_x, n_x)) for place in range(n_x)]

    def w_half(side, which):
        pieces = w_order[2 * side : 2 * side + 2]
        return jnp.concatenate(
            [piece[:, which * units : (which + 1) * units] for piece in pieces], axis=1
        )

    other = lax.ppermute(own, "row", core_swap)
    part_in, gate_part, up_part = 0.0, [], []
    for side in range(2):
        hidden_grad = jnp.where(core == side, own, other)
        gate_grad, up_grad = swiglu_grads(hidden_grad, *side_saved(side))
        gate_grad = gate_grad.reshape(group_rows, half)
        up_grad = up_grad.reshape(group_rows, half)
        part_in = part_in + contract_last(gate_grad, w_half(side, 0))
        part_in = part_in + contract_last(up_grad, w_half(side, 1))
        for slot in range(2):
            columns = slice(slot * units, (slot + 1) * units)
            gate_part.append(contract_first(token_rows, gate_grad[:, columns]))
            up_part.append(contract_first(token_rows, up_grad[:, columns]))
    unit_sum = lax.psum_scatter(
        jnp.stack(
            [jnp.concatenate(parts, axis=1) for parts in zip(gate_part, up_part)]
        ).astype(jnp.bfloat16),
        "col",
        scatter_dimension=0,
        tiled=True,
        axis_index_groups=x_groups,
    )[0]
    unit_wgrad = (unit_sum.astype(jnp.float32) * grad_scale).astype(jnp.bfloat16)
    gate_wgrad, up_wgrad = unit_wgrad[:, :units], unit_wgrad[:, units:]
    token_terms = exchange(
        part_in.astype(jnp.bfloat16).reshape(N_Z, block, features), "col", z_groups
    )
    token_grad = jnp.sum(token_terms.astype(jnp.float32), axis=0).astype(jnp.bfloat16)
    return (token_grad, gate_wgrad, up_wgrad, down_wgrad)


def solution(mesh):
    n_row, n_col = mesh.shape["row"], mesh.shape["col"]

    def device_program(*arrays):
        return local(n_row, n_col, *arrays)

    return jax.shard_map(
        device_program,
        mesh=mesh,
        in_specs=(
            P("col", "row"),
            P("col", "row"),
            P("row", "col"),
            P("row", "col"),
            P("row", "col"),
            P("row", "col"),
            P("col", "row"),
        ),
        out_specs=(P("col", "row"), P("row", "col"), P("row", "col"), P("col", "row")),
        check_vma=False,
    )
```

time: 254 us -> 233 us (0.917)
  blocking collectives: 0 us -> 21.8 us
  waiting for transfers between devices: 123 us -> 102 us
  starting transfers between devices: 66.7 us -> 50.6 us
  local copies, waits for them, and re-layouts: 18.5 us -> 8.33 us
  other arithmetic: 8.48 us -> 18.2 us
  matrix products: 21 us -> 14.1 us
    ppermute x8 -> x3, waiting for transfers between devices: 52.1 us -> 15.1 us  [the longest x1 15.1 us: local(): w_left = lax.ppermute(w_both, 'col', x_shift(1))]
    reduce_scatter x0 -> x2, waiting for transfers between devices: none -> 22.5 us  [the longest x1 22.5 us: local(): lax.psum_scatter(jnp.stack([jnp.concatenate(parts, axis=1) for parts in z...]
    all_to_all x0 -> x1, blocking collectives: none -> 21.8 us  [exchange(): lax.all_to_all(pieces, axis, 0, 0, tiled=True, axis_index_groups=groups)]
    ppermute x8 -> x3, starting transfers between devices: 25.9 us -> 14.6 us  [the longest x1 7.07 us: local(): w_left = lax.ppermute(w_both, 'col', x_shift(1))]
    dynamic_update_slice x4 -> x0, local copies, waits for them, and re-layouts: 8.37 us -> none  [local(): lax.dynamic_update_index_in_dim(all_rows, piece, lax.rem(x_here - step +...]
    dot_general x3 -> x10, matrix products: 11.9 us -> 5.74 us  [contract_first(): lax.dot_general(left_side, right_side, (((0,), (0,)), ((), ())), preferre...]
    convert_element_type x3 -> x5, other arithmetic: 3.33 us -> 9.23 us  [the longest x1 3.15 us: swiglu_grads(): return (gate_grad.astype(jnp.bfloat16), up_grad.astype(jnp.bfloat16))]
    all_to_all x4, waiting for transfers between devices: 58.3 us -> 52.4 us  [exchange(): lax.all_to_all(pieces, axis, 0, 0, tiled=True, axis_index_groups=groups)]
  transfers between devices with their start and end apart: 19 -> 15, of which waited for: 11 -> 8; matrix products, arithmetic and copies ran while one was open for 14% -> 15% of each run, Pallas kernels for 0% -> 0%
where the time goes in v4:
time: 233 us; the launch traced here: 229 us
  waiting for transfers between devices  102 us (44%)
  starting transfers between devices  50.6 us (22%)
  blocking collectives  21.8 us (9%)
  other arithmetic  18.2 us (8%)
  between operations  14.4 us (6%)
  matrix products  14.1 us (6%)
  local copies, waits for them, and re-layouts  8.33 us (4%)
    all_to_all x4, waiting for transfers between devices, exchange(): lax.all_to_all(pieces, axis, 0, 0, tiled=True, axis_index_groups=groups)  52.4 us
    all_to_all x4, starting transfers between devices, exchange(): lax.all_to_all(pieces, axis, 0, 0, tiled=True, axis_index_groups=groups)  25.1 us
    reduce_scatter x1, waiting for transfers between devices, local(): lax.psum_scatter(jnp.stack([jnp.concatenate(parts, axis=1) for parts in z...  22.5 us
    all_to_all x1, blocking collectives, exchange(): lax.all_to_all(pieces, axis, 0, 0, tiled=True, axis_index_groups=groups)  21.8 us
    ppermute x1, waiting for transfers between devices, local(): w_left = lax.ppermute(w_both, 'col', x_shift(1))  15.1 us
    ppermute x2, waiting for transfers between devices, local(): lax.ppermute(pick(saved_pieces, lax.rem(x_here + turn, 2)), ('row', 'col'...  8.74 us
    dot_general x6, matrix products, contract_last(): lax.dot_general(left_side, right_side, (((1,), (1,)), ((), ())), preferre...  8.31 us
    ppermute x1, starting transfers between devices, local(): w_left = lax.ppermute(w_both, 'col', x_shift(1))  7.07 us
  transfers between devices with their start and end apart: 15, of which 8 were waited for; matrix products, arithmetic and copies ran while one was open for 15% of the time, Pallas kernels for 0%

profile of v4, /device:TPU:6, one launch (start us, length us, event | category | flops | bytes accessed | tf_op | source)
XLA Modules:
  0.0 229.4 jit_solution(8975820079927153762)
XLA Ops:
  7.2 0.7 all-gather.3.cloned.1.call-update
  8.0 1.0 pad_maximum_fusion.4
  9.0 3.0 %collective-permute-start.1 = (bf16[72,768]{1,0:T(8,128)(2,1)S(1)}, bf16[72,768]{1,0:T(8,128)(2,1)S(1)}, u32[]{:S(2)}, u32[]{:S(2)}) collective-permute-start(bf16[72,768]{1,0:T(8,128)(2,1)S(1)} %get-tuple-element.58), channel_id=1, source_target_pairs={{0,0},{1,1},{2,2},{3,3},{4,4},{5,5},{6,6},{7,7},{8,64},{9,65},{10,... | collective-permute-start | bytes 331784 | tf_op jit(solution)/shard_map/ppermute | solution.py:89
  12.0 3.8 %collective-permute-start.2 = (bf16[72,768]{1,0:T(8,128)(2,1)S(1)}, bf16[72,768]{1,0:T(8,128)(2,1)S(1)}, u32[]{:S(2)}, u32[]{:S(2)}) collective-permute-start(bf16[72,768]{1,0:T(8,128)(2,1)S(1)} %get-tuple-element.59), channel_id=1, source_target_pairs={{0,64},{1,65},{2,66},{3,67},{4,68},{5,69},{6,70},{7,71},{8,0},{9,1... | collective-permute-start | bytes 331784 | tf_op jit(solution)/shard_map/ppermute | solution.py:89
  15.8 4.2 %collective-permute-done.1 = bf16[72,768]{1,0:T(8,128)(2,1)S(1)} collective-permute-done((bf16[72,768]{1,0:T(8,128)(2,1)S(1)}, bf16[72,768]{1,0:T(8,128)(2,1)S(1)}, u32[]{:S(2)}, u32[]{:S(2)}) %collective-permute-start.1) | collective-permute-done | bytes 110624 | tf_op jit(solution)/shard_map/ppermute | solution.py:89
  20.0 4.5 %collective-permute-done.2 = bf16[72,768]{1,0:T(8,128)(2,1)S(1)} collective-permute-done((bf16[72,768]{1,0:T(8,128)(2,1)S(1)}, bf16[72,768]{1,0:T(8,128)(2,1)S(1)}, u32[]{:S(2)}, u32[]{:S(2)}) %collective-permute-start.2) | collective-permute-done | bytes 110624 | tf_op jit(solution)/shard_map/ppermute | solution.py:89
  24.6 0.7 pad_maximum_fusion.5
  25.3 0.9 broadcast_in_dim.6
  26.2 10.3 %all-to-all-start = ((bf16[8,72,512]{2,1,0:T(8,128)(2,1)}), bf16[8,72,512]{2,1,0:T(8,128)(2,1)S(1)}, u32[]{:S(2)}, u32[]{:S(2)}) async-start(bf16[8,72,512]{2,1,0:T(8,128)(2,1)} %broadcast_in_dim.6), calls=%async_computation | async-start | bytes 1179648 | tf_op jit(solution)/shard_map/all_to_all | solution.py:39
  36.5 1.0 pad_maximum_fusion.3
  37.5 18.1 %all-to-all-done = bf16[8,72,512]{2,1,0:T(8,128)(2,1)S(1)} async-done(((bf16[8,72,512]{2,1,0:T(8,128)(2,1)}), bf16[8,72,512]{2,1,0:T(8,128)(2,1)S(1)}, u32[]{:S(2)}, u32[]{:S(2)}) %all-to-all-start) | async-done | bytes 589856 | tf_op jit(solution)/shard_map/all_to_all | solution.py:39
  55.7 3.0 %convolution_convert_fusion = bf16[576,768]{1,0:T(8,128)(2,1)} fusion(bf16[576,512]{1,0:T(8,128)(2,1)S(1)} %bitcast.186, bf16[2,768,512]{2,1,0:T(8,128)(2,1)} %bitcast.190, s32[]{:T(128)S(6)} %select_n.55), kind=kOutput, calls=%fused_computation.45 | convolution fusion | flops 453427200 | bytes 2260996 | tf_op jit(solution)/shard_map/dot_general | solution.py:11
  58.6 1.9 collective-permute-start
  60.6 0.9 broadcast_in_dim.7
  61.5 3.5 %all-to-all-start.1 = ((bf16[8,72,512]{2,1,0:T(8,128)(2,1)}), bf16[8,72,512]{2,1,0:T(8,128)(2,1)S(1)}, u32[]{:S(2)}, u32[]{:S(2)}) async-start(bf16[8,72,512]{2,1,0:T(8,128)(2,1)} %broadcast_in_dim.7), calls=%async_computation.1 | async-start | bytes 1179648 | tf_op jit(solution)/shard_map/all_to_all | solution.py:39
  65.1 2.7 %add_convert_fusion = bf16[576,768]{1,0:T(8,128)(2,1)} fusion(bf16[576,768]{1,0:T(8,128)(2,1)} %collective-permute-done, bf16[576,512]{1,0:T(8,128)(2,1)S(1)} %bitcast.187, bf16[2,768,512]{2,1,0:T(8,128)(2,1)S(1)} %bitcast.191, s32[]{:T(128)S(6)} %select_n.54), kind=kOutput, calls=%fused_computation.42 | convolution fusion | flops 455196672 | bytes 3145732 | tf_op jit(solution)/shard_map/dot_general | solution.py:11
  67.8 17.0 %all-to-all-done.1 = bf16[8,72,512]{2,1,0:T(8,128)(2,1)S(1)} async-done(((bf16[8,72,512]{2,1,0:T(8,128)(2,1)}), bf16[8,72,512]{2,1,0:T(8,128)(2,1)S(1)}, u32[]{:S(2)}, u32[]{:S(2)}) %all-to-all-start.1) | async-done | bytes 589856 | tf_op jit(solution)/shard_map/all_to_all | solution.py:39
  84.8 0.8 copy-done.9
  85.7 4.3 %all-to-all-start.2 = ((bf16[8,72,768]{2,1,0:T(8,128)(2,1)}), bf16[8,72,768]{2,1,0:T(8,128)(2,1)S(1)}, u32[]{:S(2)}, u32[]{:S(2)}) async-start(bf16[8,72,768]{2,1,0:T(8,128)(2,1)} %bitcast.5), calls=%async_computation.2 | async-start | bytes 1769472 | tf_op jit(solution)/shard_map/all_to_all | solution.py:39
  90.0 7.1 %collective-permute-start.3 = (bf16[512,768]{1,0:T(8,128)(2,1)}, bf16[512,768]{1,0:T(8,128)(2,1)}, u32[]{:S(2)}, u32[]{:S(2)}) collective-permute-start(bf16[512,768]{1,0:T(8,128)(2,1)} %pad_maximum_fusion.3), channel_id=1, source_target_pairs={{0,8},{1,9},{2,10},{3,11},{4,12},{5,13},{6,14},{7,15},{8,16},{9,17... | collective-permute-start | bytes 2359304 | tf_op jit(solution)/shard_map/ppermute | solution.py:106
  97.1 1.9 collective-permute-start.4
  99.0 15.1 %collective-permute-done.3 = bf16[512,768]{1,0:T(8,128)(2,1)} collective-permute-done((bf16[512,768]{1,0:T(8,128)(2,1)}, bf16[512,768]{1,0:T(8,128)(2,1)}, u32[]{:S(2)}, u32[]{:S(2)}) %collective-permute-start.3) | collective-permute-done | bytes 786464 | tf_op jit(solution)/shard_map/ppermute | solution.py:106
  114.1 5.6 %collective-permute-start.5 = (bf16[512,768]{1,0:T(8,128)(2,1)}, bf16[512,768]{1,0:T(8,128)(2,1)}, u32[]{:S(2)}, u32[]{:S(2)}) collective-permute-start(bf16[512,768]{1,0:T(8,128)(2,1)} %collective-permute-done.3), channel_id=1, source_target_pairs={{0,8},{1,9},{2,10},{3,11},{4,12},{5,13},{6,14},{7,15},{8,16},{9,17... | collective-permute-start | bytes 2359304 | tf_op jit(solution)/shard_map/ppermute | solution.py:108
  119.9 1.0 broadcast_in_dim.8
  120.9 6.9 %all-to-all-start.3 = ((bf16[8,72,768]{2,1,0:T(8,128)(2,1)}), bf16[8,72,768]{2,1,0:T(8,128)(2,1)}, u32[]{:S(2)}, u32[]{:S(2)}) async-start(bf16[8,72,768]{2,1,0:T(8,128)(2,1)} %broadcast_in_dim.8), calls=%async_computation.3 | async-start | bytes 1769472 | tf_op jit(solution)/shard_map/all_to_all | solution.py:39
  127.9 1.9 fusion.27
  130.4 1.1 fusion.20
  131.5 0.8 convolution_convert_fusion.3
  132.3 0.8 convolution_convert_fusion.2
  133.2 1.3 pad_maximum_fusion.2
  134.4 17.2 %all-to-all-done.3 = bf16[8,72,768]{2,1,0:T(8,128)(2,1)} async-done(((bf16[8,72,768]{2,1,0:T(8,128)(2,1)}), bf16[8,72,768]{2,1,0:T(8,128)(2,1)}, u32[]{:S(2)}, u32[]{:S(2)}) %all-to-all-start.3) | async-done | bytes 884768 | tf_op jit(solution)/shard_map/all_to_all | solution.py:39
  151.6 1.9 collective-permute-start.6
  153.8 2.5 %collective-permute-done.6 = bf16[8,72,768]{2,1,0:T(8,128)(2,1)} collective-permute-done((bf16[8,72,768]{2,1,0:T(8,128)(2,1)}, bf16[8,72,768]{2,1,0:T(8,128)(2,1)}, u32[]{:S(2)}, u32[]{:S(2)}) %collective-permute-start.6) | collective-permute-done | bytes 884768 | tf_op jit(solution)/shard_map/ppermute | solution.py:149
  156.3 3.2 %fusion.2 = (bf16[8,72,768]{2,1,0:T(8,128)(2,1)S(1)}, bf16[8,72,768]{2,1,0:T(8,128)(2,1)S(1)}, bf16[8,72,768]{2,1,0:T(8,128)(2,1)S(1)}, bf16[8,72,768]{2,1,0:T(8,128)(2,1)S(1)}) fusion(bf16[8,2,72,1536]{3,2,1,0:T(8,128)(2,1)S(1)} %bitcast.163, bf16[8,72,768]{2,1,0:T(8,128)(2,1)} %all-to-all-done.3, bf16[8,72,768]{2,1,0:T(8,128)(2,1)} %collective-permute-done.6, ...), kind=kLoop, calls=%fused_computation.8 | loop fusion | flops 15040512 | bytes 8847362 | tf_op jit(solution)/shard_map/convert_element_type | solution.py:29
  163.9 1.9 pad_maximum_fusion.1
  165.9 2.1 pad_maximum_fusion
  168.6 1.0 copy-done.8
  169.6 0.7 fusion.36
  170.3 0.7 fusion.32
  171.4 0.7 fusion.40
  172.2 0.7 fusion.26
  172.8 21.8 %all_to_all.25 = bf16[8,72,512]{2,1,0:T(8,128)(2,1)S(1)} all-to-all(bf16[8,72,512]{2,1,0:T(8,128)(2,1)S(1)} %bitcast.167), channel_id=1, replica_groups={{0,1,2,3,4,5,6,7},{8,9,10,11,12,13,14,15},{16,17,18,19,20,21,22,23},{24..., dimensions={0} | all-to-all | bytes 1179648 | tf_op jit(solution)/shard_map/all_to_all | solution.py:39
  194.7 0.7 reduce_sum.25
  195.4 1.8 multiply_convert_fusion.1
  197.2 22.5 %reduce-scatter.3.cloned.1.call-done = bf16[1,512,768]{1,2,0:T(8,128)(2,1)} async-done(((bf16[4,512,768]{1,2,0:T(8,128)(2,1)}), bf16[1,512,768]{1,2,0:T(8,128)(2,1)}) %reduce-scatter.3.cloned.1.call-update) | async-done | bytes 786448 | tf_op jit(solution)/shard_map/reduce_scatter | solution.py:162
  219.7 1.3 fusion.28
  221.1 0.9 copy.18
  222.0 0.9 copy.17
  (70 shorter events, 6.8 us)
Async XLA Ops:
  7.2 18.1 %copy-start.15 = (bf16[72,512]{1,0:T(8,128)(2,1)S(1)}, bf16[72,512]{1,0:T(8,128)(2,1)}, u32[]{:S(2)}) copy-start(bf16[72,512]{1,0:T(8,128)(2,1)} %param.8) | copy-start | bytes 221188
  7.2 48.5 %all-gather.3.cloned.1.call-start = ((), (), s32[]{:S(2)}) async-start(), calls=%async_computation.7 | async-start | bytes 1966080 | tf_op jit(solution)/shard_map/all_gather | solution.py:79
  7.9 119.9 %all-gather.5.cloned.1.call-start = ((), (), s32[]{:S(2)}) async-start(), calls=%async_computation.8 | async-start | bytes 3760128 | tf_op jit(solution)/shard_map/all_gather | solution.py:100
  9.0 27.5 %copy-start.13 = (bf16[512,384]{1,0:T(8,128)(2,1)S(1)}, bf16[512,384]{1,0:T(8,128)(2,1)}, u32[]{:S(2)}) copy-start(bf16[512,384]{1,0:T(8,128)(2,1)} %param.12) | copy-start | bytes 1179652
  9.0 27.5 %copy-start.14 = (bf16[512,384]{1,0:T(8,128)(2,1)S(1)}, bf16[512,384]{1,0:T(8,128)(2,1)}, u32[]{:S(2)}) copy-start(bf16[512,384]{1,0:T(8,128)(2,1)} %param.11) | copy-start | bytes 1179652
  9.0 11.0 %collective-permute-start.1 = (bf16[72,768]{1,0:T(8,128)(2,1)S(1)}, bf16[72,768]{1,0:T(8,128)(2,1)S(1)}, u32[]{:S(2)}, u32[]{:S(2)}) collective-permute-start(bf16[72,768]{1,0:T(8,128)(2,1)S(1)} %get-tuple-element.58), channel_id=1, source_target_pairs={{0,0},{1,1},{2,2},{3,3},{4,4},{5,5},{6,6},{7,7},{8,64},{9,65},{10,... | collective-permute-start | bytes 331784 | tf_op jit(solution)/shard_map/ppermute | solution.py:89
  12.0 12.5 %collective-permute-start.2 = (bf16[72,768]{1,0:T(8,128)(2,1)S(1)}, bf16[72,768]{1,0:T(8,128)(2,1)S(1)}, u32[]{:S(2)}, u32[]{:S(2)}) collective-permute-start(bf16[72,768]{1,0:T(8,128)(2,1)S(1)} %get-tuple-element.59), channel_id=1, source_target_pairs={{0,64},{1,65},{2,66},{3,67},{4,68},{5,69},{6,70},{7,71},{8,0},{9,1... | collective-permute-start | bytes 331784 | tf_op jit(solution)/shard_map/ppermute | solution.py:89
  26.2 29.5 %all-to-all-start = ((bf16[8,72,512]{2,1,0:T(8,128)(2,1)}), bf16[8,72,512]{2,1,0:T(8,128)(2,1)S(1)}, u32[]{:S(2)}, u32[]{:S(2)}) async-start(bf16[8,72,512]{2,1,0:T(8,128)(2,1)} %broadcast_in_dim.6), calls=%async_computation | async-start | bytes 1179648 | tf_op jit(solution)/shard_map/all_to_all | solution.py:39
  36.5 24.1 %copy-start.16 = (bf16[72,512]{1,0:T(8,128)(2,1)S(1)}, bf16[72,512]{1,0:T(8,128)(2,1)}, u32[]{:S(2)}) copy-start(bf16[72,512]{1,0:T(8,128)(2,1)} %param.7) | copy-start | bytes 221188
  55.7 9.4 %copy-start.11 = (bf16[8,72,512]{2,1,0:T(8,128)(2,1)}, bf16[8,72,512]{2,1,0:T(8,128)(2,1)S(1)}, u32[]{:S(2)}) copy-start(bf16[8,72,512]{2,1,0:T(8,128)(2,1)S(1)} %all-to-all-done) | copy-start | bytes 1769476
  55.7 9.4 %copy-start.17 = (bf16[1536,512]{1,0:T(8,128)(2,1)S(1)}, bf16[1536,512]{1,0:T(8,128)(2,1)}, u32[]{:S(2)}) copy-start(bf16[1536,512]{1,0:T(8,128)(2,1)} %all-gather.3.cloned.1.call-done) | copy-start | bytes 4718596
  58.6 6.4 %collective-permute-start = (bf16[576,768]{1,0:T(8,128)(2,1)}, bf16[576,768]{1,0:T(8,128)(2,1)}, u32[]{:S(2)}, u32[]{:S(2)}) collective-permute-start(bf16[576,768]{1,0:T(8,128)(2,1)} %convolution_convert_fusion), channel_id=1, source_target_pairs={{0,32},{32,0},{64,96},{96,64},{128,160},{160,128},{192,224},{224,1... | collective-permute-start | bytes 2654216 | tf_op jit(solution)/shard_map/ppermute | solution.py:111
  61.5 23.3 %all-to-all-start.1 = ((bf16[8,72,512]{2,1,0:T(8,128)(2,1)}), bf16[8,72,512]{2,1,0:T(8,128)(2,1)S(1)}, u32[]{:S(2)}, u32[]{:S(2)}) async-start(bf16[8,72,512]{2,1,0:T(8,128)(2,1)} %broadcast_in_dim.7), calls=%async_computation.1 | async-start | bytes 1179648 | tf_op jit(solution)/shard_map/all_to_all | solution.py:39
  84.8 0.8 copy-start.9
  85.7 34.1 %all-to-all-start.2 = ((bf16[8,72,768]{2,1,0:T(8,128)(2,1)}), bf16[8,72,768]{2,1,0:T(8,128)(2,1)S(1)}, u32[]{:S(2)}, u32[]{:S(2)}) async-start(bf16[8,72,768]{2,1,0:T(8,128)(2,1)} %bitcast.5), calls=%async_computation.2 | async-start | bytes 1769472 | tf_op jit(solution)/shard_map/all_to_all | solution.py:39
  90.0 24.1 %collective-permute-start.3 = (bf16[512,768]{1,0:T(8,128)(2,1)}, bf16[512,768]{1,0:T(8,128)(2,1)}, u32[]{:S(2)}, u32[]{:S(2)}) collective-permute-start(bf16[512,768]{1,0:T(8,128)(2,1)} %pad_maximum_fusion.3), channel_id=1, source_target_pairs={{0,8},{1,9},{2,10},{3,11},{4,12},{5,13},{6,14},{7,15},{8,16},{9,17... | collective-permute-start | bytes 2359304 | tf_op jit(solution)/shard_map/ppermute | solution.py:106
  97.1 54.5 %collective-permute-start.4 = (bf16[512,768]{1,0:T(8,128)(2,1)}, bf16[512,768]{1,0:T(8,128)(2,1)}, u32[]{:S(2)}, u32[]{:S(2)}) collective-permute-start(bf16[512,768]{1,0:T(8,128)(2,1)} %pad_maximum_fusion.3), channel_id=1, source_target_pairs={{0,24},{1,25},{2,26},{3,27},{4,28},{5,29},{6,30},{7,31},{8,0},{9,1... | collective-permute-start | bytes 2359304 | tf_op jit(solution)/shard_map/ppermute | solution.py:107
  114.1 37.5 %collective-permute-start.5 = (bf16[512,768]{1,0:T(8,128)(2,1)}, bf16[512,768]{1,0:T(8,128)(2,1)}, u32[]{:S(2)}, u32[]{:S(2)}) collective-permute-start(bf16[512,768]{1,0:T(8,128)(2,1)} %collective-permute-done.3), channel_id=1, source_target_pairs={{0,8},{1,9},{2,10},{3,11},{4,12},{5,13},{6,14},{7,15},{8,16},{9,17... | collective-permute-start | bytes 2359304 | tf_op jit(solution)/shard_map/ppermute | solution.py:108
  120.9 30.7 %all-to-all-start.3 = ((bf16[8,72,768]{2,1,0:T(8,128)(2,1)}), bf16[8,72,768]{2,1,0:T(8,128)(2,1)}, u32[]{:S(2)}, u32[]{:S(2)}) async-start(bf16[8,72,768]{2,1,0:T(8,128)(2,1)} %broadcast_in_dim.8), calls=%async_computation.3 | async-start | bytes 1769472 | tf_op jit(solution)/shard_map/all_to_all | solution.py:39
  127.8 67.6 %reduce-scatter.5.cloned.1.call-start = ((), (), s32[]{:S(2)}) async-start(), calls=%async_computation.10 | async-start | bytes 1966080 | tf_op jit(solution)/shard_map/reduce_scatter | solution.py:130
  127.9 2.5 %copy-start = (bf16[1152,1536]{1,0:T(8,128)(2,1)S(1)}, bf16[1152,1536]{1,0:T(8,128)(2,1)}, u32[]{:S(2)}) copy-start(bf16[1152,1536]{1,0:T(8,128)(2,1)} %all-gather.5.cloned.1.call-done) | copy-start | bytes 10616836
  130.4 1.1 copy-start.12
  151.6 4.7 %collective-permute-start.6 = (bf16[8,72,768]{2,1,0:T(8,128)(2,1)}, bf16[8,72,768]{2,1,0:T(8,128)(2,1)}, u32[]{:S(2)}, u32[]{:S(2)}) collective-permute-start(bf16[8,72,768]{2,1,0:T(8,128)(2,1)} %all-to-all-done.3), channel_id=1, source_target_pairs={{0,32},{32,0},{64,96},{96,64},{128,160},{160,128},{192,224},{224,1... | collective-permute-start | bytes 2654216 | tf_op jit(solution)/shard_map/ppermute | solution.py:149
  153.5 66.2 %reduce-scatter.3.cloned.1.call-start = ((), (), s32[]{:S(2)}) async-start(), calls=%async_computation.9 | async-start | bytes 3932160 | tf_op jit(solution)/shard_map/reduce_scatter | solution.py:162
  153.8 5.7 %copy-start.10 = (bf16[8,72,512]{2,1,0:T(8,128)(2,1)S(1)}, bf16[8,72,512]{2,1,0:T(8,128)(2,1)}, u32[]{:S(2)}) copy-start(bf16[8,72,512]{2,1,0:T(8,128)(2,1)} %copy-done.9) | copy-start | bytes 1769476
  159.4 1.2 copy-start.1
  159.4 1.7 copy-start.5
  159.4 3.4 %copy-start.7 = (bf16[8,72,768]{2,1,0:T(8,128)(2,1)}, bf16[8,72,768]{2,1,0:T(8,128)(2,1)S(1)}, u32[]{:S(2)}) copy-start(bf16[8,72,768]{2,1,0:T(8,128)(2,1)S(1)} %get-tuple-element.35) | copy-start | bytes 2654212
  159.4 3.9 %copy-start.3 = (bf16[8,72,768]{2,1,0:T(8,128)(2,1)}, bf16[8,72,768]{2,1,0:T(8,128)(2,1)S(1)}, u32[]{:S(2)}) copy-start(bf16[8,72,768]{2,1,0:T(8,128)(2,1)S(1)} %get-tuple-element.37) | copy-start | bytes 2654212
  168.4 1.2 copy-start.8
  168.6 1.7 copy-start.6
  170.3 1.2 copy-start.4
  170.9 1.2 copy-start.2
Sparse Core Ops, SparseCore 0:
  10.1 35.3 all-gather.2
  48.2 45.1 all-gather.4
  153.7 20.7 reduce-scatter.4
  177.2 42.4 reduce-scatter.2

commit v5 on v4

--- a/solution.py
+++ b/solution.py
@@ -81,8 +81,6 @@
     ).reshape(N_CORE, half, features)
 
     grad_rows = spread(out_grad, N_Z, "col", z_groups).reshape(group_rows, features)
-    tokens, grad_rows = lax.optimization_barrier((tokens, grad_rows))
-    token_rows = spread(tokens, N_Z, "col", z_groups).reshape(group_rows, features)
 
     saved_pieces = jnp.concatenate([gate_pre, up_pre], axis=1).reshape(2, block, half)
     moved = [
@@ -101,6 +99,12 @@
         n_y, N_CORE, block, 2 * half
     )
 
+    both = jnp.concatenate([tokens, out_grad], axis=1)
+    both, saved_share = lax.optimization_barrier((both, saved_share))
+    token_rows = lax.all_gather(both, "col", axis=0, tiled=True, axis_index_groups=z_groups)[
+        :, :features
+    ]
+
     w_both = jnp.concatenate([w_gate, w_up], axis=1)
     w_both, down_all = lax.optimization_barrier((w_both, down_all))
     w_left = lax.ppermute(w_both, "col", x_shift(1))
@@ -111,7 +115,6 @@
     got = lax.ppermute(give, "row", core_swap)
     keep = contract_last(grad_rows, pick(down_all, core)).astype(jnp.bfloat16)
     pair = (keep.astype(jnp.float32) + got.astype(jnp.float32)).astype(jnp.bfloat16)
-    pair, token_rows = lax.optimization_barrier((pair, token_rows))
     terms = exchange(pair.reshape(n_y, block, half), "row", y_groups)
     share = jnp.sum(terms.astype(jnp.float32), axis=0).astype(jnp.bfloat16)
     own = spread(share, n_y, "row", y_groups)
@@ -134,7 +137,6 @@
         tiled=True,
         axis_index_groups=x_groups,
     )
-    down_wgrad = (down_sum.astype(jnp.float32) * grad_scale).astype(jnp.bfloat16)
 
     own, w_left, w_right, w_far = lax.optimization_barrier((own, w_left, w_right, w_far))
     w_stack = jnp.stack([w_both, w_left, w_far, w_right])
@@ -159,17 +161,20 @@
             columns = slice(slot * units, (slot + 1) * units)
             gate_part.append(contract_first(token_rows, gate_grad[:, columns]))
             up_part.append(contract_first(token_rows, up_grad[:, columns]))
-    unit_sum = lax.psum_scatter(
-        jnp.stack(
-            [jnp.concatenate(parts, axis=1) for parts in zip(gate_part, up_part)]
-        ).astype(jnp.bfloat16),
-        "col",
-        scatter_dimension=0,
-        tiled=True,
-        axis_index_groups=x_groups,
-    )[0]
-    unit_wgrad = (unit_sum.astype(jnp.float32) * grad_scale).astype(jnp.bfloat16)
-    gate_wgrad, up_wgrad = unit_wgrad[:, :units], unit_wgrad[:, units:]
+    gate_wgrad, up_wgrad = (
+        lax.psum_scatter(
+            jnp.stack(parts).astype(jnp.bfloat16),
+            "col",
+            scatter_dimension=0,
+            tiled=True,
+            axis_index_groups=x_groups,
+        )[0]
+        for parts in (gate_part, up_part)
+    )
+    gate_wgrad = (gate_wgrad.astype(jnp.float32) * grad_scale).astype(jnp.bfloat16)
+    up_wgrad = (up_wgrad.astype(jnp.float32) * grad_scale).astype(jnp.bfloat16)
+    part_in, down_sum = lax.optimization_barrier((part_in, down_sum))
+    down_wgrad = (down_sum.astype(jnp.float32) * grad_scale).astype(jnp.bfloat16)
     token_terms = exchange(
         part_in.astype(jnp.bfloat16).reshape(N_Z, block, features), "col", z_groups
     )

time: 233 us -> 263 us (1.13)
  waiting for transfers between devices: 102 us -> 152 us
  blocking collectives: 21.8 us -> 0 us
  matrix products: 14.1 us -> 19.4 us
  local copies, waits for them, and re-layouts: 8.33 us -> 4.37 us
    reduce_scatter x1 -> x2, waiting for transfers between devices: 22.5 us -> 56.5 us  [local(): lax.psum_scatter(jnp.stack(parts).astype(jnp.bfloat16), 'col', scatter_di...]
    all_to_all x1 -> x0, blocking collectives: 21.8 us -> none  [exchange(): lax.all_to_all(pieces, axis, 0, 0, tiled=True, axis_index_groups=groups)]
    all_to_all x4, waiting for transfers between devices: 52.4 us -> 33.4 us  [exchange(): lax.all_to_all(pieces, axis, 0, 0, tiled=True, axis_index_groups=groups)]
    reduce_scatter x1, waiting for transfers between devices: 0.01 us -> 13.5 us  [local(): lax.psum_scatter(down_part, 'col', scatter_dimension=0, tiled=True, axis_...]
    all_gather x0 -> x1, waiting for transfers between devices: none -> 10.6 us  [local(): lax.all_gather(both, 'col', axis=0, tiled=True, axis_index_groups=z_groups)]
    all_gather x1, waiting for transfers between devices: 0.01 us -> 8.93 us  [local(): lax.all_gather(w_down, 'col', axis=0, tiled=True, axis_index_groups=x_gro...]
    dot_general x10, matrix products: 5.74 us -> 10.5 us  [contract_first(): lax.dot_general(left_side, right_side, (((0,), (0,)), ((), ())), preferre...]
    unnamed x38 -> x32, local copies, waits for them, and re-layouts: 4.93 us -> 1.95 us
  transfers between devices with their start and end apart: 15 -> 17, of which waited for: 8 -> 13; matrix products, arithmetic and copies ran while one was open for 15% -> 16% of each run, Pallas kernels for 0% -> 0%
where the time goes in v5:
time: 263 us; the launch traced here: 261 us
  waiting for transfers between devices  152 us (58%)
  starting transfers between devices  50.7 us (19%)
  other arithmetic  19.5 us (7%)
  matrix products  19.4 us (7%)
  between operations  14.7 us (6%)
  local copies, waits for them, and re-layouts  4.37 us (2%)
    reduce_scatter x2, waiting for transfers between devices, local(): lax.psum_scatter(jnp.stack(parts).astype(jnp.bfloat16), 'col', scatter_di...  56.5 us
    all_to_all x4, waiting for transfers between devices, exchange(): lax.all_to_all(pieces, axis, 0, 0, tiled=True, axis_index_groups=groups)  33.4 us
    all_to_all x4, starting transfers between devices, exchange(): lax.all_to_all(pieces, axis, 0, 0, tiled=True, axis_index_groups=groups)  25.2 us
    ppermute x1, waiting for transfers between devices, local(): w_left = lax.ppermute(w_both, 'col', x_shift(1))  14.9 us
    reduce_scatter x1, waiting for transfers between devices, local(): lax.psum_scatter(down_part, 'col', scatter_dimension=0, tiled=True, axis_...  13.5 us
    all_gather x1, waiting for transfers between devices, local(): lax.all_gather(both, 'col', axis=0, tiled=True, axis_index_groups=z_groups)  10.6 us
    dot_general x10, matrix products, contract_first(): lax.dot_general(left_side, right_side, (((0,), (0,)), ((), ())), preferre...  10.5 us
    all_gather x1, waiting for transfers between devices, local(): lax.all_gather(w_down, 'col', axis=0, tiled=True, axis_index_groups=x_gro...  8.93 us
  transfers between devices with their start and end apart: 17, of which 13 were waited for; matrix products, arithmetic and copies ran while one was open for 16% of the time, Pallas kernels for 0%

profile of v5, /device:TPU:6, one launch (start us, length us, event | category | flops | bytes accessed | tf_op | source)
XLA Modules:
  0.0 260.8 jit_solution(3803142602669096345)
XLA Ops:
  7.2 0.7 all-gather.4.cloned.1.call-update
  8.0 1.0 pad_maximum_fusion.5
  9.0 3.0 %collective-permute-start.1 = (bf16[72,768]{1,0:T(8,128)(2,1)S(1)}, bf16[72,768]{1,0:T(8,128)(2,1)S(1)}, u32[]{:S(2)}, u32[]{:S(2)}) collective-permute-start(bf16[72,768]{1,0:T(8,128)(2,1)S(1)} %get-tuple-element.42), channel_id=1, source_target_pairs={{0,0},{1,1},{2,2},{3,3},{4,4},{5,5},{6,6},{7,7},{8,64},{9,65},{10,... | collective-permute-start | bytes 331784 | tf_op jit(solution)/shard_map/ppermute | solution.py:87
  12.0 3.8 %collective-permute-start.2 = (bf16[72,768]{1,0:T(8,128)(2,1)S(1)}, bf16[72,768]{1,0:T(8,128)(2,1)S(1)}, u32[]{:S(2)}, u32[]{:S(2)}) collective-permute-start(bf16[72,768]{1,0:T(8,128)(2,1)S(1)} %get-tuple-element.43), channel_id=1, source_target_pairs={{0,64},{1,65},{2,66},{3,67},{4,68},{5,69},{6,70},{7,71},{8,0},{9,1... | collective-permute-start | bytes 331784 | tf_op jit(solution)/shard_map/ppermute | solution.py:87
  15.8 4.2 %collective-permute-done.1 = bf16[72,768]{1,0:T(8,128)(2,1)S(1)} collective-permute-done((bf16[72,768]{1,0:T(8,128)(2,1)S(1)}, bf16[72,768]{1,0:T(8,128)(2,1)S(1)}, u32[]{:S(2)}, u32[]{:S(2)}) %collective-permute-start.1) | collective-permute-done | bytes 110624 | tf_op jit(solution)/shard_map/ppermute | solution.py:87
  20.0 4.5 %collective-permute-done.2 = bf16[72,768]{1,0:T(8,128)(2,1)S(1)} collective-permute-done((bf16[72,768]{1,0:T(8,128)(2,1)S(1)}, bf16[72,768]{1,0:T(8,128)(2,1)S(1)}, u32[]{:S(2)}, u32[]{:S(2)}) %collective-permute-start.2) | collective-permute-done | bytes 110624 | tf_op jit(solution)/shard_map/ppermute | solution.py:87
  24.6 0.7 pad_maximum_fusion.6
  25.3 0.9 broadcast_in_dim.4
  26.2 10.3 %all-to-all-start = ((bf16[8,72,512]{2,1,0:T(8,128)(2,1)}), bf16[8,72,512]{2,1,0:T(8,128)(2,1)S(1)}, u32[]{:S(2)}, u32[]{:S(2)}) async-start(bf16[8,72,512]{2,1,0:T(8,128)(2,1)} %broadcast_in_dim.4), calls=%async_computation | async-start | bytes 1179648 | tf_op jit(solution)/shard_map/all_to_all | solution.py:39
  36.6 8.9 %all-gather.4.cloned.1.call-done = bf16[1536,512]{1,0:T(8,128)(2,1)} async-done(((bf16[384,512]{1,0:T(8,128)(2,1)}), bf16[1536,512]{1,0:T(8,128)(2,1)}) %all-gather.4.cloned.1.call-update) | async-done | bytes 1572880 | tf_op jit(solution)/shard_map/all_gather | solution.py:79
  45.5 10.2 %all-to-all-done = bf16[8,72,512]{2,1,0:T(8,128)(2,1)S(1)} async-done(((bf16[8,72,512]{2,1,0:T(8,128)(2,1)}), bf16[8,72,512]{2,1,0:T(8,128)(2,1)S(1)}, u32[]{:S(2)}, u32[]{:S(2)}) %all-to-all-start) | async-done | bytes 589856 | tf_op jit(solution)/shard_map/all_to_all | solution.py:39
  55.7 2.7 %fusion.21 = bf16[576,768]{1,0:T(8,128)(2,1)} fusion(bf16[576,512]{1,0:T(8,128)(2,1)S(1)} %bitcast.134, bf16[2,768,512]{2,1,0:T(8,128)(2,1)} %bitcast.136, s32[]{:T(128)S(6)} %select_n.55), kind=kOutput, calls=%fused_computation.43 | convolution fusion | flops 453427200 | bytes 2260996 | tf_op jit(solution)/shard_map/dot_general | solution.py:11
  58.4 1.9 collective-permute-start
  60.3 2.6 collective-permute-done
  62.9 2.8 %fusion.18 = bf16[576,768]{1,0:T(8,128)(2,1)} fusion(bf16[576,768]{1,0:T(8,128)(2,1)S(1)} %collective-permute-done, bf16[576,512]{1,0:T(8,128)(2,1)S(1)} %bitcast.135, bf16[2,768,512]{2,1,0:T(8,128)(2,1)} %bitcast.137, s32[]{:T(128)S(6)} %select_n.54), kind=kOutput, calls=%fused_computation.32 | convolution fusion | flops 455196672 | bytes 3145732 | tf_op jit(solution)/shard_map/dot_general | solution.py:11
  65.7 4.4 %all-to-all-start.1 = ((bf16[8,72,768]{2,1,0:T(8,128)(2,1)}), bf16[8,72,768]{2,1,0:T(8,128)(2,1)S(1)}, u32[]{:S(2)}, u32[]{:S(2)}) async-start(bf16[8,72,768]{2,1,0:T(8,128)(2,1)} %bitcast.6), calls=%async_computation.1 | async-start | bytes 1769472 | tf_op jit(solution)/shard_map/all_to_all | solution.py:39
  70.1 0.7 pad_maximum_fusion.7
  70.8 6.9 %collective-permute-start.3 = (bf16[512,768]{1,0:T(8,128)(2,1)S(1)}, bf16[512,768]{1,0:T(8,128)(2,1)S(1)}, u32[]{:S(2)}, u32[]{:S(2)}) collective-permute-start(bf16[512,768]{1,0:T(8,128)(2,1)S(1)} %pad_maximum_fusion.4), channel_id=1, source_target_pairs={{0,8},{1,9},{2,10},{3,11},{4,12},{5,13},{6,14},{7,15},{8,16},{9,17... | collective-permute-start | bytes 2359304 | tf_op jit(solution)/shard_map/ppermute | solution.py:110
  77.8 1.9 collective-permute-start.4
  79.7 14.9 %collective-permute-done.3 = bf16[512,768]{1,0:T(8,128)(2,1)S(1)} collective-permute-done((bf16[512,768]{1,0:T(8,128)(2,1)S(1)}, bf16[512,768]{1,0:T(8,128)(2,1)S(1)}, u32[]{:S(2)}, u32[]{:S(2)}) %collective-permute-start.3) | collective-permute-done | bytes 786464 | tf_op jit(solution)/shard_map/ppermute | solution.py:110
  94.6 5.6 %collective-permute-start.5 = (bf16[512,768]{1,0:T(8,128)(2,1)S(1)}, bf16[512,768]{1,0:T(8,128)(2,1)}, u32[]{:S(2)}, u32[]{:S(2)}) collective-permute-start(bf16[512,768]{1,0:T(8,128)(2,1)S(1)} %collective-permute-done.3), channel_id=1, source_target_pairs={{0,8},{1,9},{2,10},{3,11},{4,12},{5,13},{6,14},{7,15},{8,16},{9,17... | collective-permute-start | bytes 2359304 | tf_op jit(solution)/shard_map/ppermute | solution.py:112
  100.2 4.8 %all-to-all-done.1 = bf16[8,72,768]{2,1,0:T(8,128)(2,1)S(1)} async-done(((bf16[8,72,768]{2,1,0:T(8,128)(2,1)}), bf16[8,72,768]{2,1,0:T(8,128)(2,1)S(1)}, u32[]{:S(2)}, u32[]{:S(2)}) %all-to-all-start.1) | async-done | bytes 884768 | tf_op jit(solution)/shard_map/all_to_all | solution.py:39
  105.2 1.0 broadcast_in_dim.5
  106.1 3.5 %all-to-all-start.2 = ((bf16[8,72,768]{2,1,0:T(8,128)(2,1)}), bf16[8,72,768]{2,1,0:T(8,128)(2,1)S(1)}, u32[]{:S(2)}, u32[]{:S(2)}) async-start(bf16[8,72,768]{2,1,0:T(8,128)(2,1)} %broadcast_in_dim.5), calls=%async_computation.2 | async-start | bytes 1769472 | tf_op jit(solution)/shard_map/all_to_all | solution.py:39
  109.8 2.3 bitcast_convert_fusion
  112.1 2.3 bitcast_convert_fusion.1
  114.4 1.3 pad_maximum_fusion.1
  115.8 18.4 %all-to-all-done.2 = bf16[8,72,768]{2,1,0:T(8,128)(2,1)S(1)} async-done(((bf16[8,72,768]{2,1,0:T(8,128)(2,1)}), bf16[8,72,768]{2,1,0:T(8,128)(2,1)S(1)}, u32[]{:S(2)}, u32[]{:S(2)}) %all-to-all-start.2) | async-done | bytes 884768 | tf_op jit(solution)/shard_map/all_to_all | solution.py:39
  134.2 1.9 collective-permute-start.6
  136.1 2.4 collective-permute-done.6
  138.5 4.3 %fusion.9 = (bf16[8,72,768]{2,1,0:T(8,128)(2,1)S(1)}, bf16[8,72,768]{2,1,0:T(8,128)(2,1)S(1)}, bf16[8,72,768]{2,1,0:T(8,128)(2,1)}, bf16[8,72,768]{2,1,0:T(8,128)(2,1)}) fusion(bf16[8,2,72,1536]{3,2,1,0:T(8,128)(2,1)} %bitcast.118, bf16[8,72,768]{2,1,0:T(8,128)(2,1)S(1)} %all-to-all-done.2, bf16[8,72,768]{2,1,0:T(8,128)(2,1)S(1)} %collective-permute-done.6, ...), kind=kLoop, calls=%fused_computation.22 | loop fusion | flops 15040512 | bytes 8847362 | tf_op jit(solution)/shard_map/convert_element_type | solution.py:29
  142.8 10.6 %all-gather.8.cloned.1.call-done = bf16[576,1024]{1,0:T(8,128)(2,1)} async-done(((bf16[72,1024]{1,0:T(8,128)(2,1)}), bf16[576,1024]{1,0:T(8,128)(2,1)}) %all-gather.8.cloned.1.call-update) | async-done | bytes 1179664 | tf_op jit(solution)/shard_map/all_gather | solution.py:104
  153.4 1.7 fusion.25
  157.0 1.4 pad_maximum_fusion.2
  158.7 2.2 pad_maximum_fusion
  163.6 1.5 pad_maximum_fusion.3
  165.7 1.0 copy-done.8
  166.7 0.6 fusion.39
  167.4 0.7 fusion.35
  169.3 1.5 fusion.20
  170.8 13.5 %reduce-scatter.4.cloned.1.call-done = bf16[384,512]{1,0:T(8,128)(2,1)} async-done(((bf16[1536,512]{1,0:T(8,128)(2,1)}), bf16[384,512]{1,0:T(8,128)(2,1)}) %reduce-scatter.4.cloned.1.call-update) | async-done | bytes 393232 | tf_op jit(solution)/shard_map/reduce_scatter | solution.py:133
  184.4 6.9 %all-to-all-start.3 = ((bf16[8,72,512]{2,1,0:T(8,128)(2,1)}), bf16[8,72,512]{2,1,0:T(8,128)(2,1)S(1)}, u32[]{:S(2)}, u32[]{:S(2)}) async-start(bf16[8,72,512]{2,1,0:T(8,128)(2,1)} %bitcast.32), calls=%async_computation.4 | async-start | bytes 1179648 | tf_op jit(solution)/shard_map/all_to_all | solution.py:39
  191.3 1.8 multiply_convert_fusion
  193.1 24.8 %reduce-scatter.6.cloned.1.call-done = bf16[1,512,384]{2,1,0:T(8,128)(2,1)} async-done(((bf16[4,512,384]{2,1,0:T(8,128)(2,1)}), bf16[1,512,384]{2,1,0:T(8,128)(2,1)}) %reduce-scatter.6.cloned.1.call-update) | async-done | bytes 393232 | tf_op jit(solution)/shard_map/reduce_scatter | solution.py:165
  217.9 1.8 fusion.59
  219.7 31.7 %reduce-scatter.8.cloned.1.call-done = bf16[1,512,384]{2,1,0:T(8,128)(2,1)} async-done(((bf16[4,512,384]{2,1,0:T(8,128)(2,1)}), bf16[1,512,384]{2,1,0:T(8,128)(2,1)}) %reduce-scatter.8.cloned.1.call-update) | async-done | bytes 393232 | tf_op jit(solution)/shard_map/reduce_scatter | solution.py:165
  251.5 1.8 fusion.60
  253.3 0.7 reduce_sum.25
  (64 shorter events, 7.1 us)
Async XLA Ops:
  7.2 18.2 %copy-start.12 = (bf16[72,512]{1,0:T(8,128)(2,1)S(1)}, bf16[72,512]{1,0:T(8,128)(2,1)}, u32[]{:S(2)}) copy-start(bf16[72,512]{1,0:T(8,128)(2,1)} %param.8) | copy-start | bytes 221188
  7.2 38.3 %all-gather.4.cloned.1.call-start = ((), (), s32[]{:S(2)}) async-start(), calls=%async_computation.7 | async-start | bytes 1966080 | tf_op jit(solution)/shard_map/all_gather | solution.py:79
  7.9 101.9 %all-gather.6.cloned.1.call-start = ((), (), s32[]{:S(2)}) async-start(), calls=%async_computation.8 | async-start | bytes 3760128 | tf_op jit(solution)/shard_map/all_gather | solution.py:98
  9.0 27.5 %copy-start.10 = (bf16[512,384]{1,0:T(8,128)(2,1)S(1)}, bf16[512,384]{1,0:T(8,128)(2,1)}, u32[]{:S(2)}) copy-start(bf16[512,384]{1,0:T(8,128)(2,1)} %param.12) | copy-start | bytes 1179652
  9.0 27.5 %copy-start.11 = (bf16[512,384]{1,0:T(8,128)(2,1)S(1)}, bf16[512,384]{1,0:T(8,128)(2,1)}, u32[]{:S(2)}) copy-start(bf16[512,384]{1,0:T(8,128)(2,1)} %param.11) | copy-start | bytes 1179652
  9.0 11.0 %collective-permute-start.1 = (bf16[72,768]{1,0:T(8,128)(2,1)S(1)}, bf16[72,768]{1,0:T(8,128)(2,1)S(1)}, u32[]{:S(2)}, u32[]{:S(2)}) collective-permute-start(bf16[72,768]{1,0:T(8,128)(2,1)S(1)} %get-tuple-element.42), channel_id=1, source_target_pairs={{0,0},{1,1},{2,2},{3,3},{4,4},{5,5},{6,6},{7,7},{8,64},{9,65},{10,... | collective-permute-start | bytes 331784 | tf_op jit(solution)/shard_map/ppermute | solution.py:87
  12.0 12.5 %collective-permute-start.2 = (bf16[72,768]{1,0:T(8,128)(2,1)S(1)}, bf16[72,768]{1,0:T(8,128)(2,1)S(1)}, u32[]{:S(2)}, u32[]{:S(2)}) collective-permute-start(bf16[72,768]{1,0:T(8,128)(2,1)S(1)} %get-tuple-element.43), channel_id=1, source_target_pairs={{0,64},{1,65},{2,66},{3,67},{4,68},{5,69},{6,70},{7,71},{8,0},{9,1... | collective-permute-start | bytes 331784 | tf_op jit(solution)/shard_map/ppermute | solution.py:87
  26.2 29.5 %all-to-all-start = ((bf16[8,72,512]{2,1,0:T(8,128)(2,1)}), bf16[8,72,512]{2,1,0:T(8,128)(2,1)S(1)}, u32[]{:S(2)}, u32[]{:S(2)}) async-start(bf16[8,72,512]{2,1,0:T(8,128)(2,1)} %broadcast_in_dim.4), calls=%async_computation | async-start | bytes 1179648 | tf_op jit(solution)/shard_map/all_to_all | solution.py:39
  36.6 41.2 %copy-start.2 = (bf16[512,768]{1,0:T(8,128)(2,1)}, bf16[512,768]{1,0:T(8,128)(2,1)S(1)}, u32[]{:S(2)}) copy-start(bf16[512,768]{1,0:T(8,128)(2,1)S(1)} %pad_maximum_fusion.4) | copy-start | bytes 2359300
  58.4 4.5 %collective-permute-start = (bf16[576,768]{1,0:T(8,128)(2,1)}, bf16[576,768]{1,0:T(8,128)(2,1)S(1)}, u32[]{:S(2)}, u32[]{:S(2)}) collective-permute-start(bf16[576,768]{1,0:T(8,128)(2,1)} %fusion.21), channel_id=1, source_target_pairs={{0,32},{32,0},{64,96},{96,64},{128,160},{160,128},{192,224},{224,1... | collective-permute-start | bytes 2654216 | tf_op jit(solution)/shard_map/ppermute | solution.py:115
  60.3 9.8 %copy-start.13 = (bf16[72,512]{1,0:T(8,128)(2,1)S(1)}, bf16[72,512]{1,0:T(8,128)(2,1)}, u32[]{:S(2)}) copy-start(bf16[72,512]{1,0:T(8,128)(2,1)} %param.7) | copy-start | bytes 221188
  65.7 39.4 %all-to-all-start.1 = ((bf16[8,72,768]{2,1,0:T(8,128)(2,1)}), bf16[8,72,768]{2,1,0:T(8,128)(2,1)S(1)}, u32[]{:S(2)}, u32[]{:S(2)}) async-start(bf16[8,72,768]{2,1,0:T(8,128)(2,1)} %bitcast.6), calls=%async_computation.1 | async-start | bytes 1769472 | tf_op jit(solution)/shard_map/all_to_all | solution.py:39
  70.1 83.3 %all-gather.8.cloned.1.call-start = ((), (), s32[]{:S(2)}) async-start(), calls=%async_computation.10 | async-start | bytes 1327104 | tf_op jit(solution)/shard_map/all_gather | solution.py:104
  70.8 23.8 %collective-permute-start.3 = (bf16[512,768]{1,0:T(8,128)(2,1)S(1)}, bf16[512,768]{1,0:T(8,128)(2,1)S(1)}, u32[]{:S(2)}, u32[]{:S(2)}) collective-permute-start(bf16[512,768]{1,0:T(8,128)(2,1)S(1)} %pad_maximum_fusion.4), channel_id=1, source_target_pairs={{0,8},{1,9},{2,10},{3,11},{4,12},{5,13},{6,14},{7,15},{8,16},{9,17... | collective-permute-start | bytes 2359304 | tf_op jit(solution)/shard_map/ppermute | solution.py:110
  77.8 56.4 %collective-permute-start.4 = (bf16[512,768]{1,0:T(8,128)(2,1)S(1)}, bf16[512,768]{1,0:T(8,128)(2,1)}, u32[]{:S(2)}, u32[]{:S(2)}) collective-permute-start(bf16[512,768]{1,0:T(8,128)(2,1)S(1)} %pad_maximum_fusion.4), channel_id=1, source_target_pairs={{0,24},{1,25},{2,26},{3,27},{4,28},{5,29},{6,30},{7,31},{8,0},{9,1... | collective-permute-start | bytes 2359304 | tf_op jit(solution)/shard_map/ppermute | solution.py:111
  94.6 17.5 %copy-start.9 = (bf16[512,768]{1,0:T(8,128)(2,1)}, bf16[512,768]{1,0:T(8,128)(2,1)S(1)}, u32[]{:S(2)}) copy-start(bf16[512,768]{1,0:T(8,128)(2,1)S(1)} %collective-permute-done.3) | copy-start | bytes 2359300
  94.6 39.5 %collective-permute-start.5 = (bf16[512,768]{1,0:T(8,128)(2,1)S(1)}, bf16[512,768]{1,0:T(8,128)(2,1)}, u32[]{:S(2)}, u32[]{:S(2)}) collective-permute-start(bf16[512,768]{1,0:T(8,128)(2,1)S(1)} %collective-permute-done.3), channel_id=1, source_target_pairs={{0,8},{1,9},{2,10},{3,11},{4,12},{5,13},{6,14},{7,15},{8,16},{9,17... | collective-permute-start | bytes 2359304 | tf_op jit(solution)/shard_map/ppermute | solution.py:112
  106.1 28.0 %all-to-all-start.2 = ((bf16[8,72,768]{2,1,0:T(8,128)(2,1)}), bf16[8,72,768]{2,1,0:T(8,128)(2,1)S(1)}, u32[]{:S(2)}, u32[]{:S(2)}) async-start(bf16[8,72,768]{2,1,0:T(8,128)(2,1)} %broadcast_in_dim.5), calls=%async_computation.2 | async-start | bytes 1769472 | tf_op jit(solution)/shard_map/all_to_all | solution.py:39
  109.7 74.7 %reduce-scatter.4.cloned.1.call-start = ((), (), s32[]{:S(2)}) async-start(), calls=%async_computation.9 | async-start | bytes 1966080 | tf_op jit(solution)/shard_map/reduce_scatter | solution.py:133
  115.7 102.2 %reduce-scatter.6.cloned.1.call-start = ((), (), s32[]{:S(2)}) async-start(), calls=%async_computation.11 | async-start | bytes 1966080 | tf_op jit(solution)/shard_map/reduce_scatter | solution.py:165
  134.2 4.3 %collective-permute-start.6 = (bf16[8,72,768]{2,1,0:T(8,128)(2,1)S(1)}, bf16[8,72,768]{2,1,0:T(8,128)(2,1)S(1)}, u32[]{:S(2)}, u32[]{:S(2)}) collective-permute-start(bf16[8,72,768]{2,1,0:T(8,128)(2,1)S(1)} %all-to-all-done.2), channel_id=1, source_target_pairs={{0,32},{32,0},{64,96},{96,64},{128,160},{160,128},{192,224},{224,1... | collective-permute-start | bytes 2654216 | tf_op jit(solution)/shard_map/ppermute | solution.py:151
  142.8 13.0 %copy-start.7 = (bf16[8,72,768]{2,1,0:T(8,128)(2,1)}, bf16[8,72,768]{2,1,0:T(8,128)(2,1)S(1)}, u32[]{:S(2)}) copy-start(bf16[8,72,768]{2,1,0:T(8,128)(2,1)S(1)} %get-tuple-element.25) | copy-start | bytes 2654212
  142.8 13.6 %copy-start = (bf16[8,72,768]{2,1,0:T(8,128)(2,1)}, bf16[8,72,768]{2,1,0:T(8,128)(2,1)S(1)}, u32[]{:S(2)}) copy-start(bf16[8,72,768]{2,1,0:T(8,128)(2,1)S(1)} %get-tuple-element.24) | copy-start | bytes 2654212
  153.4 1.8 copy-start.14
  158.4 93.0 %reduce-scatter.8.cloned.1.call-start = ((), (), s32[]{:S(2)}) async-start(), calls=%async_computation.12 | async-start | bytes 1966080 | tf_op jit(solution)/shard_map/reduce_scatter | solution.py:165
  158.7 2.2 copy-start.5
  158.7 2.5 copy-start.15
  161.2 1.2 copy-start.3
  165.5 1.2 copy-start.8
  165.7 1.6 copy-start.6
  167.3 1.2 copy-start.4
  168.0 1.3 copy-start.1
  184.4 68.9 %all-to-all-start.3 = ((bf16[8,72,512]{2,1,0:T(8,128)(2,1)}), bf16[8,72,512]{2,1,0:T(8,128)(2,1)S(1)}, u32[]{:S(2)}, u32[]{:S(2)}) async-start(bf16[8,72,512]{2,1,0:T(8,128)(2,1)} %bitcast.32), calls=%async_computation.4 | async-start | bytes 1179648 | tf_op jit(solution)/shard_map/all_to_all | solution.py:39
Sparse Core Ops, SparseCore 0:
  10.1 35.3 all-gather.3
  48.2 58.6 all-gather.5
  109.6 43.7 all-gather.7
  156.1 28.1 reduce-scatter.3
  187.1 30.8 reduce-scatter.5
  220.6 30.7 reduce-scatter.7

commit v6 on v5

--- a/solution.py
+++ b/solution.py
@@ -76,9 +76,18 @@
                     pairs.append((r * n_col + x * N_Z + z, new_row * n_col + r // n_x * N_Z + z))
         return pairs
 
-    down_all = lax.all_gather(
-        w_down, "col", axis=0, tiled=True, axis_index_groups=x_groups
-    ).reshape(N_CORE, half, features)
+    down_stack = jnp.stack(
+        [w_down] + [lax.ppermute(w_down, "col", x_shift(step)) for step in range(1, n_x)]
+    )
+
+    def down_half(side):
+        first_block = 2 * lax.rem(core + side, 2)
+        return jnp.concatenate(
+            [
+                pick(down_stack, lax.rem(x_here - first_block - slot + n_x, n_x))
+                for slot in range(2)
+            ]
+        )
 
     grad_rows = spread(out_grad, N_Z, "col", z_groups).reshape(group_rows, features)
 
@@ -106,14 +115,14 @@
     ]
 
     w_both = jnp.concatenate([w_gate, w_up], axis=1)
-    w_both, down_all = lax.optimization_barrier((w_both, down_all))
+    w_both, grad_rows = lax.optimization_barrier((w_both, grad_rows))
     w_left = lax.ppermute(w_both, "col", x_shift(1))
     w_right = lax.ppermute(w_both, "col", x_shift(n_x - 1))
     w_far = lax.ppermute(w_left, "col", x_shift(1))
 
-    give = contract_last(grad_rows, pick(down_all, 1 - core)).astype(jnp.bfloat16)
+    give = contract_last(grad_rows, down_half(1)).astype(jnp.bfloat16)
     got = lax.ppermute(give, "row", core_swap)
-    keep = contract_last(grad_rows, pick(down_all, core)).astype(jnp.bfloat16)
+    keep = contract_last(grad_rows, down_half(0)).astype(jnp.bfloat16)
     pair = (keep.astype(jnp.float32) + got.astype(jnp.float32)).astype(jnp.bfloat16)
     terms = exchange(pair.reshape(n_y, block, half), "row", y_groups)
     share = jnp.sum(terms.astype(jnp.float32), axis=0).astype(jnp.bfloat16)
@@ -161,18 +170,20 @@
             columns = slice(slot * units, (slot + 1) * units)
             gate_part.append(contract_first(token_rows, gate_grad[:, columns]))
             up_part.append(contract_first(token_rows, up_grad[:, columns]))
-    gate_wgrad, up_wgrad = (
-        lax.psum_scatter(
-            jnp.stack(parts).astype(jnp.bfloat16),
-            "col",
-            scatter_dimension=0,
-            tiled=True,
-            axis_index_groups=x_groups,
-        )[0]
-        for parts in (gate_part, up_part)
-    )
-    gate_wgrad = (gate_wgrad.astype(jnp.float32) * grad_scale).astype(jnp.bfloat16)
-    up_wgrad = (up_wgrad.astype(jnp.float32) * grad_scale).astype(jnp.bfloat16)
+    gate_sum = lax.psum_scatter(
+        jnp.stack(gate_part).astype(jnp.bfloat16),
+        "col",
+        scatter_dimension=0,
+        tiled=True,
+        axis_index_groups=x_groups,
+    )[0]
+    gate_wgrad = (gate_sum.astype(jnp.float32) * grad_scale).astype(jnp.bfloat16)
+    up_stack = jnp.stack(up_part)
+    up_sum = pick(up_stack, x_here)
+    for step in range(1, n_x):
+        piece = pick(up_stack, lax.rem(x_here + step, n_x)).astype(jnp.bfloat16)
+        up_sum = up_sum + lax.ppermute(piece, "col", x_shift(step)).astype(jnp.float32)
+    up_wgrad = (up_sum * grad_scale).astype(jnp.bfloat16)
     part_in, down_sum = lax.optimization_barrier((part_in, down_sum))
     down_wgrad = (down_sum.astype(jnp.float32) * grad_scale).astype(jnp.bfloat16)
     token_terms = exchange(

time: 263 us -> 210 us (0.80)
  waiting for transfers between devices: 152 us -> 74.6 us
  starting transfers between devices: 50.7 us -> 71.8 us
  matrix products: 19.4 us -> 13.4 us
  local copies, waits for them, and re-layouts: 4.37 us -> 9.56 us
  other arithmetic: 19.5 us -> 22.4 us
    reduce_scatter x2 -> x1, waiting for transfers between devices: 56.5 us -> 1.29 us  [local(): lax.psum_scatter(jnp.stack(gate_part).astype(jnp.bfloat16), 'col', scatte...]
    ppermute x0 -> x6, waiting for transfers between devices: none -> 30.5 us  [the longest x3 15.7 us: local(): lax.ppermute(piece, 'col', x_shift(step)).astype(jnp.float32)]
    ppermute x0 -> x6, starting transfers between devices: none -> 18.1 us  [the longest x3 9.1 us: local(): lax.ppermute(piece, 'col', x_shift(step)).astype(jnp.float32)]
    all_to_all x4, waiting for transfers between devices: 33.4 us -> 17.1 us  [exchange(): lax.all_to_all(pieces, axis, 0, 0, tiled=True, axis_index_groups=groups)]
    reduce_scatter x1, waiting for transfers between devices: 13.5 us -> 0.01 us  [local(): lax.psum_scatter(down_part, 'col', scatter_dimension=0, tiled=True, axis_...]
    all_gather x1, waiting for transfers between devices: 10.6 us -> 0.02 us  [local(): lax.all_gather(both, 'col', axis=0, tiled=True, axis_index_groups=z_groups)]
    all_gather x1 -> x0, waiting for transfers between devices: 8.93 us -> none  [local(): lax.all_gather(w_down, 'col', axis=0, tiled=True, axis_index_groups=x_gro...]
    all_to_all x4, starting transfers between devices: 25.2 us -> 30.8 us  [exchange(): lax.all_to_all(pieces, axis, 0, 0, tiled=True, axis_index_groups=groups)]
  transfers between devices with their start and end apart: 17 -> 21, of which waited for: 13 -> 11; matrix products, arithmetic and copies ran while one was open for 16% -> 19% of each run, Pallas kernels for 0% -> 0%
where the time goes in v6:
time: 210 us; the launch traced here: 206 us
  waiting for transfers between devices  74.6 us (36%)
  starting transfers between devices  71.8 us (34%)
  other arithmetic  22.4 us (11%)
  between operations  14.5 us (7%)
  matrix products  13.4 us (6%)
  local copies, waits for them, and re-layouts  9.56 us (5%)
    all_to_all x4, starting transfers between devices, exchange(): lax.all_to_all(pieces, axis, 0, 0, tiled=True, axis_index_groups=groups)  30.8 us
    all_to_all x4, waiting for transfers between devices, exchange(): lax.all_to_all(pieces, axis, 0, 0, tiled=True, axis_index_groups=groups)  17.1 us
    ppermute x3, waiting for transfers between devices, local(): lax.ppermute(piece, 'col', x_shift(step)).astype(jnp.float32)  15.7 us
    ppermute x3, waiting for transfers between devices, local(): lax.ppermute(w_down, 'col', x_shift(step))  14.9 us
    ppermute x1, waiting for transfers between devices, local(): w_left = lax.ppermute(w_both, 'col', x_shift(1))  14.5 us
    ppermute x3, starting transfers between devices, local(): lax.ppermute(piece, 'col', x_shift(step)).astype(jnp.float32)  9.1 us
    ppermute x3, starting transfers between devices, local(): lax.ppermute(w_down, 'col', x_shift(step))  8.97 us
    ppermute x2, waiting for transfers between devices, local(): lax.ppermute(pick(saved_pieces, lax.rem(x_here + turn, 2)), ('row', 'col'...  8.72 us
  transfers between devices with their start and end apart: 21, of which 11 were waited for; matrix products, arithmetic and copies ran while one was open for 19% of the time, Pallas kernels for 0%

profile of v6, /device:TPU:6, one launch (start us, length us, event | category | flops | bytes accessed | tf_op | source)
XLA Modules:
  0.0 206.4 jit_solution(4269267060445955851)
XLA Ops:
  7.3 1.0 pad_maximum_fusion.6
  8.3 3.0 %collective-permute-start.4 = (bf16[72,768]{1,0:T(8,128)(2,1)S(1)}, bf16[72,768]{1,0:T(8,128)(2,1)S(1)}, u32[]{:S(2)}, u32[]{:S(2)}) collective-permute-start(bf16[72,768]{1,0:T(8,128)(2,1)S(1)} %get-tuple-element.53), channel_id=1, source_target_pairs={{0,0},{1,1},{2,2},{3,3},{4,4},{5,5},{6,6},{7,7},{8,64},{9,65},{10,... | collective-permute-start | bytes 331784 | tf_op jit(solution)/shard_map/ppermute | solution.py:96
  11.3 3.8 %collective-permute-start.5 = (bf16[72,768]{1,0:T(8,128)(2,1)S(1)}, bf16[72,768]{1,0:T(8,128)(2,1)S(1)}, u32[]{:S(2)}, u32[]{:S(2)}) collective-permute-start(bf16[72,768]{1,0:T(8,128)(2,1)S(1)} %get-tuple-element.54), channel_id=1, source_target_pairs={{0,64},{1,65},{2,66},{3,67},{4,68},{5,69},{6,70},{7,71},{8,0},{9,1... | collective-permute-start | bytes 331784 | tf_op jit(solution)/shard_map/ppermute | solution.py:96
  15.1 4.2 %collective-permute-done.4 = bf16[72,768]{1,0:T(8,128)(2,1)S(1)} collective-permute-done((bf16[72,768]{1,0:T(8,128)(2,1)S(1)}, bf16[72,768]{1,0:T(8,128)(2,1)S(1)}, u32[]{:S(2)}, u32[]{:S(2)}) %collective-permute-start.4) | collective-permute-done | bytes 110624 | tf_op jit(solution)/shard_map/ppermute | solution.py:96
  19.3 4.5 %collective-permute-done.5 = bf16[72,768]{1,0:T(8,128)(2,1)S(1)} collective-permute-done((bf16[72,768]{1,0:T(8,128)(2,1)S(1)}, bf16[72,768]{1,0:T(8,128)(2,1)S(1)}, u32[]{:S(2)}, u32[]{:S(2)}) %collective-permute-start.5) | collective-permute-done | bytes 110624 | tf_op jit(solution)/shard_map/ppermute | solution.py:96
  25.4 10.3 %all-to-all-start = ((bf16[8,72,512]{2,1,0:T(8,128)(2,1)}), bf16[8,72,512]{2,1,0:T(8,128)(2,1)S(1)}, u32[]{:S(2)}, u32[]{:S(2)}) async-start(bf16[8,72,512]{2,1,0:T(8,128)(2,1)} %broadcast_in_dim.4), calls=%async_computation | async-start | bytes 1179648 | tf_op jit(solution)/shard_map/all_to_all | solution.py:39
  35.8 2.1 collective-permute-start.2
  37.8 2.1 %collective-permute-start.1 = (bf16[384,512]{1,0:T(8,128)(2,1)S(1)}, bf16[384,512]{1,0:T(8,128)(2,1)S(1)}, u32[]{:S(2)}, u32[]{:S(2)}) collective-permute-start(bf16[384,512]{1,0:T(8,128)(2,1)S(1)} %copy-done.12), channel_id=1, source_target_pairs={{0,16},{1,17},{2,18},{3,19},{4,20},{5,21},{6,22},{7,23},{8,24},{9,... | collective-permute-start | bytes 1179656 | tf_op jit(solution)/shard_map/ppermute | solution.py:80
  39.9 4.8 %collective-permute-start = (bf16[384,512]{1,0:T(8,128)(2,1)S(1)}, bf16[384,512]{1,0:T(8,128)(2,1)S(1)}, u32[]{:S(2)}, u32[]{:S(2)}) collective-permute-start(bf16[384,512]{1,0:T(8,128)(2,1)S(1)} %copy-done.12), channel_id=1, source_target_pairs={{0,8},{1,9},{2,10},{3,11},{4,12},{5,13},{6,14},{7,15},{8,16},{9,17... | collective-permute-start | bytes 1179656 | tf_op jit(solution)/shard_map/ppermute | solution.py:80
  45.8 12.3 %collective-permute-done.2 = bf16[384,512]{1,0:T(8,128)(2,1)S(1)} collective-permute-done((bf16[384,512]{1,0:T(8,128)(2,1)S(1)}, bf16[384,512]{1,0:T(8,128)(2,1)S(1)}, u32[]{:S(2)}, u32[]{:S(2)}) %collective-permute-start.2) | collective-permute-done | bytes 393248 | tf_op jit(solution)/shard_map/ppermute | solution.py:80
  58.2 2.5 %collective-permute-done = bf16[384,512]{1,0:T(8,128)(2,1)S(1)} collective-permute-done((bf16[384,512]{1,0:T(8,128)(2,1)S(1)}, bf16[384,512]{1,0:T(8,128)(2,1)S(1)}, u32[]{:S(2)}, u32[]{:S(2)}) %collective-permute-start) | collective-permute-done | bytes 393248 | tf_op jit(solution)/shard_map/ppermute | solution.py:80
  61.7 1.9 collective-permute-start.3
  63.6 2.4 %collective-permute-done.3 = bf16[576,768]{1,0:T(8,128)(2,1)S(1)} collective-permute-done((bf16[576,768]{1,0:T(8,128)(2,1)S(1)}, bf16[576,768]{1,0:T(8,128)(2,1)S(1)}, u32[]{:S(2)}, u32[]{:S(2)}) %collective-permute-start.3) | collective-permute-done | bytes 884768 | tf_op jit(solution)/shard_map/ppermute | solution.py:124
  66.0 1.6 add_convert_fusion
  67.6 6.7 %all-to-all-start.1 = ((bf16[8,72,768]{2,1,0:T(8,128)(2,1)}), bf16[8,72,768]{2,1,0:T(8,128)(2,1)S(1)}, u32[]{:S(2)}, u32[]{:S(2)}) async-start(bf16[8,72,768]{2,1,0:T(8,128)(2,1)} %bitcast.9), calls=%async_computation.1 | async-start | bytes 1769472 | tf_op jit(solution)/shard_map/all_to_all | solution.py:39
  74.3 4.5 %collective-permute-start.6 = (bf16[512,768]{1,0:T(8,128)(2,1)}, bf16[512,768]{1,0:T(8,128)(2,1)}, u32[]{:S(2)}, u32[]{:S(2)}) collective-permute-start(bf16[512,768]{1,0:T(8,128)(2,1)} %pad_maximum_fusion.5), channel_id=1, source_target_pairs={{0,8},{1,9},{2,10},{3,11},{4,12},{5,13},{6,14},{7,15},{8,16},{9,17... | collective-permute-start | bytes 2359304 | tf_op jit(solution)/shard_map/ppermute | solution.py:119
  79.6 1.9 collective-permute-start.7
  81.5 14.5 %collective-permute-done.6 = bf16[512,768]{1,0:T(8,128)(2,1)} collective-permute-done((bf16[512,768]{1,0:T(8,128)(2,1)}, bf16[512,768]{1,0:T(8,128)(2,1)}, u32[]{:S(2)}, u32[]{:S(2)}) %collective-permute-start.6) | collective-permute-done | bytes 786464 | tf_op jit(solution)/shard_map/ppermute | solution.py:119
  96.0 5.6 %collective-permute-start.8 = (bf16[512,768]{1,0:T(8,128)(2,1)}, bf16[512,768]{1,0:T(8,128)(2,1)}, u32[]{:S(2)}, u32[]{:S(2)}) collective-permute-start(bf16[512,768]{1,0:T(8,128)(2,1)} %collective-permute-done.6), channel_id=1, source_target_pairs={{0,8},{1,9},{2,10},{3,11},{4,12},{5,13},{6,14},{7,15},{8,16},{9,17... | collective-permute-start | bytes 2359304 | tf_op jit(solution)/shard_map/ppermute | solution.py:121
  101.7 1.0 broadcast_in_dim.5
  102.7 6.9 %all-to-all-start.2 = ((bf16[8,72,768]{2,1,0:T(8,128)(2,1)}), bf16[8,72,768]{2,1,0:T(8,128)(2,1)}, u32[]{:S(2)}, u32[]{:S(2)}) async-start(bf16[8,72,768]{2,1,0:T(8,128)(2,1)} %broadcast_in_dim.5), calls=%async_computation.2 | async-start | bytes 1769472 | tf_op jit(solution)/shard_map/all_to_all | solution.py:39
  109.7 1.9 fusion.30
  112.2 1.1 fusion.20
  115.0 1.3 pad_maximum_fusion.3
  116.4 17.1 %all-to-all-done.2 = bf16[8,72,768]{2,1,0:T(8,128)(2,1)} async-done(((bf16[8,72,768]{2,1,0:T(8,128)(2,1)}), bf16[8,72,768]{2,1,0:T(8,128)(2,1)}, u32[]{:S(2)}, u32[]{:S(2)}) %all-to-all-start.2) | async-done | bytes 884768 | tf_op jit(solution)/shard_map/all_to_all | solution.py:39
  133.5 2.1 %collective-permute-start.9 = (bf16[8,72,768]{2,1,0:T(8,128)(2,1)}, bf16[8,72,768]{2,1,0:T(8,128)(2,1)S(1)}, u32[]{:S(2)}, u32[]{:S(2)}) collective-permute-start(bf16[8,72,768]{2,1,0:T(8,128)(2,1)} %all-to-all-done.2), channel_id=1, source_target_pairs={{0,32},{32,0},{64,96},{96,64},{128,160},{160,128},{192,224},{224,1... | collective-permute-start | bytes 2654216 | tf_op jit(solution)/shard_map/ppermute | solution.py:160
  135.6 2.0 pad_maximum_fusion
  137.7 1.1 dynamic-slice_bitcast_fusion.3
  138.8 1.0 fusion.85
  139.7 1.0 fusion.84
  140.7 1.0 fusion.83
  141.7 4.3 %fusion.2 = (bf16[8,72,768]{2,1,0:T(8,128)(2,1)}, bf16[8,72,768]{2,1,0:T(8,128)(2,1)}, bf16[8,72,768]{2,1,0:T(8,128)(2,1)}, bf16[8,72,768]{2,1,0:T(8,128)(2,1)}) fusion(bf16[8,2,72,1536]{3,2,1,0:T(8,128)(2,1)S(1)} %bitcast.183, bf16[8,72,768]{2,1,0:T(8,128)(2,1)} %all-to-all-done.2, bf16[8,72,768]{2,1,0:T(8,128)(2,1)S(1)} %collective-permute-done.9, ...), kind=kLoop, calls=%fused_computation.8 | loop fusion | flops 15040512 | bytes 8847362 | tf_op jit(solution)/shard_map/convert_element_type | solution.py:29
  146.0 1.9 fusion.29
  149.7 1.4 pad_maximum_fusion.4
  151.2 1.0 copy-done.8
  154.9 1.0 fusion.65
  156.0 2.0 collective-permute-start.12
  158.0 3.7 %collective-permute-start.11 = (bf16[512,384]{1,0:T(8,128)(2,1)}, bf16[512,384]{1,0:T(8,128)(2,1)}, u32[]{:S(2)}, u32[]{:S(2)}) collective-permute-start(bf16[512,384]{1,0:T(8,128)(2,1)} %get-tuple-element.34), channel_id=1, source_target_pairs={{0,16},{1,17},{2,18},{3,19},{4,20},{5,21},{6,22},{7,23},{8,24},{9,... | collective-permute-start | bytes 1179656 | tf_op jit(solution)/shard_map/ppermute | solution.py:185
  161.7 3.4 %collective-permute-start.10 = (bf16[512,384]{1,0:T(8,128)(2,1)S(1)}, bf16[512,384]{1,0:T(8,128)(2,1)}, u32[]{:S(2)}, u32[]{:S(2)}) collective-permute-start(bf16[512,384]{1,0:T(8,128)(2,1)S(1)} %get-tuple-element.32), channel_id=1, source_target_pairs={{0,8},{1,9},{2,10},{3,11},{4,12},{5,13},{6,14},{7,15},{8,16},{9,17... | collective-permute-start | bytes 1179656 | tf_op jit(solution)/shard_map/ppermute | solution.py:185
  167.8 1.6 fusion.25
  169.4 6.9 %all-to-all-start.3 = ((bf16[8,72,512]{2,1,0:T(8,128)(2,1)}), bf16[8,72,512]{2,1,0:T(8,128)(2,1)}, u32[]{:S(2)}, u32[]{:S(2)}) async-start(bf16[8,72,512]{2,1,0:T(8,128)(2,1)} %bitcast.187), calls=%async_computation.4 | async-start | bytes 1179648 | tf_op jit(solution)/shard_map/all_to_all | solution.py:39
  176.3 3.1 %collective-permute-done.12 = bf16[512,384]{1,0:T(8,128)(2,1)} collective-permute-done((bf16[512,384]{1,0:T(8,128)(2,1)}, bf16[512,384]{1,0:T(8,128)(2,1)}, u32[]{:S(2)}, u32[]{:S(2)}) %collective-permute-start.12) | collective-permute-done | bytes 393248 | tf_op jit(solution)/shard_map/ppermute | solution.py:185
  179.4 3.7 %collective-permute-done.11 = bf16[512,384]{1,0:T(8,128)(2,1)} collective-permute-done((bf16[512,384]{1,0:T(8,128)(2,1)}, bf16[512,384]{1,0:T(8,128)(2,1)}, u32[]{:S(2)}, u32[]{:S(2)}) %collective-permute-start.11) | collective-permute-done | bytes 393248 | tf_op jit(solution)/shard_map/ppermute | solution.py:185
  183.1 8.8 %collective-permute-done.10 = bf16[512,384]{1,0:T(8,128)(2,1)} collective-permute-done((bf16[512,384]{1,0:T(8,128)(2,1)S(1)}, bf16[512,384]{1,0:T(8,128)(2,1)}, u32[]{:S(2)}, u32[]{:S(2)}) %collective-permute-start.10) | collective-permute-done | bytes 393248 | tf_op jit(solution)/shard_map/ppermute | solution.py:185
  191.9 2.2 %fusion.55 = bf16[512,384]{1,0:T(8,128)(2,1)} fusion(bf16[512,384]{1,0:T(8,128)(2,1)} %collective-permute-done.12, bf16[512,384]{1,0:T(8,128)(2,1)} %collective-permute-done.11, bf16[512,384]{1,0:T(8,128)(2,1)} %collective-permute-done.10, f32[4,512,384]{2,1,0:T(8,128)S(1)} %pad_maximum_fusion.1, s32[]{:T(128)S(6)} %select_n.83), kind=kLoop, calls=%fused_computation.98 | loop fusion | flops 1572864 | bytes 2359300 | tf_op jit(solution)/shard_map/convert_element_type | solution.py:186
  194.9 1.3 reduce-scatter.5.cloned.1.call-done
  196.2 1.8 fusion.64
  198.1 1.8 reduce_sum.25
  (91 shorter events, 14.8 us)
Async XLA Ops:
  7.2 17.4 %copy-start.21 = (bf16[72,512]{1,0:T(8,128)(2,1)S(1)}, bf16[72,512]{1,0:T(8,128)(2,1)}, u32[]{:S(2)}) copy-start(bf16[72,512]{1,0:T(8,128)(2,1)} %param.8) | copy-start | bytes 221188
  7.2 102.5 %all-gather.3.cloned.1.call-start = ((), (), s32[]{:S(2)}) async-start(), calls=%async_computation.6 | async-start | bytes 3760128 | tf_op jit(solution)/shard_map/all_gather | solution.py:107
  8.3 27.5 %copy-start.12 = (bf16[384,512]{1,0:T(8,128)(2,1)S(1)}, bf16[384,512]{1,0:T(8,128)(2,1)}, u32[]{:S(2)}) copy-start(bf16[384,512]{1,0:T(8,128)(2,1)} %param.13) | copy-start | bytes 1179652
  8.3 11.0 %collective-permute-start.4 = (bf16[72,768]{1,0:T(8,128)(2,1)S(1)}, bf16[72,768]{1,0:T(8,128)(2,1)S(1)}, u32[]{:S(2)}, u32[]{:S(2)}) collective-permute-start(bf16[72,768]{1,0:T(8,128)(2,1)S(1)} %get-tuple-element.53), channel_id=1, source_target_pairs={{0,0},{1,1},{2,2},{3,3},{4,4},{5,5},{6,6},{7,7},{8,64},{9,65},{10,... | collective-permute-start | bytes 331784 | tf_op jit(solution)/shard_map/ppermute | solution.py:96
  11.3 12.5 %collective-permute-start.5 = (bf16[72,768]{1,0:T(8,128)(2,1)S(1)}, bf16[72,768]{1,0:T(8,128)(2,1)S(1)}, u32[]{:S(2)}, u32[]{:S(2)}) collective-permute-start(bf16[72,768]{1,0:T(8,128)(2,1)S(1)} %get-tuple-element.54), channel_id=1, source_target_pairs={{0,64},{1,65},{2,66},{3,67},{4,68},{5,69},{6,70},{7,71},{8,0},{9,1... | collective-permute-start | bytes 331784 | tf_op jit(solution)/shard_map/ppermute | solution.py:96
  15.0 29.8 %copy-start.14 = (bf16[512,384]{1,0:T(8,128)(2,1)S(1)}, bf16[512,384]{1,0:T(8,128)(2,1)}, u32[]{:S(2)}) copy-start(bf16[512,384]{1,0:T(8,128)(2,1)} %param.12) | copy-start | bytes 1179652
  15.0 29.8 %copy-start.15 = (bf16[512,384]{1,0:T(8,128)(2,1)S(1)}, bf16[512,384]{1,0:T(8,128)(2,1)}, u32[]{:S(2)}) copy-start(bf16[512,384]{1,0:T(8,128)(2,1)} %param.11) | copy-start | bytes 1179652
  25.4 35.6 %all-to-all-start = ((bf16[8,72,512]{2,1,0:T(8,128)(2,1)}), bf16[8,72,512]{2,1,0:T(8,128)(2,1)S(1)}, u32[]{:S(2)}, u32[]{:S(2)}) async-start(bf16[8,72,512]{2,1,0:T(8,128)(2,1)} %broadcast_in_dim.4), calls=%async_computation | async-start | bytes 1179648 | tf_op jit(solution)/shard_map/all_to_all | solution.py:39
  35.8 22.4 %collective-permute-start.2 = (bf16[384,512]{1,0:T(8,128)(2,1)S(1)}, bf16[384,512]{1,0:T(8,128)(2,1)S(1)}, u32[]{:S(2)}, u32[]{:S(2)}) collective-permute-start(bf16[384,512]{1,0:T(8,128)(2,1)S(1)} %copy-done.12), channel_id=1, source_target_pairs={{0,24},{1,25},{2,26},{3,27},{4,28},{5,29},{6,30},{7,31},{8,0},{9,1... | collective-permute-start | bytes 1179656 | tf_op jit(solution)/shard_map/ppermute | solution.py:80
  37.8 20.3 %collective-permute-start.1 = (bf16[384,512]{1,0:T(8,128)(2,1)S(1)}, bf16[384,512]{1,0:T(8,128)(2,1)S(1)}, u32[]{:S(2)}, u32[]{:S(2)}) collective-permute-start(bf16[384,512]{1,0:T(8,128)(2,1)S(1)} %copy-done.12), channel_id=1, source_target_pairs={{0,16},{1,17},{2,18},{3,19},{4,20},{5,21},{6,22},{7,23},{8,24},{9,... | collective-permute-start | bytes 1179656 | tf_op jit(solution)/shard_map/ppermute | solution.py:80
  39.9 20.8 %collective-permute-start = (bf16[384,512]{1,0:T(8,128)(2,1)S(1)}, bf16[384,512]{1,0:T(8,128)(2,1)S(1)}, u32[]{:S(2)}, u32[]{:S(2)}) collective-permute-start(bf16[384,512]{1,0:T(8,128)(2,1)S(1)} %copy-done.12), channel_id=1, source_target_pairs={{0,8},{1,9},{2,10},{3,11},{4,12},{5,13},{6,14},{7,15},{8,16},{9,17... | collective-permute-start | bytes 1179656 | tf_op jit(solution)/shard_map/ppermute | solution.py:80
  61.0 6.6 %copy-start.10 = (bf16[8,72,512]{2,1,0:T(8,128)(2,1)}, bf16[8,72,512]{2,1,0:T(8,128)(2,1)S(1)}, u32[]{:S(2)}) copy-start(bf16[8,72,512]{2,1,0:T(8,128)(2,1)S(1)} %all-to-all-done) | copy-start | bytes 1769476
  61.7 4.3 %collective-permute-start.3 = (bf16[576,768]{1,0:T(8,128)(2,1)S(1)}, bf16[576,768]{1,0:T(8,128)(2,1)S(1)}, u32[]{:S(2)}, u32[]{:S(2)}) collective-permute-start(bf16[576,768]{1,0:T(8,128)(2,1)S(1)} %convolution_convert_fusion), channel_id=1, source_target_pairs={{0,32},{32,0},{64,96},{96,64},{128,160},{160,128},{192,224},{224,1... | collective-permute-start | bytes 2654216 | tf_op jit(solution)/shard_map/ppermute | solution.py:124
  67.6 11.3 %copy-start.22 = (bf16[72,512]{1,0:T(8,128)(2,1)S(1)}, bf16[72,512]{1,0:T(8,128)(2,1)}, u32[]{:S(2)}) copy-start(bf16[72,512]{1,0:T(8,128)(2,1)} %param.7) | copy-start | bytes 221188
  67.6 34.0 %all-to-all-start.1 = ((bf16[8,72,768]{2,1,0:T(8,128)(2,1)}), bf16[8,72,768]{2,1,0:T(8,128)(2,1)S(1)}, u32[]{:S(2)}, u32[]{:S(2)}) async-start(bf16[8,72,768]{2,1,0:T(8,128)(2,1)} %bitcast.9), calls=%async_computation.1 | async-start | bytes 1769472 | tf_op jit(solution)/shard_map/all_to_all | solution.py:39
  74.3 71.7 %all-gather.5.cloned.1.call-start = ((), (), s32[]{:S(2)}) async-start(), calls=%async_computation.8 | async-start | bytes 1327104 | tf_op jit(solution)/shard_map/all_gather | solution.py:113
  74.3 21.7 %collective-permute-start.6 = (bf16[512,768]{1,0:T(8,128)(2,1)}, bf16[512,768]{1,0:T(8,128)(2,1)}, u32[]{:S(2)}, u32[]{:S(2)}) collective-permute-start(bf16[512,768]{1,0:T(8,128)(2,1)} %pad_maximum_fusion.5), channel_id=1, source_target_pairs={{0,8},{1,9},{2,10},{3,11},{4,12},{5,13},{6,14},{7,15},{8,16},{9,17... | collective-permute-start | bytes 2359304 | tf_op jit(solution)/shard_map/ppermute | solution.py:119
  79.6 53.9 %collective-permute-start.7 = (bf16[512,768]{1,0:T(8,128)(2,1)}, bf16[512,768]{1,0:T(8,128)(2,1)}, u32[]{:S(2)}, u32[]{:S(2)}) collective-permute-start(bf16[512,768]{1,0:T(8,128)(2,1)} %pad_maximum_fusion.5), channel_id=1, source_target_pairs={{0,24},{1,25},{2,26},{3,27},{4,28},{5,29},{6,30},{7,31},{8,0},{9,1... | collective-permute-start | bytes 2359304 | tf_op jit(solution)/shard_map/ppermute | solution.py:120
  96.0 37.5 %collective-permute-start.8 = (bf16[512,768]{1,0:T(8,128)(2,1)}, bf16[512,768]{1,0:T(8,128)(2,1)}, u32[]{:S(2)}, u32[]{:S(2)}) collective-permute-start(bf16[512,768]{1,0:T(8,128)(2,1)} %collective-permute-done.6), channel_id=1, source_target_pairs={{0,8},{1,9},{2,10},{3,11},{4,12},{5,13},{6,14},{7,15},{8,16},{9,17... | collective-permute-start | bytes 2359304 | tf_op jit(solution)/shard_map/ppermute | solution.py:121
  102.7 30.8 %all-to-all-start.2 = ((bf16[8,72,768]{2,1,0:T(8,128)(2,1)}), bf16[8,72,768]{2,1,0:T(8,128)(2,1)}, u32[]{:S(2)}, u32[]{:S(2)}) async-start(bf16[8,72,768]{2,1,0:T(8,128)(2,1)} %broadcast_in_dim.5), calls=%async_computation.2 | async-start | bytes 1769472 | tf_op jit(solution)/shard_map/all_to_all | solution.py:39
  109.6 59.7 %reduce-scatter.3.cloned.1.call-start = ((), (), s32[]{:S(2)}) async-start(), calls=%async_computation.7 | async-start | bytes 1966080 | tf_op jit(solution)/shard_map/reduce_scatter | solution.py:142
  109.7 2.6 %copy-start = (bf16[1152,1536]{1,0:T(8,128)(2,1)S(1)}, bf16[1152,1536]{1,0:T(8,128)(2,1)}, u32[]{:S(2)}) copy-start(bf16[1152,1536]{1,0:T(8,128)(2,1)} %all-gather.3.cloned.1.call-done) | copy-start | bytes 10616836
  112.2 1.1 copy-start.11
  116.3 79.9 %reduce-scatter.5.cloned.1.call-start = ((), (), s32[]{:S(2)}) async-start(), calls=%async_computation.9 | async-start | bytes 1966080 | tf_op jit(solution)/shard_map/reduce_scatter | solution.py:173
  133.5 8.2 %collective-permute-start.9 = (bf16[8,72,768]{2,1,0:T(8,128)(2,1)}, bf16[8,72,768]{2,1,0:T(8,128)(2,1)S(1)}, u32[]{:S(2)}, u32[]{:S(2)}) collective-permute-start(bf16[8,72,768]{2,1,0:T(8,128)(2,1)} %all-to-all-done.2), channel_id=1, source_target_pairs={{0,32},{32,0},{64,96},{96,64},{128,160},{160,128},{192,224},{224,1... | collective-permute-start | bytes 2654216 | tf_op jit(solution)/shard_map/ppermute | solution.py:160
  145.9 2.0 copy-start.6
  145.9 2.0 copy-start.23
  146.0 2.6 %copy-start.1 = (bf16[8,72,768]{2,1,0:T(8,128)(2,1)S(1)}, bf16[8,72,768]{2,1,0:T(8,128)(2,1)}, u32[]{:S(2)}) copy-start(bf16[8,72,768]{2,1,0:T(8,128)(2,1)} %get-tuple-element.24) | copy-start | bytes 2654212
  149.7 1.4 copy-start.3
  151.1 1.2 copy-start.8
  152.3 1.2 copy-start.5
  154.9 10.2 %copy-start.9 = (bf16[8,72,768]{2,1,0:T(8,128)(2,1)S(1)}, bf16[8,72,768]{2,1,0:T(8,128)(2,1)}, u32[]{:S(2)}) copy-start(bf16[8,72,768]{2,1,0:T(8,128)(2,1)} %get-tuple-element.27) | copy-start | bytes 2654212
  154.9 10.2 %copy-start.19 = (bf16[512,384]{1,0:T(8,128)(2,1)S(1)}, bf16[512,384]{1,0:T(8,128)(2,1)}, u32[]{:S(2)}) copy-start(bf16[512,384]{1,0:T(8,128)(2,1)} %get-tuple-element.50) | copy-start | bytes 1179652
  154.9 10.2 %copy-start.20 = (bf16[512,384]{1,0:T(8,128)(2,1)S(1)}, bf16[512,384]{1,0:T(8,128)(2,1)}, u32[]{:S(2)}) copy-start(bf16[512,384]{1,0:T(8,128)(2,1)} %get-tuple-element.48) | copy-start | bytes 1179652
  156.0 9.8 %copy-start.7 = (bf16[8,72,768]{2,1,0:T(8,128)(2,1)S(1)}, bf16[8,72,768]{2,1,0:T(8,128)(2,1)}, u32[]{:S(2)}) copy-start(bf16[8,72,768]{2,1,0:T(8,128)(2,1)} %get-tuple-element.25) | copy-start | bytes 2654212
  156.0 9.8 %copy-start.16 = (bf16[512,384]{1,0:T(8,128)(2,1)S(1)}, bf16[512,384]{1,0:T(8,128)(2,1)}, u32[]{:S(2)}) copy-start(bf16[512,384]{1,0:T(8,128)(2,1)} %get-tuple-element.49) | copy-start | bytes 1179652
  156.0 9.8 %copy-start.18 = (bf16[512,384]{1,0:T(8,128)(2,1)S(1)}, bf16[512,384]{1,0:T(8,128)(2,1)}, u32[]{:S(2)}) copy-start(bf16[512,384]{1,0:T(8,128)(2,1)} %get-tuple-element.47) | copy-start | bytes 1179652
  156.0 23.5 %collective-permute-start.12 = (bf16[512,384]{1,0:T(8,128)(2,1)}, bf16[512,384]{1,0:T(8,128)(2,1)}, u32[]{:S(2)}, u32[]{:S(2)}) collective-permute-start(bf16[512,384]{1,0:T(8,128)(2,1)} %get-tuple-element.33), channel_id=1, source_target_pairs={{0,24},{1,25},{2,26},{3,27},{4,28},{5,29},{6,30},{7,31},{8,0},{9,1... | collective-permute-start | bytes 1179656 | tf_op jit(solution)/shard_map/ppermute | solution.py:185
  158.0 25.1 %collective-permute-start.11 = (bf16[512,384]{1,0:T(8,128)(2,1)}, bf16[512,384]{1,0:T(8,128)(2,1)}, u32[]{:S(2)}, u32[]{:S(2)}) collective-permute-start(bf16[512,384]{1,0:T(8,128)(2,1)} %get-tuple-element.34), channel_id=1, source_target_pairs={{0,16},{1,17},{2,18},{3,19},{4,20},{5,21},{6,22},{7,23},{8,24},{9,... | collective-permute-start | bytes 1179656 | tf_op jit(solution)/shard_map/ppermute | solution.py:185
  161.7 30.3 %collective-permute-start.10 = (bf16[512,384]{1,0:T(8,128)(2,1)S(1)}, bf16[512,384]{1,0:T(8,128)(2,1)}, u32[]{:S(2)}, u32[]{:S(2)}) collective-permute-start(bf16[512,384]{1,0:T(8,128)(2,1)S(1)} %get-tuple-element.32), channel_id=1, source_target_pairs={{0,8},{1,9},{2,10},{3,11},{4,12},{5,13},{6,14},{7,15},{8,16},{9,17... | collective-permute-start | bytes 1179656 | tf_op jit(solution)/shard_map/ppermute | solution.py:185
  165.8 1.0 copy-start.17
  166.5 1.2 copy-start.2
  166.5 1.3 copy-start.4
  169.4 28.7 %all-to-all-start.3 = ((bf16[8,72,512]{2,1,0:T(8,128)(2,1)}), bf16[8,72,512]{2,1,0:T(8,128)(2,1)}, u32[]{:S(2)}, u32[]{:S(2)}) async-start(bf16[8,72,512]{2,1,0:T(8,128)(2,1)} %bitcast.187), calls=%async_computation.4 | async-start | bytes 1179648 | tf_op jit(solution)/shard_map/all_to_all | solution.py:39
  176.3 17.9 %copy-start.13 = (bf16[384,512]{1,0:T(8,128)(2,1)S(1)}, bf16[384,512]{1,0:T(8,128)(2,1)}, u32[]{:S(2)}) copy-start(bf16[384,512]{1,0:T(8,128)(2,1)} %reduce-scatter.3.cloned.1.call-done) | copy-start | bytes 1179652
Sparse Core Ops, SparseCore 0:
  24.7 48.2 all-gather.2
  79.7 43.3 all-gather.4
  125.9 27.8 reduce-scatter.2
  156.5 39.6 reduce-scatter.4

commit v7 on v6

--- a/solution.py
+++ b/solution.py
@@ -1,6 +1,8 @@
 import jax
 import jax.numpy as jnp
 from jax import lax
+from jax.experimental import pallas as pl
+from jax.experimental.pallas import tpu as pltpu
 from jax.sharding import PartitionSpec as P
 
 N_CORE = 2
@@ -33,6 +35,109 @@
     gate_float = gate_pre.astype(jnp.float32)
     swish_gate = gate_float * jax.nn.sigmoid(gate_float)
     return (swish_gate * up_pre.astype(jnp.float32)).astype(jnp.bfloat16)
+
+
+def unit_block_kernel(
+    place_ref, own_ref, other_ref, gate_ref, up_ref, tokens_ref,
+    part_ref, gate_grad_ref, up_grad_ref, grad_ref,
+):
+    mine = pl.program_id(0) // 2 == place_ref[0]
+
+    @pl.when(mine)
+    def _():
+        grad_ref[...] = own_ref[...].astype(jnp.float32)
+
+    @pl.when(jnp.logical_not(mine))
+    def _():
+        grad_ref[...] = other_ref[...].astype(jnp.float32)
+
+    shape = grad_ref.shape
+    gate_grad, up_grad = swiglu_grads(
+        grad_ref[...],
+        gate_ref[...].astype(jnp.float32).reshape(shape),
+        up_ref[...].astype(jnp.float32).reshape(shape),
+    )
+    gate_grad_ref[0] = gate_grad
+    up_grad_ref[0] = up_grad
+    token_columns = tokens_ref[...]
+    units = shape[-1]
+    for which, grads in enumerate((gate_grad, up_grad)):
+        part_ref[0, :, which * units : (which + 1) * units] = jnp.dot(
+            token_columns, grads, preferred_element_type=jnp.float32
+        ).astype(jnp.bfloat16)
+
+
+def unit_blocks(place, own, other, saved, token_columns):
+    n_y, _, block, width = saved.shape
+    units = width // 4
+    features, group_rows = token_columns.shape
+    n_block = 4
+
+    def half_spec():
+        return pl.BlockSpec((group_rows, units), lambda j, place: (0, j % 2))
+
+    def saved_spec(first):
+        return pl.BlockSpec(
+            (n_y, 1, block, units), lambda j, place: (0, j // 2, 0, first + j % 2)
+        )
+
+    def out_spec(rows, width):
+        return pl.BlockSpec((1, rows, width), lambda j, place: (j, 0, 0))
+
+    part = jax.ShapeDtypeStruct((n_block, features, 2 * units), jnp.bfloat16)
+    grads = jax.ShapeDtypeStruct((n_block, group_rows, units), jnp.bfloat16)
+    return pl.pallas_call(
+        unit_block_kernel,
+        out_shape=(part, grads, grads),
+        grid_spec=pltpu.PrefetchScalarGridSpec(
+            num_scalar_prefetch=1,
+            grid=(n_block,),
+            in_specs=[
+                half_spec(),
+                half_spec(),
+                saved_spec(0),
+                saved_spec(2),
+                pl.BlockSpec((features, group_rows), lambda j, place: (0, 0)),
+            ],
+            out_specs=[out_spec(features, 2 * units)] + [out_spec(group_rows, units)] * 2,
+            scratch_shapes=[pltpu.VMEM((group_rows, units), jnp.float32)],
+        ),
+        compiler_params=pltpu.CompilerParams(vmem_limit_bytes=32 * 1024 * 1024),
+        cost_estimate=pl.CostEstimate(
+            flops=4 * n_block * features * units * group_rows,
+            bytes_accessed=14_000_000,
+            transcendentals=n_block * group_rows * units,
+        ),
+    )(place, own, other, saved, saved, token_columns)
+
+
+def input_grad_kernel(order_ref, gate_ref, up_ref, *refs):
+    weights, out_ref = refs[:-1], refs[-1]
+    units = gate_ref.shape[-1]
+    total = 0.0
+    for step, weight_ref in enumerate(weights):
+        place = order_ref[step]
+        total = total + contract_last(gate_ref[place], weight_ref[:, :units])
+        total = total + contract_last(up_ref[place], weight_ref[:, units:])
+    out_ref[...] = total.astype(jnp.bfloat16)
+
+
+def input_grad_part(order, gate_grad, up_grad, weights):
+    n_block, group_rows, units = gate_grad.shape
+    features = weights[0].shape[0]
+    vmem = pl.BlockSpec(memory_space=pltpu.VMEM)
+    return pl.pallas_call(
+        input_grad_kernel,
+        out_shape=jax.ShapeDtypeStruct((group_rows, features), jnp.bfloat16),
+        in_specs=[pl.BlockSpec(memory_space=pltpu.SMEM)] + [vmem] * (2 + n_block),
+        out_specs=vmem,
+        compiler_params=pltpu.CompilerParams(vmem_limit_bytes=32 * 1024 * 1024),
+        cost_estimate=pl.CostEstimate(
+            flops=4 * n_block * features * units * group_rows,
+            bytes_accessed=7_000_000,
+            transcendentals=0,
+        ),
+    )(order, gate_grad, up_grad, *weights)
 
 
 def exchange(pieces, axis, groups):
@@ -66,6 +171,13 @@
             (x * N_Z + z, (x + step) % n_x * N_Z + z) for x in range(n_x) for z in range(N_Z)
         ]
 
+    def sum_over_x(parts):
+        total = pick(parts, x_here).astype(jnp.float32)
+        for step in range(1, n_x):
+            piece = pick(parts, lax.rem(x_here + step, n_x))
+            total = total + lax.ppermute(piece, "col", x_shift(step)).astype(jnp.float32)
+        return total
+
     def to_group(turn):
         pairs = []
         for r in range(n_row):
@@ -126,7 +238,7 @@
     pair = (keep.astype(jnp.float32) + got.astype(jnp.float32)).astype(jnp.bfloat16)
     terms = exchange(pair.reshape(n_y, block, half), "row", y_groups)
     share = jnp.sum(terms.astype(jnp.float32), axis=0).astype(jnp.bfloat16)
-    own = spread(share, n_y, "row", y_groups)
+    own = spread(share, n_y, "row", y_groups).reshape(group_rows, half)
 
     grad_scale = (rows * n_row) ** (-0.5)
 
@@ -137,57 +249,27 @@
     for side in range(2):
         hidden = swiglu_hidden(*side_saved(side)).reshape(group_rows, half)
         down_part.append(contract_first(hidden, grad_rows).astype(jnp.bfloat16))
-    down_part = jnp.concatenate(down_part, axis=0)
+    down_part = jnp.concatenate(down_part, axis=0).reshape(n_x, units, features)
     own, _ = lax.optimization_barrier((own, down_part))
     down_sum = lax.psum_scatter(
-        down_part,
-        "col",
-        scatter_dimension=0,
-        tiled=True,
-        axis_index_groups=x_groups,
-    )
+        down_part, "col", scatter_dimension=0, tiled=True, axis_index_groups=x_groups
+    )[0]
 
     own, w_left, w_right, w_far = lax.optimization_barrier((own, w_left, w_right, w_far))
-    w_stack = jnp.stack([w_both, w_left, w_far, w_right])
-    w_order = [pick(w_stack, lax.rem(x_here - place + n_x, n_x)) for place in range(n_x)]
-
-    def w_half(side, which):
-        pieces = w_order[2 * side : 2 * side + 2]
-        return jnp.concatenate(
-            [piece[:, which * units : (which + 1) * units] for piece in pieces], axis=1
-        )
+    weights = [w_both, w_left, w_far, w_right]
+    order = jnp.stack([lax.rem(x_here - step + n_x, n_x) for step in range(n_x)])
 
     other = lax.ppermute(own, "row", core_swap)
-    part_in, gate_part, up_part = 0.0, [], []
-    for side in range(2):
-        hidden_grad = jnp.where(core == side, own, other)
-        gate_grad, up_grad = swiglu_grads(hidden_grad, *side_saved(side))
-        gate_grad = gate_grad.reshape(group_rows, half)
-        up_grad = up_grad.reshape(group_rows, half)
-        part_in = part_in + contract_last(gate_grad, w_half(side, 0))
-        part_in = part_in + contract_last(up_grad, w_half(side, 1))
-        for slot in range(2):
-            columns = slice(slot * units, (slot + 1) * units)
-            gate_part.append(contract_first(token_rows, gate_grad[:, columns]))
-            up_part.append(contract_first(token_rows, up_grad[:, columns]))
-    gate_sum = lax.psum_scatter(
-        jnp.stack(gate_part).astype(jnp.bfloat16),
-        "col",
-        scatter_dimension=0,
-        tiled=True,
-        axis_index_groups=x_groups,
-    )[0]
-    gate_wgrad = (gate_sum.astype(jnp.float32) * grad_scale).astype(jnp.bfloat16)
-    up_stack = jnp.stack(up_part)
-    up_sum = pick(up_stack, x_here)
-    for step in range(1, n_x):
-        piece = pick(up_stack, lax.rem(x_here + step, n_x)).astype(jnp.bfloat16)
-        up_sum = up_sum + lax.ppermute(piece, "col", x_shift(step)).astype(jnp.float32)
-    up_wgrad = (up_sum * grad_scale).astype(jnp.bfloat16)
+    unit_part, gate_grad, up_grad = unit_blocks(
+        core.reshape(1), own, other, saved, token_rows.swapaxes(0, 1)
+    )
+    unit_wgrad = (sum_over_x(unit_part) * grad_scale).astype(jnp.bfloat16)
+    gate_wgrad, up_wgrad = unit_wgrad[:, :units], unit_wgrad[:, units:]
+    part_in = input_grad_part(order, gate_grad, up_grad, weights)
     part_in, down_sum = lax.optimization_barrier((part_in, down_sum))
     down_wgrad = (down_sum.astype(jnp.float32) * grad_scale).astype(jnp.bfloat16)
     token_terms = exchange(
-        part_in.astype(jnp.bfloat16).reshape(N_Z, block, features), "col", z_groups
+        part_in.reshape(N_Z, block, features), "col", z_groups
     )
     token_grad = jnp.sum(token_terms.astype(jnp.float32), axis=0).astype(jnp.bfloat16)
     return (token_grad, gate_wgrad, up_wgrad, down_wgrad)

time: 210 us -> 215 us (1.024); the launches traced: 206 us -> 214 us
  waiting for transfers between devices: 74.6 us -> 88.6 us
  other arithmetic: 22.4 us -> 10.2 us
  Pallas kernels: 0 us -> 11.4 us
  matrix products: 13.4 us -> 3.89 us
  local copies, waits for them, and re-layouts: 9.56 us -> 15.7 us
  starting transfers between devices: 71.8 us -> 69.5 us
    all_to_all x4, waiting for transfers between devices: 17.1 us -> 34.5 us  [exchange(): lax.all_to_all(pieces, axis, 0, 0, tiled=True, axis_index_groups=groups)]
    ppermute x1, waiting for transfers between devices: 14.5 us -> 0.01 us  [local(): w_left = lax.ppermute(w_both, 'col', x_shift(1))]
    pallas_call x0 -> x2, Pallas kernels: none -> 11.4 us  [the longest x1 6.07 us: unit_blocks(): pl.pallas_call(unit_block_kernel, out_shape=(part, grads, grads), grid_sp...]
    ppermute x3, waiting for transfers between devices: 15.7 us -> 22.3 us  [sum_over_x(): lax.ppermute(piece, 'col', x_shift(step)).astype(jnp.float32)]
    dot_general x10 -> x2, matrix products: 7.65 us -> 1.61 us  [contract_first(): lax.dot_general(left_side, right_side, (((0,), (0,)), ((), ())), preferre...]
    convert_element_type x3 -> x1, other arithmetic: 8.26 us -> 2.28 us  [local(): unit_wgrad = (sum_over_x(unit_part) * grad_scale).astype(jnp.bfloat16)]
    unnamed x48 -> x27, local copies, waits for them, and re-layouts: 2.41 us -> 7.1 us
    ppermute x1, waiting for transfers between devices: 0.01 us -> 4.12 us  [local(): w_right = lax.ppermute(w_both, 'col', x_shift(n_x - 1))]
  transfers between devices with their start and end apart: 21 -> 20, of which waited for: 11 -> 11; matrix products, arithmetic and copies ran while one was open for 19% -> 11% of each run, Pallas kernels for 0% -> 5%
where the time goes in v7:
time: 215 us; the launch traced here: 214 us
  waiting for transfers between devices  88.6 us (41%)
  starting transfers between devices  69.5 us (32%)
  local copies, waits for them, and re-layouts  15.7 us (7%)
  between operations  14.3 us (7%)
  Pallas kernels  11.4 us (5%)
  other arithmetic  10.2 us (5%)
  matrix products  3.89 us (2%)
    all_to_all x4, waiting for transfers between devices, exchange(): lax.all_to_all(pieces, axis, 0, 0, tiled=True, axis_index_groups=groups)  34.5 us
    all_to_all x4, starting transfers between devices, exchange(): lax.all_to_all(pieces, axis, 0, 0, tiled=True, axis_index_groups=groups)  30.8 us
    ppermute x3, waiting for transfers between devices, sum_over_x(): lax.ppermute(piece, 'col', x_shift(step)).astype(jnp.float32)  22.3 us
    ppermute x3, waiting for transfers between devices, local(): lax.ppermute(w_down, 'col', x_shift(step))  15.3 us
    ppermute x3, starting transfers between devices, sum_over_x(): lax.ppermute(piece, 'col', x_shift(step)).astype(jnp.float32)  11 us
    ppermute x2, waiting for transfers between devices, local(): lax.ppermute(pick(saved_pieces, lax.rem(x_here + turn, 2)), ('row', 'col'...  8.74 us
    ppermute x3, starting transfers between devices, local(): lax.ppermute(w_down, 'col', x_shift(step))  7.95 us
    unnamed x27, local copies, waits for them, and re-layouts  7.1 us
  transfers between devices with their start and end apart: 20, of which 11 were waited for; matrix products, arithmetic and copies ran while one was open for 11% of the time, Pallas kernels for 5%

profile of v7, /device:TPU:6, one launch (start us, length us, event | category | flops | bytes accessed | tf_op | source)
XLA Modules:
  0.0 213.6 jit_solution(9983990517948932982)
XLA Ops:
  7.3 1.0 pad_maximum_fusion.3
  8.3 2.8 %collective-permute-start.4 = (bf16[72,768]{1,0:T(8,128)(2,1)S(1)}, bf16[72,768]{1,0:T(8,128)(2,1)S(1)}, u32[]{:S(2)}, u32[]{:S(2)}) collective-permute-start(bf16[72,768]{1,0:T(8,128)(2,1)S(1)} %get-tuple-element.45), channel_id=1, source_target_pairs={{0,0},{1,1},{2,2},{3,3},{4,4},{5,5},{6,6},{7,7},{8,64},{9,65},{10,... | collective-permute-start | bytes 331784 | tf_op jit(solution)/shard_map/ppermute | solution.py:208
  11.1 3.8 %collective-permute-start.5 = (bf16[72,768]{1,0:T(8,128)(2,1)S(1)}, bf16[72,768]{1,0:T(8,128)(2,1)S(1)}, u32[]{:S(2)}, u32[]{:S(2)}) collective-permute-start(bf16[72,768]{1,0:T(8,128)(2,1)S(1)} %get-tuple-element.46), channel_id=1, source_target_pairs={{0,64},{1,65},{2,66},{3,67},{4,68},{5,69},{6,70},{7,71},{8,0},{9,1... | collective-permute-start | bytes 331784 | tf_op jit(solution)/shard_map/ppermute | solution.py:208
  14.9 4.2 %collective-permute-done.4 = bf16[72,768]{1,0:T(8,128)(2,1)S(1)} collective-permute-done((bf16[72,768]{1,0:T(8,128)(2,1)S(1)}, bf16[72,768]{1,0:T(8,128)(2,1)S(1)}, u32[]{:S(2)}, u32[]{:S(2)}) %collective-permute-start.4) | collective-permute-done | bytes 110624 | tf_op jit(solution)/shard_map/ppermute | solution.py:208
  19.1 4.5 %collective-permute-done.5 = bf16[72,768]{1,0:T(8,128)(2,1)S(1)} collective-permute-done((bf16[72,768]{1,0:T(8,128)(2,1)S(1)}, bf16[72,768]{1,0:T(8,128)(2,1)S(1)}, u32[]{:S(2)}, u32[]{:S(2)}) %collective-permute-start.5) | collective-permute-done | bytes 110624 | tf_op jit(solution)/shard_map/ppermute | solution.py:208
  24.5 0.9 broadcast_in_dim.4
  25.3 10.3 %all-to-all-start = ((bf16[8,72,512]{2,1,0:T(8,128)(2,1)}), bf16[8,72,512]{2,1,0:T(8,128)(2,1)S(1)}, u32[]{:S(2)}, u32[]{:S(2)}) async-start(bf16[8,72,512]{2,1,0:T(8,128)(2,1)} %broadcast_in_dim.4), calls=%async_computation | async-start | bytes 1179648 | tf_op jit(solution)/shard_map/all_to_all | solution.py:144
  35.7 1.9 collective-permute-start
  37.6 3.9 %collective-permute-start.2 = (bf16[384,512]{1,0:T(8,128)(2,1)S(1)}, bf16[384,512]{1,0:T(8,128)(2,1)S(1)}, u32[]{:S(2)}, u32[]{:S(2)}) collective-permute-start(bf16[384,512]{1,0:T(8,128)(2,1)S(1)} %copy-done.7), channel_id=1, source_target_pairs={{0,24},{1,25},{2,26},{3,27},{4,28},{5,29},{6,30},{7,31},{8,0},{9,1... | collective-permute-start | bytes 1179656 | tf_op jit(solution)/shard_map/ppermute | solution.py:192
  41.5 2.1 collective-permute-start.1
  43.7 1.0 pad_maximum_fusion.2.refs_0_
  44.7 4.8 %collective-permute-done = bf16[384,512]{1,0:T(8,128)(2,1)S(1)} collective-permute-done((bf16[384,512]{1,0:T(8,128)(2,1)S(1)}, bf16[384,512]{1,0:T(8,128)(2,1)S(1)}, u32[]{:S(2)}, u32[]{:S(2)}) %collective-permute-start) | collective-permute-done | bytes 393248 | tf_op jit(solution)/shard_map/ppermute | solution.py:192
  49.6 10.4 %collective-permute-done.2 = bf16[384,512]{1,0:T(8,128)(2,1)S(1)} collective-permute-done((bf16[384,512]{1,0:T(8,128)(2,1)S(1)}, bf16[384,512]{1,0:T(8,128)(2,1)S(1)}, u32[]{:S(2)}, u32[]{:S(2)}) %collective-permute-start.2) | collective-permute-done | bytes 393248 | tf_op jit(solution)/shard_map/ppermute | solution.py:192
  61.0 1.9 collective-permute-start.3
  62.9 2.4 %collective-permute-done.3 = bf16[576,768]{1,0:T(8,128)(2,1)S(1)} collective-permute-done((bf16[576,768]{1,0:T(8,128)(2,1)S(1)}, bf16[576,768]{1,0:T(8,128)(2,1)S(1)}, u32[]{:S(2)}, u32[]{:S(2)}) %collective-permute-start.3) | collective-permute-done | bytes 884768 | tf_op jit(solution)/shard_map/ppermute | solution.py:236
  65.3 1.6 add_convert_fusion
  66.9 9.3 %all-to-all-start.1 = ((bf16[8,72,768]{2,1,0:T(8,128)(2,1)}), bf16[8,72,768]{2,1,0:T(8,128)(2,1)S(1)}, u32[]{:S(2)}, u32[]{:S(2)}) async-start(bf16[8,72,768]{2,1,0:T(8,128)(2,1)} %bitcast.14), calls=%async_computation.1 | async-start | bytes 1769472 | tf_op jit(solution)/shard_map/all_to_all | solution.py:144
  77.0 1.9 collective-permute-start.6
  78.9 22.8 %all-to-all-done.1 = bf16[8,72,768]{2,1,0:T(8,128)(2,1)S(1)} async-done(((bf16[8,72,768]{2,1,0:T(8,128)(2,1)}), bf16[8,72,768]{2,1,0:T(8,128)(2,1)S(1)}, u32[]{:S(2)}, u32[]{:S(2)}) %all-to-all-start.1) | async-done | bytes 884768 | tf_op jit(solution)/shard_map/all_to_all | solution.py:144
  101.9 1.0 broadcast_in_dim.5
  102.9 4.2 %all-to-all-start.2 = ((bf16[8,72,768]{2,1,0:T(8,128)(2,1)}), bf16[8,72,768]{2,1,0:T(8,128)(2,1)}, u32[]{:S(2)}, u32[]{:S(2)}) async-start(bf16[8,72,768]{2,1,0:T(8,128)(2,1)} %broadcast_in_dim.5), calls=%async_computation.2 | async-start | bytes 1769472 | tf_op jit(solution)/shard_map/all_to_all | solution.py:144
  107.2 2.2 %fusion.22 = (bf16[8,1,72,768]{3,2,1,0:T(8,128)(2,1)S(1)}, bf16[8,1,72,768]{3,2,1,0:T(8,128)(2,1)S(1)}, bf16[8,1,72,768]{3,2,1,0:T(8,128)(2,1)S(1)}, bf16[8,1,72,768]{3,2,1,0:T(8,128)(2,1)S(1)}) fusion(bf16[8,2,72,1536]{3,2,1,0:T(8,128)(2,1)} %bitcast.57), kind=kLoop, calls=%fused_computation.51 | loop fusion | bytes 7077888 | tf_op jit(solution)/shard_map/slice | solution.py:246
  110.1 0.8 convolution_convert_fusion.3
  112.4 1.3 pad_maximum_fusion.1
  113.8 2.2 %collective-permute-start.7 = (bf16[512,768]{1,0:T(8,128)(2,1)}, bf16[512,768]{1,0:T(8,128)(2,1)}, u32[]{:S(2)}, u32[]{:S(2)}) collective-permute-start(bf16[512,768]{1,0:T(8,128)(2,1)} %pad_maximum_fusion.2.refs_0_), channel_id=1, source_target_pairs={{0,24},{1,25},{2,26},{3,27},{4,28},{5,29},{6,30},{7,31},{8,0},{9,1... | collective-permute-start | bytes 2359304 | tf_op jit(solution)/shard_map/ppermute | solution.py:232
  116.0 5.1 %collective-permute-start.8 = (bf16[512,768]{1,0:T(8,128)(2,1)}, bf16[512,768]{1,0:T(8,128)(2,1)}, u32[]{:S(2)}, u32[]{:S(2)}) collective-permute-start(bf16[512,768]{1,0:T(8,128)(2,1)} %collective-permute-done.6.refs_1_), channel_id=1, source_target_pairs={{0,8},{1,9},{2,10},{3,11},{4,12},{5,13},{6,14},{7,15},{8,16},{9,17... | collective-permute-start | bytes 2359304 | tf_op jit(solution)/shard_map/ppermute | solution.py:233
  121.1 11.7 %all-to-all-done.2 = bf16[8,72,768]{2,1,0:T(8,128)(2,1)} async-done(((bf16[8,72,768]{2,1,0:T(8,128)(2,1)}), bf16[8,72,768]{2,1,0:T(8,128)(2,1)}, u32[]{:S(2)}, u32[]{:S(2)}) %all-to-all-start.2) | async-done | bytes 884768 | tf_op jit(solution)/shard_map/all_to_all | solution.py:144
  132.8 4.1 %collective-permute-done.7.refs_3_ = bf16[512,768]{1,0:T(8,128)(2,1)} collective-permute-done((bf16[512,768]{1,0:T(8,128)(2,1)}, bf16[512,768]{1,0:T(8,128)(2,1)}, u32[]{:S(2)}, u32[]{:S(2)}) %collective-permute-start.7) | collective-permute-done | bytes 786464 | tf_op jit(solution)/shard_map/ppermute | solution.py:232
  136.9 1.2 collective-permute-done.8.refs_2_
  138.1 1.9 collective-permute-start.9
  140.1 1.9 slice.52
  142.0 2.2 %copy.14 = bf16[576,512]{0,1:T(8,128)(2,1)} copy(bf16[576,512]{1,0:T(8,128)(2,1)} %slice.52) | data formatting | bytes 1179648
  144.2 1.1 copy-done.2
  145.3 6.1 %shard_map.102 = (bf16[4,512,768]{2,1,0:T(8,128)(2,1)S(1)}, bf16[4,576,384]{2,1,0:T(8,128)(2,1)S(1)}, bf16[4,576,384]{2,1,0:T(8,128)(2,1)S(1)}) custom-call(s32[1]{0:T(128)} %bitcast.4.place_ref, bf16[576,768]{1,0:T(8,128)(2,1)} %bitcast.15.own_ref, bf16[576,768]{1,0:T(8,128)(2,1)} %collective-permute-done.9.other_ref, ...), custom_call_target="tpu_custom_call" | custom-call | flops 1811939328 | bytes 14000000 | tf_op jit(solution)/shard_map/pallas_call | solution.py:89
  151.4 1.2 copy-done.3
  152.6 1.2 copy-done.5
  153.8 1.5 dynamic-slice_bitcast_fusion.2
  155.3 1.3 copy-done.1
  156.6 5.7 %collective-permute-start.10 = (bf16[512,768]{1,0:T(8,128)(2,1)}, bf16[512,768]{1,0:T(8,128)(2,1)}, u32[]{:S(2)}, u32[]{:S(2)}) collective-permute-start(bf16[512,768]{1,0:T(8,128)(2,1)} %get-tuple-element.34), channel_id=1, source_target_pairs={{0,8},{1,9},{2,10},{3,11},{4,12},{5,13},{6,14},{7,15},{8,16},{9,17... | collective-permute-start | bytes 2359304 | tf_op jit(solution)/shard_map/ppermute | solution.py:178
  162.3 1.9 collective-permute-start.12
  164.3 3.4 %collective-permute-start.11 = (bf16[512,768]{1,0:T(8,128)(2,1)}, bf16[512,768]{1,0:T(8,128)(2,1)}, u32[]{:S(2)}, u32[]{:S(2)}) collective-permute-start(bf16[512,768]{1,0:T(8,128)(2,1)} %get-tuple-element.36), channel_id=1, source_target_pairs={{0,16},{1,17},{2,18},{3,19},{4,20},{5,21},{6,22},{7,23},{8,24},{9,... | collective-permute-start | bytes 2359304 | tf_op jit(solution)/shard_map/ppermute | solution.py:178
  167.7 5.3 %shard_map.103 = bf16[576,512]{1,0:T(8,128)(2,1)} custom-call(s32[4]{0:T(128)S(1)} %pad_add_fusion.order_ref, bf16[4,576,384]{2,1,0:T(8,128)(2,1)S(1)} %copy-done.4, bf16[4,576,384]{2,1,0:T(8,128)(2,1)S(1)} %copy-done.6, bf16[512,768]{1,0:T(8,128)(2,1)} %pad_maximum_fusion.2.refs_0_, bf16[512,768]{1,0:T(8,128)(2,1)} %collective-permute-done.6.refs_1_, ...), custom_call_target="tpu_custom_call" | custom-call | flops 1811939328 | bytes 7000000 | tf_op jit(solution)/shard_map/pallas_call | solution.py:129
  173.0 6.9 %all-to-all-start.3 = ((bf16[8,72,512]{2,1,0:T(8,128)(2,1)}), bf16[8,72,512]{2,1,0:T(8,128)(2,1)S(1)}, u32[]{:S(2)}, u32[]{:S(2)}) async-start(bf16[8,72,512]{2,1,0:T(8,128)(2,1)} %bitcast.29), calls=%async_computation.4 | async-start | bytes 1179648 | tf_op jit(solution)/shard_map/all_to_all | solution.py:144
  180.0 17.0 %collective-permute-done.10 = bf16[512,768]{1,0:T(8,128)(2,1)} collective-permute-done((bf16[512,768]{1,0:T(8,128)(2,1)}, bf16[512,768]{1,0:T(8,128)(2,1)}, u32[]{:S(2)}, u32[]{:S(2)}) %collective-permute-start.10) | collective-permute-done | bytes 786464 | tf_op jit(solution)/shard_map/ppermute | solution.py:178
  196.9 5.3 %collective-permute-done.12 = bf16[512,768]{1,0:T(8,128)(2,1)} collective-permute-done((bf16[512,768]{1,0:T(8,128)(2,1)}, bf16[512,768]{1,0:T(8,128)(2,1)}, u32[]{:S(2)}, u32[]{:S(2)}) %collective-permute-start.12) | collective-permute-done | bytes 786464 | tf_op jit(solution)/shard_map/ppermute | solution.py:178
  202.3 2.3 %fusion.13 = bf16[512,768]{1,0:T(8,128)(2,1)S(1)} fusion(bf16[512,768]{1,0:T(8,128)(2,1)} %collective-permute-done.12, bf16[512,768]{1,0:T(8,128)(2,1)} %collective-permute-done.11, bf16[512,768]{1,0:T(8,128)(2,1)} %collective-permute-done.10, bf16[4,512,768]{2,1,0:T(8,128)(2,1)} %copy-done.1, s32[]{:T(128)S(6)} %select_n.54), kind=kLoop, calls=%fused_computation.21 | loop fusion | flops 3538944 | bytes 3932164 | tf_op jit(solution)/shard_map/convert_element_type | solution.py:266
  204.6 1.0 fusion.23
  205.6 0.8 multiply_convert_fusion
  (51 shorter events, 5.8 us)
Async XLA Ops:
  7.2 17.3 %copy-start.11 = (bf16[72,512]{1,0:T(8,128)(2,1)S(1)}, bf16[72,512]{1,0:T(8,128)(2,1)}, u32[]{:S(2)}) copy-start(bf16[72,512]{1,0:T(8,128)(2,1)} %param.8) | copy-start | bytes 221188
  7.2 100.0 %all-gather.3.cloned.1.call-start = ((), (), s32[]{:S(2)}) async-start(), calls=%async_computation.5 | async-start | bytes 3760128 | tf_op jit(solution)/shard_map/all_gather | solution.py:219
  8.3 10.9 %collective-permute-start.4 = (bf16[72,768]{1,0:T(8,128)(2,1)S(1)}, bf16[72,768]{1,0:T(8,128)(2,1)S(1)}, u32[]{:S(2)}, u32[]{:S(2)}) collective-permute-start(bf16[72,768]{1,0:T(8,128)(2,1)S(1)} %get-tuple-element.45), channel_id=1, source_target_pairs={{0,0},{1,1},{2,2},{3,3},{4,4},{5,5},{6,6},{7,7},{8,64},{9,65},{10,... | collective-permute-start | bytes 331784 | tf_op jit(solution)/shard_map/ppermute | solution.py:208
  11.1 12.5 %collective-permute-start.5 = (bf16[72,768]{1,0:T(8,128)(2,1)S(1)}, bf16[72,768]{1,0:T(8,128)(2,1)S(1)}, u32[]{:S(2)}, u32[]{:S(2)}) collective-permute-start(bf16[72,768]{1,0:T(8,128)(2,1)S(1)} %get-tuple-element.46), channel_id=1, source_target_pairs={{0,64},{1,65},{2,66},{3,67},{4,68},{5,69},{6,70},{7,71},{8,0},{9,1... | collective-permute-start | bytes 331784 | tf_op jit(solution)/shard_map/ppermute | solution.py:208
  23.7 12.0 %copy-start.7 = (bf16[384,512]{1,0:T(8,128)(2,1)S(1)}, bf16[384,512]{1,0:T(8,128)(2,1)}, u32[]{:S(2)}) copy-start(bf16[384,512]{1,0:T(8,128)(2,1)} %param.13) | copy-start | bytes 1179652
  23.7 20.0 %copy-start.9 = (bf16[512,384]{1,0:T(8,128)(2,1)S(1)}, bf16[512,384]{1,0:T(8,128)(2,1)}, u32[]{:S(2)}) copy-start(bf16[512,384]{1,0:T(8,128)(2,1)} %param.12) | copy-start | bytes 1179652
  23.7 20.0 %copy-start.10 = (bf16[512,384]{1,0:T(8,128)(2,1)S(1)}, bf16[512,384]{1,0:T(8,128)(2,1)}, u32[]{:S(2)}) copy-start(bf16[512,384]{1,0:T(8,128)(2,1)} %param.11) | copy-start | bytes 1179652
  25.3 35.0 %all-to-all-start = ((bf16[8,72,512]{2,1,0:T(8,128)(2,1)}), bf16[8,72,512]{2,1,0:T(8,128)(2,1)S(1)}, u32[]{:S(2)}, u32[]{:S(2)}) async-start(bf16[8,72,512]{2,1,0:T(8,128)(2,1)} %broadcast_in_dim.4), calls=%async_computation | async-start | bytes 1179648 | tf_op jit(solution)/shard_map/all_to_all | solution.py:144
  35.7 13.9 %collective-permute-start = (bf16[384,512]{1,0:T(8,128)(2,1)S(1)}, bf16[384,512]{1,0:T(8,128)(2,1)S(1)}, u32[]{:S(2)}, u32[]{:S(2)}) collective-permute-start(bf16[384,512]{1,0:T(8,128)(2,1)S(1)} %copy-done.7), channel_id=1, source_target_pairs={{0,8},{1,9},{2,10},{3,11},{4,12},{5,13},{6,14},{7,15},{8,16},{9,17... | collective-permute-start | bytes 1179656 | tf_op jit(solution)/shard_map/ppermute | solution.py:192
  37.6 22.4 %collective-permute-start.2 = (bf16[384,512]{1,0:T(8,128)(2,1)S(1)}, bf16[384,512]{1,0:T(8,128)(2,1)S(1)}, u32[]{:S(2)}, u32[]{:S(2)}) collective-permute-start(bf16[384,512]{1,0:T(8,128)(2,1)S(1)} %copy-done.7), channel_id=1, source_target_pairs={{0,24},{1,25},{2,26},{3,27},{4,28},{5,29},{6,30},{7,31},{8,0},{9,1... | collective-permute-start | bytes 1179656 | tf_op jit(solution)/shard_map/ppermute | solution.py:192
  41.5 18.5 %collective-permute-start.1 = (bf16[384,512]{1,0:T(8,128)(2,1)S(1)}, bf16[384,512]{1,0:T(8,128)(2,1)S(1)}, u32[]{:S(2)}, u32[]{:S(2)}) collective-permute-start(bf16[384,512]{1,0:T(8,128)(2,1)S(1)} %copy-done.7), channel_id=1, source_target_pairs={{0,16},{1,17},{2,18},{3,19},{4,20},{5,21},{6,22},{7,23},{8,24},{9,... | collective-permute-start | bytes 1179656 | tf_op jit(solution)/shard_map/ppermute | solution.py:192
  61.0 4.3 %collective-permute-start.3 = (bf16[576,768]{1,0:T(8,128)(2,1)S(1)}, bf16[576,768]{1,0:T(8,128)(2,1)S(1)}, u32[]{:S(2)}, u32[]{:S(2)}) collective-permute-start(bf16[576,768]{1,0:T(8,128)(2,1)S(1)} %convolution_convert_fusion), channel_id=1, source_target_pairs={{0,32},{32,0},{64,96},{96,64},{128,160},{160,128},{192,224},{224,1... | collective-permute-start | bytes 2654216 | tf_op jit(solution)/shard_map/ppermute | solution.py:236
  66.9 9.4 %copy-start.12 = (bf16[72,512]{1,0:T(8,128)(2,1)S(1)}, bf16[72,512]{1,0:T(8,128)(2,1)}, u32[]{:S(2)}) copy-start(bf16[72,512]{1,0:T(8,128)(2,1)} %param.7) | copy-start | bytes 221188
  66.9 34.8 %all-to-all-start.1 = ((bf16[8,72,768]{2,1,0:T(8,128)(2,1)}), bf16[8,72,768]{2,1,0:T(8,128)(2,1)S(1)}, u32[]{:S(2)}, u32[]{:S(2)}) async-start(bf16[8,72,768]{2,1,0:T(8,128)(2,1)} %bitcast.14), calls=%async_computation.1 | async-start | bytes 1769472 | tf_op jit(solution)/shard_map/all_to_all | solution.py:144
  76.2 63.8 %all-gather.5.cloned.1.call-start = ((), (), s32[]{:S(2)}) async-start(), calls=%async_computation.6 | async-start | bytes 1327104 | tf_op jit(solution)/shard_map/all_gather | solution.py:225
  77.0 39.0 %collective-permute-start.6 = (bf16[512,768]{1,0:T(8,128)(2,1)}, bf16[512,768]{1,0:T(8,128)(2,1)}, u32[]{:S(2)}, u32[]{:S(2)}) collective-permute-start(bf16[512,768]{1,0:T(8,128)(2,1)} %pad_maximum_fusion.2.refs_0_), channel_id=1, source_target_pairs={{0,8},{1,9},{2,10},{3,11},{4,12},{5,13},{6,14},{7,15},{8,16},{9,17... | collective-permute-start | bytes 2359304 | tf_op jit(solution)/shard_map/ppermute | solution.py:231
  102.9 29.9 %all-to-all-start.2 = ((bf16[8,72,768]{2,1,0:T(8,128)(2,1)}), bf16[8,72,768]{2,1,0:T(8,128)(2,1)}, u32[]{:S(2)}, u32[]{:S(2)}) async-start(bf16[8,72,768]{2,1,0:T(8,128)(2,1)} %broadcast_in_dim.5), calls=%async_computation.2 | async-start | bytes 1769472 | tf_op jit(solution)/shard_map/all_to_all | solution.py:144
  107.1 65.9 %reduce-scatter.2.cloned.1.call-start = ((), (), s32[]{:S(2)}) async-start(), calls=%async_computation.7 | async-start | bytes 1966080 | tf_op jit(solution)/shard_map/reduce_scatter | solution.py:254
  113.7 30.4 %copy-start = (bf16[1152,1536]{1,0:T(8,128)(2,1)S(1)}, bf16[1152,1536]{1,0:T(8,128)(2,1)}, u32[]{:S(2)}) copy-start(bf16[1152,1536]{1,0:T(8,128)(2,1)} %all-gather.3.cloned.1.call-done) | copy-start | bytes 10616836
  113.8 23.1 %collective-permute-start.7 = (bf16[512,768]{1,0:T(8,128)(2,1)}, bf16[512,768]{1,0:T(8,128)(2,1)}, u32[]{:S(2)}, u32[]{:S(2)}) collective-permute-start(bf16[512,768]{1,0:T(8,128)(2,1)} %pad_maximum_fusion.2.refs_0_), channel_id=1, source_target_pairs={{0,24},{1,25},{2,26},{3,27},{4,28},{5,29},{6,30},{7,31},{8,0},{9,1... | collective-permute-start | bytes 2359304 | tf_op jit(solution)/shard_map/ppermute | solution.py:232
  116.0 22.1 %collective-permute-start.8 = (bf16[512,768]{1,0:T(8,128)(2,1)}, bf16[512,768]{1,0:T(8,128)(2,1)}, u32[]{:S(2)}, u32[]{:S(2)}) collective-permute-start(bf16[512,768]{1,0:T(8,128)(2,1)} %collective-permute-done.6.refs_1_), channel_id=1, source_target_pairs={{0,8},{1,9},{2,10},{3,11},{4,12},{5,13},{6,14},{7,15},{8,16},{9,17... | collective-permute-start | bytes 2359304 | tf_op jit(solution)/shard_map/ppermute | solution.py:233
  138.1 6.1 %collective-permute-start.9 = (bf16[576,768]{1,0:T(8,128)(2,1)}, bf16[576,768]{1,0:T(8,128)(2,1)}, u32[]{:S(2)}, u32[]{:S(2)}) collective-permute-start(bf16[576,768]{1,0:T(8,128)(2,1)} %bitcast.15.own_ref), channel_id=1, source_target_pairs={{0,32},{32,0},{64,96},{96,64},{128,160},{160,128},{192,224},{224,1... | collective-permute-start | bytes 2654216 | tf_op jit(solution)/shard_map/ppermute | solution.py:262
  144.2 1.1 copy-start.2
  151.4 1.2 copy-start.3
  152.6 1.2 copy-start.5
  153.8 2.8 %copy-start.1 = (bf16[4,512,768]{2,1,0:T(8,128)(2,1)}, bf16[4,512,768]{2,1,0:T(8,128)(2,1)S(1)}, u32[]{:S(2)}) copy-start(bf16[4,512,768]{2,1,0:T(8,128)(2,1)S(1)} %get-tuple-element.28) | copy-start | bytes 9437188
  153.8 13.9 %copy-start.4 = (bf16[4,576,384]{2,1,0:T(8,128)(2,1)S(1)}, bf16[4,576,384]{2,1,0:T(8,128)(2,1)}, u32[]{:S(2)}) copy-start(bf16[4,576,384]{2,1,0:T(8,128)(2,1)} %copy-done.3) | copy-start | bytes 5308420
  153.8 13.9 %copy-start.6 = (bf16[4,576,384]{2,1,0:T(8,128)(2,1)S(1)}, bf16[4,576,384]{2,1,0:T(8,128)(2,1)}, u32[]{:S(2)}) copy-start(bf16[4,576,384]{2,1,0:T(8,128)(2,1)} %copy-done.5) | copy-start | bytes 5308420
  156.6 40.4 %collective-permute-start.10 = (bf16[512,768]{1,0:T(8,128)(2,1)}, bf16[512,768]{1,0:T(8,128)(2,1)}, u32[]{:S(2)}, u32[]{:S(2)}) collective-permute-start(bf16[512,768]{1,0:T(8,128)(2,1)} %get-tuple-element.34), channel_id=1, source_target_pairs={{0,8},{1,9},{2,10},{3,11},{4,12},{5,13},{6,14},{7,15},{8,16},{9,17... | collective-permute-start | bytes 2359304 | tf_op jit(solution)/shard_map/ppermute | solution.py:178
  162.3 39.9 %collective-permute-start.12 = (bf16[512,768]{1,0:T(8,128)(2,1)}, bf16[512,768]{1,0:T(8,128)(2,1)}, u32[]{:S(2)}, u32[]{:S(2)}) collective-permute-start(bf16[512,768]{1,0:T(8,128)(2,1)} %get-tuple-element.35), channel_id=1, source_target_pairs={{0,24},{1,25},{2,26},{3,27},{4,28},{5,29},{6,30},{7,31},{8,0},{9,1... | collective-permute-start | bytes 2359304 | tf_op jit(solution)/shard_map/ppermute | solution.py:178
  164.3 38.0 %collective-permute-start.11 = (bf16[512,768]{1,0:T(8,128)(2,1)}, bf16[512,768]{1,0:T(8,128)(2,1)}, u32[]{:S(2)}, u32[]{:S(2)}) collective-permute-start(bf16[512,768]{1,0:T(8,128)(2,1)} %get-tuple-element.36), channel_id=1, source_target_pairs={{0,16},{1,17},{2,18},{3,19},{4,20},{5,21},{6,22},{7,23},{8,24},{9,... | collective-permute-start | bytes 2359304 | tf_op jit(solution)/shard_map/ppermute | solution.py:178
  173.0 33.4 %all-to-all-start.3 = ((bf16[8,72,512]{2,1,0:T(8,128)(2,1)}), bf16[8,72,512]{2,1,0:T(8,128)(2,1)S(1)}, u32[]{:S(2)}, u32[]{:S(2)}) async-start(bf16[8,72,512]{2,1,0:T(8,128)(2,1)} %bitcast.29), calls=%async_computation.4 | async-start | bytes 1179648 | tf_op jit(solution)/shard_map/all_to_all | solution.py:144
  204.6 1.0 copy-start.8
Sparse Core Ops, SparseCore 0:
  24.6 48.2 all-gather.2
  79.7 43.3 all-gather.4
  126.0 28.1 reduce-scatter.1

commit v8 on v7

--- a/solution.py
+++ b/solution.py
@@ -38,10 +38,18 @@
 
 
 def unit_block_kernel(
-    place_ref, own_ref, other_ref, gate_ref, up_ref, tokens_ref,
-    part_ref, gate_grad_ref, up_grad_ref, grad_ref,
+    place_ref, own_ref, other_ref, gate_ref, up_ref, tokens_ref, *refs
 ):
-    mine = pl.program_id(0) // 2 == place_ref[0]
+    n_block = pl.num_programs(0)
+    weights, parts = refs[:4], refs[4:8]
+    input_part_ref, grad_ref, columns_ref, total_ref = refs[8:]
+    step = pl.program_id(0)
+    mine = lax.rem(place_ref[1] + step, n_block) // 2 == place_ref[0]
+
+    @pl.when(step == 0)
+    def _():
+        columns_ref[...] = tokens_ref[...].T
+        total_ref[...] = jnp.zeros_like(total_ref)
 
     @pl.when(mine)
     def _():
@@ -52,92 +60,82 @@
         grad_ref[...] = other_ref[...].astype(jnp.float32)
 
     shape = grad_ref.shape
+    units = shape[-1]
     gate_grad, up_grad = swiglu_grads(
         grad_ref[...],
         gate_ref[...].astype(jnp.float32).reshape(shape),
         up_ref[...].astype(jnp.float32).reshape(shape),
     )
-    gate_grad_ref[0] = gate_grad
-    up_grad_ref[0] = up_grad
-    token_columns = tokens_ref[...]
-    units = shape[-1]
-    for which, grads in enumerate((gate_grad, up_grad)):
-        part_ref[0, :, which * units : (which + 1) * units] = jnp.dot(
-            token_columns, grads, preferred_element_type=jnp.float32
-        ).astype(jnp.bfloat16)
-
-
-def unit_blocks(place, own, other, saved, token_columns):
+    for k, part_ref in enumerate(parts):
+
+        @pl.when(step == k)
+        def _():
+            weight_ref = weights[(len(parts) - k) % len(parts)]
+            total = total_ref[...]
+            for which, grads in enumerate((gate_grad, up_grad)):
+                columns = slice(which * units, (which + 1) * units)
+                part_ref[:, columns] = jnp.dot(
+                    columns_ref[...], grads, preferred_element_type=jnp.float32
+                ).astype(jnp.bfloat16)
+                total = total + contract_last(grads, weight_ref[:, columns])
+            total_ref[...] = total
+
+    @pl.when(step == n_block - 1)
+    def _():
+        input_part_ref[...] = total_ref[...].astype(jnp.bfloat16)
+
+
+def unit_blocks(place, own, other, saved, rows, weights):
     n_y, _, block, width = saved.shape
     units = width // 4
-    features, group_rows = token_columns.shape
-    n_block = 4
+    group_rows = own.shape[0]
+    features = weights[0].shape[0]
+    n_block = len(weights)
+
+    def block_of(j, place):
+        return lax.rem(place[1] + j, n_block)
 
     def half_spec():
-        return pl.BlockSpec((group_rows, units), lambda j, place: (0, j % 2))
+        return pl.BlockSpec(
+            (group_rows, units), lambda j, place: (0, lax.rem(block_of(j, place), 2))
+        )
 
     def saved_spec(first):
-        return pl.BlockSpec(
-            (n_y, 1, block, units), lambda j, place: (0, j // 2, 0, first + j % 2)
-        )
-
-    def out_spec(rows, width):
-        return pl.BlockSpec((1, rows, width), lambda j, place: (j, 0, 0))
-
-    part = jax.ShapeDtypeStruct((n_block, features, 2 * units), jnp.bfloat16)
-    grads = jax.ShapeDtypeStruct((n_block, group_rows, units), jnp.bfloat16)
+        def index(j, place):
+            which = block_of(j, place)
+            return (0, lax.div(which, 2), 0, first + lax.rem(which, 2))
+
+        return pl.BlockSpec((n_y, 1, block, units), index)
+
+    def fixed_spec(*shape):
+        return pl.BlockSpec(shape, lambda j, place: (0, 0))
+
+    part = jax.ShapeDtypeStruct((features, 2 * units), jnp.bfloat16)
+    input_part = jax.ShapeDtypeStruct((group_rows, features), jnp.bfloat16)
     return pl.pallas_call(
         unit_block_kernel,
-        out_shape=(part, grads, grads),
+        out_shape=(part,) * n_block + (input_part,),
         grid_spec=pltpu.PrefetchScalarGridSpec(
             num_scalar_prefetch=1,
             grid=(n_block,),
-            in_specs=[
-                half_spec(),
-                half_spec(),
-                saved_spec(0),
-                saved_spec(2),
-                pl.BlockSpec((features, group_rows), lambda j, place: (0, 0)),
+            in_specs=[half_spec(), half_spec(), saved_spec(0), saved_spec(2)]
+            + [fixed_spec(group_rows, features)]
+            + [fixed_spec(features, 2 * units)] * n_block,
+            out_specs=[fixed_spec(features, 2 * units)] * n_block
+            + [fixed_spec(group_rows, features)],
+            scratch_shapes=[
+                pltpu.VMEM((group_rows, units), jnp.float32),
+                pltpu.VMEM((features, group_rows), jnp.bfloat16),
+                pltpu.VMEM((group_rows, features), jnp.float32),
             ],
-            out_specs=[out_spec(features, 2 * units)] + [out_spec(group_rows, units)] * 2,
-            scratch_shapes=[pltpu.VMEM((group_rows, units), jnp.float32)],
         ),
-        compiler_params=pltpu.CompilerParams(vmem_limit_bytes=32 * 1024 * 1024),
+        compiler_params=pltpu.CompilerParams(vmem_limit_bytes=40 * 1024 * 1024),
         cost_estimate=pl.CostEstimate(
-            flops=4 * n_block * features * units * group_rows,
+            flops=8 * n_block * features * units * group_rows,
             bytes_accessed=14_000_000,
             transcendentals=n_block * group_rows * units,
         ),
-    )(place, own, other, saved, saved, token_columns)
-
-
-def input_grad_kernel(order_ref, gate_ref, up_ref, *refs):
-    weights, out_ref = refs[:-1], refs[-1]
-    units = gate_ref.shape[-1]
-    total = 0.0
-    for step, weight_ref in enumerate(weights):
-        place = order_ref[step]
-        total = total + contract_last(gate_ref[place], weight_ref[:, :units])
-        total = total + contract_last(up_ref[place], weight_ref[:, units:])
-    out_ref[...] = total.astype(jnp.bfloat16)
-
-
-def input_grad_part(order, gate_grad, up_grad, weights):
-    n_block, group_rows, units = gate_grad.shape
-    features = weights[0].shape[0]
-    vmem = pl.BlockSpec(memory_space=pltpu.VMEM)
-    return pl.pallas_call(
-        input_grad_kernel,
-        out_shape=jax.ShapeDtypeStruct((group_rows, features), jnp.bfloat16),
-        in_specs=[pl.BlockSpec(memory_space=pltpu.SMEM)] + [vmem] * (2 + n_block),
-        out_specs=vmem,
-        compiler_params=pltpu.CompilerParams(vmem_limit_bytes=32 * 1024 * 1024),
-        cost_estimate=pl.CostEstimate(
-            flops=4 * n_block * features * units * group_rows,
-            bytes_accessed=7_000_000,
-            transcendentals=0,
-        ),
-    )(order, gate_grad, up_grad, *weights)
+    )(place, own, other, saved, saved, rows, *weights)
 
 
 def exchange(pieces, axis, groups):
@@ -171,13 +169,6 @@
             (x * N_Z + z, (x + step) % n_x * N_Z + z) for x in range(n_x) for z in range(N_Z)
         ]
 
-    def sum_over_x(parts):
-        total = pick(parts, x_here).astype(jnp.float32)
-        for step in range(1, n_x):
-            piece = pick(parts, lax.rem(x_here + step, n_x))
-            total = total + lax.ppermute(piece, "col", x_shift(step)).astype(jnp.float32)
-        return total
-
     def to_group(turn):
         pairs = []
         for r in range(n_row):
@@ -222,15 +213,12 @@
 
     both = jnp.concatenate([tokens, out_grad], axis=1)
     both, saved_share = lax.optimization_barrier((both, saved_share))
-    token_rows = lax.all_gather(both, "col", axis=0, tiled=True, axis_index_groups=z_groups)[
-        :, :features
-    ]
+    both_rows = lax.all_gather(both, "col", axis=0, tiled=True, axis_index_groups=z_groups)
 
     w_both = jnp.concatenate([w_gate, w_up], axis=1)
     w_both, grad_rows = lax.optimization_barrier((w_both, grad_rows))
     w_left = lax.ppermute(w_both, "col", x_shift(1))
     w_right = lax.ppermute(w_both, "col", x_shift(n_x - 1))
-    w_far = lax.ppermute(w_left, "col", x_shift(1))
 
     give = contract_last(grad_rows, down_half(1)).astype(jnp.bfloat16)
     got = lax.ppermute(give, "row", core_swap)
@@ -238,6 +226,8 @@
     pair = (keep.astype(jnp.float32) + got.astype(jnp.float32)).astype(jnp.bfloat16)
     terms = exchange(pair.reshape(n_y, block, half), "row", y_groups)
     share = jnp.sum(terms.astype(jnp.float32), axis=0).astype(jnp.bfloat16)
+    share, w_left, w_right = lax.optimization_barrier((share, w_left, w_right))
+    w_far = lax.ppermute(w_left, "col", x_shift(1))
     own = spread(share, n_y, "row", y_groups).reshape(group_rows, half)
 
     grad_scale = (rows * n_row) ** (-0.5)
@@ -255,17 +245,19 @@
         down_part, "col", scatter_dimension=0, tiled=True, axis_index_groups=x_groups
     )[0]
 
-    own, w_left, w_right, w_far = lax.optimization_barrier((own, w_left, w_right, w_far))
+    own, w_far = lax.optimization_barrier((own, w_far))
     weights = [w_both, w_left, w_far, w_right]
-    order = jnp.stack([lax.rem(x_here - step + n_x, n_x) for step in range(n_x)])
 
     other = lax.ppermute(own, "row", core_swap)
-    unit_part, gate_grad, up_grad = unit_blocks(
-        core.reshape(1), own, other, saved, token_rows.swapaxes(0, 1)
-    )
-    unit_wgrad = (sum_over_x(unit_part) * grad_scale).astype(jnp.bfloat16)
+    *unit_parts, part_in = unit_blocks(
+        jnp.stack([core, x_here]), own, other, saved, both_rows, weights
+    )
+    unit_sum = unit_parts[0].astype(jnp.float32)
+    for step in range(1, n_x):
+        moved_part = lax.ppermute(unit_parts[step], "col", x_shift(step))
+        unit_sum = unit_sum + moved_part.astype(jnp.float32)
+    unit_wgrad = (unit_sum * grad_scale).astype(jnp.bfloat16)
     gate_wgrad, up_wgrad = unit_wgrad[:, :units], unit_wgrad[:, units:]
-    part_in = input_grad_part(order, gate_grad, up_grad, weights)
     part_in, down_sum = lax.optimization_barrier((part_in, down_sum))
     down_wgrad = (down_sum.astype(jnp.float32) * grad_scale).astype(jnp.bfloat16)
     token_terms = exchange(

time: 215 us -> 219 us (1.019)
  starting transfers between devices: 69.5 us -> 73 us
  local copies, waits for them, and re-layouts: 15.7 us -> 12.6 us
  Pallas kernels: 11.4 us -> 14 us
    ppermute x3, waiting for transfers between devices: 22.3 us -> 28.1 us  [local(): moved_part = lax.ppermute(unit_parts[step], 'col', x_shift(step))]
    all_to_all x4, waiting for transfers between devices: 34.5 us -> 30 us  [exchange(): lax.all_to_all(pieces, axis, 0, 0, tiled=True, axis_index_groups=groups)]
    ppermute x1, waiting for transfers between devices: 4.12 us -> 0.01 us  [local(): w_right = lax.ppermute(w_both, 'col', x_shift(n_x - 1))]
    ppermute x1, starting transfers between devices: 1.92 us -> 5.13 us  [local(): w_left = lax.ppermute(w_both, 'col', x_shift(1))]
    pallas_call x2 -> x1, Pallas kernels: 11.4 us -> 14 us  [unit_blocks(): pl.pallas_call(unit_block_kernel, out_shape=(part,) * n_block + (input_pa...]
    ppermute x1, waiting for transfers between devices: 0.01 us -> 2.47 us  [local(): other = lax.ppermute(own, 'row', core_swap)]
    unnamed x27 -> x36, local copies, waits for them, and re-layouts: 7.1 us -> 7.13 us
  transfers between devices with their start and end apart: 20 -> 20, of which waited for: 11 -> 11; matrix products, arithmetic and copies ran while one was open for 11% -> 8% of each run, Pallas kernels for 5% -> 6%
where the time goes in v8:
time: 219 us; the launch traced here: 217 us
  waiting for transfers between devices  90.2 us (41%)
  starting transfers between devices  73 us (33%)
  between operations  14.2 us (6%)
  Pallas kernels  14 us (6%)
  local copies, waits for them, and re-layouts  12.6 us (6%)
  other arithmetic  9.54 us (4%)
  matrix products  3.84 us (2%)
    all_to_all x4, starting transfers between devices, exchange(): lax.all_to_all(pieces, axis, 0, 0, tiled=True, axis_index_groups=groups)  31.5 us
    all_to_all x4, waiting for transfers between devices, exchange(): lax.all_to_all(pieces, axis, 0, 0, tiled=True, axis_index_groups=groups)  30 us
    ppermute x3, waiting for transfers between devices, local(): moved_part = lax.ppermute(unit_parts[step], 'col', x_shift(step))  28.1 us
    ppermute x3, waiting for transfers between devices, local(): lax.ppermute(w_down, 'col', x_shift(step))  15.2 us
    pallas_call x1, Pallas kernels, unit_blocks(): pl.pallas_call(unit_block_kernel, out_shape=(part,) * n_block + (input_pa...  14 us
    ppermute x3, starting transfers between devices, local(): moved_part = lax.ppermute(unit_parts[step], 'col', x_shift(step))  10.1 us
    ppermute x2, waiting for transfers between devices, local(): lax.ppermute(pick(saved_pieces, lax.rem(x_here + turn, 2)), ('row', 'col'...  8.74 us
    ppermute x3, starting transfers between devices, local(): lax.ppermute(w_down, 'col', x_shift(step))  7.95 us
  transfers between devices with their start and end apart: 20, of which 11 were waited for; matrix products, arithmetic and copies ran while one was open for 8% of the time, Pallas kernels for 6%

profile of v8, /device:TPU:6, one launch (start us, length us, event | category | flops | bytes accessed | tf_op | source)
XLA Modules:
  0.0 217.4 jit_solution(12440689854584327283)
XLA Ops:
  7.3 1.0 pad_maximum_fusion.3
  8.3 2.8 %collective-permute-start.6 = (bf16[72,768]{1,0:T(8,128)(2,1)S(1)}, bf16[72,768]{1,0:T(8,128)(2,1)S(1)}, u32[]{:S(2)}, u32[]{:S(2)}) collective-permute-start(bf16[72,768]{1,0:T(8,128)(2,1)S(1)} %get-tuple-element.48), channel_id=1, source_target_pairs={{0,0},{1,1},{2,2},{3,3},{4,4},{5,5},{6,6},{7,7},{8,64},{9,65},{10,... | collective-permute-start | bytes 331784 | tf_op jit(solution)/shard_map/ppermute | solution.py:199
  11.1 3.8 %collective-permute-start.7 = (bf16[72,768]{1,0:T(8,128)(2,1)S(1)}, bf16[72,768]{1,0:T(8,128)(2,1)S(1)}, u32[]{:S(2)}, u32[]{:S(2)}) collective-permute-start(bf16[72,768]{1,0:T(8,128)(2,1)S(1)} %get-tuple-element.49), channel_id=1, source_target_pairs={{0,64},{1,65},{2,66},{3,67},{4,68},{5,69},{6,70},{7,71},{8,0},{9,1... | collective-permute-start | bytes 331784 | tf_op jit(solution)/shard_map/ppermute | solution.py:199
  14.9 4.2 %collective-permute-done.6 = bf16[72,768]{1,0:T(8,128)(2,1)S(1)} collective-permute-done((bf16[72,768]{1,0:T(8,128)(2,1)S(1)}, bf16[72,768]{1,0:T(8,128)(2,1)S(1)}, u32[]{:S(2)}, u32[]{:S(2)}) %collective-permute-start.6) | collective-permute-done | bytes 110624 | tf_op jit(solution)/shard_map/ppermute | solution.py:199
  19.1 4.5 %collective-permute-done.7 = bf16[72,768]{1,0:T(8,128)(2,1)S(1)} collective-permute-done((bf16[72,768]{1,0:T(8,128)(2,1)S(1)}, bf16[72,768]{1,0:T(8,128)(2,1)S(1)}, u32[]{:S(2)}, u32[]{:S(2)}) %collective-permute-start.7) | collective-permute-done | bytes 110624 | tf_op jit(solution)/shard_map/ppermute | solution.py:199
  24.5 0.9 broadcast_in_dim.4
  25.3 10.3 %all-to-all-start = ((bf16[8,72,512]{2,1,0:T(8,128)(2,1)}), bf16[8,72,512]{2,1,0:T(8,128)(2,1)S(1)}, u32[]{:S(2)}, u32[]{:S(2)}) async-start(bf16[8,72,512]{2,1,0:T(8,128)(2,1)} %broadcast_in_dim.4), calls=%async_computation | async-start | bytes 1179648 | tf_op jit(solution)/shard_map/all_to_all | solution.py:142
  35.6 1.9 collective-permute-start
  37.6 3.9 %collective-permute-start.2 = (bf16[384,512]{1,0:T(8,128)(2,1)S(1)}, bf16[384,512]{1,0:T(8,128)(2,1)S(1)}, u32[]{:S(2)}, u32[]{:S(2)}) collective-permute-start(bf16[384,512]{1,0:T(8,128)(2,1)S(1)} %copy-done.13), channel_id=1, source_target_pairs={{0,24},{1,25},{2,26},{3,27},{4,28},{5,29},{6,30},{7,31},{8,0},{9,1... | collective-permute-start | bytes 1179656 | tf_op jit(solution)/shard_map/ppermute | solution.py:183
  41.5 2.1 collective-permute-start.1
  43.7 1.1 pad_maximum_fusion.2.refs_0_
  44.8 4.8 %collective-permute-done = bf16[384,512]{1,0:T(8,128)(2,1)S(1)} collective-permute-done((bf16[384,512]{1,0:T(8,128)(2,1)S(1)}, bf16[384,512]{1,0:T(8,128)(2,1)S(1)}, u32[]{:S(2)}, u32[]{:S(2)}) %collective-permute-start) | collective-permute-done | bytes 393248 | tf_op jit(solution)/shard_map/ppermute | solution.py:183
  49.5 10.4 %collective-permute-done.2 = bf16[384,512]{1,0:T(8,128)(2,1)S(1)} collective-permute-done((bf16[384,512]{1,0:T(8,128)(2,1)S(1)}, bf16[384,512]{1,0:T(8,128)(2,1)S(1)}, u32[]{:S(2)}, u32[]{:S(2)}) %collective-permute-start.2) | collective-permute-done | bytes 393248 | tf_op jit(solution)/shard_map/ppermute | solution.py:183
  61.0 1.9 collective-permute-start.3
  62.9 2.4 %collective-permute-done.3 = bf16[576,768]{1,0:T(8,128)(2,1)S(1)} collective-permute-done((bf16[576,768]{1,0:T(8,128)(2,1)S(1)}, bf16[576,768]{1,0:T(8,128)(2,1)S(1)}, u32[]{:S(2)}, u32[]{:S(2)}) %collective-permute-start.3) | collective-permute-done | bytes 884768 | tf_op jit(solution)/shard_map/ppermute | solution.py:224
  65.3 1.6 add_convert_fusion
  66.9 9.3 %all-to-all-start.1 = ((bf16[8,72,768]{2,1,0:T(8,128)(2,1)}), bf16[8,72,768]{2,1,0:T(8,128)(2,1)S(1)}, u32[]{:S(2)}, u32[]{:S(2)}) async-start(bf16[8,72,768]{2,1,0:T(8,128)(2,1)} %bitcast.11), calls=%async_computation.1 | async-start | bytes 1769472 | tf_op jit(solution)/shard_map/all_to_all | solution.py:142
  76.2 1.9 collective-permute-start.5
  78.2 5.1 %collective-permute-start.4 = (bf16[512,768]{1,0:T(8,128)(2,1)S(1)}, bf16[512,768]{1,0:T(8,128)(2,1)S(1)}, u32[]{:S(2)}, u32[]{:S(2)}) collective-permute-start(bf16[512,768]{1,0:T(8,128)(2,1)S(1)} %pad_maximum_fusion.2.refs_0_), channel_id=1, source_target_pairs={{0,8},{1,9},{2,10},{3,11},{4,12},{5,13},{6,14},{7,15},{8,16},{9,17... | collective-permute-start | bytes 2359304 | tf_op jit(solution)/shard_map/ppermute | solution.py:220
  84.0 17.7 %all-to-all-done.1 = bf16[8,72,768]{2,1,0:T(8,128)(2,1)S(1)} async-done(((bf16[8,72,768]{2,1,0:T(8,128)(2,1)}), bf16[8,72,768]{2,1,0:T(8,128)(2,1)S(1)}, u32[]{:S(2)}, u32[]{:S(2)}) %all-to-all-start.1) | async-done | bytes 884768 | tf_op jit(solution)/shard_map/all_to_all | solution.py:142
  101.9 1.2 broadcast_in_dim.5
  103.1 4.8 %all-to-all-start.2 = ((bf16[8,72,768]{2,1,0:T(8,128)(2,1)}), bf16[8,72,768]{2,1,0:T(8,128)(2,1)}, u32[]{:S(2)}, u32[]{:S(2)}) async-start(bf16[8,72,768]{2,1,0:T(8,128)(2,1)} %broadcast_in_dim.5), calls=%async_computation.2 | async-start | bytes 1769472 | tf_op jit(solution)/shard_map/all_to_all | solution.py:142
  107.9 2.3 %fusion.18 = (bf16[8,1,72,768]{3,2,1,0:T(8,128)(2,1)S(1)}, bf16[8,1,72,768]{3,2,1,0:T(8,128)(2,1)S(1)}, bf16[8,1,72,768]{3,2,1,0:T(8,128)(2,1)S(1)}, bf16[8,1,72,768]{3,2,1,0:T(8,128)(2,1)S(1)}) fusion(bf16[8,2,72,1536]{3,2,1,0:T(8,128)(2,1)} %bitcast.44), kind=kLoop, calls=%fused_computation.44 | loop fusion | bytes 7077888 | tf_op jit(solution)/shard_map/slice | solution.py:236
  111.3 0.8 convolution_convert_fusion.3
  112.8 0.8 convolution_convert_fusion.2
  113.6 1.3 pad_maximum_fusion.1
  114.9 5.7 %collective-permute-start.8 = (bf16[512,768]{1,0:T(8,128)(2,1)}, bf16[512,768]{1,0:T(8,128)(2,1)}, u32[]{:S(2)}, u32[]{:S(2)}) collective-permute-start(bf16[512,768]{1,0:T(8,128)(2,1)} %copy-done.9), channel_id=1, source_target_pairs={{0,8},{1,9},{2,10},{3,11},{4,12},{5,13},{6,14},{7,15},{8,16},{9,17... | collective-permute-start | bytes 2359304 | tf_op jit(solution)/shard_map/ppermute | solution.py:230
  120.6 12.3 %all-to-all-done.2 = bf16[8,72,768]{2,1,0:T(8,128)(2,1)} async-done(((bf16[8,72,768]{2,1,0:T(8,128)(2,1)}), bf16[8,72,768]{2,1,0:T(8,128)(2,1)}, u32[]{:S(2)}, u32[]{:S(2)}) %all-to-all-start.2) | async-done | bytes 884768 | tf_op jit(solution)/shard_map/all_to_all | solution.py:142
  133.0 3.2 %collective-permute-done.8.refs_2_ = bf16[512,768]{1,0:T(8,128)(2,1)} collective-permute-done((bf16[512,768]{1,0:T(8,128)(2,1)}, bf16[512,768]{1,0:T(8,128)(2,1)}, u32[]{:S(2)}, u32[]{:S(2)}) %collective-permute-start.8) | collective-permute-done | bytes 786464 | tf_op jit(solution)/shard_map/ppermute | solution.py:230
  136.1 2.1 collective-permute-start.9
  138.3 2.5 %collective-permute-done.9.other_ref = bf16[576,768]{1,0:T(8,128)(2,1)} collective-permute-done((bf16[576,768]{1,0:T(8,128)(2,1)}, bf16[576,768]{1,0:T(8,128)(2,1)}, u32[]{:S(2)}, u32[]{:S(2)}) %collective-permute-start.9) | collective-permute-done | bytes 884768 | tf_op jit(solution)/shard_map/ppermute | solution.py:251
  140.8 1.1 copy-done.2
  141.9 1.4 copy-done.6
  143.4 1.1 copy-done.8
  144.5 1.1 copy-done.10
  145.6 14.0 %shard_map.102 = (bf16[512,768]{1,0:T(8,128)(2,1)S(1)}, bf16[512,768]{1,0:T(8,128)(2,1)}, bf16[512,768]{1,0:T(8,128)(2,1)}, bf16[512,768]{1,0:T(8,128)(2,1)}, bf16[576,512]{1,0:T(8,128)(2,1)S(1)}) custom-call(s32[2]{0:T(128)S(1)} %pad_add_fusion.place_ref, bf16[576,768]{1,0:T(8,128)(2,1)} %bitcast.12.own_ref, ...), custom_call_target="tpu_custom_call" | custom-call | flops 3623878656 | bytes 14000000 | tf_op jit(solution)/shard_map/pallas_call | solution.py:115
  159.6 0.9 copy-done.3
  160.6 0.9 copy-done.5
  161.4 5.4 %collective-permute-start.10 = (bf16[512,768]{1,0:T(8,128)(2,1)}, bf16[512,768]{1,0:T(8,128)(2,1)S(1)}, u32[]{:S(2)}, u32[]{:S(2)}) collective-permute-start(bf16[512,768]{1,0:T(8,128)(2,1)} %get-tuple-element.32), channel_id=1, source_target_pairs={{0,8},{1,9},{2,10},{3,11},{4,12},{5,13},{6,14},{7,15},{8,16},{9,17... | collective-permute-start | bytes 2359304 | tf_op jit(solution)/shard_map/ppermute | solution.py:257
  166.9 1.9 collective-permute-start.11
  168.8 2.8 %collective-permute-start.12 = (bf16[512,768]{1,0:T(8,128)(2,1)}, bf16[512,768]{1,0:T(8,128)(2,1)}, u32[]{:S(2)}, u32[]{:S(2)}) collective-permute-start(bf16[512,768]{1,0:T(8,128)(2,1)} %get-tuple-element.34), channel_id=1, source_target_pairs={{0,24},{1,25},{2,26},{3,27},{4,28},{5,29},{6,30},{7,31},{8,0},{9,1... | collective-permute-start | bytes 2359304 | tf_op jit(solution)/shard_map/ppermute | solution.py:257
  171.6 7.0 %all-to-all-start.3 = ((bf16[8,72,512]{2,1,0:T(8,128)(2,1)}), bf16[8,72,512]{2,1,0:T(8,128)(2,1)S(1)}, u32[]{:S(2)}, u32[]{:S(2)}) async-start(bf16[8,72,512]{2,1,0:T(8,128)(2,1)} %bitcast.47), calls=%async_computation.4 | async-start | bytes 1179648 | tf_op jit(solution)/shard_map/all_to_all | solution.py:142
  178.6 22.5 %collective-permute-done.10 = bf16[512,768]{1,0:T(8,128)(2,1)S(1)} collective-permute-done((bf16[512,768]{1,0:T(8,128)(2,1)}, bf16[512,768]{1,0:T(8,128)(2,1)S(1)}, u32[]{:S(2)}, u32[]{:S(2)}) %collective-permute-start.10) | collective-permute-done | bytes 786464 | tf_op jit(solution)/shard_map/ppermute | solution.py:257
  201.1 5.6 %collective-permute-done.12 = bf16[512,768]{1,0:T(8,128)(2,1)} collective-permute-done((bf16[512,768]{1,0:T(8,128)(2,1)}, bf16[512,768]{1,0:T(8,128)(2,1)}, u32[]{:S(2)}, u32[]{:S(2)}) %collective-permute-start.12) | collective-permute-done | bytes 786464 | tf_op jit(solution)/shard_map/ppermute | solution.py:257
  206.7 1.6 multiply_convert_fusion
  208.3 1.0 fusion.19
  209.3 0.8 multiply_convert_fusion.1
  210.1 0.7 reduce_sum.25
  (57 shorter events, 4.7 us)
Async XLA Ops:
  7.2 17.3 %copy-start.16 = (bf16[72,512]{1,0:T(8,128)(2,1)S(1)}, bf16[72,512]{1,0:T(8,128)(2,1)}, u32[]{:S(2)}) copy-start(bf16[72,512]{1,0:T(8,128)(2,1)} %param.8) | copy-start | bytes 221188
  7.2 100.7 %all-gather.3.cloned.1.call-start = ((), (), s32[]{:S(2)}) async-start(), calls=%async_computation.5 | async-start | bytes 3760128 | tf_op jit(solution)/shard_map/all_gather | solution.py:210
  8.3 10.9 %collective-permute-start.6 = (bf16[72,768]{1,0:T(8,128)(2,1)S(1)}, bf16[72,768]{1,0:T(8,128)(2,1)S(1)}, u32[]{:S(2)}, u32[]{:S(2)}) collective-permute-start(bf16[72,768]{1,0:T(8,128)(2,1)S(1)} %get-tuple-element.48), channel_id=1, source_target_pairs={{0,0},{1,1},{2,2},{3,3},{4,4},{5,5},{6,6},{7,7},{8,64},{9,65},{10,... | collective-permute-start | bytes 331784 | tf_op jit(solution)/shard_map/ppermute | solution.py:199
  11.1 12.5 %collective-permute-start.7 = (bf16[72,768]{1,0:T(8,128)(2,1)S(1)}, bf16[72,768]{1,0:T(8,128)(2,1)S(1)}, u32[]{:S(2)}, u32[]{:S(2)}) collective-permute-start(bf16[72,768]{1,0:T(8,128)(2,1)S(1)} %get-tuple-element.49), channel_id=1, source_target_pairs={{0,64},{1,65},{2,66},{3,67},{4,68},{5,69},{6,70},{7,71},{8,0},{9,1... | collective-permute-start | bytes 331784 | tf_op jit(solution)/shard_map/ppermute | solution.py:199
  23.7 12.0 %copy-start.13 = (bf16[384,512]{1,0:T(8,128)(2,1)S(1)}, bf16[384,512]{1,0:T(8,128)(2,1)}, u32[]{:S(2)}) copy-start(bf16[384,512]{1,0:T(8,128)(2,1)} %param.13) | copy-start | bytes 1179652
  23.7 20.0 %copy-start.15 = (bf16[512,384]{1,0:T(8,128)(2,1)S(1)}, bf16[512,384]{1,0:T(8,128)(2,1)}, u32[]{:S(2)}) copy-start(bf16[512,384]{1,0:T(8,128)(2,1)} %param.12) | copy-start | bytes 1179652
  25.3 35.0 %all-to-all-start = ((bf16[8,72,512]{2,1,0:T(8,128)(2,1)}), bf16[8,72,512]{2,1,0:T(8,128)(2,1)S(1)}, u32[]{:S(2)}, u32[]{:S(2)}) async-start(bf16[8,72,512]{2,1,0:T(8,128)(2,1)} %broadcast_in_dim.4), calls=%async_computation | async-start | bytes 1179648 | tf_op jit(solution)/shard_map/all_to_all | solution.py:142
  35.6 13.9 %collective-permute-start = (bf16[384,512]{1,0:T(8,128)(2,1)S(1)}, bf16[384,512]{1,0:T(8,128)(2,1)S(1)}, u32[]{:S(2)}, u32[]{:S(2)}) collective-permute-start(bf16[384,512]{1,0:T(8,128)(2,1)S(1)} %copy-done.13), channel_id=1, source_target_pairs={{0,8},{1,9},{2,10},{3,11},{4,12},{5,13},{6,14},{7,15},{8,16},{9,17... | collective-permute-start | bytes 1179656 | tf_op jit(solution)/shard_map/ppermute | solution.py:183
  37.6 22.4 %collective-permute-start.2 = (bf16[384,512]{1,0:T(8,128)(2,1)S(1)}, bf16[384,512]{1,0:T(8,128)(2,1)S(1)}, u32[]{:S(2)}, u32[]{:S(2)}) collective-permute-start(bf16[384,512]{1,0:T(8,128)(2,1)S(1)} %copy-done.13), channel_id=1, source_target_pairs={{0,24},{1,25},{2,26},{3,27},{4,28},{5,29},{6,30},{7,31},{8,0},{9,1... | collective-permute-start | bytes 1179656 | tf_op jit(solution)/shard_map/ppermute | solution.py:183
  41.5 18.5 %collective-permute-start.1 = (bf16[384,512]{1,0:T(8,128)(2,1)S(1)}, bf16[384,512]{1,0:T(8,128)(2,1)S(1)}, u32[]{:S(2)}, u32[]{:S(2)}) collective-permute-start(bf16[384,512]{1,0:T(8,128)(2,1)S(1)} %copy-done.13), channel_id=1, source_target_pairs={{0,16},{1,17},{2,18},{3,19},{4,20},{5,21},{6,22},{7,23},{8,24},{9,... | collective-permute-start | bytes 1179656 | tf_op jit(solution)/shard_map/ppermute | solution.py:183
  44.8 33.4 %copy-start.1 = (bf16[512,768]{1,0:T(8,128)(2,1)}, bf16[512,768]{1,0:T(8,128)(2,1)S(1)}, u32[]{:S(2)}) copy-start(bf16[512,768]{1,0:T(8,128)(2,1)S(1)} %pad_maximum_fusion.2.refs_0_) | copy-start | bytes 2359300
  60.3 6.6 %copy-start.11 = (bf16[8,72,512]{2,1,0:T(8,128)(2,1)}, bf16[8,72,512]{2,1,0:T(8,128)(2,1)S(1)}, u32[]{:S(2)}) copy-start(bf16[8,72,512]{2,1,0:T(8,128)(2,1)S(1)} %all-to-all-done) | copy-start | bytes 1769476
  61.0 4.3 %collective-permute-start.3 = (bf16[576,768]{1,0:T(8,128)(2,1)S(1)}, bf16[576,768]{1,0:T(8,128)(2,1)S(1)}, u32[]{:S(2)}, u32[]{:S(2)}) collective-permute-start(bf16[576,768]{1,0:T(8,128)(2,1)S(1)} %convolution_convert_fusion), channel_id=1, source_target_pairs={{0,32},{32,0},{64,96},{96,64},{128,160},{160,128},{192,224},{224,1... | collective-permute-start | bytes 2654216 | tf_op jit(solution)/shard_map/ppermute | solution.py:224
  66.9 16.5 %copy-start.17 = (bf16[72,512]{1,0:T(8,128)(2,1)S(1)}, bf16[72,512]{1,0:T(8,128)(2,1)}, u32[]{:S(2)}) copy-start(bf16[72,512]{1,0:T(8,128)(2,1)} %param.7) | copy-start | bytes 221188
  66.9 34.8 %all-to-all-start.1 = ((bf16[8,72,768]{2,1,0:T(8,128)(2,1)}), bf16[8,72,768]{2,1,0:T(8,128)(2,1)S(1)}, u32[]{:S(2)}, u32[]{:S(2)}) async-start(bf16[8,72,768]{2,1,0:T(8,128)(2,1)} %bitcast.11), calls=%async_computation.1 | async-start | bytes 1769472 | tf_op jit(solution)/shard_map/all_to_all | solution.py:142
  76.2 62.1 %all-gather.5.cloned.1.call-start = ((), (), s32[]{:S(2)}) async-start(), calls=%async_computation.6 | async-start | bytes 1327104 | tf_op jit(solution)/shard_map/all_gather | solution.py:216
  76.2 25.6 %collective-permute-start.5 = (bf16[512,768]{1,0:T(8,128)(2,1)S(1)}, bf16[512,768]{1,0:T(8,128)(2,1)S(1)}, u32[]{:S(2)}, u32[]{:S(2)}) collective-permute-start(bf16[512,768]{1,0:T(8,128)(2,1)S(1)} %pad_maximum_fusion.2.refs_0_), channel_id=1, source_target_pairs={{0,24},{1,25},{2,26},{3,27},{4,28},{5,29},{6,30},{7,31},{8,0},{9,1... | collective-permute-start | bytes 2359304 | tf_op jit(solution)/shard_map/ppermute | solution.py:221
  78.2 23.7 %collective-permute-start.4 = (bf16[512,768]{1,0:T(8,128)(2,1)S(1)}, bf16[512,768]{1,0:T(8,128)(2,1)S(1)}, u32[]{:S(2)}, u32[]{:S(2)}) collective-permute-start(bf16[512,768]{1,0:T(8,128)(2,1)S(1)} %pad_maximum_fusion.2.refs_0_), channel_id=1, source_target_pairs={{0,8},{1,9},{2,10},{3,11},{4,12},{5,13},{6,14},{7,15},{8,16},{9,17... | collective-permute-start | bytes 2359304 | tf_op jit(solution)/shard_map/ppermute | solution.py:220
  101.8 8.4 %copy-start.7 = (bf16[512,768]{1,0:T(8,128)(2,1)}, bf16[512,768]{1,0:T(8,128)(2,1)S(1)}, u32[]{:S(2)}) copy-start(bf16[512,768]{1,0:T(8,128)(2,1)S(1)} %collective-permute-done.5.refs_3_) | copy-start | bytes 2359300
  101.9 8.4 %copy-start.9 = (bf16[512,768]{1,0:T(8,128)(2,1)}, bf16[512,768]{1,0:T(8,128)(2,1)S(1)}, u32[]{:S(2)}) copy-start(bf16[512,768]{1,0:T(8,128)(2,1)S(1)} %collective-permute-done.4.refs_1_) | copy-start | bytes 2359300
  103.1 29.9 %all-to-all-start.2 = ((bf16[8,72,768]{2,1,0:T(8,128)(2,1)}), bf16[8,72,768]{2,1,0:T(8,128)(2,1)}, u32[]{:S(2)}, u32[]{:S(2)}) async-start(bf16[8,72,768]{2,1,0:T(8,128)(2,1)} %broadcast_in_dim.5), calls=%async_computation.2 | async-start | bytes 1769472 | tf_op jit(solution)/shard_map/all_to_all | solution.py:142
  107.9 63.7 %reduce-scatter.2.cloned.1.call-start = ((), (), s32[]{:S(2)}) async-start(), calls=%async_computation.7 | async-start | bytes 1966080 | tf_op jit(solution)/shard_map/reduce_scatter | solution.py:244
  110.2 1.1 copy-start.12
  113.6 27.2 %copy-start = (bf16[1152,1536]{1,0:T(8,128)(2,1)S(1)}, bf16[1152,1536]{1,0:T(8,128)(2,1)}, u32[]{:S(2)}) copy-start(bf16[1152,1536]{1,0:T(8,128)(2,1)} %all-gather.3.cloned.1.call-done) | copy-start | bytes 10616836
  114.9 21.2 %collective-permute-start.8 = (bf16[512,768]{1,0:T(8,128)(2,1)}, bf16[512,768]{1,0:T(8,128)(2,1)}, u32[]{:S(2)}, u32[]{:S(2)}) collective-permute-start(bf16[512,768]{1,0:T(8,128)(2,1)} %copy-done.9), channel_id=1, source_target_pairs={{0,8},{1,9},{2,10},{3,11},{4,12},{5,13},{6,14},{7,15},{8,16},{9,17... | collective-permute-start | bytes 2359304 | tf_op jit(solution)/shard_map/ppermute | solution.py:230
  136.1 4.7 %collective-permute-start.9 = (bf16[576,768]{1,0:T(8,128)(2,1)}, bf16[576,768]{1,0:T(8,128)(2,1)}, u32[]{:S(2)}, u32[]{:S(2)}) collective-permute-start(bf16[576,768]{1,0:T(8,128)(2,1)} %bitcast.12.own_ref), channel_id=1, source_target_pairs={{0,32},{32,0},{64,96},{96,64},{128,160},{160,128},{192,224},{224,1... | collective-permute-start | bytes 2654216 | tf_op jit(solution)/shard_map/ppermute | solution.py:251
  140.8 1.1 copy-start.2
  141.9 1.4 copy-start.6
  143.4 1.1 copy-start.8
  144.5 1.1 copy-start.10
  159.6 0.9 copy-start.3
  160.5 0.9 copy-start.5
  161.4 45.3 %copy-start.4 = (bf16[512,768]{1,0:T(8,128)(2,1)S(1)}, bf16[512,768]{1,0:T(8,128)(2,1)}, u32[]{:S(2)}) copy-start(bf16[512,768]{1,0:T(8,128)(2,1)} %copy-done.3) | copy-start | bytes 2359300
  161.4 39.6 %collective-permute-start.10 = (bf16[512,768]{1,0:T(8,128)(2,1)}, bf16[512,768]{1,0:T(8,128)(2,1)S(1)}, u32[]{:S(2)}, u32[]{:S(2)}) collective-permute-start(bf16[512,768]{1,0:T(8,128)(2,1)} %get-tuple-element.32), channel_id=1, source_target_pairs={{0,8},{1,9},{2,10},{3,11},{4,12},{5,13},{6,14},{7,15},{8,16},{9,17... | collective-permute-start | bytes 2359304 | tf_op jit(solution)/shard_map/ppermute | solution.py:257
  166.9 34.2 %collective-permute-start.11 = (bf16[512,768]{1,0:T(8,128)(2,1)}, bf16[512,768]{1,0:T(8,128)(2,1)S(1)}, u32[]{:S(2)}, u32[]{:S(2)}) collective-permute-start(bf16[512,768]{1,0:T(8,128)(2,1)} %get-tuple-element.33), channel_id=1, source_target_pairs={{0,16},{1,17},{2,18},{3,19},{4,20},{5,21},{6,22},{7,23},{8,24},{9,... | collective-permute-start | bytes 2359304 | tf_op jit(solution)/shard_map/ppermute | solution.py:257
  168.8 37.9 %collective-permute-start.12 = (bf16[512,768]{1,0:T(8,128)(2,1)}, bf16[512,768]{1,0:T(8,128)(2,1)}, u32[]{:S(2)}, u32[]{:S(2)}) collective-permute-start(bf16[512,768]{1,0:T(8,128)(2,1)} %get-tuple-element.34), channel_id=1, source_target_pairs={{0,24},{1,25},{2,26},{3,27},{4,28},{5,29},{6,30},{7,31},{8,0},{9,1... | collective-permute-start | bytes 2359304 | tf_op jit(solution)/shard_map/ppermute | solution.py:257
  171.6 38.5 %all-to-all-start.3 = ((bf16[8,72,512]{2,1,0:T(8,128)(2,1)}), bf16[8,72,512]{2,1,0:T(8,128)(2,1)S(1)}, u32[]{:S(2)}, u32[]{:S(2)}) async-start(bf16[8,72,512]{2,1,0:T(8,128)(2,1)} %bitcast.47), calls=%async_computation.4 | async-start | bytes 1179648 | tf_op jit(solution)/shard_map/all_to_all | solution.py:142
  208.3 1.0 copy-start.14
Sparse Core Ops, SparseCore 0:
  24.6 48.2 all-gather.2
  84.2 43.2 all-gather.4
  130.3 28.1 reduce-scatter.1

commit v9 on v8

--- a/solution.py
+++ b/solution.py
@@ -37,19 +37,14 @@
     return (swish_gate * up_pre.astype(jnp.float32)).astype(jnp.bfloat16)
 
 
-def unit_block_kernel(
-    place_ref, own_ref, other_ref, gate_ref, up_ref, tokens_ref, *refs
-):
-    n_block = pl.num_programs(0)
-    weights, parts = refs[:4], refs[4:8]
-    input_part_ref, grad_ref, columns_ref, total_ref = refs[8:]
+def unit_block_kernel(place_ref, own_ref, other_ref, gate_ref, up_ref, tokens_ref, *refs):
+    *parts, grads_ref, grad_ref, columns_ref = refs
     step = pl.program_id(0)
-    mine = lax.rem(place_ref[1] + step, n_block) // 2 == place_ref[0]
+    mine = lax.rem(place_ref[1] + step, len(parts)) // 2 == place_ref[0]
 
     @pl.when(step == 0)
     def _():
         columns_ref[...] = tokens_ref[...].T
-        total_ref[...] = jnp.zeros_like(total_ref)
 
     @pl.when(mine)
     def _():
@@ -66,31 +61,22 @@
         gate_ref[...].astype(jnp.float32).reshape(shape),
         up_ref[...].astype(jnp.float32).reshape(shape),
     )
+    grads_ref[:, :units] = gate_grad
+    grads_ref[:, units:] = up_grad
     for k, part_ref in enumerate(parts):
 
         @pl.when(step == k)
         def _():
-            weight_ref = weights[(len(parts) - k) % len(parts)]
-            total = total_ref[...]
-            for which, grads in enumerate((gate_grad, up_grad)):
-                columns = slice(which * units, (which + 1) * units)
-                part_ref[:, columns] = jnp.dot(
-                    columns_ref[...], grads, preferred_element_type=jnp.float32
-                ).astype(jnp.bfloat16)
-                total = total + contract_last(grads, weight_ref[:, columns])
-            total_ref[...] = total
-
-    @pl.when(step == n_block - 1)
-    def _():
-        input_part_ref[...] = total_ref[...].astype(jnp.bfloat16)
-
-
-def unit_blocks(place, own, other, saved, rows, weights):
+            part_ref[...] = jnp.dot(
+                columns_ref[...], grads_ref[...], preferred_element_type=jnp.float32
+            ).astype(jnp.bfloat16)
+
+
+def unit_blocks(place, own, other, saved, rows, n_block):
     n_y, _, block, width = saved.shape
     units = width // 4
     group_rows = own.shape[0]
-    features = weights[0].shape[0]
-    n_block = len(weights)
+    features = rows.shape[1] // 2
 
     def block_of(j, place):
         return lax.rem(place[1] + j, n_block)
@@ -111,31 +97,29 @@
         return pl.BlockSpec(shape, lambda j, place: (0, 0))
 
     part = jax.ShapeDtypeStruct((features, 2 * units), jnp.bfloat16)
-    input_part = jax.ShapeDtypeStruct((group_rows, features), jnp.bfloat16)
+    grads = jax.ShapeDtypeStruct((group_rows, 2 * units * n_block), jnp.bfloat16)
     return pl.pallas_call(
         unit_block_kernel,
-        out_shape=(part,) * n_block + (input_part,),
+        out_shape=(part,) * n_block + (grads,),
         grid_spec=pltpu.PrefetchScalarGridSpec(
             num_scalar_prefetch=1,
             grid=(n_block,),
             in_specs=[half_spec(), half_spec(), saved_spec(0), saved_spec(2)]
-            + [fixed_spec(group_rows, features)]
-            + [fixed_spec(features, 2 * units)] * n_block,
+            + [fixed_spec(group_rows, features)],
             out_specs=[fixed_spec(features, 2 * units)] * n_block
-            + [fixed_spec(group_rows, features)],
+            + [pl.BlockSpec((group_rows, 2 * units), lambda j, place: (0, j))],
             scratch_shapes=[
                 pltpu.VMEM((group_rows, units), jnp.float32),
                 pltpu.VMEM((features, group_rows), jnp.bfloat16),
-                pltpu.VMEM((group_rows, features), jnp.float32),
             ],
         ),
-        compiler_params=pltpu.CompilerParams(vmem_limit_bytes=40 * 1024 * 1024),
+        compiler_params=pltpu.CompilerParams(vmem_limit_bytes=32 * 1024 * 1024),
         cost_estimate=pl.CostEstimate(
-            flops=8 * n_block * features * units * group_rows,
+            flops=4 * n_block * features * units * group_rows,
             bytes_accessed=14_000_000,
             transcendentals=n_block * group_rows * units,
         ),
-    )(place, own, other, saved, saved, rows, *weights)
+    )(place, own, other, saved, saved, rows)
 
 
 def exchange(pieces, axis, groups):
@@ -240,18 +224,18 @@
         hidden = swiglu_hidden(*side_saved(side)).reshape(group_rows, half)
         down_part.append(contract_first(hidden, grad_rows).astype(jnp.bfloat16))
     down_part = jnp.concatenate(down_part, axis=0).reshape(n_x, units, features)
-    own, _ = lax.optimization_barrier((own, down_part))
+    down_part, w_far = lax.optimization_barrier((down_part, w_far))
+    weights = jnp.concatenate([w_both, w_right, w_far, w_left], axis=1)
     down_sum = lax.psum_scatter(
         down_part, "col", scatter_dimension=0, tiled=True, axis_index_groups=x_groups
     )[0]
-
-    own, w_far = lax.optimization_barrier((own, w_far))
-    weights = [w_both, w_left, w_far, w_right]
+    own, weights, _ = lax.optimization_barrier((own, weights, down_part))
 
     other = lax.ppermute(own, "row", core_swap)
-    *unit_parts, part_in = unit_blocks(
-        jnp.stack([core, x_here]), own, other, saved, both_rows, weights
-    )
+    *unit_parts, unit_grads = unit_blocks(
+        jnp.stack([core, x_here]), own, other, saved, both_rows, n_x
+    )
+    part_in = contract_last(unit_grads, weights).astype(jnp.bfloat16)
     unit_sum = unit_parts[0].astype(jnp.float32)
     for step in range(1, n_x):
         moved_part = lax.ppermute(unit_parts[step], "col", x_shift(step))

time: 219 us -> 208 us (0.950)
  waiting for transfers between devices: 90.2 us -> 79.1 us
  Pallas kernels: 14 us -> 9.53 us
  local copies, waits for them, and re-layouts: 12.6 us -> 8.86 us
  other arithmetic: 9.54 us -> 13 us
  matrix products: 3.84 us -> 6.69 us
    all_to_all x4, waiting for transfers between devices: 30 us -> 17.7 us  [exchange(): lax.all_to_all(pieces, axis, 0, 0, tiled=True, axis_index_groups=groups)]
    ppermute x3, waiting for transfers between devices: 28.1 us -> 21.5 us  [local(): moved_part = lax.ppermute(unit_parts[step], 'col', x_shift(step))]
    ppermute x1, waiting for transfers between devices: 3.16 us -> 8.15 us  [local(): w_far = lax.ppermute(w_left, 'col', x_shift(1))]
    pallas_call x1, Pallas kernels: 14 us -> 9.53 us  [unit_blocks(): pl.pallas_call(unit_block_kernel, out_shape=(part,) * n_block + (grads,),...]
    unnamed x36 -> x32, local copies, waits for them, and re-layouts: 7.13 us -> 3.58 us
    concatenate x0 -> x1, other arithmetic: none -> 3.38 us  [local(): weights = jnp.concatenate([w_both, w_right, w_far, w_left], axis=1)]
    dot_general x2 -> x3, matrix products: 2.23 us -> 5.08 us  [contract_last(): lax.dot_general(left_side, right_side, (((1,), (1,)), ((), ())), preferre...]
    reduce_scatter x1, waiting for transfers between devices: 0.02 us -> 2.69 us  [local(): lax.psum_scatter(down_part, 'col', scatter_dimension=0, tiled=True, axis_...]
  transfers between devices with their start and end apart: 20 -> 20, of which waited for: 11 -> 12; matrix products, arithmetic and copies ran while one was open for 8% -> 11% of each run, Pallas kernels for 6% -> 5%
where the time goes in v9:
time: 208 us; the launch traced here: 205 us
  waiting for transfers between devices  79.1 us (38%)
  starting transfers between devices  74 us (36%)
  between operations  14.2 us (7%)
  other arithmetic  13 us (6%)
  Pallas kernels  9.53 us (5%)
  local copies, waits for them, and re-layouts  8.86 us (4%)
  matrix products  6.69 us (3%)
    all_to_all x4, starting transfers between devices, exchange(): lax.all_to_all(pieces, axis, 0, 0, tiled=True, axis_index_groups=groups)  32.4 us
    ppermute x3, waiting for transfers between devices, local(): moved_part = lax.ppermute(unit_parts[step], 'col', x_shift(step))  21.5 us
    all_to_all x4, waiting for transfers between devices, exchange(): lax.all_to_all(pieces, axis, 0, 0, tiled=True, axis_index_groups=groups)  17.7 us
    ppermute x3, waiting for transfers between devices, local(): lax.ppermute(w_down, 'col', x_shift(step))  15.2 us
    ppermute x3, starting transfers between devices, local(): moved_part = lax.ppermute(unit_parts[step], 'col', x_shift(step))  10.3 us
    pallas_call x1, Pallas kernels, unit_blocks(): pl.pallas_call(unit_block_kernel, out_shape=(part,) * n_block + (grads,),...  9.53 us
    ppermute x2, waiting for transfers between devices, local(): lax.ppermute(pick(saved_pieces, lax.rem(x_here + turn, 2)), ('row', 'col'...  8.73 us
    ppermute x1, waiting for transfers between devices, local(): w_far = lax.ppermute(w_left, 'col', x_shift(1))  8.15 us
  transfers between devices with their start and end apart: 20, of which 12 were waited for; matrix products, arithmetic and copies ran while one was open for 11% of the time, Pallas kernels for 5%

profile of v9, /device:TPU:6, one launch (start us, length us, event | category | flops | bytes accessed | tf_op | source)
XLA Modules:
  0.0 205.4 jit_solution(4659950516214505460)
XLA Ops:
  7.3 1.0 pad_maximum_fusion.4
  8.3 3.0 %collective-permute-start.6 = (bf16[72,768]{1,0:T(8,128)(2,1)S(1)}, bf16[72,768]{1,0:T(8,128)(2,1)S(1)}, u32[]{:S(2)}, u32[]{:S(2)}) collective-permute-start(bf16[72,768]{1,0:T(8,128)(2,1)S(1)} %get-tuple-element.50), channel_id=1, source_target_pairs={{0,0},{1,1},{2,2},{3,3},{4,4},{5,5},{6,6},{7,7},{8,64},{9,65},{10,... | collective-permute-start | bytes 331784 | tf_op jit(solution)/shard_map/ppermute | solution.py:183
  11.3 3.8 %collective-permute-start.7 = (bf16[72,768]{1,0:T(8,128)(2,1)S(1)}, bf16[72,768]{1,0:T(8,128)(2,1)S(1)}, u32[]{:S(2)}, u32[]{:S(2)}) collective-permute-start(bf16[72,768]{1,0:T(8,128)(2,1)S(1)} %get-tuple-element.51), channel_id=1, source_target_pairs={{0,64},{1,65},{2,66},{3,67},{4,68},{5,69},{6,70},{7,71},{8,0},{9,1... | collective-permute-start | bytes 331784 | tf_op jit(solution)/shard_map/ppermute | solution.py:183
  15.1 4.2 %collective-permute-done.6 = bf16[72,768]{1,0:T(8,128)(2,1)S(1)} collective-permute-done((bf16[72,768]{1,0:T(8,128)(2,1)S(1)}, bf16[72,768]{1,0:T(8,128)(2,1)S(1)}, u32[]{:S(2)}, u32[]{:S(2)}) %collective-permute-start.6) | collective-permute-done | bytes 110624 | tf_op jit(solution)/shard_map/ppermute | solution.py:183
  19.3 4.5 %collective-permute-done.7 = bf16[72,768]{1,0:T(8,128)(2,1)S(1)} collective-permute-done((bf16[72,768]{1,0:T(8,128)(2,1)S(1)}, bf16[72,768]{1,0:T(8,128)(2,1)S(1)}, u32[]{:S(2)}, u32[]{:S(2)}) %collective-permute-start.7) | collective-permute-done | bytes 110624 | tf_op jit(solution)/shard_map/ppermute | solution.py:183
  24.6 0.9 broadcast_in_dim.4
  25.4 10.3 %all-to-all-start = ((bf16[8,72,512]{2,1,0:T(8,128)(2,1)}), bf16[8,72,512]{2,1,0:T(8,128)(2,1)S(1)}, u32[]{:S(2)}, u32[]{:S(2)}) async-start(bf16[8,72,512]{2,1,0:T(8,128)(2,1)} %broadcast_in_dim.4), calls=%async_computation | async-start | bytes 1179648 | tf_op jit(solution)/shard_map/all_to_all | solution.py:126
  35.8 1.9 collective-permute-start
  37.7 3.9 %collective-permute-start.2 = (bf16[384,512]{1,0:T(8,128)(2,1)S(1)}, bf16[384,512]{1,0:T(8,128)(2,1)S(1)}, u32[]{:S(2)}, u32[]{:S(2)}) collective-permute-start(bf16[384,512]{1,0:T(8,128)(2,1)S(1)} %copy-done.11), channel_id=1, source_target_pairs={{0,24},{1,25},{2,26},{3,27},{4,28},{5,29},{6,30},{7,31},{8,0},{9,1... | collective-permute-start | bytes 1179656 | tf_op jit(solution)/shard_map/ppermute | solution.py:167
  41.6 2.1 %collective-permute-start.1 = (bf16[384,512]{1,0:T(8,128)(2,1)S(1)}, bf16[384,512]{1,0:T(8,128)(2,1)S(1)}, u32[]{:S(2)}, u32[]{:S(2)}) collective-permute-start(bf16[384,512]{1,0:T(8,128)(2,1)S(1)} %copy-done.11), channel_id=1, source_target_pairs={{0,16},{1,17},{2,18},{3,19},{4,20},{5,21},{6,22},{7,23},{8,24},{9,... | collective-permute-start | bytes 1179656 | tf_op jit(solution)/shard_map/ppermute | solution.py:167
  43.8 1.1 pad_maximum_fusion.3
  44.9 4.8 %collective-permute-done = bf16[384,512]{1,0:T(8,128)(2,1)S(1)} collective-permute-done((bf16[384,512]{1,0:T(8,128)(2,1)S(1)}, bf16[384,512]{1,0:T(8,128)(2,1)S(1)}, u32[]{:S(2)}, u32[]{:S(2)}) %collective-permute-start) | collective-permute-done | bytes 393248 | tf_op jit(solution)/shard_map/ppermute | solution.py:167
  49.7 10.4 %collective-permute-done.2 = bf16[384,512]{1,0:T(8,128)(2,1)S(1)} collective-permute-done((bf16[384,512]{1,0:T(8,128)(2,1)S(1)}, bf16[384,512]{1,0:T(8,128)(2,1)S(1)}, u32[]{:S(2)}, u32[]{:S(2)}) %collective-permute-start.2) | collective-permute-done | bytes 393248 | tf_op jit(solution)/shard_map/ppermute | solution.py:167
  61.1 1.9 collective-permute-start.3
  63.0 2.4 %collective-permute-done.3 = bf16[576,768]{1,0:T(8,128)(2,1)S(1)} collective-permute-done((bf16[576,768]{1,0:T(8,128)(2,1)S(1)}, bf16[576,768]{1,0:T(8,128)(2,1)S(1)}, u32[]{:S(2)}, u32[]{:S(2)}) %collective-permute-start.3) | collective-permute-done | bytes 884768 | tf_op jit(solution)/shard_map/ppermute | solution.py:208
  65.4 1.6 add_convert_fusion
  67.0 9.3 %all-to-all-start.1 = ((bf16[8,72,768]{2,1,0:T(8,128)(2,1)}), bf16[8,72,768]{2,1,0:T(8,128)(2,1)S(1)}, u32[]{:S(2)}, u32[]{:S(2)}) async-start(bf16[8,72,768]{2,1,0:T(8,128)(2,1)} %bitcast.11), calls=%async_computation.1 | async-start | bytes 1769472 | tf_op jit(solution)/shard_map/all_to_all | solution.py:126
  76.4 1.9 collective-permute-start.5
  78.3 5.1 %collective-permute-start.4 = (bf16[512,768]{1,0:T(8,128)(2,1)S(1)}, bf16[512,768]{1,0:T(8,128)(2,1)S(1)}, u32[]{:S(2)}, u32[]{:S(2)}) collective-permute-start(bf16[512,768]{1,0:T(8,128)(2,1)S(1)} %pad_maximum_fusion.3), channel_id=1, source_target_pairs={{0,8},{1,9},{2,10},{3,11},{4,12},{5,13},{6,14},{7,15},{8,16},{9,17... | collective-permute-start | bytes 2359304 | tf_op jit(solution)/shard_map/ppermute | solution.py:204
  84.1 17.7 %all-to-all-done.1 = bf16[8,72,768]{2,1,0:T(8,128)(2,1)S(1)} async-done(((bf16[8,72,768]{2,1,0:T(8,128)(2,1)}), bf16[8,72,768]{2,1,0:T(8,128)(2,1)S(1)}, u32[]{:S(2)}, u32[]{:S(2)}) %all-to-all-start.1) | async-done | bytes 884768 | tf_op jit(solution)/shard_map/all_to_all | solution.py:126
  102.0 1.1 broadcast_in_dim.5
  103.1 4.9 %all-to-all-start.2 = ((bf16[8,72,768]{2,1,0:T(8,128)(2,1)}), bf16[8,72,768]{2,1,0:T(8,128)(2,1)}, u32[]{:S(2)}, u32[]{:S(2)}) async-start(bf16[8,72,768]{2,1,0:T(8,128)(2,1)} %broadcast_in_dim.5), calls=%async_computation.2 | async-start | bytes 1769472 | tf_op jit(solution)/shard_map/all_to_all | solution.py:126
  108.0 5.6 %collective-permute-start.8 = (bf16[512,768]{1,0:T(8,128)(2,1)S(1)}, bf16[512,768]{1,0:T(8,128)(2,1)S(1)}, u32[]{:S(2)}, u32[]{:S(2)}) collective-permute-start(bf16[512,768]{1,0:T(8,128)(2,1)S(1)} %collective-permute-done.4), channel_id=1, source_target_pairs={{0,8},{1,9},{2,10},{3,11},{4,12},{5,13},{6,14},{7,15},{8,16},{9,17... | collective-permute-start | bytes 2359304 | tf_op jit(solution)/shard_map/ppermute | solution.py:214
  113.6 2.2 %fusion.18 = (bf16[8,1,72,768]{3,2,1,0:T(8,128)(2,1)S(1)}, bf16[8,1,72,768]{3,2,1,0:T(8,128)(2,1)S(1)}, bf16[8,1,72,768]{3,2,1,0:T(8,128)(2,1)S(1)}, bf16[8,1,72,768]{3,2,1,0:T(8,128)(2,1)S(1)}) fusion(bf16[8,2,72,1536]{3,2,1,0:T(8,128)(2,1)} %bitcast.46), kind=kLoop, calls=%fused_computation.46 | loop fusion | bytes 7077888 | tf_op jit(solution)/shard_map/slice | solution.py:220
  117.6 0.8 convolution_convert_fusion.3
  118.4 0.8 convolution_convert_fusion.2
  119.2 1.4 pad_maximum_fusion.2
  120.6 8.1 %collective-permute-done.8 = bf16[512,768]{1,0:T(8,128)(2,1)S(1)} collective-permute-done((bf16[512,768]{1,0:T(8,128)(2,1)S(1)}, bf16[512,768]{1,0:T(8,128)(2,1)S(1)}, u32[]{:S(2)}, u32[]{:S(2)}) %collective-permute-start.8) | collective-permute-done | bytes 786464 | tf_op jit(solution)/shard_map/ppermute | solution.py:214
  128.7 0.9 copy-done.8
  129.7 3.4 %pad_maximum_fusion = bf16[512,3072]{1,0:T(8,128)(2,1)} fusion(bf16[512,768]{1,0:T(8,128)(2,1)} %copy-done.7, bf16[512,768]{1,0:T(8,128)(2,1)} %copy-done.8, bf16[512,768]{1,0:T(8,128)(2,1)} %copy-done.6, bf16[512,768]{1,0:T(8,128)(2,1)} %copy-done.4), kind=kLoop, calls=%fused_computation | loop fusion | flops 12582912 | bytes 6291456 | tf_op jit(solution)/shard_map/concatenate | solution.py:228
  133.0 1.9 collective-permute-start.9
  135.0 2.7 %collective-permute-done.9.other_ref = bf16[576,768]{1,0:T(8,128)(2,1)} collective-permute-done((bf16[576,768]{1,0:T(8,128)(2,1)}, bf16[576,768]{1,0:T(8,128)(2,1)}, u32[]{:S(2)}, u32[]{:S(2)}) %collective-permute-start.9) | collective-permute-done | bytes 884768 | tf_op jit(solution)/shard_map/ppermute | solution.py:234
  137.7 1.3 copy-done.1
  139.0 9.5 %shard_map.102 = (bf16[512,768]{1,0:T(8,128)(2,1)S(1)}, bf16[512,768]{1,0:T(8,128)(2,1)}, bf16[512,768]{1,0:T(8,128)(2,1)}, bf16[512,768]{1,0:T(8,128)(2,1)}, bf16[576,3072]{1,0:T(8,128)(2,1)S(1)}) custom-call(s32[2]{0:T(128)S(1)} %pad_add_fusion.place_ref, bf16[576,768]{1,0:T(8,128)(2,1)} %bitcast.12.own_ref, ...), custom_call_target="tpu_custom_call" | custom-call | flops 1811939328 | bytes 14000000 | tf_op jit(solution)/shard_map/pallas_call | solution.py:101
  148.5 0.9 copy-done.2
  149.4 5.5 %collective-permute-start.10 = (bf16[512,768]{1,0:T(8,128)(2,1)}, bf16[512,768]{1,0:T(8,128)(2,1)S(1)}, u32[]{:S(2)}, u32[]{:S(2)}) collective-permute-start(bf16[512,768]{1,0:T(8,128)(2,1)} %get-tuple-element.34), channel_id=1, source_target_pairs={{0,8},{1,9},{2,10},{3,11},{4,12},{5,13},{6,14},{7,15},{8,16},{9,17... | collective-permute-start | bytes 2359304 | tf_op jit(solution)/shard_map/ppermute | solution.py:241
  154.9 1.9 collective-permute-start.11
  156.8 2.9 %collective-permute-start.12 = (bf16[512,768]{1,0:T(8,128)(2,1)}, bf16[512,768]{1,0:T(8,128)(2,1)}, u32[]{:S(2)}, u32[]{:S(2)}) collective-permute-start(bf16[512,768]{1,0:T(8,128)(2,1)} %get-tuple-element.36), channel_id=1, source_target_pairs={{0,24},{1,25},{2,26},{3,27},{4,28},{5,29},{6,30},{7,31},{8,0},{9,1... | collective-permute-start | bytes 2359304 | tf_op jit(solution)/shard_map/ppermute | solution.py:241
  159.8 2.9 %convolution_convert_fusion.4 = bf16[576,512]{1,0:T(8,128)(2,1)} fusion(bf16[576,3072]{1,0:T(8,128)(2,1)S(1)} %get-tuple-element.30, bf16[512,3072]{1,0:T(8,128)(2,1)S(1)} %copy-done.5), kind=kOutput, calls=%fused_computation.23 | convolution fusion | flops 1812234240 | bytes 7274496 | tf_op jit(solution)/shard_map/dot_general | solution.py:13
  162.6 2.7 %reduce-scatter.2.cloned.1.call-done = bf16[1,384,512]{2,1,0:T(8,128)(2,1)} async-done(((bf16[4,384,512]{2,1,0:T(8,128)(2,1)}), bf16[1,384,512]{2,1,0:T(8,128)(2,1)}) %reduce-scatter.2.cloned.1.call-update) | async-done | bytes 393232 | tf_op jit(solution)/shard_map/reduce_scatter | solution.py:229
  165.3 7.9 %all-to-all-start.3 = ((bf16[8,72,512]{2,1,0:T(8,128)(2,1)}), bf16[8,72,512]{2,1,0:T(8,128)(2,1)S(1)}, u32[]{:S(2)}, u32[]{:S(2)}) async-start(bf16[8,72,512]{2,1,0:T(8,128)(2,1)} %bitcast.25), calls=%async_computation.4 | async-start | bytes 1179648 | tf_op jit(solution)/shard_map/all_to_all | solution.py:126
  173.2 3.2 %collective-permute-done.10 = bf16[512,768]{1,0:T(8,128)(2,1)S(1)} collective-permute-done((bf16[512,768]{1,0:T(8,128)(2,1)}, bf16[512,768]{1,0:T(8,128)(2,1)S(1)}, u32[]{:S(2)}, u32[]{:S(2)}) %collective-permute-start.10) | collective-permute-done | bytes 786464 | tf_op jit(solution)/shard_map/ppermute | solution.py:241
  176.4 2.5 %collective-permute-done.11 = bf16[512,768]{1,0:T(8,128)(2,1)S(1)} collective-permute-done((bf16[512,768]{1,0:T(8,128)(2,1)}, bf16[512,768]{1,0:T(8,128)(2,1)S(1)}, u32[]{:S(2)}, u32[]{:S(2)}) %collective-permute-start.11) | collective-permute-done | bytes 786464 | tf_op jit(solution)/shard_map/ppermute | solution.py:241
  179.0 15.8 %collective-permute-done.12 = bf16[512,768]{1,0:T(8,128)(2,1)} collective-permute-done((bf16[512,768]{1,0:T(8,128)(2,1)}, bf16[512,768]{1,0:T(8,128)(2,1)}, u32[]{:S(2)}, u32[]{:S(2)}) %collective-permute-start.12) | collective-permute-done | bytes 786464 | tf_op jit(solution)/shard_map/ppermute | solution.py:241
  194.8 1.6 multiply_convert_fusion
  196.3 1.0 fusion.19
  197.3 0.8 multiply_convert_fusion.1
  198.2 0.7 reduce_sum.25
  (55 shorter events, 4.6 us)
Async XLA Ops:
  7.2 17.4 %copy-start.14 = (bf16[72,512]{1,0:T(8,128)(2,1)S(1)}, bf16[72,512]{1,0:T(8,128)(2,1)}, u32[]{:S(2)}) copy-start(bf16[72,512]{1,0:T(8,128)(2,1)} %param.8) | copy-start | bytes 221188
  7.2 106.4 %all-gather.3.cloned.1.call-start = ((), (), s32[]{:S(2)}) async-start(), calls=%async_computation.5 | async-start | bytes 3760128 | tf_op jit(solution)/shard_map/all_gather | solution.py:194
  8.3 27.5 %copy-start.11 = (bf16[384,512]{1,0:T(8,128)(2,1)S(1)}, bf16[384,512]{1,0:T(8,128)(2,1)}, u32[]{:S(2)}) copy-start(bf16[384,512]{1,0:T(8,128)(2,1)} %param.13) | copy-start | bytes 1179652
  8.3 11.0 %collective-permute-start.6 = (bf16[72,768]{1,0:T(8,128)(2,1)S(1)}, bf16[72,768]{1,0:T(8,128)(2,1)S(1)}, u32[]{:S(2)}, u32[]{:S(2)}) collective-permute-start(bf16[72,768]{1,0:T(8,128)(2,1)S(1)} %get-tuple-element.50), channel_id=1, source_target_pairs={{0,0},{1,1},{2,2},{3,3},{4,4},{5,5},{6,6},{7,7},{8,64},{9,65},{10,... | collective-permute-start | bytes 331784 | tf_op jit(solution)/shard_map/ppermute | solution.py:183
  11.3 12.5 %collective-permute-start.7 = (bf16[72,768]{1,0:T(8,128)(2,1)S(1)}, bf16[72,768]{1,0:T(8,128)(2,1)S(1)}, u32[]{:S(2)}, u32[]{:S(2)}) collective-permute-start(bf16[72,768]{1,0:T(8,128)(2,1)S(1)} %get-tuple-element.51), channel_id=1, source_target_pairs={{0,64},{1,65},{2,66},{3,67},{4,68},{5,69},{6,70},{7,71},{8,0},{9,1... | collective-permute-start | bytes 331784 | tf_op jit(solution)/shard_map/ppermute | solution.py:183
  15.0 28.8 %copy-start.13 = (bf16[512,384]{1,0:T(8,128)(2,1)S(1)}, bf16[512,384]{1,0:T(8,128)(2,1)}, u32[]{:S(2)}) copy-start(bf16[512,384]{1,0:T(8,128)(2,1)} %param.12) | copy-start | bytes 1179652
  25.4 35.0 %all-to-all-start = ((bf16[8,72,512]{2,1,0:T(8,128)(2,1)}), bf16[8,72,512]{2,1,0:T(8,128)(2,1)S(1)}, u32[]{:S(2)}, u32[]{:S(2)}) async-start(bf16[8,72,512]{2,1,0:T(8,128)(2,1)} %broadcast_in_dim.4), calls=%async_computation | async-start | bytes 1179648 | tf_op jit(solution)/shard_map/all_to_all | solution.py:126
  35.8 13.9 %collective-permute-start = (bf16[384,512]{1,0:T(8,128)(2,1)S(1)}, bf16[384,512]{1,0:T(8,128)(2,1)S(1)}, u32[]{:S(2)}, u32[]{:S(2)}) collective-permute-start(bf16[384,512]{1,0:T(8,128)(2,1)S(1)} %copy-done.11), channel_id=1, source_target_pairs={{0,8},{1,9},{2,10},{3,11},{4,12},{5,13},{6,14},{7,15},{8,16},{9,17... | collective-permute-start | bytes 1179656 | tf_op jit(solution)/shard_map/ppermute | solution.py:167
  37.7 22.4 %collective-permute-start.2 = (bf16[384,512]{1,0:T(8,128)(2,1)S(1)}, bf16[384,512]{1,0:T(8,128)(2,1)S(1)}, u32[]{:S(2)}, u32[]{:S(2)}) collective-permute-start(bf16[384,512]{1,0:T(8,128)(2,1)S(1)} %copy-done.11), channel_id=1, source_target_pairs={{0,24},{1,25},{2,26},{3,27},{4,28},{5,29},{6,30},{7,31},{8,0},{9,1... | collective-permute-start | bytes 1179656 | tf_op jit(solution)/shard_map/ppermute | solution.py:167
  41.6 18.5 %collective-permute-start.1 = (bf16[384,512]{1,0:T(8,128)(2,1)S(1)}, bf16[384,512]{1,0:T(8,128)(2,1)S(1)}, u32[]{:S(2)}, u32[]{:S(2)}) collective-permute-start(bf16[384,512]{1,0:T(8,128)(2,1)S(1)} %copy-done.11), channel_id=1, source_target_pairs={{0,16},{1,17},{2,18},{3,19},{4,20},{5,21},{6,22},{7,23},{8,24},{9,... | collective-permute-start | bytes 1179656 | tf_op jit(solution)/shard_map/ppermute | solution.py:167
  44.9 33.4 %copy-start.4 = (bf16[512,768]{1,0:T(8,128)(2,1)}, bf16[512,768]{1,0:T(8,128)(2,1)S(1)}, u32[]{:S(2)}) copy-start(bf16[512,768]{1,0:T(8,128)(2,1)S(1)} %pad_maximum_fusion.3) | copy-start | bytes 2359300
  60.4 6.6 %copy-start.9 = (bf16[8,72,512]{2,1,0:T(8,128)(2,1)}, bf16[8,72,512]{2,1,0:T(8,128)(2,1)S(1)}, u32[]{:S(2)}) copy-start(bf16[8,72,512]{2,1,0:T(8,128)(2,1)S(1)} %all-to-all-done) | copy-start | bytes 1769476
  61.1 4.3 %collective-permute-start.3 = (bf16[576,768]{1,0:T(8,128)(2,1)S(1)}, bf16[576,768]{1,0:T(8,128)(2,1)S(1)}, u32[]{:S(2)}, u32[]{:S(2)}) collective-permute-start(bf16[576,768]{1,0:T(8,128)(2,1)S(1)} %convolution_convert_fusion), channel_id=1, source_target_pairs={{0,32},{32,0},{64,96},{96,64},{128,160},{160,128},{192,224},{224,1... | collective-permute-start | bytes 2654216 | tf_op jit(solution)/shard_map/ppermute | solution.py:208
  67.0 16.4 %copy-start.15 = (bf16[72,512]{1,0:T(8,128)(2,1)S(1)}, bf16[72,512]{1,0:T(8,128)(2,1)}, u32[]{:S(2)}) copy-start(bf16[72,512]{1,0:T(8,128)(2,1)} %param.7) | copy-start | bytes 221188
  67.0 34.8 %all-to-all-start.1 = ((bf16[8,72,768]{2,1,0:T(8,128)(2,1)}), bf16[8,72,768]{2,1,0:T(8,128)(2,1)S(1)}, u32[]{:S(2)}, u32[]{:S(2)}) async-start(bf16[8,72,768]{2,1,0:T(8,128)(2,1)} %bitcast.11), calls=%async_computation.1 | async-start | bytes 1769472 | tf_op jit(solution)/shard_map/all_to_all | solution.py:126
  76.3 58.7 %all-gather.5.cloned.1.call-start = ((), (), s32[]{:S(2)}) async-start(), calls=%async_computation.6 | async-start | bytes 1327104 | tf_op jit(solution)/shard_map/all_gather | solution.py:200
  76.4 25.6 %collective-permute-start.5 = (bf16[512,768]{1,0:T(8,128)(2,1)S(1)}, bf16[512,768]{1,0:T(8,128)(2,1)S(1)}, u32[]{:S(2)}, u32[]{:S(2)}) collective-permute-start(bf16[512,768]{1,0:T(8,128)(2,1)S(1)} %pad_maximum_fusion.3), channel_id=1, source_target_pairs={{0,24},{1,25},{2,26},{3,27},{4,28},{5,29},{6,30},{7,31},{8,0},{9,1... | collective-permute-start | bytes 2359304 | tf_op jit(solution)/shard_map/ppermute | solution.py:205
  78.3 23.7 %collective-permute-start.4 = (bf16[512,768]{1,0:T(8,128)(2,1)S(1)}, bf16[512,768]{1,0:T(8,128)(2,1)S(1)}, u32[]{:S(2)}, u32[]{:S(2)}) collective-permute-start(bf16[512,768]{1,0:T(8,128)(2,1)S(1)} %pad_maximum_fusion.3), channel_id=1, source_target_pairs={{0,8},{1,9},{2,10},{3,11},{4,12},{5,13},{6,14},{7,15},{8,16},{9,17... | collective-permute-start | bytes 2359304 | tf_op jit(solution)/shard_map/ppermute | solution.py:204
  102.0 13.9 %copy-start.6 = (bf16[512,768]{1,0:T(8,128)(2,1)}, bf16[512,768]{1,0:T(8,128)(2,1)S(1)}, u32[]{:S(2)}) copy-start(bf16[512,768]{1,0:T(8,128)(2,1)S(1)} %collective-permute-done.5) | copy-start | bytes 2359300
  102.0 13.9 %copy-start.7 = (bf16[512,768]{1,0:T(8,128)(2,1)}, bf16[512,768]{1,0:T(8,128)(2,1)S(1)}, u32[]{:S(2)}) copy-start(bf16[512,768]{1,0:T(8,128)(2,1)S(1)} %collective-permute-done.4) | copy-start | bytes 2359300
  103.1 30.0 %all-to-all-start.2 = ((bf16[8,72,768]{2,1,0:T(8,128)(2,1)}), bf16[8,72,768]{2,1,0:T(8,128)(2,1)}, u32[]{:S(2)}, u32[]{:S(2)}) async-start(bf16[8,72,768]{2,1,0:T(8,128)(2,1)} %broadcast_in_dim.5), calls=%async_computation.2 | async-start | bytes 1769472 | tf_op jit(solution)/shard_map/all_to_all | solution.py:126
  107.9 57.4 %reduce-scatter.2.cloned.1.call-start = ((), (), s32[]{:S(2)}) async-start(), calls=%async_computation.7 | async-start | bytes 1966080 | tf_op jit(solution)/shard_map/reduce_scatter | solution.py:229
  108.0 20.7 %collective-permute-start.8 = (bf16[512,768]{1,0:T(8,128)(2,1)S(1)}, bf16[512,768]{1,0:T(8,128)(2,1)S(1)}, u32[]{:S(2)}, u32[]{:S(2)}) collective-permute-start(bf16[512,768]{1,0:T(8,128)(2,1)S(1)} %collective-permute-done.4), channel_id=1, source_target_pairs={{0,8},{1,9},{2,10},{3,11},{4,12},{5,13},{6,14},{7,15},{8,16},{9,17... | collective-permute-start | bytes 2359304 | tf_op jit(solution)/shard_map/ppermute | solution.py:214
  116.5 1.1 copy-start.10
  128.7 0.9 copy-start.8
  129.6 8.1 %copy-start = (bf16[1152,1536]{1,0:T(8,128)(2,1)S(1)}, bf16[1152,1536]{1,0:T(8,128)(2,1)}, u32[]{:S(2)}) copy-start(bf16[1152,1536]{1,0:T(8,128)(2,1)} %all-gather.3.cloned.1.call-done) | copy-start | bytes 10616836
  133.0 4.7 %collective-permute-start.9 = (bf16[576,768]{1,0:T(8,128)(2,1)}, bf16[576,768]{1,0:T(8,128)(2,1)}, u32[]{:S(2)}, u32[]{:S(2)}) collective-permute-start(bf16[576,768]{1,0:T(8,128)(2,1)} %bitcast.12.own_ref), channel_id=1, source_target_pairs={{0,32},{32,0},{64,96},{96,64},{128,160},{160,128},{192,224},{224,1... | collective-permute-start | bytes 2654216 | tf_op jit(solution)/shard_map/ppermute | solution.py:234
  137.7 1.3 copy-start.1
  139.0 20.8 %copy-start.5 = (bf16[512,3072]{1,0:T(8,128)(2,1)S(1)}, bf16[512,3072]{1,0:T(8,128)(2,1)}, u32[]{:S(2)}) copy-start(bf16[512,3072]{1,0:T(8,128)(2,1)} %pad_maximum_fusion) | copy-start | bytes 9437188
  148.5 0.9 copy-start.2
  149.4 27.0 %collective-permute-start.10 = (bf16[512,768]{1,0:T(8,128)(2,1)}, bf16[512,768]{1,0:T(8,128)(2,1)S(1)}, u32[]{:S(2)}, u32[]{:S(2)}) collective-permute-start(bf16[512,768]{1,0:T(8,128)(2,1)} %get-tuple-element.34), channel_id=1, source_target_pairs={{0,8},{1,9},{2,10},{3,11},{4,12},{5,13},{6,14},{7,15},{8,16},{9,17... | collective-permute-start | bytes 2359304 | tf_op jit(solution)/shard_map/ppermute | solution.py:241
  154.9 24.1 %collective-permute-start.11 = (bf16[512,768]{1,0:T(8,128)(2,1)}, bf16[512,768]{1,0:T(8,128)(2,1)S(1)}, u32[]{:S(2)}, u32[]{:S(2)}) collective-permute-start(bf16[512,768]{1,0:T(8,128)(2,1)} %get-tuple-element.35), channel_id=1, source_target_pairs={{0,16},{1,17},{2,18},{3,19},{4,20},{5,21},{6,22},{7,23},{8,24},{9,... | collective-permute-start | bytes 2359304 | tf_op jit(solution)/shard_map/ppermute | solution.py:241
  156.8 37.9 %collective-permute-start.12 = (bf16[512,768]{1,0:T(8,128)(2,1)}, bf16[512,768]{1,0:T(8,128)(2,1)}, u32[]{:S(2)}, u32[]{:S(2)}) collective-permute-start(bf16[512,768]{1,0:T(8,128)(2,1)} %get-tuple-element.36), channel_id=1, source_target_pairs={{0,24},{1,25},{2,26},{3,27},{4,28},{5,29},{6,30},{7,31},{8,0},{9,1... | collective-permute-start | bytes 2359304 | tf_op jit(solution)/shard_map/ppermute | solution.py:241
  159.8 35.0 %copy-start.3 = (bf16[512,768]{1,0:T(8,128)(2,1)S(1)}, bf16[512,768]{1,0:T(8,128)(2,1)}, u32[]{:S(2)}) copy-start(bf16[512,768]{1,0:T(8,128)(2,1)} %copy-done.2) | copy-start | bytes 2359300
  165.3 32.8 %all-to-all-start.3 = ((bf16[8,72,512]{2,1,0:T(8,128)(2,1)}), bf16[8,72,512]{2,1,0:T(8,128)(2,1)S(1)}, u32[]{:S(2)}, u32[]{:S(2)}) async-start(bf16[8,72,512]{2,1,0:T(8,128)(2,1)} %bitcast.25), calls=%async_computation.4 | async-start | bytes 1179648 | tf_op jit(solution)/shard_map/all_to_all | solution.py:126
  196.3 1.0 copy-start.12
Sparse Core Ops, SparseCore 0:
  24.7 48.2 all-gather.2
  84.3 43.2 all-gather.4
  130.4 34.8 reduce-scatter.1

commit v10 on v9

--- a/solution.py
+++ b/solution.py
@@ -38,13 +38,9 @@
 
 
 def unit_block_kernel(place_ref, own_ref, other_ref, gate_ref, up_ref, tokens_ref, *refs):
-    *parts, grads_ref, grad_ref, columns_ref = refs
+    *parts, grads_ref, grad_ref = refs
     step = pl.program_id(0)
-    mine = lax.rem(place_ref[1] + step, len(parts)) // 2 == place_ref[0]
-
-    @pl.when(step == 0)
-    def _():
-        columns_ref[...] = tokens_ref[...].T
+    mine = lax.rem(place_ref[1] + step, pl.num_programs(0)) // 2 == place_ref[0]
 
     @pl.when(mine)
     def _():
@@ -68,15 +64,15 @@
         @pl.when(step == k)
         def _():
             part_ref[...] = jnp.dot(
-                columns_ref[...], grads_ref[...], preferred_element_type=jnp.float32
+                tokens_ref[...], grads_ref[...], preferred_element_type=jnp.float32
             ).astype(jnp.bfloat16)
 
 
-def unit_blocks(place, own, other, saved, rows, n_block):
+def unit_blocks(place, own, other, saved, token_columns, n_block):
     n_y, _, block, width = saved.shape
     units = width // 4
     group_rows = own.shape[0]
-    features = rows.shape[1] // 2
+    features = token_columns.shape[0]
 
     def block_of(j, place):
         return lax.rem(place[1] + j, n_block)
@@ -105,13 +101,10 @@
             num_scalar_prefetch=1,
             grid=(n_block,),
             in_specs=[half_spec(), half_spec(), saved_spec(0), saved_spec(2)]
-            + [fixed_spec(group_rows, features)],
+            + [fixed_spec(features, group_rows)],
             out_specs=[fixed_spec(features, 2 * units)] * n_block
             + [pl.BlockSpec((group_rows, 2 * units), lambda j, place: (0, j))],
-            scratch_shapes=[
-                pltpu.VMEM((group_rows, units), jnp.float32),
-                pltpu.VMEM((features, group_rows), jnp.bfloat16),
-            ],
+            scratch_shapes=[pltpu.VMEM((group_rows, units), jnp.float32)],
         ),
         compiler_params=pltpu.CompilerParams(vmem_limit_bytes=32 * 1024 * 1024),
         cost_estimate=pl.CostEstimate(
@@ -119,7 +112,7 @@
             bytes_accessed=14_000_000,
             transcendentals=n_block * group_rows * units,
         ),
-    )(place, own, other, saved, saved, rows)
+    )(place, own, other, saved, saved, token_columns)
 
 
 def exchange(pieces, axis, groups):
@@ -195,10 +188,6 @@
         n_y, N_CORE, block, 2 * half
     )
 
-    both = jnp.concatenate([tokens, out_grad], axis=1)
-    both, saved_share = lax.optimization_barrier((both, saved_share))
-    both_rows = lax.all_gather(both, "col", axis=0, tiled=True, axis_index_groups=z_groups)
-
     w_both = jnp.concatenate([w_gate, w_up], axis=1)
     w_both, grad_rows = lax.optimization_barrier((w_both, grad_rows))
     w_left = lax.ppermute(w_both, "col", x_shift(1))
@@ -208,6 +197,10 @@
     got = lax.ppermute(give, "row", core_swap)
     keep = contract_last(grad_rows, down_half(0)).astype(jnp.bfloat16)
     pair = (keep.astype(jnp.float32) + got.astype(jnp.float32)).astype(jnp.bfloat16)
+
+    both = jnp.concatenate([tokens, out_grad], axis=1)
+    both, pair = lax.optimization_barrier((both, pair))
+    both_rows = lax.all_gather(both, "col", axis=0, tiled=True, axis_index_groups=z_groups)
     terms = exchange(pair.reshape(n_y, block, half), "row", y_groups)
     share = jnp.sum(terms.astype(jnp.float32), axis=0).astype(jnp.bfloat16)
     share, w_left, w_right = lax.optimization_barrier((share, w_left, w_right))
@@ -225,17 +218,22 @@
         down_part.append(contract_first(hidden, grad_rows).astype(jnp.bfloat16))
     down_part = jnp.concatenate(down_part, axis=0).reshape(n_x, units, features)
     down_part, w_far = lax.optimization_barrier((down_part, w_far))
-    weights = jnp.concatenate([w_both, w_right, w_far, w_left], axis=1)
+    weights = [w_both, w_right, w_far, w_left]
     down_sum = lax.psum_scatter(
         down_part, "col", scatter_dimension=0, tiled=True, axis_index_groups=x_groups
     )[0]
-    own, weights, _ = lax.optimization_barrier((own, weights, down_part))
+    token_columns = both_rows[:, :features].swapaxes(0, 1)
+    own, token_columns, _ = lax.optimization_barrier((own, token_columns, down_part))
 
     other = lax.ppermute(own, "row", core_swap)
     *unit_parts, unit_grads = unit_blocks(
-        jnp.stack([core, x_here]), own, other, saved, both_rows, n_x
-    )
-    part_in = contract_last(unit_grads, weights).astype(jnp.bfloat16)
+        jnp.stack([core, x_here]), own, other, saved, token_columns, n_x
+    )
+    part_in = 0.0
+    for step, weight in enumerate(weights):
+        columns = slice(2 * step * units, 2 * (step + 1) * units)
+        part_in = part_in + contract_last(unit_grads[:, columns], weight)
+    part_in = part_in.astype(jnp.bfloat16)
     unit_sum = unit_parts[0].astype(jnp.float32)
     for step in range(1, n_x):
         moved_part = lax.ppermute(unit_parts[step], "col", x_shift(step))

time: 208 us -> 210 us (level)
  local copies, waits for them, and re-layouts: 8.86 us -> 13.1 us
  other arithmetic: 13 us -> 9.54 us
  matrix products: 6.69 us -> 9.4 us
    concatenate x1 -> x0, other arithmetic: 3.38 us -> none  [local(): weights = jnp.concatenate([w_both, w_right, w_far, w_left], axis=1)]
    dot_general x3 -> x6, matrix products: 5.08 us -> 7.8 us  [contract_last(): lax.dot_general(left_side, right_side, (((1,), (1,)), ((), ())), preferre...]
    unnamed x32 -> x39, local copies, waits for them, and re-layouts: 3.58 us -> 5.56 us
  transfers between devices with their start and end apart: 20 -> 20, of which waited for: 12 -> 12; matrix products, arithmetic and copies ran while one was open for 11% -> 13% of each run, Pallas kernels for 5% -> 4%
where the time goes in v10:
time: 210 us; the launch traced here: 207 us
  waiting for transfers between devices  78.4 us (37%)
  starting transfers between devices  73.7 us (35%)
  between operations  14.3 us (7%)
  local copies, waits for them, and re-layouts  13.1 us (6%)
  other arithmetic  9.54 us (5%)
  matrix products  9.4 us (4%)
  Pallas kernels  8.9 us (4%)
    all_to_all x4, starting transfers between devices, exchange(): lax.all_to_all(pieces, axis, 0, 0, tiled=True, axis_index_groups=groups)  32.1 us
    ppermute x3, waiting for transfers between devices, local(): moved_part = lax.ppermute(unit_parts[step], 'col', x_shift(step))  20.5 us
    all_to_all x4, waiting for transfers between devices, exchange(): lax.all_to_all(pieces, axis, 0, 0, tiled=True, axis_index_groups=groups)  18.4 us
    ppermute x3, waiting for transfers between devices, local(): lax.ppermute(w_down, 'col', x_shift(step))  15.2 us
    ppermute x3, starting transfers between devices, local(): moved_part = lax.ppermute(unit_parts[step], 'col', x_shift(step))  10.4 us
    pallas_call x1, Pallas kernels, unit_blocks(): pl.pallas_call(unit_block_kernel, out_shape=(part,) * n_block + (grads,),...  8.9 us
    ppermute x2, waiting for transfers between devices, local(): lax.ppermute(pick(saved_pieces, lax.rem(x_here + turn, 2)), ('row', 'col'...  8.74 us
    ppermute x1, waiting for transfers between devices, local(): w_far = lax.ppermute(w_left, 'col', x_shift(1))  8.28 us
  transfers between devices with their start and end apart: 20, of which 12 were waited for; matrix products, arithmetic and copies ran while one was open for 13% of the time, Pallas kernels for 4%

profile of v10, /device:TPU:6, one launch (start us, length us, event | category | flops | bytes accessed | tf_op | source)
XLA Modules:
  0.0 207.2 jit_solution(3765387006277611704)
XLA Ops:
  7.3 1.0 pad_maximum_fusion.3
  8.3 2.8 %collective-permute-start.6 = (bf16[72,768]{1,0:T(8,128)(2,1)S(1)}, bf16[72,768]{1,0:T(8,128)(2,1)S(1)}, u32[]{:S(2)}, u32[]{:S(2)}) collective-permute-start(bf16[72,768]{1,0:T(8,128)(2,1)S(1)} %get-tuple-element.52), channel_id=1, source_target_pairs={{0,0},{1,1},{2,2},{3,3},{4,4},{5,5},{6,6},{7,7},{8,64},{9,65},{10,... | collective-permute-start | bytes 331784 | tf_op jit(solution)/shard_map/ppermute | solution.py:176
  11.1 3.8 %collective-permute-start.7 = (bf16[72,768]{1,0:T(8,128)(2,1)S(1)}, bf16[72,768]{1,0:T(8,128)(2,1)S(1)}, u32[]{:S(2)}, u32[]{:S(2)}) collective-permute-start(bf16[72,768]{1,0:T(8,128)(2,1)S(1)} %get-tuple-element.53), channel_id=1, source_target_pairs={{0,64},{1,65},{2,66},{3,67},{4,68},{5,69},{6,70},{7,71},{8,0},{9,1... | collective-permute-start | bytes 331784 | tf_op jit(solution)/shard_map/ppermute | solution.py:176
  14.9 4.2 %collective-permute-done.6 = bf16[72,768]{1,0:T(8,128)(2,1)S(1)} collective-permute-done((bf16[72,768]{1,0:T(8,128)(2,1)S(1)}, bf16[72,768]{1,0:T(8,128)(2,1)S(1)}, u32[]{:S(2)}, u32[]{:S(2)}) %collective-permute-start.6) | collective-permute-done | bytes 110624 | tf_op jit(solution)/shard_map/ppermute | solution.py:176
  19.1 4.5 %collective-permute-done.7 = bf16[72,768]{1,0:T(8,128)(2,1)S(1)} collective-permute-done((bf16[72,768]{1,0:T(8,128)(2,1)S(1)}, bf16[72,768]{1,0:T(8,128)(2,1)S(1)}, u32[]{:S(2)}, u32[]{:S(2)}) %collective-permute-start.7) | collective-permute-done | bytes 110624 | tf_op jit(solution)/shard_map/ppermute | solution.py:176
  24.5 0.9 broadcast_in_dim.4
  25.3 10.3 %all-to-all-start = ((bf16[8,72,512]{2,1,0:T(8,128)(2,1)}), bf16[8,72,512]{2,1,0:T(8,128)(2,1)S(1)}, u32[]{:S(2)}, u32[]{:S(2)}) async-start(bf16[8,72,512]{2,1,0:T(8,128)(2,1)} %broadcast_in_dim.4), calls=%async_computation | async-start | bytes 1179648 | tf_op jit(solution)/shard_map/all_to_all | solution.py:119
  35.6 1.9 collective-permute-start
  37.6 3.9 %collective-permute-start.2 = (bf16[384,512]{1,0:T(8,128)(2,1)S(1)}, bf16[384,512]{1,0:T(8,128)(2,1)S(1)}, u32[]{:S(2)}, u32[]{:S(2)}) collective-permute-start(bf16[384,512]{1,0:T(8,128)(2,1)S(1)} %copy-done.14), channel_id=1, source_target_pairs={{0,24},{1,25},{2,26},{3,27},{4,28},{5,29},{6,30},{7,31},{8,0},{9,1... | collective-permute-start | bytes 1179656 | tf_op jit(solution)/shard_map/ppermute | solution.py:160
  41.5 2.1 %collective-permute-start.1 = (bf16[384,512]{1,0:T(8,128)(2,1)S(1)}, bf16[384,512]{1,0:T(8,128)(2,1)S(1)}, u32[]{:S(2)}, u32[]{:S(2)}) collective-permute-start(bf16[384,512]{1,0:T(8,128)(2,1)S(1)} %copy-done.14), channel_id=1, source_target_pairs={{0,16},{1,17},{2,18},{3,19},{4,20},{5,21},{6,22},{7,23},{8,24},{9,... | collective-permute-start | bytes 1179656 | tf_op jit(solution)/shard_map/ppermute | solution.py:160
  43.7 1.1 pad_maximum_fusion.2
  44.8 4.8 %collective-permute-done = bf16[384,512]{1,0:T(8,128)(2,1)S(1)} collective-permute-done((bf16[384,512]{1,0:T(8,128)(2,1)S(1)}, bf16[384,512]{1,0:T(8,128)(2,1)S(1)}, u32[]{:S(2)}, u32[]{:S(2)}) %collective-permute-start) | collective-permute-done | bytes 393248 | tf_op jit(solution)/shard_map/ppermute | solution.py:160
  49.5 10.4 %collective-permute-done.2 = bf16[384,512]{1,0:T(8,128)(2,1)S(1)} collective-permute-done((bf16[384,512]{1,0:T(8,128)(2,1)S(1)}, bf16[384,512]{1,0:T(8,128)(2,1)S(1)}, u32[]{:S(2)}, u32[]{:S(2)}) %collective-permute-start.2) | collective-permute-done | bytes 393248 | tf_op jit(solution)/shard_map/ppermute | solution.py:160
  60.3 1.6 convolution_convert_fusion
  61.9 1.9 collective-permute-start.3
  64.5 2.0 collective-permute-done.3
  66.6 2.7 %add_convert_fusion = bf16[576,768]{1,0:T(8,128)(2,1)} fusion(bf16[576,768]{1,0:T(8,128)(2,1)} %collective-permute-done.3, bf16[576,512]{1,0:T(8,128)(2,1)S(1)} %bitcast.56, bf16[384,512]{1,0:T(8,128)(2,1)S(1)} %get-tuple-element.47, bf16[384,512]{1,0:T(8,128)(2,1)S(1)} %get-tuple-element.44), kind=kOutput, calls=%fused_computation.12 | convolution fusion | flops 456769536 | bytes 3145728 | tf_op jit(solution)/shard_map/dot_general | solution.py:13
  69.3 9.2 %all-to-all-start.1 = ((bf16[8,72,768]{2,1,0:T(8,128)(2,1)}), bf16[8,72,768]{2,1,0:T(8,128)(2,1)S(1)}, u32[]{:S(2)}, u32[]{:S(2)}) async-start(bf16[8,72,768]{2,1,0:T(8,128)(2,1)} %bitcast.11), calls=%async_computation.1 | async-start | bytes 1769472 | tf_op jit(solution)/shard_map/all_to_all | solution.py:119
  78.6 1.9 collective-permute-start.5
  80.5 5.1 %collective-permute-start.4 = (bf16[512,768]{1,0:T(8,128)(2,1)S(1)}, bf16[512,768]{1,0:T(8,128)(2,1)S(1)}, u32[]{:S(2)}, u32[]{:S(2)}) collective-permute-start(bf16[512,768]{1,0:T(8,128)(2,1)S(1)} %pad_maximum_fusion.2), channel_id=1, source_target_pairs={{0,8},{1,9},{2,10},{3,11},{4,12},{5,13},{6,14},{7,15},{8,16},{9,17... | collective-permute-start | bytes 2359304 | tf_op jit(solution)/shard_map/ppermute | solution.py:193
  85.7 18.4 %all-to-all-done.1 = bf16[8,72,768]{2,1,0:T(8,128)(2,1)S(1)} async-done(((bf16[8,72,768]{2,1,0:T(8,128)(2,1)}), bf16[8,72,768]{2,1,0:T(8,128)(2,1)S(1)}, u32[]{:S(2)}, u32[]{:S(2)}) %all-to-all-start.1) | async-done | bytes 884768 | tf_op jit(solution)/shard_map/all_to_all | solution.py:119
  104.2 1.2 broadcast_in_dim.5
  105.4 4.8 %all-to-all-start.2 = ((bf16[8,72,768]{2,1,0:T(8,128)(2,1)}), bf16[8,72,768]{2,1,0:T(8,128)(2,1)}, u32[]{:S(2)}, u32[]{:S(2)}) async-start(bf16[8,72,768]{2,1,0:T(8,128)(2,1)} %broadcast_in_dim.5), calls=%async_computation.2 | async-start | bytes 1769472 | tf_op jit(solution)/shard_map/all_to_all | solution.py:119
  110.2 5.6 %collective-permute-start.8 = (bf16[512,768]{1,0:T(8,128)(2,1)S(1)}, bf16[512,768]{1,0:T(8,128)(2,1)S(1)}, u32[]{:S(2)}, u32[]{:S(2)}) collective-permute-start(bf16[512,768]{1,0:T(8,128)(2,1)S(1)} %collective-permute-done.4), channel_id=1, source_target_pairs={{0,8},{1,9},{2,10},{3,11},{4,12},{5,13},{6,14},{7,15},{8,16},{9,17... | collective-permute-start | bytes 2359304 | tf_op jit(solution)/shard_map/ppermute | solution.py:207
  115.8 2.2 %fusion.28 = (bf16[8,1,72,768]{3,2,1,0:T(8,128)(2,1)S(1)}, bf16[8,1,72,768]{3,2,1,0:T(8,128)(2,1)S(1)}, bf16[8,1,72,768]{3,2,1,0:T(8,128)(2,1)S(1)}, bf16[8,1,72,768]{3,2,1,0:T(8,128)(2,1)S(1)}) fusion(bf16[8,2,72,1536]{3,2,1,0:T(8,128)(2,1)} %bitcast.49), kind=kLoop, calls=%fused_computation.55 | loop fusion | bytes 7077888 | tf_op jit(solution)/shard_map/slice | solution.py:213
  119.8 0.8 convolution_convert_fusion.3
  120.7 0.8 convolution_convert_fusion.2
  121.5 1.3 pad_maximum_fusion.1
  122.7 8.3 %collective-permute-done.8 = bf16[512,768]{1,0:T(8,128)(2,1)S(1)} collective-permute-done((bf16[512,768]{1,0:T(8,128)(2,1)S(1)}, bf16[512,768]{1,0:T(8,128)(2,1)S(1)}, u32[]{:S(2)}, u32[]{:S(2)}) %collective-permute-start.8) | collective-permute-done | bytes 786464 | tf_op jit(solution)/shard_map/ppermute | solution.py:207
  131.0 0.9 copy-done.10
  131.9 2.1 %slice.60 = bf16[576,512]{1,0:T(8,128)(2,1)} slice(bf16[576,1024]{1,0:T(8,128)(2,1)} %all-gather.3.cloned.1.call-done), slice={[0:576], [0:512]} | slice | bytes 1179648 | tf_op jit(solution)/shard_map/slice | solution.py:225
  134.0 2.1 %copy.14 = bf16[576,512]{0,1:T(8,128)(2,1)} copy(bf16[576,512]{1,0:T(8,128)(2,1)} %slice.60) | data formatting | bytes 1179648
  136.2 1.9 collective-permute-start.9
  138.2 2.5 %collective-permute-done.9.other_ref = bf16[576,768]{1,0:T(8,128)(2,1)S(1)} collective-permute-done((bf16[576,768]{1,0:T(8,128)(2,1)}, bf16[576,768]{1,0:T(8,128)(2,1)S(1)}, u32[]{:S(2)}, u32[]{:S(2)}) %collective-permute-start.9) | collective-permute-done | bytes 884768 | tf_op jit(solution)/shard_map/ppermute | solution.py:228
  140.7 1.1 copy-done.1
  141.8 8.9 %shard_map.102 = (bf16[512,768]{1,0:T(8,128)(2,1)S(1)}, bf16[512,768]{1,0:T(8,128)(2,1)}, bf16[512,768]{1,0:T(8,128)(2,1)}, bf16[512,768]{1,0:T(8,128)(2,1)}, bf16[576,3072]{1,0:T(8,128)(2,1)S(1)}) custom-call(s32[2]{0:T(128)S(1)} %pad_add_fusion.place_ref, bf16[576,768]{1,0:T(8,128)(2,1)} %bitcast.12.own_ref, ...), custom_call_target="tpu_custom_call" | custom-call | flops 1811939328 | bytes 14000000 | tf_op jit(solution)/shard_map/pallas_call | solution.py:97
  150.7 5.5 %collective-permute-start.10 = (bf16[512,768]{1,0:T(8,128)(2,1)}, bf16[512,768]{1,0:T(8,128)(2,1)S(1)}, u32[]{:S(2)}, u32[]{:S(2)}) collective-permute-start(bf16[512,768]{1,0:T(8,128)(2,1)} %get-tuple-element.36), channel_id=1, source_target_pairs={{0,8},{1,9},{2,10},{3,11},{4,12},{5,13},{6,14},{7,15},{8,16},{9,17... | collective-permute-start | bytes 2359304 | tf_op jit(solution)/shard_map/ppermute | solution.py:239
  156.2 1.9 collective-permute-start.11
  158.2 2.9 %collective-permute-start.12 = (bf16[512,768]{1,0:T(8,128)(2,1)}, bf16[512,768]{1,0:T(8,128)(2,1)}, u32[]{:S(2)}, u32[]{:S(2)}) collective-permute-start(bf16[512,768]{1,0:T(8,128)(2,1)} %get-tuple-element.38), channel_id=1, source_target_pairs={{0,24},{1,25},{2,26},{3,27},{4,28},{5,29},{6,30},{7,31},{8,0},{9,1... | collective-permute-start | bytes 2359304 | tf_op jit(solution)/shard_map/ppermute | solution.py:239
  164.1 1.5 fusion.12
  165.6 2.7 %reduce-scatter.2.cloned.1.call-done = bf16[1,384,512]{2,1,0:T(8,128)(2,1)} async-done(((bf16[4,384,512]{2,1,0:T(8,128)(2,1)}), bf16[1,384,512]{2,1,0:T(8,128)(2,1)}) %reduce-scatter.2.cloned.1.call-update) | async-done | bytes 393232 | tf_op jit(solution)/shard_map/reduce_scatter | solution.py:222
  168.2 7.8 %all-to-all-start.3 = ((bf16[8,72,512]{2,1,0:T(8,128)(2,1)}), bf16[8,72,512]{2,1,0:T(8,128)(2,1)S(1)}, u32[]{:S(2)}, u32[]{:S(2)}) async-start(bf16[8,72,512]{2,1,0:T(8,128)(2,1)} %bitcast.26), calls=%async_computation.4 | async-start | bytes 1179648 | tf_op jit(solution)/shard_map/all_to_all | solution.py:119
  176.1 2.5 %collective-permute-done.10 = bf16[512,768]{1,0:T(8,128)(2,1)S(1)} collective-permute-done((bf16[512,768]{1,0:T(8,128)(2,1)}, bf16[512,768]{1,0:T(8,128)(2,1)S(1)}, u32[]{:S(2)}, u32[]{:S(2)}) %collective-permute-start.10) | collective-permute-done | bytes 786464 | tf_op jit(solution)/shard_map/ppermute | solution.py:239
  178.6 1.8 collective-permute-done.11
  180.4 16.2 %collective-permute-done.12 = bf16[512,768]{1,0:T(8,128)(2,1)} collective-permute-done((bf16[512,768]{1,0:T(8,128)(2,1)}, bf16[512,768]{1,0:T(8,128)(2,1)}, u32[]{:S(2)}, u32[]{:S(2)}) %collective-permute-start.12) | collective-permute-done | bytes 786464 | tf_op jit(solution)/shard_map/ppermute | solution.py:239
  196.6 1.6 multiply_convert_fusion
  198.2 1.0 fusion.29
  199.2 0.8 multiply_convert_fusion.1
  (65 shorter events, 7.6 us)
Async XLA Ops:
  7.2 17.3 %copy-start.17 = (bf16[72,512]{1,0:T(8,128)(2,1)S(1)}, bf16[72,512]{1,0:T(8,128)(2,1)}, u32[]{:S(2)}) copy-start(bf16[72,512]{1,0:T(8,128)(2,1)} %param.8) | copy-start | bytes 221188
  7.2 108.7 %all-gather.5.cloned.1.call-start = ((), (), s32[]{:S(2)}) async-start(), calls=%async_computation.6 | async-start | bytes 3760128 | tf_op jit(solution)/shard_map/all_gather | solution.py:187
  8.3 10.9 %collective-permute-start.6 = (bf16[72,768]{1,0:T(8,128)(2,1)S(1)}, bf16[72,768]{1,0:T(8,128)(2,1)S(1)}, u32[]{:S(2)}, u32[]{:S(2)}) collective-permute-start(bf16[72,768]{1,0:T(8,128)(2,1)S(1)} %get-tuple-element.52), channel_id=1, source_target_pairs={{0,0},{1,1},{2,2},{3,3},{4,4},{5,5},{6,6},{7,7},{8,64},{9,65},{10,... | collective-permute-start | bytes 331784 | tf_op jit(solution)/shard_map/ppermute | solution.py:176
  11.1 12.5 %collective-permute-start.7 = (bf16[72,768]{1,0:T(8,128)(2,1)S(1)}, bf16[72,768]{1,0:T(8,128)(2,1)S(1)}, u32[]{:S(2)}, u32[]{:S(2)}) collective-permute-start(bf16[72,768]{1,0:T(8,128)(2,1)S(1)} %get-tuple-element.53), channel_id=1, source_target_pairs={{0,64},{1,65},{2,66},{3,67},{4,68},{5,69},{6,70},{7,71},{8,0},{9,1... | collective-permute-start | bytes 331784 | tf_op jit(solution)/shard_map/ppermute | solution.py:176
  23.7 12.0 %copy-start.14 = (bf16[384,512]{1,0:T(8,128)(2,1)S(1)}, bf16[384,512]{1,0:T(8,128)(2,1)}, u32[]{:S(2)}) copy-start(bf16[384,512]{1,0:T(8,128)(2,1)} %param.13) | copy-start | bytes 1179652
  23.7 20.0 %copy-start.16 = (bf16[512,384]{1,0:T(8,128)(2,1)S(1)}, bf16[512,384]{1,0:T(8,128)(2,1)}, u32[]{:S(2)}) copy-start(bf16[512,384]{1,0:T(8,128)(2,1)} %param.12) | copy-start | bytes 1179652
  25.3 35.0 %all-to-all-start = ((bf16[8,72,512]{2,1,0:T(8,128)(2,1)}), bf16[8,72,512]{2,1,0:T(8,128)(2,1)S(1)}, u32[]{:S(2)}, u32[]{:S(2)}) async-start(bf16[8,72,512]{2,1,0:T(8,128)(2,1)} %broadcast_in_dim.4), calls=%async_computation | async-start | bytes 1179648 | tf_op jit(solution)/shard_map/all_to_all | solution.py:119
  35.6 13.9 %collective-permute-start = (bf16[384,512]{1,0:T(8,128)(2,1)S(1)}, bf16[384,512]{1,0:T(8,128)(2,1)S(1)}, u32[]{:S(2)}, u32[]{:S(2)}) collective-permute-start(bf16[384,512]{1,0:T(8,128)(2,1)S(1)} %copy-done.14), channel_id=1, source_target_pairs={{0,8},{1,9},{2,10},{3,11},{4,12},{5,13},{6,14},{7,15},{8,16},{9,17... | collective-permute-start | bytes 1179656 | tf_op jit(solution)/shard_map/ppermute | solution.py:160
  37.6 22.4 %collective-permute-start.2 = (bf16[384,512]{1,0:T(8,128)(2,1)S(1)}, bf16[384,512]{1,0:T(8,128)(2,1)S(1)}, u32[]{:S(2)}, u32[]{:S(2)}) collective-permute-start(bf16[384,512]{1,0:T(8,128)(2,1)S(1)} %copy-done.14), channel_id=1, source_target_pairs={{0,24},{1,25},{2,26},{3,27},{4,28},{5,29},{6,30},{7,31},{8,0},{9,1... | collective-permute-start | bytes 1179656 | tf_op jit(solution)/shard_map/ppermute | solution.py:160
  41.5 18.5 %collective-permute-start.1 = (bf16[384,512]{1,0:T(8,128)(2,1)S(1)}, bf16[384,512]{1,0:T(8,128)(2,1)S(1)}, u32[]{:S(2)}, u32[]{:S(2)}) collective-permute-start(bf16[384,512]{1,0:T(8,128)(2,1)S(1)} %copy-done.14), channel_id=1, source_target_pairs={{0,16},{1,17},{2,18},{3,19},{4,20},{5,21},{6,22},{7,23},{8,24},{9,... | collective-permute-start | bytes 1179656 | tf_op jit(solution)/shard_map/ppermute | solution.py:160
  44.8 35.7 %copy-start.4 = (bf16[512,768]{1,0:T(8,128)(2,1)}, bf16[512,768]{1,0:T(8,128)(2,1)S(1)}, u32[]{:S(2)}) copy-start(bf16[512,768]{1,0:T(8,128)(2,1)S(1)} %pad_maximum_fusion.2) | copy-start | bytes 2359300
  60.3 3.6 %copy-start.18 = (bf16[72,512]{1,0:T(8,128)(2,1)S(1)}, bf16[72,512]{1,0:T(8,128)(2,1)}, u32[]{:S(2)}) copy-start(bf16[72,512]{1,0:T(8,128)(2,1)} %param.7) | copy-start | bytes 221188
  60.3 6.3 %copy-start.12 = (bf16[8,72,512]{2,1,0:T(8,128)(2,1)}, bf16[8,72,512]{2,1,0:T(8,128)(2,1)S(1)}, u32[]{:S(2)}) copy-start(bf16[8,72,512]{2,1,0:T(8,128)(2,1)S(1)} %all-to-all-done) | copy-start | bytes 1769476
  61.9 4.7 %collective-permute-start.3 = (bf16[576,768]{1,0:T(8,128)(2,1)}, bf16[576,768]{1,0:T(8,128)(2,1)}, u32[]{:S(2)}, u32[]{:S(2)}) collective-permute-start(bf16[576,768]{1,0:T(8,128)(2,1)} %convolution_convert_fusion), channel_id=1, source_target_pairs={{0,32},{32,0},{64,96},{96,64},{128,160},{160,128},{192,224},{224,1... | collective-permute-start | bytes 2654216 | tf_op jit(solution)/shard_map/ppermute | solution.py:197
  69.3 34.7 %all-to-all-start.1 = ((bf16[8,72,768]{2,1,0:T(8,128)(2,1)}), bf16[8,72,768]{2,1,0:T(8,128)(2,1)S(1)}, u32[]{:S(2)}, u32[]{:S(2)}) async-start(bf16[8,72,768]{2,1,0:T(8,128)(2,1)} %bitcast.11), calls=%async_computation.1 | async-start | bytes 1769472 | tf_op jit(solution)/shard_map/all_to_all | solution.py:119
  78.5 53.4 %all-gather.3.cloned.1.call-start = ((), (), s32[]{:S(2)}) async-start(), calls=%async_computation.5 | async-start | bytes 1327104 | tf_op jit(solution)/shard_map/all_gather | solution.py:203
  78.6 25.6 %collective-permute-start.5 = (bf16[512,768]{1,0:T(8,128)(2,1)S(1)}, bf16[512,768]{1,0:T(8,128)(2,1)S(1)}, u32[]{:S(2)}, u32[]{:S(2)}) collective-permute-start(bf16[512,768]{1,0:T(8,128)(2,1)S(1)} %pad_maximum_fusion.2), channel_id=1, source_target_pairs={{0,24},{1,25},{2,26},{3,27},{4,28},{5,29},{6,30},{7,31},{8,0},{9,1... | collective-permute-start | bytes 2359304 | tf_op jit(solution)/shard_map/ppermute | solution.py:194
  80.5 23.7 %collective-permute-start.4 = (bf16[512,768]{1,0:T(8,128)(2,1)S(1)}, bf16[512,768]{1,0:T(8,128)(2,1)S(1)}, u32[]{:S(2)}, u32[]{:S(2)}) collective-permute-start(bf16[512,768]{1,0:T(8,128)(2,1)S(1)} %pad_maximum_fusion.2), channel_id=1, source_target_pairs={{0,8},{1,9},{2,10},{3,11},{4,12},{5,13},{6,14},{7,15},{8,16},{9,17... | collective-permute-start | bytes 2359304 | tf_op jit(solution)/shard_map/ppermute | solution.py:193
  104.2 13.9 %copy-start.6 = (bf16[512,768]{1,0:T(8,128)(2,1)}, bf16[512,768]{1,0:T(8,128)(2,1)S(1)}, u32[]{:S(2)}) copy-start(bf16[512,768]{1,0:T(8,128)(2,1)S(1)} %collective-permute-done.5) | copy-start | bytes 2359300
  104.2 13.9 %copy-start.8 = (bf16[512,768]{1,0:T(8,128)(2,1)}, bf16[512,768]{1,0:T(8,128)(2,1)S(1)}, u32[]{:S(2)}) copy-start(bf16[512,768]{1,0:T(8,128)(2,1)S(1)} %collective-permute-done.4) | copy-start | bytes 2359300
  105.4 30.8 %all-to-all-start.2 = ((bf16[8,72,768]{2,1,0:T(8,128)(2,1)}), bf16[8,72,768]{2,1,0:T(8,128)(2,1)}, u32[]{:S(2)}, u32[]{:S(2)}) async-start(bf16[8,72,768]{2,1,0:T(8,128)(2,1)} %broadcast_in_dim.5), calls=%async_computation.2 | async-start | bytes 1769472 | tf_op jit(solution)/shard_map/all_to_all | solution.py:119
  110.2 58.1 %reduce-scatter.2.cloned.1.call-start = ((), (), s32[]{:S(2)}) async-start(), calls=%async_computation.7 | async-start | bytes 1966080 | tf_op jit(solution)/shard_map/reduce_scatter | solution.py:222
  110.2 20.8 %collective-permute-start.8 = (bf16[512,768]{1,0:T(8,128)(2,1)S(1)}, bf16[512,768]{1,0:T(8,128)(2,1)S(1)}, u32[]{:S(2)}, u32[]{:S(2)}) collective-permute-start(bf16[512,768]{1,0:T(8,128)(2,1)S(1)} %collective-permute-done.4), channel_id=1, source_target_pairs={{0,8},{1,9},{2,10},{3,11},{4,12},{5,13},{6,14},{7,15},{8,16},{9,17... | collective-permute-start | bytes 2359304 | tf_op jit(solution)/shard_map/ppermute | solution.py:207
  118.8 1.1 copy-start.13
  131.0 0.9 copy-start.10
  131.9 8.8 %copy-start = (bf16[1152,1536]{1,0:T(8,128)(2,1)S(1)}, bf16[1152,1536]{1,0:T(8,128)(2,1)}, u32[]{:S(2)}) copy-start(bf16[1152,1536]{1,0:T(8,128)(2,1)} %all-gather.5.cloned.1.call-done) | copy-start | bytes 10616836
  136.2 4.5 %collective-permute-start.9 = (bf16[576,768]{1,0:T(8,128)(2,1)}, bf16[576,768]{1,0:T(8,128)(2,1)S(1)}, u32[]{:S(2)}, u32[]{:S(2)}) collective-permute-start(bf16[576,768]{1,0:T(8,128)(2,1)} %bitcast.12.own_ref), channel_id=1, source_target_pairs={{0,32},{32,0},{64,96},{96,64},{128,160},{160,128},{192,224},{224,1... | collective-permute-start | bytes 2654216 | tf_op jit(solution)/shard_map/ppermute | solution.py:228
  140.7 1.1 copy-start.1
  141.8 19.3 %copy-start.9 = (bf16[512,768]{1,0:T(8,128)(2,1)S(1)}, bf16[512,768]{1,0:T(8,128)(2,1)}, u32[]{:S(2)}) copy-start(bf16[512,768]{1,0:T(8,128)(2,1)} %copy-done.8) | copy-start | bytes 2359300
  150.7 11.8 %copy-start.2 = (bf16[512,768]{1,0:T(8,128)(2,1)}, bf16[512,768]{1,0:T(8,128)(2,1)S(1)}, u32[]{:S(2)}) copy-start(bf16[512,768]{1,0:T(8,128)(2,1)S(1)} %get-tuple-element.35) | copy-start | bytes 2359300
  150.7 11.1 %copy-start.11 = (bf16[512,768]{1,0:T(8,128)(2,1)S(1)}, bf16[512,768]{1,0:T(8,128)(2,1)}, u32[]{:S(2)}) copy-start(bf16[512,768]{1,0:T(8,128)(2,1)} %copy-done.10) | copy-start | bytes 2359300
  150.7 27.9 %collective-permute-start.10 = (bf16[512,768]{1,0:T(8,128)(2,1)}, bf16[512,768]{1,0:T(8,128)(2,1)S(1)}, u32[]{:S(2)}, u32[]{:S(2)}) collective-permute-start(bf16[512,768]{1,0:T(8,128)(2,1)} %get-tuple-element.36), channel_id=1, source_target_pairs={{0,8},{1,9},{2,10},{3,11},{4,12},{5,13},{6,14},{7,15},{8,16},{9,17... | collective-permute-start | bytes 2359304 | tf_op jit(solution)/shard_map/ppermute | solution.py:239
  156.2 24.2 %collective-permute-start.11 = (bf16[512,768]{1,0:T(8,128)(2,1)}, bf16[512,768]{1,0:T(8,128)(2,1)S(1)}, u32[]{:S(2)}, u32[]{:S(2)}) collective-permute-start(bf16[512,768]{1,0:T(8,128)(2,1)} %get-tuple-element.37), channel_id=1, source_target_pairs={{0,16},{1,17},{2,18},{3,19},{4,20},{5,21},{6,22},{7,23},{8,24},{9,... | collective-permute-start | bytes 2359304 | tf_op jit(solution)/shard_map/ppermute | solution.py:239
  158.2 38.4 %collective-permute-start.12 = (bf16[512,768]{1,0:T(8,128)(2,1)}, bf16[512,768]{1,0:T(8,128)(2,1)}, u32[]{:S(2)}, u32[]{:S(2)}) collective-permute-start(bf16[512,768]{1,0:T(8,128)(2,1)} %get-tuple-element.38), channel_id=1, source_target_pairs={{0,24},{1,25},{2,26},{3,27},{4,28},{5,29},{6,30},{7,31},{8,0},{9,1... | collective-permute-start | bytes 2359304 | tf_op jit(solution)/shard_map/ppermute | solution.py:239
  161.8 1.1 copy-start.7
  162.9 1.1 copy-start.5
  165.6 31.0 %copy-start.3 = (bf16[512,768]{1,0:T(8,128)(2,1)S(1)}, bf16[512,768]{1,0:T(8,128)(2,1)}, u32[]{:S(2)}) copy-start(bf16[512,768]{1,0:T(8,128)(2,1)} %copy-done.2) | copy-start | bytes 2359300
  168.2 31.8 %all-to-all-start.3 = ((bf16[8,72,512]{2,1,0:T(8,128)(2,1)}), bf16[8,72,512]{2,1,0:T(8,128)(2,1)S(1)}, u32[]{:S(2)}, u32[]{:S(2)}) async-start(bf16[8,72,512]{2,1,0:T(8,128)(2,1)} %bitcast.26), calls=%async_computation.4 | async-start | bytes 1179648 | tf_op jit(solution)/shard_map/all_to_all | solution.py:119
  198.2 1.0 copy-start.15
Sparse Core Ops, SparseCore 0:
  24.6 48.2 all-gather.4
  85.8 43.2 all-gather.2
  132.0 36.1 reduce-scatter.1

commit v11 on v10

--- a/solution.py
+++ b/solution.py
@@ -21,58 +21,62 @@
     )
 
 
-def swiglu_grads(hidden_grad, gate_pre, up_pre):
+def swiglu_factors(gate_pre, up_pre):
     gate_float = gate_pre.astype(jnp.float32)
     up_float = up_pre.astype(jnp.float32)
-    grad_float = hidden_grad.astype(jnp.float32)
     sigmoid_gate = jax.nn.sigmoid(gate_float)
-    gate_grad = grad_float * up_float * sigmoid_gate * (1.0 + gate_float * (1.0 - sigmoid_gate))
-    up_grad = grad_float * (gate_float * sigmoid_gate)
-    return gate_grad.astype(jnp.bfloat16), up_grad.astype(jnp.bfloat16)
-
-
-def swiglu_hidden(gate_pre, up_pre):
-    gate_float = gate_pre.astype(jnp.float32)
-    swish_gate = gate_float * jax.nn.sigmoid(gate_float)
-    return (swish_gate * up_pre.astype(jnp.float32)).astype(jnp.bfloat16)
+    swish_gate = gate_float * sigmoid_gate
+    gate_factor = up_float * sigmoid_gate * (1.0 + gate_float * (1.0 - sigmoid_gate))
+    return (
+        gate_factor.astype(jnp.bfloat16),
+        swish_gate.astype(jnp.bfloat16),
+        (swish_gate * up_float).astype(jnp.bfloat16),
+    )
 
 
 def unit_block_kernel(place_ref, own_ref, other_ref, gate_ref, up_ref, tokens_ref, *refs):
-    *parts, grads_ref, grad_ref = refs
-    step = pl.program_id(0)
-    mine = lax.rem(place_ref[1] + step, pl.num_programs(0)) // 2 == place_ref[0]
-
-    @pl.when(mine)
+    *outs, grads_ref, parts_ref, columns_ref, sems = refs
+    step, n_block = pl.program_id(0), pl.num_programs(0)
+    mine = lax.rem(place_ref[1] + step, n_block) // 2 == place_ref[0]
+
+    @pl.when(step == 0)
     def _():
-        grad_ref[...] = own_ref[...].astype(jnp.float32)
-
-    @pl.when(jnp.logical_not(mine))
-    def _():
-        grad_ref[...] = other_ref[...].astype(jnp.float32)
-
-    shape = grad_ref.shape
+        columns_ref[...] = tokens_ref[...].T
+
+    hidden_grad = jnp.where(
+        mine, own_ref[...].astype(jnp.float32), other_ref[...].astype(jnp.float32)
+    )
+    shape = hidden_grad.shape
     units = shape[-1]
-    gate_grad, up_grad = swiglu_grads(
-        grad_ref[...],
-        gate_ref[...].astype(jnp.float32).reshape(shape),
-        up_ref[...].astype(jnp.float32).reshape(shape),
-    )
-    grads_ref[:, :units] = gate_grad
-    grads_ref[:, units:] = up_grad
-    for k, part_ref in enumerate(parts):
+    for which, factor_ref in enumerate((gate_ref, up_ref)):
+        factor = factor_ref[...].astype(jnp.float32).reshape(shape)
+        grads_ref[:, which * units : (which + 1) * units] = (hidden_grad * factor).astype(
+            jnp.bfloat16
+        )
+    copies = [
+        pltpu.make_async_copy(parts_ref.at[k], out_ref, sems.at[k])
+        for k, out_ref in enumerate(outs)
+    ]
+    for k, copy in enumerate(copies):
 
         @pl.when(step == k)
         def _():
-            part_ref[...] = jnp.dot(
-                tokens_ref[...], grads_ref[...], preferred_element_type=jnp.float32
+            parts_ref[k] = jnp.dot(
+                columns_ref[...], grads_ref[...], preferred_element_type=jnp.float32
             ).astype(jnp.bfloat16)
-
-
-def unit_blocks(place, own, other, saved, token_columns, n_block):
-    n_y, _, block, width = saved.shape
-    units = width // 4
+            copy.start()
+
+    @pl.when(step == n_block - 1)
+    def _():
+        for copy in copies:
+            copy.wait()
+
+
+def unit_blocks(place, own, other, gate_factor, up_factor, rows, n_block):
+    n_y, _, block, half = gate_factor.shape
+    units = half // 2
     group_rows = own.shape[0]
-    features = token_columns.shape[0]
+    features = rows.shape[1] // 2
 
     def block_of(j, place):
         return lax.rem(place[1] + j, n_block)
@@ -82,15 +86,12 @@
             (group_rows, units), lambda j, place: (0, lax.rem(block_of(j, place), 2))
         )
 
-    def saved_spec(first):
+    def factor_spec():
         def index(j, place):
             which = block_of(j, place)
-            return (0, lax.div(which, 2), 0, first + lax.rem(which, 2))
+            return (0, lax.div(which, 2), 0, lax.rem(which, 2))
 
         return pl.BlockSpec((n_y, 1, block, units), index)
-
-    def fixed_spec(*shape):
-        return pl.BlockSpec(shape, lambda j, place: (0, 0))
 
     part = jax.ShapeDtypeStruct((features, 2 * units), jnp.bfloat16)
     grads = jax.ShapeDtypeStruct((group_rows, 2 * units * n_block), jnp.bfloat16)
@@ -100,19 +101,23 @@
         grid_spec=pltpu.PrefetchScalarGridSpec(
             num_scalar_prefetch=1,
             grid=(n_block,),
-            in_specs=[half_spec(), half_spec(), saved_spec(0), saved_spec(2)]
-            + [fixed_spec(features, group_rows)],
-            out_specs=[fixed_spec(features, 2 * units)] * n_block
+            in_specs=[half_spec(), half_spec(), factor_spec(), factor_spec()]
+            + [pl.BlockSpec((group_rows, features), lambda j, place: (0, 0))],
+            out_specs=[pl.BlockSpec(memory_space=pl.ANY)] * n_block
             + [pl.BlockSpec((group_rows, 2 * units), lambda j, place: (0, j))],
-            scratch_shapes=[pltpu.VMEM((group_rows, units), jnp.float32)],
+            scratch_shapes=[
+                pltpu.VMEM((n_block, features, 2 * units), jnp.bfloat16),
+                pltpu.VMEM((features, group_rows), jnp.bfloat16),
+                pltpu.SemaphoreType.DMA((n_block,)),
+            ],
         ),
         compiler_params=pltpu.CompilerParams(vmem_limit_bytes=32 * 1024 * 1024),
         cost_estimate=pl.CostEstimate(
             flops=4 * n_block * features * units * group_rows,
             bytes_accessed=14_000_000,
-            transcendentals=n_block * group_rows * units,
+            transcendentals=0,
         ),
-    )(place, own, other, saved, saved, token_columns)
+    )(place, own, other, gate_factor, up_factor, rows)
 
 
 def exchange(pieces, axis, groups):
@@ -209,25 +214,24 @@
 
     grad_scale = (rows * n_row) ** (-0.5)
 
-    def side_saved(side):
-        return saved[:, side, :, :half], saved[:, side, :, half:]
-
-    down_part = []
-    for side in range(2):
-        hidden = swiglu_hidden(*side_saved(side)).reshape(group_rows, half)
-        down_part.append(contract_first(hidden, grad_rows).astype(jnp.bfloat16))
+    gate_factor, up_factor, hidden = swiglu_factors(saved[..., :half], saved[..., half:])
+    down_part = [
+        contract_first(hidden[:, side].reshape(group_rows, half), grad_rows).astype(jnp.bfloat16)
+        for side in range(2)
+    ]
     down_part = jnp.concatenate(down_part, axis=0).reshape(n_x, units, features)
     down_part, w_far = lax.optimization_barrier((down_part, w_far))
     weights = [w_both, w_right, w_far, w_left]
     down_sum = lax.psum_scatter(
         down_part, "col", scatter_dimension=0, tiled=True, axis_index_groups=x_groups
     )[0]
-    token_columns = both_rows[:, :features].swapaxes(0, 1)
-    own, token_columns, _ = lax.optimization_barrier((own, token_columns, down_part))
+    own, gate_factor, up_factor, _ = lax.optimization_barrier(
+        (own, gate_factor, up_factor, down_part)
+    )
 
     other = lax.ppermute(own, "row", core_swap)
     *unit_parts, unit_grads = unit_blocks(
-        jnp.stack([core, x_here]), own, other, saved, token_columns, n_x
+        jnp.stack([core, x_here]), own, other, gate_factor, up_factor, both_rows, n_x
     )
     part_in = 0.0
     for step, weight in enumerate(weights):

time: 210 us -> 219 us (1.043)
  waiting for transfers between devices: 78.4 us -> 90.6 us
  local copies, waits for them, and re-layouts: 13.1 us -> 5.94 us
  matrix products: 9.4 us -> 11.8 us
    ppermute x3, waiting for transfers between devices: 20.5 us -> 6.12 us  [local(): moved_part = lax.ppermute(unit_parts[step], 'col', x_shift(step))]
    reduce_scatter x1, waiting for transfers between devices: 2.66 us -> 17 us  [local(): lax.psum_scatter(down_part, 'col', scatter_dimension=0, tiled=True, axis_...]
    all_to_all x4, waiting for transfers between devices: 18.4 us -> 30.9 us  [exchange(): lax.all_to_all(pieces, axis, 0, 0, tiled=True, axis_index_groups=groups)]
    slice x2 -> x1, local copies, waits for them, and re-layouts: 4.32 us -> 0.12 us  [local(): hidden[:, side].reshape(group_rows, half)]
    unnamed x39 -> x28, local copies, waits for them, and re-layouts: 5.56 us -> 2.79 us
    dot_general x6, matrix products: 7.8 us -> 10.2 us  [contract_last(): lax.dot_general(left_side, right_side, (((1,), (1,)), ((), ())), preferre...]
    convert_element_type x2 -> x1, other arithmetic: 1.34 us -> 3.53 us  [swiglu_factors(): (swish_gate * up_float).astype(jnp.bfloat16)]
  transfers between devices with their start and end apart: 20 -> 20, of which waited for: 12 -> 12; matrix products, arithmetic and copies ran while one was open for 13% -> 11% of each run, Pallas kernels for 4% -> 4%
where the time goes in v11:
time: 219 us; the launch traced here: 215 us
  waiting for transfers between devices  90.6 us (41%)
  starting transfers between devices  72.6 us (33%)
  between operations  14.3 us (7%)
  matrix products  11.8 us (5%)
  other arithmetic  11.7 us (5%)
  Pallas kernels  7.84 us (4%)
  local copies, waits for them, and re-layouts  5.94 us (3%)
    all_to_all x4, starting transfers between devices, exchange(): lax.all_to_all(pieces, axis, 0, 0, tiled=True, axis_index_groups=groups)  32.1 us
    all_to_all x4, waiting for transfers between devices, exchange(): lax.all_to_all(pieces, axis, 0, 0, tiled=True, axis_index_groups=groups)  30.9 us
    reduce_scatter x1, waiting for transfers between devices, local(): lax.psum_scatter(down_part, 'col', scatter_dimension=0, tiled=True, axis_...  17 us
    ppermute x3, waiting for transfers between devices, local(): lax.ppermute(w_down, 'col', x_shift(step))  15.2 us
    dot_general x6, matrix products, contract_last(): lax.dot_general(left_side, right_side, (((1,), (1,)), ((), ())), preferre...  10.2 us
    ppermute x3, starting transfers between devices, local(): moved_part = lax.ppermute(unit_parts[step], 'col', x_shift(step))  9.24 us
    ppermute x2, waiting for transfers between devices, local(): lax.ppermute(pick(saved_pieces, lax.rem(x_here + turn, 2)), ('row', 'col'...  8.74 us
    ppermute x3, starting transfers between devices, local(): lax.ppermute(w_down, 'col', x_shift(step))  7.95 us
  transfers between devices with their start and end apart: 20, of which 12 were waited for; matrix products, arithmetic and copies ran while one was open for 11% of the time, Pallas kernels for 4%

profile of v11, /device:TPU:6, one launch (start us, length us, event | category | flops | bytes accessed | tf_op | source)
XLA Modules:
  0.0 214.7 jit_solution(15051208375387624558)
XLA Ops:
  7.3 1.0 pad_maximum_fusion.3
  8.3 2.8 %collective-permute-start.6 = (bf16[72,768]{1,0:T(8,128)(2,1)S(1)}, bf16[72,768]{1,0:T(8,128)(2,1)S(1)}, u32[]{:S(2)}, u32[]{:S(2)}) collective-permute-start(bf16[72,768]{1,0:T(8,128)(2,1)S(1)} %get-tuple-element.55), channel_id=1, source_target_pairs={{0,0},{1,1},{2,2},{3,3},{4,4},{5,5},{6,6},{7,7},{8,64},{9,65},{10,... | collective-permute-start | bytes 331784 | tf_op jit(solution)/shard_map/ppermute | solution.py:181
  11.1 3.8 %collective-permute-start.7 = (bf16[72,768]{1,0:T(8,128)(2,1)S(1)}, bf16[72,768]{1,0:T(8,128)(2,1)S(1)}, u32[]{:S(2)}, u32[]{:S(2)}) collective-permute-start(bf16[72,768]{1,0:T(8,128)(2,1)S(1)} %get-tuple-element.56), channel_id=1, source_target_pairs={{0,64},{1,65},{2,66},{3,67},{4,68},{5,69},{6,70},{7,71},{8,0},{9,1... | collective-permute-start | bytes 331784 | tf_op jit(solution)/shard_map/ppermute | solution.py:181
  14.9 4.2 %collective-permute-done.6 = bf16[72,768]{1,0:T(8,128)(2,1)S(1)} collective-permute-done((bf16[72,768]{1,0:T(8,128)(2,1)S(1)}, bf16[72,768]{1,0:T(8,128)(2,1)S(1)}, u32[]{:S(2)}, u32[]{:S(2)}) %collective-permute-start.6) | collective-permute-done | bytes 110624 | tf_op jit(solution)/shard_map/ppermute | solution.py:181
  19.1 4.5 %collective-permute-done.7 = bf16[72,768]{1,0:T(8,128)(2,1)S(1)} collective-permute-done((bf16[72,768]{1,0:T(8,128)(2,1)S(1)}, bf16[72,768]{1,0:T(8,128)(2,1)S(1)}, u32[]{:S(2)}, u32[]{:S(2)}) %collective-permute-start.7) | collective-permute-done | bytes 110624 | tf_op jit(solution)/shard_map/ppermute | solution.py:181
  24.5 0.9 broadcast_in_dim.4
  25.3 10.3 %all-to-all-start = ((bf16[8,72,512]{2,1,0:T(8,128)(2,1)}), bf16[8,72,512]{2,1,0:T(8,128)(2,1)S(1)}, u32[]{:S(2)}, u32[]{:S(2)}) async-start(bf16[8,72,512]{2,1,0:T(8,128)(2,1)} %broadcast_in_dim.4), calls=%async_computation | async-start | bytes 1179648 | tf_op jit(solution)/shard_map/all_to_all | solution.py:124
  35.6 1.9 collective-permute-start
  37.6 3.9 %collective-permute-start.2 = (bf16[384,512]{1,0:T(8,128)(2,1)S(1)}, bf16[384,512]{1,0:T(8,128)(2,1)S(1)}, u32[]{:S(2)}, u32[]{:S(2)}) collective-permute-start(bf16[384,512]{1,0:T(8,128)(2,1)S(1)} %copy-done.9), channel_id=1, source_target_pairs={{0,24},{1,25},{2,26},{3,27},{4,28},{5,29},{6,30},{7,31},{8,0},{9,1... | collective-permute-start | bytes 1179656 | tf_op jit(solution)/shard_map/ppermute | solution.py:165
  41.5 2.1 collective-permute-start.1
  43.7 1.1 pad_maximum_fusion.2
  44.8 4.8 %collective-permute-done = bf16[384,512]{1,0:T(8,128)(2,1)S(1)} collective-permute-done((bf16[384,512]{1,0:T(8,128)(2,1)S(1)}, bf16[384,512]{1,0:T(8,128)(2,1)S(1)}, u32[]{:S(2)}, u32[]{:S(2)}) %collective-permute-start) | collective-permute-done | bytes 393248 | tf_op jit(solution)/shard_map/ppermute | solution.py:165
  49.5 10.4 %collective-permute-done.2 = bf16[384,512]{1,0:T(8,128)(2,1)S(1)} collective-permute-done((bf16[384,512]{1,0:T(8,128)(2,1)S(1)}, bf16[384,512]{1,0:T(8,128)(2,1)S(1)}, u32[]{:S(2)}, u32[]{:S(2)}) %collective-permute-start.2) | collective-permute-done | bytes 393248 | tf_op jit(solution)/shard_map/ppermute | solution.py:165
  60.3 1.6 convolution_convert_fusion
  61.9 1.9 collective-permute-start.3
  64.5 2.0 collective-permute-done.3
  66.6 2.8 %add_convert_fusion = bf16[576,768]{1,0:T(8,128)(2,1)} fusion(bf16[576,768]{1,0:T(8,128)(2,1)} %collective-permute-done.3, bf16[576,512]{1,0:T(8,128)(2,1)S(1)} %bitcast.44, bf16[384,512]{1,0:T(8,128)(2,1)S(1)} %get-tuple-element.50, bf16[384,512]{1,0:T(8,128)(2,1)S(1)} %get-tuple-element.47), kind=kOutput, calls=%fused_computation.12 | convolution fusion | flops 456769536 | bytes 3145728 | tf_op jit(solution)/shard_map/dot_general | solution.py:13
  69.4 9.2 %all-to-all-start.1 = ((bf16[8,72,768]{2,1,0:T(8,128)(2,1)}), bf16[8,72,768]{2,1,0:T(8,128)(2,1)S(1)}, u32[]{:S(2)}, u32[]{:S(2)}) async-start(bf16[8,72,768]{2,1,0:T(8,128)(2,1)} %bitcast.11), calls=%async_computation.1 | async-start | bytes 1769472 | tf_op jit(solution)/shard_map/all_to_all | solution.py:124
  78.6 1.9 collective-permute-start.5
  80.5 5.1 %collective-permute-start.4 = (bf16[512,768]{1,0:T(8,128)(2,1)S(1)}, bf16[512,768]{1,0:T(8,128)(2,1)}, u32[]{:S(2)}, u32[]{:S(2)}) collective-permute-start(bf16[512,768]{1,0:T(8,128)(2,1)S(1)} %pad_maximum_fusion.2), channel_id=1, source_target_pairs={{0,8},{1,9},{2,10},{3,11},{4,12},{5,13},{6,14},{7,15},{8,16},{9,17... | collective-permute-start | bytes 2359304 | tf_op jit(solution)/shard_map/ppermute | solution.py:198
  85.7 18.4 %all-to-all-done.1 = bf16[8,72,768]{2,1,0:T(8,128)(2,1)S(1)} async-done(((bf16[8,72,768]{2,1,0:T(8,128)(2,1)}), bf16[8,72,768]{2,1,0:T(8,128)(2,1)S(1)}, u32[]{:S(2)}, u32[]{:S(2)}) %all-to-all-start.1) | async-done | bytes 884768 | tf_op jit(solution)/shard_map/all_to_all | solution.py:124
  104.2 1.0 broadcast_in_dim.5
  105.3 4.8 %all-to-all-start.2 = ((bf16[8,72,768]{2,1,0:T(8,128)(2,1)}), bf16[8,72,768]{2,1,0:T(8,128)(2,1)}, u32[]{:S(2)}, u32[]{:S(2)}) async-start(bf16[8,72,768]{2,1,0:T(8,128)(2,1)} %broadcast_in_dim.5), calls=%async_computation.2 | async-start | bytes 1769472 | tf_op jit(solution)/shard_map/all_to_all | solution.py:124
  110.1 5.7 %collective-permute-start.8 = (bf16[512,768]{1,0:T(8,128)(2,1)}, bf16[512,768]{1,0:T(8,128)(2,1)}, u32[]{:S(2)}, u32[]{:S(2)}) collective-permute-start(bf16[512,768]{1,0:T(8,128)(2,1)} %collective-permute-done.4), channel_id=1, source_target_pairs={{0,8},{1,9},{2,10},{3,11},{4,12},{5,13},{6,14},{7,15},{8,16},{9,17... | collective-permute-start | bytes 2359304 | tf_op jit(solution)/shard_map/ppermute | solution.py:212
  115.8 3.5 %fusion.2 = (bf16[8,2,72,768]{3,2,1,0:T(8,128)(2,1)S(1)}, bf16[8,2,72,768]{3,2,1,0:T(8,128)(2,1)S(1)}, bf16[8,2,72,768]{3,2,1,0:T(8,128)(2,1)S(1)}) fusion(bf16[8,2,72,1536]{3,2,1,0:T(8,128)(2,1)} %bitcast.39), kind=kLoop, calls=%fused_computation.7 | loop fusion | flops 13271040 | bytes 8847360 | tf_op jit(solution)/shard_map/convert_element_type | solution.py:33
  119.5 0.9 copy-done.8
  120.5 0.8 convolution_convert_fusion.3
  121.3 0.8 convolution_convert_fusion.2
  122.1 1.3 pad_maximum_fusion.1
  123.3 7.9 %collective-permute-done.8 = bf16[512,768]{1,0:T(8,128)(2,1)} collective-permute-done((bf16[512,768]{1,0:T(8,128)(2,1)}, bf16[512,768]{1,0:T(8,128)(2,1)}, u32[]{:S(2)}, u32[]{:S(2)}) %collective-permute-start.8) | collective-permute-done | bytes 786464 | tf_op jit(solution)/shard_map/ppermute | solution.py:212
  131.3 3.9 %all-to-all-done.2 = bf16[8,72,768]{2,1,0:T(8,128)(2,1)} async-done(((bf16[8,72,768]{2,1,0:T(8,128)(2,1)}), bf16[8,72,768]{2,1,0:T(8,128)(2,1)}, u32[]{:S(2)}, u32[]{:S(2)}) %all-to-all-start.2) | async-done | bytes 884768 | tf_op jit(solution)/shard_map/all_to_all | solution.py:124
  135.2 1.9 collective-permute-start.9
  137.2 2.6 %collective-permute-done.9.other_ref = bf16[576,768]{1,0:T(8,128)(2,1)} collective-permute-done((bf16[576,768]{1,0:T(8,128)(2,1)}, bf16[576,768]{1,0:T(8,128)(2,1)}, u32[]{:S(2)}, u32[]{:S(2)}) %collective-permute-start.9) | collective-permute-done | bytes 884768 | tf_op jit(solution)/shard_map/ppermute | solution.py:232
  139.8 1.3 copy-done.2
  141.1 7.8 %shard_map.102 = (bf16[512,768]{1,0:T(8,128)(2,1)S(1)}, bf16[512,768]{1,0:T(8,128)(2,1)}, bf16[512,768]{1,0:T(8,128)(2,1)}, bf16[512,768]{1,0:T(8,128)(2,1)}, bf16[576,3072]{1,0:T(8,128)(2,1)S(1)}) custom-call(s32[2]{0:T(128)S(1)} %pad_add_fusion.place_ref, bf16[576,768]{1,0:T(8,128)(2,1)} %bitcast.12.own_ref, ...), custom_call_target="tpu_custom_call" | custom-call | flops 1811939328 | bytes 14000000 | tf_op jit(solution)/shard_map/pallas_call | solution.py:98
  149.0 4.5 %collective-permute-start.10 = (bf16[512,768]{1,0:T(8,128)(2,1)}, bf16[512,768]{1,0:T(8,128)(2,1)S(1)}, u32[]{:S(2)}, u32[]{:S(2)}) collective-permute-start(bf16[512,768]{1,0:T(8,128)(2,1)} %get-tuple-element.38), channel_id=1, source_target_pairs={{0,8},{1,9},{2,10},{3,11},{4,12},{5,13},{6,14},{7,15},{8,16},{9,17... | collective-permute-start | bytes 2359304 | tf_op jit(solution)/shard_map/ppermute | solution.py:243
  153.5 1.9 collective-permute-start.11
  155.4 2.8 %collective-permute-start.12 = (bf16[512,768]{1,0:T(8,128)(2,1)}, bf16[512,768]{1,0:T(8,128)(2,1)}, u32[]{:S(2)}, u32[]{:S(2)}) collective-permute-start(bf16[512,768]{1,0:T(8,128)(2,1)} %get-tuple-element.40), channel_id=1, source_target_pairs={{0,24},{1,25},{2,26},{3,27},{4,28},{5,29},{6,30},{7,31},{8,0},{9,1... | collective-permute-start | bytes 2359304 | tf_op jit(solution)/shard_map/ppermute | solution.py:243
  158.2 1.8 fusion.11
  160.0 1.9 fusion.13
  163.1 1.5 fusion.9
  164.6 17.0 %reduce-scatter.2.cloned.1.call-done = bf16[1,384,512]{2,1,0:T(8,128)(2,1)} async-done(((bf16[4,384,512]{2,1,0:T(8,128)(2,1)}), bf16[1,384,512]{2,1,0:T(8,128)(2,1)}) %reduce-scatter.2.cloned.1.call-update) | async-done | bytes 393232 | tf_op jit(solution)/shard_map/reduce_scatter | solution.py:225
  181.5 7.8 %all-to-all-start.3 = ((bf16[8,72,512]{2,1,0:T(8,128)(2,1)}), bf16[8,72,512]{2,1,0:T(8,128)(2,1)S(1)}, u32[]{:S(2)}, u32[]{:S(2)}) async-start(bf16[8,72,512]{2,1,0:T(8,128)(2,1)} %bitcast.21), calls=%async_computation.4 | async-start | bytes 1179648 | tf_op jit(solution)/shard_map/all_to_all | solution.py:124
  189.4 6.1 %collective-permute-done.12 = bf16[512,768]{1,0:T(8,128)(2,1)} collective-permute-done((bf16[512,768]{1,0:T(8,128)(2,1)}, bf16[512,768]{1,0:T(8,128)(2,1)}, u32[]{:S(2)}, u32[]{:S(2)}) %collective-permute-start.12) | collective-permute-done | bytes 786464 | tf_op jit(solution)/shard_map/ppermute | solution.py:243
  195.5 1.6 multiply_convert_fusion
  197.1 1.0 fusion.27
  198.1 0.8 multiply_convert_fusion.1
  198.9 8.6 %all-to-all-done.3 = bf16[8,72,512]{2,1,0:T(8,128)(2,1)S(1)} async-done(((bf16[8,72,512]{2,1,0:T(8,128)(2,1)}), bf16[8,72,512]{2,1,0:T(8,128)(2,1)S(1)}, u32[]{:S(2)}, u32[]{:S(2)}) %all-to-all-start.3) | async-done | bytes 589856 | tf_op jit(solution)/shard_map/all_to_all | solution.py:124
  (52 shorter events, 4.2 us)
Async XLA Ops:
  7.2 17.3 %copy-start.12 = (bf16[72,512]{1,0:T(8,128)(2,1)S(1)}, bf16[72,512]{1,0:T(8,128)(2,1)}, u32[]{:S(2)}) copy-start(bf16[72,512]{1,0:T(8,128)(2,1)} %param.8) | copy-start | bytes 221188
  7.2 108.6 %all-gather.3.cloned.1.call-start = ((), (), s32[]{:S(2)}) async-start(), calls=%async_computation.5 | async-start | bytes 3760128 | tf_op jit(solution)/shard_map/all_gather | solution.py:192
  8.3 10.9 %collective-permute-start.6 = (bf16[72,768]{1,0:T(8,128)(2,1)S(1)}, bf16[72,768]{1,0:T(8,128)(2,1)S(1)}, u32[]{:S(2)}, u32[]{:S(2)}) collective-permute-start(bf16[72,768]{1,0:T(8,128)(2,1)S(1)} %get-tuple-element.55), channel_id=1, source_target_pairs={{0,0},{1,1},{2,2},{3,3},{4,4},{5,5},{6,6},{7,7},{8,64},{9,65},{10,... | collective-permute-start | bytes 331784 | tf_op jit(solution)/shard_map/ppermute | solution.py:181
  11.1 12.5 %collective-permute-start.7 = (bf16[72,768]{1,0:T(8,128)(2,1)S(1)}, bf16[72,768]{1,0:T(8,128)(2,1)S(1)}, u32[]{:S(2)}, u32[]{:S(2)}) collective-permute-start(bf16[72,768]{1,0:T(8,128)(2,1)S(1)} %get-tuple-element.56), channel_id=1, source_target_pairs={{0,64},{1,65},{2,66},{3,67},{4,68},{5,69},{6,70},{7,71},{8,0},{9,1... | collective-permute-start | bytes 331784 | tf_op jit(solution)/shard_map/ppermute | solution.py:181
  23.7 12.0 %copy-start.9 = (bf16[384,512]{1,0:T(8,128)(2,1)S(1)}, bf16[384,512]{1,0:T(8,128)(2,1)}, u32[]{:S(2)}) copy-start(bf16[384,512]{1,0:T(8,128)(2,1)} %param.13) | copy-start | bytes 1179652
  23.7 20.0 %copy-start.11 = (bf16[512,384]{1,0:T(8,128)(2,1)S(1)}, bf16[512,384]{1,0:T(8,128)(2,1)}, u32[]{:S(2)}) copy-start(bf16[512,384]{1,0:T(8,128)(2,1)} %param.12) | copy-start | bytes 1179652
  25.3 35.0 %all-to-all-start = ((bf16[8,72,512]{2,1,0:T(8,128)(2,1)}), bf16[8,72,512]{2,1,0:T(8,128)(2,1)S(1)}, u32[]{:S(2)}, u32[]{:S(2)}) async-start(bf16[8,72,512]{2,1,0:T(8,128)(2,1)} %broadcast_in_dim.4), calls=%async_computation | async-start | bytes 1179648 | tf_op jit(solution)/shard_map/all_to_all | solution.py:124
  35.6 13.9 %collective-permute-start = (bf16[384,512]{1,0:T(8,128)(2,1)S(1)}, bf16[384,512]{1,0:T(8,128)(2,1)S(1)}, u32[]{:S(2)}, u32[]{:S(2)}) collective-permute-start(bf16[384,512]{1,0:T(8,128)(2,1)S(1)} %copy-done.9), channel_id=1, source_target_pairs={{0,8},{1,9},{2,10},{3,11},{4,12},{5,13},{6,14},{7,15},{8,16},{9,17... | collective-permute-start | bytes 1179656 | tf_op jit(solution)/shard_map/ppermute | solution.py:165
  37.6 22.4 %collective-permute-start.2 = (bf16[384,512]{1,0:T(8,128)(2,1)S(1)}, bf16[384,512]{1,0:T(8,128)(2,1)S(1)}, u32[]{:S(2)}, u32[]{:S(2)}) collective-permute-start(bf16[384,512]{1,0:T(8,128)(2,1)S(1)} %copy-done.9), channel_id=1, source_target_pairs={{0,24},{1,25},{2,26},{3,27},{4,28},{5,29},{6,30},{7,31},{8,0},{9,1... | collective-permute-start | bytes 1179656 | tf_op jit(solution)/shard_map/ppermute | solution.py:165
  41.5 18.5 %collective-permute-start.1 = (bf16[384,512]{1,0:T(8,128)(2,1)S(1)}, bf16[384,512]{1,0:T(8,128)(2,1)S(1)}, u32[]{:S(2)}, u32[]{:S(2)}) collective-permute-start(bf16[384,512]{1,0:T(8,128)(2,1)S(1)} %copy-done.9), channel_id=1, source_target_pairs={{0,16},{1,17},{2,18},{3,19},{4,20},{5,21},{6,22},{7,23},{8,24},{9,... | collective-permute-start | bytes 1179656 | tf_op jit(solution)/shard_map/ppermute | solution.py:165
  44.8 35.8 %copy-start.3 = (bf16[512,768]{1,0:T(8,128)(2,1)}, bf16[512,768]{1,0:T(8,128)(2,1)S(1)}, u32[]{:S(2)}) copy-start(bf16[512,768]{1,0:T(8,128)(2,1)S(1)} %pad_maximum_fusion.2) | copy-start | bytes 2359300
  60.3 3.6 %copy-start.13 = (bf16[72,512]{1,0:T(8,128)(2,1)S(1)}, bf16[72,512]{1,0:T(8,128)(2,1)}, u32[]{:S(2)}) copy-start(bf16[72,512]{1,0:T(8,128)(2,1)} %param.7) | copy-start | bytes 221188
  60.3 6.3 %copy-start.7 = (bf16[8,72,512]{2,1,0:T(8,128)(2,1)}, bf16[8,72,512]{2,1,0:T(8,128)(2,1)S(1)}, u32[]{:S(2)}) copy-start(bf16[8,72,512]{2,1,0:T(8,128)(2,1)S(1)} %all-to-all-done) | copy-start | bytes 1769476
  61.9 4.7 %collective-permute-start.3 = (bf16[576,768]{1,0:T(8,128)(2,1)}, bf16[576,768]{1,0:T(8,128)(2,1)}, u32[]{:S(2)}, u32[]{:S(2)}) collective-permute-start(bf16[576,768]{1,0:T(8,128)(2,1)} %convolution_convert_fusion), channel_id=1, source_target_pairs={{0,32},{32,0},{64,96},{96,64},{128,160},{160,128},{192,224},{224,1... | collective-permute-start | bytes 2654216 | tf_op jit(solution)/shard_map/ppermute | solution.py:202
  69.4 34.7 %all-to-all-start.1 = ((bf16[8,72,768]{2,1,0:T(8,128)(2,1)}), bf16[8,72,768]{2,1,0:T(8,128)(2,1)S(1)}, u32[]{:S(2)}, u32[]{:S(2)}) async-start(bf16[8,72,768]{2,1,0:T(8,128)(2,1)} %bitcast.11), calls=%async_computation.1 | async-start | bytes 1769472 | tf_op jit(solution)/shard_map/all_to_all | solution.py:124
  78.6 58.6 %all-gather.5.cloned.1.call-start = ((), (), s32[]{:S(2)}) async-start(), calls=%async_computation.6 | async-start | bytes 1327104 | tf_op jit(solution)/shard_map/all_gather | solution.py:208
  78.6 25.6 %collective-permute-start.5 = (bf16[512,768]{1,0:T(8,128)(2,1)S(1)}, bf16[512,768]{1,0:T(8,128)(2,1)S(1)}, u32[]{:S(2)}, u32[]{:S(2)}) collective-permute-start(bf16[512,768]{1,0:T(8,128)(2,1)S(1)} %pad_maximum_fusion.2), channel_id=1, source_target_pairs={{0,24},{1,25},{2,26},{3,27},{4,28},{5,29},{6,30},{7,31},{8,0},{9,1... | collective-permute-start | bytes 2359304 | tf_op jit(solution)/shard_map/ppermute | solution.py:199
  80.5 23.7 %collective-permute-start.4 = (bf16[512,768]{1,0:T(8,128)(2,1)S(1)}, bf16[512,768]{1,0:T(8,128)(2,1)}, u32[]{:S(2)}, u32[]{:S(2)}) collective-permute-start(bf16[512,768]{1,0:T(8,128)(2,1)S(1)} %pad_maximum_fusion.2), channel_id=1, source_target_pairs={{0,8},{1,9},{2,10},{3,11},{4,12},{5,13},{6,14},{7,15},{8,16},{9,17... | collective-permute-start | bytes 2359304 | tf_op jit(solution)/shard_map/ppermute | solution.py:198
  104.2 11.6 %copy-start.5 = (bf16[512,768]{1,0:T(8,128)(2,1)}, bf16[512,768]{1,0:T(8,128)(2,1)S(1)}, u32[]{:S(2)}) copy-start(bf16[512,768]{1,0:T(8,128)(2,1)S(1)} %collective-permute-done.5) | copy-start | bytes 2359300
  105.3 29.9 %all-to-all-start.2 = ((bf16[8,72,768]{2,1,0:T(8,128)(2,1)}), bf16[8,72,768]{2,1,0:T(8,128)(2,1)}, u32[]{:S(2)}, u32[]{:S(2)}) async-start(bf16[8,72,768]{2,1,0:T(8,128)(2,1)} %broadcast_in_dim.5), calls=%async_computation.2 | async-start | bytes 1769472 | tf_op jit(solution)/shard_map/all_to_all | solution.py:124
  110.0 71.5 %reduce-scatter.2.cloned.1.call-start = ((), (), s32[]{:S(2)}) async-start(), calls=%async_computation.7 | async-start | bytes 1966080 | tf_op jit(solution)/shard_map/reduce_scatter | solution.py:225
  110.1 21.1 %collective-permute-start.8 = (bf16[512,768]{1,0:T(8,128)(2,1)}, bf16[512,768]{1,0:T(8,128)(2,1)}, u32[]{:S(2)}, u32[]{:S(2)}) collective-permute-start(bf16[512,768]{1,0:T(8,128)(2,1)} %collective-permute-done.4), channel_id=1, source_target_pairs={{0,8},{1,9},{2,10},{3,11},{4,12},{5,13},{6,14},{7,15},{8,16},{9,17... | collective-permute-start | bytes 2359304 | tf_op jit(solution)/shard_map/ppermute | solution.py:212
  119.4 1.1 copy-start.8
  135.2 4.7 %collective-permute-start.9 = (bf16[576,768]{1,0:T(8,128)(2,1)}, bf16[576,768]{1,0:T(8,128)(2,1)}, u32[]{:S(2)}, u32[]{:S(2)}) collective-permute-start(bf16[576,768]{1,0:T(8,128)(2,1)} %bitcast.12.own_ref), channel_id=1, source_target_pairs={{0,32},{32,0},{64,96},{96,64},{128,160},{160,128},{192,224},{224,1... | collective-permute-start | bytes 2654216 | tf_op jit(solution)/shard_map/ppermute | solution.py:232
  139.8 1.3 copy-start.2
  148.9 12.9 %copy-start = (bf16[512,768]{1,0:T(8,128)(2,1)}, bf16[512,768]{1,0:T(8,128)(2,1)S(1)}, u32[]{:S(2)}) copy-start(bf16[512,768]{1,0:T(8,128)(2,1)S(1)} %get-tuple-element.37) | copy-start | bytes 2359300
  149.0 40.4 %collective-permute-start.10 = (bf16[512,768]{1,0:T(8,128)(2,1)}, bf16[512,768]{1,0:T(8,128)(2,1)S(1)}, u32[]{:S(2)}, u32[]{:S(2)}) collective-permute-start(bf16[512,768]{1,0:T(8,128)(2,1)} %get-tuple-element.38), channel_id=1, source_target_pairs={{0,8},{1,9},{2,10},{3,11},{4,12},{5,13},{6,14},{7,15},{8,16},{9,17... | collective-permute-start | bytes 2359304 | tf_op jit(solution)/shard_map/ppermute | solution.py:243
  153.5 35.8 %collective-permute-start.11 = (bf16[512,768]{1,0:T(8,128)(2,1)}, bf16[512,768]{1,0:T(8,128)(2,1)S(1)}, u32[]{:S(2)}, u32[]{:S(2)}) collective-permute-start(bf16[512,768]{1,0:T(8,128)(2,1)} %get-tuple-element.39), channel_id=1, source_target_pairs={{0,16},{1,17},{2,18},{3,19},{4,20},{5,21},{6,22},{7,23},{8,24},{9,... | collective-permute-start | bytes 2359304 | tf_op jit(solution)/shard_map/ppermute | solution.py:243
  155.4 40.0 %collective-permute-start.12 = (bf16[512,768]{1,0:T(8,128)(2,1)}, bf16[512,768]{1,0:T(8,128)(2,1)}, u32[]{:S(2)}, u32[]{:S(2)}) collective-permute-start(bf16[512,768]{1,0:T(8,128)(2,1)} %get-tuple-element.40), channel_id=1, source_target_pairs={{0,24},{1,25},{2,26},{3,27},{4,28},{5,29},{6,30},{7,31},{8,0},{9,1... | collective-permute-start | bytes 2359304 | tf_op jit(solution)/shard_map/ppermute | solution.py:243
  160.0 1.9 copy-start.6
  161.9 1.1 copy-start.4
  164.6 30.9 %copy-start.1 = (bf16[512,768]{1,0:T(8,128)(2,1)S(1)}, bf16[512,768]{1,0:T(8,128)(2,1)}, u32[]{:S(2)}) copy-start(bf16[512,768]{1,0:T(8,128)(2,1)} %copy-done) | copy-start | bytes 2359300
  181.5 26.0 %all-to-all-start.3 = ((bf16[8,72,512]{2,1,0:T(8,128)(2,1)}), bf16[8,72,512]{2,1,0:T(8,128)(2,1)S(1)}, u32[]{:S(2)}, u32[]{:S(2)}) async-start(bf16[8,72,512]{2,1,0:T(8,128)(2,1)} %bitcast.21), calls=%async_computation.4 | async-start | bytes 1179648 | tf_op jit(solution)/shard_map/all_to_all | solution.py:124
  197.1 1.0 copy-start.10
Sparse Core Ops, SparseCore 0:
  24.6 48.2 all-gather.2
  85.8 43.2 all-gather.4
  132.0 49.5 reduce-scatter.1

commit v12 on v11

--- a/solution.py
+++ b/solution.py
@@ -193,6 +193,10 @@
         n_y, N_CORE, block, 2 * half
     )
 
+    both = jnp.concatenate([tokens, out_grad], axis=1)
+    both, saved_share = lax.optimization_barrier((both, saved_share))
+    both_rows = lax.all_gather(both, "col", axis=0, tiled=True, axis_index_groups=z_groups)
+
     w_both = jnp.concatenate([w_gate, w_up], axis=1)
     w_both, grad_rows = lax.optimization_barrier((w_both, grad_rows))
     w_left = lax.ppermute(w_both, "col", x_shift(1))
@@ -203,9 +207,6 @@
     keep = contract_last(grad_rows, down_half(0)).astype(jnp.bfloat16)
     pair = (keep.astype(jnp.float32) + got.astype(jnp.float32)).astype(jnp.bfloat16)
 
-    both = jnp.concatenate([tokens, out_grad], axis=1)
-    both, pair = lax.optimization_barrier((both, pair))
-    both_rows = lax.all_gather(both, "col", axis=0, tiled=True, axis_index_groups=z_groups)
     terms = exchange(pair.reshape(n_y, block, half), "row", y_groups)
     share = jnp.sum(terms.astype(jnp.float32), axis=0).astype(jnp.bfloat16)
     share, w_left, w_right = lax.optimization_barrier((share, w_left, w_right))
@@ -220,19 +221,19 @@
         for side in range(2)
     ]
     down_part = jnp.concatenate(down_part, axis=0).reshape(n_x, units, features)
-    down_part, w_far = lax.optimization_barrier((down_part, w_far))
-    weights = [w_both, w_right, w_far, w_left]
     down_sum = lax.psum_scatter(
         down_part, "col", scatter_dimension=0, tiled=True, axis_index_groups=x_groups
     )[0]
-    own, gate_factor, up_factor, _ = lax.optimization_barrier(
-        (own, gate_factor, up_factor, down_part)
-    )
+    own, gate_factor, up_factor, w_far, _ = lax.optimization_barrier(
+        (own, gate_factor, up_factor, w_far, down_part)
+    )
+    weights = [w_both, w_right, w_far, w_left]
 
     other = lax.ppermute(own, "row", core_swap)
     *unit_parts, unit_grads = unit_blocks(
         jnp.stack([core, x_here]), own, other, gate_factor, up_factor, both_rows, n_x
     )
+    unit_grads, down_sum = lax.optimization_barrier((unit_grads, down_sum))
     part_in = 0.0
     for step, weight in enumerate(weights):
         columns = slice(2 * step * units, 2 * (step + 1) * units)
@@ -244,7 +245,6 @@
         unit_sum = unit_sum + moved_part.astype(jnp.float32)
     unit_wgrad = (unit_sum * grad_scale).astype(jnp.bfloat16)
     gate_wgrad, up_wgrad = unit_wgrad[:, :units], unit_wgrad[:, units:]
-    part_in, down_sum = lax.optimization_barrier((part_in, down_sum))
     down_wgrad = (down_sum.astype(jnp.float32) * grad_scale).astype(jnp.bfloat16)
     token_terms = exchange(
         part_in.reshape(N_Z, block, features), "col", z_groups

time: 219 us -> 217 us (level)
  local copies, waits for them, and re-layouts: 5.94 us -> 14.9 us
  starting transfers between devices: 72.6 us -> 65.1 us
  waiting for transfers between devices: 90.6 us -> 87.9 us
    reduce_scatter x1, waiting for transfers between devices: 17 us -> 0.02 us  [local(): lax.psum_scatter(down_part, 'col', scatter_dimension=0, tiled=True, axis_...]
    ppermute x1, waiting for transfers between devices: 7.88 us -> 24.1 us  [local(): w_far = lax.ppermute(w_left, 'col', x_shift(1))]
    ppermute x3, waiting for transfers between devices: 6.12 us -> 21.7 us  [local(): moved_part = lax.ppermute(unit_parts[step], 'col', x_shift(step))]
    all_to_all x4, waiting for transfers between devices: 30.9 us -> 16.5 us  [exchange(): lax.all_to_all(pieces, axis, 0, 0, tiled=True, axis_index_groups=groups)]
    unnamed x28 -> x42, local copies, waits for them, and re-layouts: 2.79 us -> 10.8 us
    ppermute x1, starting transfers between devices: 5.71 us -> 2.2 us  [local(): w_far = lax.ppermute(w_left, 'col', x_shift(1))]
    all_to_all x4, starting transfers between devices: 32.1 us -> 29.6 us  [exchange(): lax.all_to_all(pieces, axis, 0, 0, tiled=True, axis_index_groups=groups)]
  transfers between devices with their start and end apart: 20 -> 20, of which waited for: 12 -> 10; matrix products, arithmetic and copies ran while one was open for 11% -> 13% of each run, Pallas kernels for 4% -> 3%
where the time goes in v12:
time: 217 us; the launch traced here: 215 us
  waiting for transfers between devices  87.9 us (41%)
  starting transfers between devices  65.1 us (30%)
  local copies, waits for them, and re-layouts  14.9 us (7%)
  between operations  14.3 us (7%)
  other arithmetic  13.4 us (6%)
  matrix products  12 us (6%)
  Pallas kernels  7.34 us (3%)
    all_to_all x4, starting transfers between devices, exchange(): lax.all_to_all(pieces, axis, 0, 0, tiled=True, axis_index_groups=groups)  29.6 us
    ppermute x1, waiting for transfers between devices, local(): w_far = lax.ppermute(w_left, 'col', x_shift(1))  24.1 us
    ppermute x3, waiting for transfers between devices, local(): moved_part = lax.ppermute(unit_parts[step], 'col', x_shift(step))  21.7 us
    all_to_all x4, waiting for transfers between devices, exchange(): lax.all_to_all(pieces, axis, 0, 0, tiled=True, axis_index_groups=groups)  16.5 us
    ppermute x3, waiting for transfers between devices, local(): lax.ppermute(w_down, 'col', x_shift(step))  15.2 us
    unnamed x42, local copies, waits for them, and re-layouts  10.8 us
    dot_general x6, matrix products, contract_last(): lax.dot_general(left_side, right_side, (((1,), (1,)), ((), ())), preferre...  10.4 us
    ppermute x2, waiting for transfers between devices, local(): lax.ppermute(pick(saved_pieces, lax.rem(x_here + turn, 2)), ('row', 'col'...  8.74 us
  transfers between devices with their start and end apart: 20, of which 10 were waited for; matrix products, arithmetic and copies ran while one was open for 13% of the time, Pallas kernels for 3%

profile of v12, /device:TPU:6, one launch (start us, length us, event | category | flops | bytes accessed | tf_op | source)
XLA Modules:
  0.0 214.8 jit_solution(3179077234403693940)
XLA Ops:
  7.3 1.0 pad_maximum_fusion.3
  8.3 2.8 %collective-permute-start.6 = (bf16[72,768]{1,0:T(8,128)(2,1)S(1)}, bf16[72,768]{1,0:T(8,128)(2,1)S(1)}, u32[]{:S(2)}, u32[]{:S(2)}) collective-permute-start(bf16[72,768]{1,0:T(8,128)(2,1)S(1)} %get-tuple-element.51), channel_id=1, source_target_pairs={{0,0},{1,1},{2,2},{3,3},{4,4},{5,5},{6,6},{7,7},{8,64},{9,65},{10,... | collective-permute-start | bytes 331784 | tf_op jit(solution)/shard_map/ppermute | solution.py:181
  11.1 3.8 %collective-permute-start.7 = (bf16[72,768]{1,0:T(8,128)(2,1)S(1)}, bf16[72,768]{1,0:T(8,128)(2,1)S(1)}, u32[]{:S(2)}, u32[]{:S(2)}) collective-permute-start(bf16[72,768]{1,0:T(8,128)(2,1)S(1)} %get-tuple-element.52), channel_id=1, source_target_pairs={{0,64},{1,65},{2,66},{3,67},{4,68},{5,69},{6,70},{7,71},{8,0},{9,1... | collective-permute-start | bytes 331784 | tf_op jit(solution)/shard_map/ppermute | solution.py:181
  14.9 4.2 %collective-permute-done.6 = bf16[72,768]{1,0:T(8,128)(2,1)S(1)} collective-permute-done((bf16[72,768]{1,0:T(8,128)(2,1)S(1)}, bf16[72,768]{1,0:T(8,128)(2,1)S(1)}, u32[]{:S(2)}, u32[]{:S(2)}) %collective-permute-start.6) | collective-permute-done | bytes 110624 | tf_op jit(solution)/shard_map/ppermute | solution.py:181
  19.1 4.5 %collective-permute-done.7 = bf16[72,768]{1,0:T(8,128)(2,1)S(1)} collective-permute-done((bf16[72,768]{1,0:T(8,128)(2,1)S(1)}, bf16[72,768]{1,0:T(8,128)(2,1)S(1)}, u32[]{:S(2)}, u32[]{:S(2)}) %collective-permute-start.7) | collective-permute-done | bytes 110624 | tf_op jit(solution)/shard_map/ppermute | solution.py:181
  25.3 10.3 %all-to-all-start = ((bf16[8,72,512]{2,1,0:T(8,128)(2,1)}), bf16[8,72,512]{2,1,0:T(8,128)(2,1)S(1)}, u32[]{:S(2)}, u32[]{:S(2)}) async-start(bf16[8,72,512]{2,1,0:T(8,128)(2,1)} %broadcast_in_dim.4), calls=%async_computation | async-start | bytes 1179648 | tf_op jit(solution)/shard_map/all_to_all | solution.py:124
  35.7 1.9 collective-permute-start
  37.6 3.9 %collective-permute-start.2 = (bf16[384,512]{1,0:T(8,128)(2,1)S(1)}, bf16[384,512]{1,0:T(8,128)(2,1)S(1)}, u32[]{:S(2)}, u32[]{:S(2)}) collective-permute-start(bf16[384,512]{1,0:T(8,128)(2,1)S(1)} %copy-done.16), channel_id=1, source_target_pairs={{0,24},{1,25},{2,26},{3,27},{4,28},{5,29},{6,30},{7,31},{8,0},{9,1... | collective-permute-start | bytes 1179656 | tf_op jit(solution)/shard_map/ppermute | solution.py:165
  41.5 2.1 collective-permute-start.1
  43.7 1.1 pad_maximum_fusion.2
  44.8 4.8 %collective-permute-done = bf16[384,512]{1,0:T(8,128)(2,1)S(1)} collective-permute-done((bf16[384,512]{1,0:T(8,128)(2,1)S(1)}, bf16[384,512]{1,0:T(8,128)(2,1)S(1)}, u32[]{:S(2)}, u32[]{:S(2)}) %collective-permute-start) | collective-permute-done | bytes 393248 | tf_op jit(solution)/shard_map/ppermute | solution.py:165
  49.6 10.4 %collective-permute-done.2 = bf16[384,512]{1,0:T(8,128)(2,1)S(1)} collective-permute-done((bf16[384,512]{1,0:T(8,128)(2,1)S(1)}, bf16[384,512]{1,0:T(8,128)(2,1)S(1)}, u32[]{:S(2)}, u32[]{:S(2)}) %collective-permute-start.2) | collective-permute-done | bytes 393248 | tf_op jit(solution)/shard_map/ppermute | solution.py:165
  60.2 1.0 dynamic-slice_bitcast_fusion.3
  61.2 1.6 convolution_convert_fusion
  62.8 1.9 collective-permute-start.3
  65.4 1.9 collective-permute-start.5
  67.4 5.1 %collective-permute-start.4 = (bf16[512,768]{1,0:T(8,128)(2,1)S(1)}, bf16[512,768]{1,0:T(8,128)(2,1)S(1)}, u32[]{:S(2)}, u32[]{:S(2)}) collective-permute-start(bf16[512,768]{1,0:T(8,128)(2,1)S(1)} %pad_maximum_fusion.2), channel_id=1, source_target_pairs={{0,8},{1,9},{2,10},{3,11},{4,12},{5,13},{6,14},{7,15},{8,16},{9,17... | collective-permute-start | bytes 2359304 | tf_op jit(solution)/shard_map/ppermute | solution.py:202
  72.5 3.0 %add_convert_fusion = bf16[576,768]{1,0:T(8,128)(2,1)} fusion(bf16[576,768]{1,0:T(8,128)(2,1)} %collective-permute-done.3, bf16[576,512]{1,0:T(8,128)(2,1)S(1)} %bitcast.47, bf16[384,512]{1,0:T(8,128)(2,1)} %get-tuple-element.46, bf16[384,512]{1,0:T(8,128)(2,1)} %get-tuple-element.43), kind=kOutput, calls=%fused_computation.12 | convolution fusion | flops 456769536 | bytes 3145728 | tf_op jit(solution)/shard_map/dot_general | solution.py:13
  75.5 9.2 %all-to-all-start.1 = ((bf16[8,72,768]{2,1,0:T(8,128)(2,1)}), bf16[8,72,768]{2,1,0:T(8,128)(2,1)S(1)}, u32[]{:S(2)}, u32[]{:S(2)}) async-start(bf16[8,72,768]{2,1,0:T(8,128)(2,1)} %bitcast.11), calls=%async_computation.1 | async-start | bytes 1769472 | tf_op jit(solution)/shard_map/all_to_all | solution.py:124
  84.8 4.7 %fusion.2 = (bf16[8,2,72,768]{3,2,1,0:T(8,128)(2,1)S(1)}, bf16[8,2,72,768]{3,2,1,0:T(8,128)(2,1)}, bf16[8,2,72,768]{3,2,1,0:T(8,128)(2,1)}) fusion(bf16[8,2,72,1536]{3,2,1,0:T(8,128)(2,1)} %bitcast.41), kind=kLoop, calls=%fused_computation.7 | loop fusion | flops 13271040 | bytes 8847360 | tf_op jit(solution)/shard_map/convert_element_type | solution.py:33
  89.7 0.9 copy-done.15
  92.2 1.3 pad_maximum_fusion.1
  93.5 16.5 %all-to-all-done.1 = bf16[8,72,768]{2,1,0:T(8,128)(2,1)S(1)} async-done(((bf16[8,72,768]{2,1,0:T(8,128)(2,1)}), bf16[8,72,768]{2,1,0:T(8,128)(2,1)S(1)}, u32[]{:S(2)}, u32[]{:S(2)}) %all-to-all-start.1) | async-done | bytes 884768 | tf_op jit(solution)/shard_map/all_to_all | solution.py:124
  110.2 1.1 broadcast_in_dim.5
  111.3 3.5 %all-to-all-start.2 = ((bf16[8,72,768]{2,1,0:T(8,128)(2,1)}), bf16[8,72,768]{2,1,0:T(8,128)(2,1)S(1)}, u32[]{:S(2)}, u32[]{:S(2)}) async-start(bf16[8,72,768]{2,1,0:T(8,128)(2,1)} %broadcast_in_dim.5), calls=%async_computation.2 | async-start | bytes 1769472 | tf_op jit(solution)/shard_map/all_to_all | solution.py:124
  114.9 2.2 %collective-permute-start.8 = (bf16[512,768]{1,0:T(8,128)(2,1)S(1)}, bf16[512,768]{1,0:T(8,128)(2,1)}, u32[]{:S(2)}, u32[]{:S(2)}) collective-permute-start(bf16[512,768]{1,0:T(8,128)(2,1)S(1)} %collective-permute-done.4), channel_id=1, source_target_pairs={{0,8},{1,9},{2,10},{3,11},{4,12},{5,13},{6,14},{7,15},{8,16},{9,17... | collective-permute-start | bytes 2359304 | tf_op jit(solution)/shard_map/ppermute | solution.py:213
  117.1 24.1 %collective-permute-done.8 = bf16[512,768]{1,0:T(8,128)(2,1)} collective-permute-done((bf16[512,768]{1,0:T(8,128)(2,1)S(1)}, bf16[512,768]{1,0:T(8,128)(2,1)}, u32[]{:S(2)}, u32[]{:S(2)}) %collective-permute-start.8) | collective-permute-done | bytes 786464 | tf_op jit(solution)/shard_map/ppermute | solution.py:213
  141.2 1.9 collective-permute-start.9
  143.2 0.9 copy-done.2
  144.1 1.4 collective-permute-done.9.other_ref
  145.5 0.9 copy-done.7
  146.5 1.5 copy-done
  148.0 1.5 copy-done.1
  149.5 1.2 copy-done.3
  150.6 1.3 copy-done.6
  151.9 1.2 copy-done.8
  153.1 7.3 %shard_map.102 = (bf16[512,768]{1,0:T(8,128)(2,1)S(1)}, bf16[512,768]{1,0:T(8,128)(2,1)}, bf16[512,768]{1,0:T(8,128)(2,1)}, bf16[512,768]{1,0:T(8,128)(2,1)}, bf16[576,3072]{1,0:T(8,128)(2,1)S(1)}) custom-call(s32[2]{0:T(128)S(1)} %pad_add_fusion.place_ref, bf16[576,768]{1,0:T(8,128)(2,1)S(1)} %bitcast.39, bf16[576,768]{1,0:T(8,128)(2,1)S(1)} %copy-done.8, ...), custom_call_target="tpu_custom_call" | custom-call | flops 1811939328 | bytes 14000000 | tf_op jit(solution)/shard_map/pallas_call | solution.py:98
  161.3 2.5 %collective-permute-start.10 = (bf16[512,768]{1,0:T(8,128)(2,1)}, bf16[512,768]{1,0:T(8,128)(2,1)}, u32[]{:S(2)}, u32[]{:S(2)}) collective-permute-start(bf16[512,768]{1,0:T(8,128)(2,1)} %get-tuple-element.34), channel_id=1, source_target_pairs={{0,8},{1,9},{2,10},{3,11},{4,12},{5,13},{6,14},{7,15},{8,16},{9,17... | collective-permute-start | bytes 2359304 | tf_op jit(solution)/shard_map/ppermute | solution.py:244
  163.8 2.8 %collective-permute-start.11 = (bf16[512,768]{1,0:T(8,128)(2,1)}, bf16[512,768]{1,0:T(8,128)(2,1)}, u32[]{:S(2)}, u32[]{:S(2)}) collective-permute-start(bf16[512,768]{1,0:T(8,128)(2,1)} %get-tuple-element.35), channel_id=1, source_target_pairs={{0,16},{1,17},{2,18},{3,19},{4,20},{5,21},{6,22},{7,23},{8,24},{9,... | collective-permute-start | bytes 2359304 | tf_op jit(solution)/shard_map/ppermute | solution.py:244
  166.6 2.4 %collective-permute-start.12 = (bf16[512,768]{1,0:T(8,128)(2,1)}, bf16[512,768]{1,0:T(8,128)(2,1)}, u32[]{:S(2)}, u32[]{:S(2)}) collective-permute-start(bf16[512,768]{1,0:T(8,128)(2,1)} %get-tuple-element.36), channel_id=1, source_target_pairs={{0,24},{1,25},{2,26},{3,27},{4,28},{5,29},{6,30},{7,31},{8,0},{9,1... | collective-permute-start | bytes 2359304 | tf_op jit(solution)/shard_map/ppermute | solution.py:244
  169.1 1.9 fusion.14
  172.8 2.6 %fusion.8 = bf16[576,512]{1,0:T(8,128)(2,1)} fusion(f32[576,512]{1,0:T(8,128)S(1)} %fusion.10, f32[576,512]{1,0:T(8,128)S(1)} %convolution_add_fusion.1, bf16[512,768]{1,0:T(8,128)(2,1)} %collective-permute-done.8, bf16[576,3072]{1,0:T(8,128)(2,1)S(1)} %get-tuple-element.30), kind=kOutput, calls=%fused_computation.23 | convolution fusion | flops 453869568 | bytes 4620288 | tf_op jit(solution)/shard_map/dot_general | solution.py:13
  175.4 6.5 %all-to-all-start.3 = ((bf16[8,72,512]{2,1,0:T(8,128)(2,1)}), bf16[8,72,512]{2,1,0:T(8,128)(2,1)S(1)}, u32[]{:S(2)}, u32[]{:S(2)}) async-start(bf16[8,72,512]{2,1,0:T(8,128)(2,1)} %bitcast.42), calls=%async_computation.4 | async-start | bytes 1179648 | tf_op jit(solution)/shard_map/all_to_all | solution.py:124
  182.0 1.9 collective-permute-done.10
  183.9 4.1 %collective-permute-done.11 = bf16[512,768]{1,0:T(8,128)(2,1)} collective-permute-done((bf16[512,768]{1,0:T(8,128)(2,1)}, bf16[512,768]{1,0:T(8,128)(2,1)}, u32[]{:S(2)}, u32[]{:S(2)}) %collective-permute-start.11) | collective-permute-done | bytes 786464 | tf_op jit(solution)/shard_map/ppermute | solution.py:244
  188.0 15.7 %collective-permute-done.12 = bf16[512,768]{1,0:T(8,128)(2,1)} collective-permute-done((bf16[512,768]{1,0:T(8,128)(2,1)}, bf16[512,768]{1,0:T(8,128)(2,1)}, u32[]{:S(2)}, u32[]{:S(2)}) %collective-permute-start.12) | collective-permute-done | bytes 786464 | tf_op jit(solution)/shard_map/ppermute | solution.py:244
  203.7 2.0 multiply_convert_fusion
  205.8 1.0 fusion.25
  (66 shorter events, 8.9 us)
Async XLA Ops:
  7.2 17.3 %copy-start.19 = (bf16[72,512]{1,0:T(8,128)(2,1)S(1)}, bf16[72,512]{1,0:T(8,128)(2,1)}, u32[]{:S(2)}) copy-start(bf16[72,512]{1,0:T(8,128)(2,1)} %param.8) | copy-start | bytes 221188
  7.2 77.6 %all-gather.3.cloned.1.call-start = ((), (), s32[]{:S(2)}) async-start(), calls=%async_computation.5 | async-start | bytes 3760128 | tf_op jit(solution)/shard_map/all_gather | solution.py:192
  8.3 10.9 %collective-permute-start.6 = (bf16[72,768]{1,0:T(8,128)(2,1)S(1)}, bf16[72,768]{1,0:T(8,128)(2,1)S(1)}, u32[]{:S(2)}, u32[]{:S(2)}) collective-permute-start(bf16[72,768]{1,0:T(8,128)(2,1)S(1)} %get-tuple-element.51), channel_id=1, source_target_pairs={{0,0},{1,1},{2,2},{3,3},{4,4},{5,5},{6,6},{7,7},{8,64},{9,65},{10,... | collective-permute-start | bytes 331784 | tf_op jit(solution)/shard_map/ppermute | solution.py:181
  11.1 12.5 %collective-permute-start.7 = (bf16[72,768]{1,0:T(8,128)(2,1)S(1)}, bf16[72,768]{1,0:T(8,128)(2,1)S(1)}, u32[]{:S(2)}, u32[]{:S(2)}) collective-permute-start(bf16[72,768]{1,0:T(8,128)(2,1)S(1)} %get-tuple-element.52), channel_id=1, source_target_pairs={{0,64},{1,65},{2,66},{3,67},{4,68},{5,69},{6,70},{7,71},{8,0},{9,1... | collective-permute-start | bytes 331784 | tf_op jit(solution)/shard_map/ppermute | solution.py:181
  23.7 12.0 %copy-start.16 = (bf16[384,512]{1,0:T(8,128)(2,1)S(1)}, bf16[384,512]{1,0:T(8,128)(2,1)}, u32[]{:S(2)}) copy-start(bf16[384,512]{1,0:T(8,128)(2,1)} %param.13) | copy-start | bytes 1179652
  23.7 20.1 %copy-start.18 = (bf16[512,384]{1,0:T(8,128)(2,1)S(1)}, bf16[512,384]{1,0:T(8,128)(2,1)}, u32[]{:S(2)}) copy-start(bf16[512,384]{1,0:T(8,128)(2,1)} %param.12) | copy-start | bytes 1179652
  25.3 35.9 %all-to-all-start = ((bf16[8,72,512]{2,1,0:T(8,128)(2,1)}), bf16[8,72,512]{2,1,0:T(8,128)(2,1)S(1)}, u32[]{:S(2)}, u32[]{:S(2)}) async-start(bf16[8,72,512]{2,1,0:T(8,128)(2,1)} %broadcast_in_dim.4), calls=%async_computation | async-start | bytes 1179648 | tf_op jit(solution)/shard_map/all_to_all | solution.py:124
  35.6 108.5 %all-gather.5.cloned.1.call-start = ((), (), s32[]{:S(2)}) async-start(), calls=%async_computation.6 | async-start | bytes 1327104 | tf_op jit(solution)/shard_map/all_gather | solution.py:198
  35.7 13.9 %collective-permute-start = (bf16[384,512]{1,0:T(8,128)(2,1)S(1)}, bf16[384,512]{1,0:T(8,128)(2,1)S(1)}, u32[]{:S(2)}, u32[]{:S(2)}) collective-permute-start(bf16[384,512]{1,0:T(8,128)(2,1)S(1)} %copy-done.16), channel_id=1, source_target_pairs={{0,8},{1,9},{2,10},{3,11},{4,12},{5,13},{6,14},{7,15},{8,16},{9,17... | collective-permute-start | bytes 1179656 | tf_op jit(solution)/shard_map/ppermute | solution.py:165
  37.6 22.4 %collective-permute-start.2 = (bf16[384,512]{1,0:T(8,128)(2,1)S(1)}, bf16[384,512]{1,0:T(8,128)(2,1)S(1)}, u32[]{:S(2)}, u32[]{:S(2)}) collective-permute-start(bf16[384,512]{1,0:T(8,128)(2,1)S(1)} %copy-done.16), channel_id=1, source_target_pairs={{0,24},{1,25},{2,26},{3,27},{4,28},{5,29},{6,30},{7,31},{8,0},{9,1... | collective-permute-start | bytes 1179656 | tf_op jit(solution)/shard_map/ppermute | solution.py:165
  41.5 18.5 %collective-permute-start.1 = (bf16[384,512]{1,0:T(8,128)(2,1)S(1)}, bf16[384,512]{1,0:T(8,128)(2,1)S(1)}, u32[]{:S(2)}, u32[]{:S(2)}) collective-permute-start(bf16[384,512]{1,0:T(8,128)(2,1)S(1)} %copy-done.16), channel_id=1, source_target_pairs={{0,16},{1,17},{2,18},{3,19},{4,20},{5,21},{6,22},{7,23},{8,24},{9,... | collective-permute-start | bytes 1179656 | tf_op jit(solution)/shard_map/ppermute | solution.py:165
  44.8 22.6 %copy-start.9 = (bf16[512,768]{1,0:T(8,128)(2,1)}, bf16[512,768]{1,0:T(8,128)(2,1)S(1)}, u32[]{:S(2)}) copy-start(bf16[512,768]{1,0:T(8,128)(2,1)S(1)} %pad_maximum_fusion.2) | copy-start | bytes 2359300
  61.2 3.5 %copy-start.20 = (bf16[72,512]{1,0:T(8,128)(2,1)S(1)}, bf16[72,512]{1,0:T(8,128)(2,1)}, u32[]{:S(2)}) copy-start(bf16[72,512]{1,0:T(8,128)(2,1)} %param.7) | copy-start | bytes 221188
  61.2 11.3 %copy-start.14 = (bf16[8,72,512]{2,1,0:T(8,128)(2,1)}, bf16[8,72,512]{2,1,0:T(8,128)(2,1)S(1)}, u32[]{:S(2)}) copy-start(bf16[8,72,512]{2,1,0:T(8,128)(2,1)S(1)} %all-to-all-done) | copy-start | bytes 1769476
  62.8 9.7 %collective-permute-start.3 = (bf16[576,768]{1,0:T(8,128)(2,1)}, bf16[576,768]{1,0:T(8,128)(2,1)}, u32[]{:S(2)}, u32[]{:S(2)}) collective-permute-start(bf16[576,768]{1,0:T(8,128)(2,1)} %convolution_convert_fusion), channel_id=1, source_target_pairs={{0,32},{32,0},{64,96},{96,64},{128,160},{160,128},{192,224},{224,1... | collective-permute-start | bytes 2654216 | tf_op jit(solution)/shard_map/ppermute | solution.py:206
  65.4 44.8 %collective-permute-start.5 = (bf16[512,768]{1,0:T(8,128)(2,1)S(1)}, bf16[512,768]{1,0:T(8,128)(2,1)S(1)}, u32[]{:S(2)}, u32[]{:S(2)}) collective-permute-start(bf16[512,768]{1,0:T(8,128)(2,1)S(1)} %pad_maximum_fusion.2), channel_id=1, source_target_pairs={{0,24},{1,25},{2,26},{3,27},{4,28},{5,29},{6,30},{7,31},{8,0},{9,1... | collective-permute-start | bytes 2359304 | tf_op jit(solution)/shard_map/ppermute | solution.py:203
  67.4 42.8 %collective-permute-start.4 = (bf16[512,768]{1,0:T(8,128)(2,1)S(1)}, bf16[512,768]{1,0:T(8,128)(2,1)S(1)}, u32[]{:S(2)}, u32[]{:S(2)}) collective-permute-start(bf16[512,768]{1,0:T(8,128)(2,1)S(1)} %pad_maximum_fusion.2), channel_id=1, source_target_pairs={{0,8},{1,9},{2,10},{3,11},{4,12},{5,13},{6,14},{7,15},{8,16},{9,17... | collective-permute-start | bytes 2359304 | tf_op jit(solution)/shard_map/ppermute | solution.py:202
  75.5 34.5 %all-to-all-start.1 = ((bf16[8,72,768]{2,1,0:T(8,128)(2,1)}), bf16[8,72,768]{2,1,0:T(8,128)(2,1)S(1)}, u32[]{:S(2)}, u32[]{:S(2)}) async-start(bf16[8,72,768]{2,1,0:T(8,128)(2,1)} %bitcast.11), calls=%async_computation.1 | async-start | bytes 1769472 | tf_op jit(solution)/shard_map/all_to_all | solution.py:124
  84.7 84.4 %reduce-scatter.2.cloned.1.call-start = ((), (), s32[]{:S(2)}) async-start(), calls=%async_computation.7 | async-start | bytes 1966080 | tf_op jit(solution)/shard_map/reduce_scatter | solution.py:224
  89.5 1.1 copy-start.15
  110.2 34.0 %copy-start.12 = (bf16[512,768]{1,0:T(8,128)(2,1)}, bf16[512,768]{1,0:T(8,128)(2,1)S(1)}, u32[]{:S(2)}) copy-start(bf16[512,768]{1,0:T(8,128)(2,1)S(1)} %collective-permute-done.5) | copy-start | bytes 2359300
  110.2 31.0 %copy-start.10 = (bf16[512,768]{1,0:T(8,128)(2,1)}, bf16[512,768]{1,0:T(8,128)(2,1)S(1)}, u32[]{:S(2)}) copy-start(bf16[512,768]{1,0:T(8,128)(2,1)S(1)} %collective-permute-done.4) | copy-start | bytes 2359300
  111.3 29.9 %all-to-all-start.2 = ((bf16[8,72,768]{2,1,0:T(8,128)(2,1)}), bf16[8,72,768]{2,1,0:T(8,128)(2,1)S(1)}, u32[]{:S(2)}, u32[]{:S(2)}) async-start(bf16[8,72,768]{2,1,0:T(8,128)(2,1)} %broadcast_in_dim.5), calls=%async_computation.2 | async-start | bytes 1769472 | tf_op jit(solution)/shard_map/all_to_all | solution.py:124
  114.9 26.4 %collective-permute-start.8 = (bf16[512,768]{1,0:T(8,128)(2,1)S(1)}, bf16[512,768]{1,0:T(8,128)(2,1)}, u32[]{:S(2)}, u32[]{:S(2)}) collective-permute-start(bf16[512,768]{1,0:T(8,128)(2,1)S(1)} %collective-permute-done.4), channel_id=1, source_target_pairs={{0,8},{1,9},{2,10},{3,11},{4,12},{5,13},{6,14},{7,15},{8,16},{9,17... | collective-permute-start | bytes 2359304 | tf_op jit(solution)/shard_map/ppermute | solution.py:213
  141.2 4.3 %collective-permute-start.9 = (bf16[576,768]{1,0:T(8,128)(2,1)S(1)}, bf16[576,768]{1,0:T(8,128)(2,1)S(1)}, u32[]{:S(2)}, u32[]{:S(2)}) collective-permute-start(bf16[576,768]{1,0:T(8,128)(2,1)S(1)} %bitcast.38), channel_id=1, source_target_pairs={{0,32},{32,0},{64,96},{96,64},{128,160},{160,128},{192,224},{224,1... | collective-permute-start | bytes 2654216 | tf_op jit(solution)/shard_map/ppermute | solution.py:232
  143.1 0.9 copy-start.2
  145.5 0.9 copy-start.7
  146.5 1.5 copy-start
  148.0 1.5 copy-start.1
  149.5 1.2 copy-start.3
  150.6 1.3 copy-start.6
  151.9 1.2 copy-start.8
  160.4 0.9 copy-start.4
  161.3 22.6 %collective-permute-start.10 = (bf16[512,768]{1,0:T(8,128)(2,1)}, bf16[512,768]{1,0:T(8,128)(2,1)}, u32[]{:S(2)}, u32[]{:S(2)}) collective-permute-start(bf16[512,768]{1,0:T(8,128)(2,1)} %get-tuple-element.34), channel_id=1, source_target_pairs={{0,8},{1,9},{2,10},{3,11},{4,12},{5,13},{6,14},{7,15},{8,16},{9,17... | collective-permute-start | bytes 2359304 | tf_op jit(solution)/shard_map/ppermute | solution.py:244
  163.8 24.2 %collective-permute-start.11 = (bf16[512,768]{1,0:T(8,128)(2,1)}, bf16[512,768]{1,0:T(8,128)(2,1)}, u32[]{:S(2)}, u32[]{:S(2)}) collective-permute-start(bf16[512,768]{1,0:T(8,128)(2,1)} %get-tuple-element.35), channel_id=1, source_target_pairs={{0,16},{1,17},{2,18},{3,19},{4,20},{5,21},{6,22},{7,23},{8,24},{9,... | collective-permute-start | bytes 2359304 | tf_op jit(solution)/shard_map/ppermute | solution.py:244
  166.6 37.1 %collective-permute-start.12 = (bf16[512,768]{1,0:T(8,128)(2,1)}, bf16[512,768]{1,0:T(8,128)(2,1)}, u32[]{:S(2)}, u32[]{:S(2)}) collective-permute-start(bf16[512,768]{1,0:T(8,128)(2,1)} %get-tuple-element.36), channel_id=1, source_target_pairs={{0,24},{1,25},{2,26},{3,27},{4,28},{5,29},{6,30},{7,31},{8,0},{9,1... | collective-permute-start | bytes 2359304 | tf_op jit(solution)/shard_map/ppermute | solution.py:244
  169.1 1.9 copy-start.13
  171.0 1.1 copy-start.11
  175.4 28.3 %copy-start.5 = (bf16[512,768]{1,0:T(8,128)(2,1)S(1)}, bf16[512,768]{1,0:T(8,128)(2,1)}, u32[]{:S(2)}) copy-start(bf16[512,768]{1,0:T(8,128)(2,1)} %copy-done.4) | copy-start | bytes 2359300
  175.4 32.2 %all-to-all-start.3 = ((bf16[8,72,512]{2,1,0:T(8,128)(2,1)}), bf16[8,72,512]{2,1,0:T(8,128)(2,1)S(1)}, u32[]{:S(2)}, u32[]{:S(2)}) async-start(bf16[8,72,512]{2,1,0:T(8,128)(2,1)} %bitcast.42), calls=%async_computation.4 | async-start | bytes 1179648 | tf_op jit(solution)/shard_map/all_to_all | solution.py:124
  205.8 1.0 copy-start.17
Sparse Core Ops, SparseCore 0:
  24.6 48.2 all-gather.2
  75.0 41.2 all-gather.4
  119.1 30.7 reduce-scatter.1

commit v13 on v12

--- a/solution.py
+++ b/solution.py
@@ -194,7 +194,7 @@
     )
 
     both = jnp.concatenate([tokens, out_grad], axis=1)
-    both, saved_share = lax.optimization_barrier((both, saved_share))
+    both, _ = lax.optimization_barrier((both, grad_rows))
     both_rows = lax.all_gather(both, "col", axis=0, tiled=True, axis_index_groups=z_groups)
 
     w_both = jnp.concatenate([w_gate, w_up], axis=1)
@@ -221,19 +221,19 @@
         for side in range(2)
     ]
     down_part = jnp.concatenate(down_part, axis=0).reshape(n_x, units, features)
+    down_part, w_far = lax.optimization_barrier((down_part, w_far))
+    weights = [w_both, w_right, w_far, w_left]
     down_sum = lax.psum_scatter(
         down_part, "col", scatter_dimension=0, tiled=True, axis_index_groups=x_groups
     )[0]
-    own, gate_factor, up_factor, w_far, _ = lax.optimization_barrier(
-        (own, gate_factor, up_factor, w_far, down_part)
-    )
-    weights = [w_both, w_right, w_far, w_left]
+    own, gate_factor, up_factor, both_rows, _ = lax.optimization_barrier(
+        (own, gate_factor, up_factor, both_rows, down_part)
+    )
 
     other = lax.ppermute(own, "row", core_swap)
     *unit_parts, unit_grads = unit_blocks(
         jnp.stack([core, x_here]), own, other, gate_factor, up_factor, both_rows, n_x
     )
-    unit_grads, down_sum = lax.optimization_barrier((unit_grads, down_sum))
     part_in = 0.0
     for step, weight in enumerate(weights):
         columns = slice(2 * step * units, 2 * (step + 1) * units)

time: 217 us -> 210 us (0.968)
  local copies, waits for them, and re-layouts: 14.9 us -> 5.88 us
  starting transfers between devices: 65.1 us -> 71.8 us
  waiting for transfers between devices: 87.9 us -> 84.6 us
  matrix products: 12 us -> 9.73 us
    ppermute x1, waiting for transfers between devices: 24.1 us -> 7.9 us  [local(): w_far = lax.ppermute(w_left, 'col', x_shift(1))]
    unnamed x42 -> x26, local copies, waits for them, and re-layouts: 10.8 us -> 2.71 us
    all_to_all x4, waiting for transfers between devices: 16.5 us -> 21.6 us  [exchange(): lax.all_to_all(pieces, axis, 0, 0, tiled=True, axis_index_groups=groups)]
    ppermute x3, waiting for transfers between devices: 21.7 us -> 26.1 us  [local(): moved_part = lax.ppermute(unit_parts[step], 'col', x_shift(step))]
    ppermute x1, starting transfers between devices: 2.2 us -> 5.71 us  [local(): w_far = lax.ppermute(w_left, 'col', x_shift(1))]
    ppermute x1, waiting for transfers between devices: 0.01 us -> 2.39 us  [local(): got = lax.ppermute(give, 'row', core_swap)]
    dot_general x6, matrix products: 10.4 us -> 8.12 us  [contract_last(): lax.dot_general(left_side, right_side, (((1,), (1,)), ((), ())), preferre...]
  transfers between devices with their start and end apart: 20 -> 20, of which waited for: 10 -> 12; matrix products, arithmetic and copies ran while one was open for 13% -> 11% of each run, Pallas kernels for 3% -> 4%
where the time goes in v13:
time: 210 us; the launch traced here: 207 us
  waiting for transfers between devices  84.6 us (40%)
  starting transfers between devices  71.8 us (34%)
  between operations  14.3 us (7%)
  other arithmetic  12.7 us (6%)
  matrix products  9.73 us (5%)
  Pallas kernels  7.84 us (4%)
  local copies, waits for them, and re-layouts  5.88 us (3%)
    all_to_all x4, starting transfers between devices, exchange(): lax.all_to_all(pieces, axis, 0, 0, tiled=True, axis_index_groups=groups)  31.4 us
    ppermute x3, waiting for transfers between devices, local(): moved_part = lax.ppermute(unit_parts[step], 'col', x_shift(step))  26.1 us
    all_to_all x4, waiting for transfers between devices, exchange(): lax.all_to_all(pieces, axis, 0, 0, tiled=True, axis_index_groups=groups)  21.6 us
    ppermute x3, waiting for transfers between devices, local(): lax.ppermute(w_down, 'col', x_shift(step))  15.2 us
    ppermute x3, starting transfers between devices, local(): moved_part = lax.ppermute(unit_parts[step], 'col', x_shift(step))  9.1 us
    ppermute x2, waiting for transfers between devices, local(): lax.ppermute(pick(saved_pieces, lax.rem(x_here + turn, 2)), ('row', 'col'...  8.74 us
    dot_general x6, matrix products, contract_last(): lax.dot_general(left_side, right_side, (((1,), (1,)), ((), ())), preferre...  8.12 us
    ppermute x3, starting transfers between devices, local(): lax.ppermute(w_down, 'col', x_shift(step))  7.95 us
  transfers between devices with their start and end apart: 20, of which 12 were waited for; matrix products, arithmetic and copies ran while one was open for 11% of the time, Pallas kernels for 4%

profile of v13, /device:TPU:6, one launch (start us, length us, event | category | flops | bytes accessed | tf_op | source)
XLA Modules:
  0.0 206.8 jit_solution(13697838552287301220)
XLA Ops:
  7.3 1.0 pad_maximum_fusion.3
  8.3 2.8 %collective-permute-start.6 = (bf16[72,768]{1,0:T(8,128)(2,1)S(1)}, bf16[72,768]{1,0:T(8,128)(2,1)S(1)}, u32[]{:S(2)}, u32[]{:S(2)}) collective-permute-start(bf16[72,768]{1,0:T(8,128)(2,1)S(1)} %get-tuple-element.51), channel_id=1, source_target_pairs={{0,0},{1,1},{2,2},{3,3},{4,4},{5,5},{6,6},{7,7},{8,64},{9,65},{10,... | collective-permute-start | bytes 331784 | tf_op jit(solution)/shard_map/ppermute | solution.py:181
  11.1 3.8 %collective-permute-start.7 = (bf16[72,768]{1,0:T(8,128)(2,1)S(1)}, bf16[72,768]{1,0:T(8,128)(2,1)S(1)}, u32[]{:S(2)}, u32[]{:S(2)}) collective-permute-start(bf16[72,768]{1,0:T(8,128)(2,1)S(1)} %get-tuple-element.52), channel_id=1, source_target_pairs={{0,64},{1,65},{2,66},{3,67},{4,68},{5,69},{6,70},{7,71},{8,0},{9,1... | collective-permute-start | bytes 331784 | tf_op jit(solution)/shard_map/ppermute | solution.py:181
  14.9 4.2 %collective-permute-done.6 = bf16[72,768]{1,0:T(8,128)(2,1)S(1)} collective-permute-done((bf16[72,768]{1,0:T(8,128)(2,1)S(1)}, bf16[72,768]{1,0:T(8,128)(2,1)S(1)}, u32[]{:S(2)}, u32[]{:S(2)}) %collective-permute-start.6) | collective-permute-done | bytes 110624 | tf_op jit(solution)/shard_map/ppermute | solution.py:181
  19.1 4.5 %collective-permute-done.7 = bf16[72,768]{1,0:T(8,128)(2,1)S(1)} collective-permute-done((bf16[72,768]{1,0:T(8,128)(2,1)S(1)}, bf16[72,768]{1,0:T(8,128)(2,1)S(1)}, u32[]{:S(2)}, u32[]{:S(2)}) %collective-permute-start.7) | collective-permute-done | bytes 110624 | tf_op jit(solution)/shard_map/ppermute | solution.py:181
  24.5 0.9 broadcast_in_dim.4
  25.3 10.3 %all-to-all-start = ((bf16[8,72,512]{2,1,0:T(8,128)(2,1)}), bf16[8,72,512]{2,1,0:T(8,128)(2,1)S(1)}, u32[]{:S(2)}, u32[]{:S(2)}) async-start(bf16[8,72,512]{2,1,0:T(8,128)(2,1)} %broadcast_in_dim.4), calls=%async_computation | async-start | bytes 1179648 | tf_op jit(solution)/shard_map/all_to_all | solution.py:124
  35.6 1.9 collective-permute-start
  37.6 3.9 %collective-permute-start.2 = (bf16[384,512]{1,0:T(8,128)(2,1)S(1)}, bf16[384,512]{1,0:T(8,128)(2,1)S(1)}, u32[]{:S(2)}, u32[]{:S(2)}) collective-permute-start(bf16[384,512]{1,0:T(8,128)(2,1)S(1)} %copy-done.9), channel_id=1, source_target_pairs={{0,24},{1,25},{2,26},{3,27},{4,28},{5,29},{6,30},{7,31},{8,0},{9,1... | collective-permute-start | bytes 1179656 | tf_op jit(solution)/shard_map/ppermute | solution.py:165
  41.5 2.1 %collective-permute-start.1 = (bf16[384,512]{1,0:T(8,128)(2,1)S(1)}, bf16[384,512]{1,0:T(8,128)(2,1)S(1)}, u32[]{:S(2)}, u32[]{:S(2)}) collective-permute-start(bf16[384,512]{1,0:T(8,128)(2,1)S(1)} %copy-done.9), channel_id=1, source_target_pairs={{0,16},{1,17},{2,18},{3,19},{4,20},{5,21},{6,22},{7,23},{8,24},{9,... | collective-permute-start | bytes 1179656 | tf_op jit(solution)/shard_map/ppermute | solution.py:165
  43.7 1.1 pad_maximum_fusion.2
  44.8 4.8 %collective-permute-done = bf16[384,512]{1,0:T(8,128)(2,1)S(1)} collective-permute-done((bf16[384,512]{1,0:T(8,128)(2,1)S(1)}, bf16[384,512]{1,0:T(8,128)(2,1)S(1)}, u32[]{:S(2)}, u32[]{:S(2)}) %collective-permute-start) | collective-permute-done | bytes 393248 | tf_op jit(solution)/shard_map/ppermute | solution.py:165
  49.5 10.4 %collective-permute-done.2 = bf16[384,512]{1,0:T(8,128)(2,1)S(1)} collective-permute-done((bf16[384,512]{1,0:T(8,128)(2,1)S(1)}, bf16[384,512]{1,0:T(8,128)(2,1)S(1)}, u32[]{:S(2)}, u32[]{:S(2)}) %collective-permute-start.2) | collective-permute-done | bytes 393248 | tf_op jit(solution)/shard_map/ppermute | solution.py:165
  61.0 1.9 collective-permute-start.3
  62.9 2.4 %collective-permute-done.3 = bf16[576,768]{1,0:T(8,128)(2,1)S(1)} collective-permute-done((bf16[576,768]{1,0:T(8,128)(2,1)S(1)}, bf16[576,768]{1,0:T(8,128)(2,1)S(1)}, u32[]{:S(2)}, u32[]{:S(2)}) %collective-permute-start.3) | collective-permute-done | bytes 884768 | tf_op jit(solution)/shard_map/ppermute | solution.py:206
  65.3 1.6 add_convert_fusion
  66.9 9.3 %all-to-all-start.1 = ((bf16[8,72,768]{2,1,0:T(8,128)(2,1)}), bf16[8,72,768]{2,1,0:T(8,128)(2,1)S(1)}, u32[]{:S(2)}, u32[]{:S(2)}) async-start(bf16[8,72,768]{2,1,0:T(8,128)(2,1)} %bitcast.11), calls=%async_computation.1 | async-start | bytes 1769472 | tf_op jit(solution)/shard_map/all_to_all | solution.py:124
  76.3 1.9 collective-permute-start.5
  78.2 5.1 %collective-permute-start.4 = (bf16[512,768]{1,0:T(8,128)(2,1)S(1)}, bf16[512,768]{1,0:T(8,128)(2,1)}, u32[]{:S(2)}, u32[]{:S(2)}) collective-permute-start(bf16[512,768]{1,0:T(8,128)(2,1)S(1)} %pad_maximum_fusion.2), channel_id=1, source_target_pairs={{0,8},{1,9},{2,10},{3,11},{4,12},{5,13},{6,14},{7,15},{8,16},{9,17... | collective-permute-start | bytes 2359304 | tf_op jit(solution)/shard_map/ppermute | solution.py:202
  84.1 17.7 %all-to-all-done.1 = bf16[8,72,768]{2,1,0:T(8,128)(2,1)S(1)} async-done(((bf16[8,72,768]{2,1,0:T(8,128)(2,1)}), bf16[8,72,768]{2,1,0:T(8,128)(2,1)S(1)}, u32[]{:S(2)}, u32[]{:S(2)}) %all-to-all-start.1) | async-done | bytes 884768 | tf_op jit(solution)/shard_map/all_to_all | solution.py:124
  101.9 1.1 broadcast_in_dim.5
  103.0 4.8 %all-to-all-start.2 = ((bf16[8,72,768]{2,1,0:T(8,128)(2,1)}), bf16[8,72,768]{2,1,0:T(8,128)(2,1)}, u32[]{:S(2)}, u32[]{:S(2)}) async-start(bf16[8,72,768]{2,1,0:T(8,128)(2,1)} %broadcast_in_dim.5), calls=%async_computation.2 | async-start | bytes 1769472 | tf_op jit(solution)/shard_map/all_to_all | solution.py:124
  107.8 5.7 %collective-permute-start.8 = (bf16[512,768]{1,0:T(8,128)(2,1)}, bf16[512,768]{1,0:T(8,128)(2,1)}, u32[]{:S(2)}, u32[]{:S(2)}) collective-permute-start(bf16[512,768]{1,0:T(8,128)(2,1)} %collective-permute-done.4), channel_id=1, source_target_pairs={{0,8},{1,9},{2,10},{3,11},{4,12},{5,13},{6,14},{7,15},{8,16},{9,17... | collective-permute-start | bytes 2359304 | tf_op jit(solution)/shard_map/ppermute | solution.py:213
  113.5 3.5 %fusion.2 = (bf16[8,2,72,768]{3,2,1,0:T(8,128)(2,1)S(1)}, bf16[8,2,72,768]{3,2,1,0:T(8,128)(2,1)S(1)}, bf16[8,2,72,768]{3,2,1,0:T(8,128)(2,1)S(1)}) fusion(bf16[8,2,72,1536]{3,2,1,0:T(8,128)(2,1)} %bitcast.40), kind=kLoop, calls=%fused_computation.7 | loop fusion | flops 13271040 | bytes 8847360 | tf_op jit(solution)/shard_map/convert_element_type | solution.py:33
  117.2 0.9 copy-done.8
  118.1 0.8 convolution_convert_fusion.3
  118.9 0.8 convolution_convert_fusion.2
  119.8 1.3 pad_maximum_fusion.1
  121.0 7.9 %collective-permute-done.8 = bf16[512,768]{1,0:T(8,128)(2,1)} collective-permute-done((bf16[512,768]{1,0:T(8,128)(2,1)}, bf16[512,768]{1,0:T(8,128)(2,1)}, u32[]{:S(2)}, u32[]{:S(2)}) %collective-permute-start.8) | collective-permute-done | bytes 786464 | tf_op jit(solution)/shard_map/ppermute | solution.py:213
  128.9 3.9 %all-to-all-done.2 = bf16[8,72,768]{2,1,0:T(8,128)(2,1)} async-done(((bf16[8,72,768]{2,1,0:T(8,128)(2,1)}), bf16[8,72,768]{2,1,0:T(8,128)(2,1)}, u32[]{:S(2)}, u32[]{:S(2)}) %all-to-all-start.2) | async-done | bytes 884768 | tf_op jit(solution)/shard_map/all_to_all | solution.py:124
  132.9 1.9 collective-permute-start.9
  134.9 2.6 %collective-permute-done.9.other_ref = bf16[576,768]{1,0:T(8,128)(2,1)} collective-permute-done((bf16[576,768]{1,0:T(8,128)(2,1)}, bf16[576,768]{1,0:T(8,128)(2,1)}, u32[]{:S(2)}, u32[]{:S(2)}) %collective-permute-start.9) | collective-permute-done | bytes 884768 | tf_op jit(solution)/shard_map/ppermute | solution.py:233
  137.5 1.3 copy-done.2
  138.8 7.8 %shard_map.102 = (bf16[512,768]{1,0:T(8,128)(2,1)S(1)}, bf16[512,768]{1,0:T(8,128)(2,1)}, bf16[512,768]{1,0:T(8,128)(2,1)}, bf16[512,768]{1,0:T(8,128)(2,1)}, bf16[576,3072]{1,0:T(8,128)(2,1)S(1)}) custom-call(s32[2]{0:T(128)S(1)} %pad_add_fusion.place_ref, bf16[576,768]{1,0:T(8,128)(2,1)} %bitcast.12.own_ref, ...), custom_call_target="tpu_custom_call" | custom-call | flops 1811939328 | bytes 14000000 | tf_op jit(solution)/shard_map/pallas_call | solution.py:98
  146.7 4.4 %collective-permute-start.10 = (bf16[512,768]{1,0:T(8,128)(2,1)}, bf16[512,768]{1,0:T(8,128)(2,1)S(1)}, u32[]{:S(2)}, u32[]{:S(2)}) collective-permute-start(bf16[512,768]{1,0:T(8,128)(2,1)} %get-tuple-element.35), channel_id=1, source_target_pairs={{0,8},{1,9},{2,10},{3,11},{4,12},{5,13},{6,14},{7,15},{8,16},{9,17... | collective-permute-start | bytes 2359304 | tf_op jit(solution)/shard_map/ppermute | solution.py:244
  151.1 1.9 collective-permute-start.11
  153.0 2.8 %collective-permute-start.12 = (bf16[512,768]{1,0:T(8,128)(2,1)}, bf16[512,768]{1,0:T(8,128)(2,1)}, u32[]{:S(2)}, u32[]{:S(2)}) collective-permute-start(bf16[512,768]{1,0:T(8,128)(2,1)} %get-tuple-element.37), channel_id=1, source_target_pairs={{0,24},{1,25},{2,26},{3,27},{4,28},{5,29},{6,30},{7,31},{8,0},{9,1... | collective-permute-start | bytes 2359304 | tf_op jit(solution)/shard_map/ppermute | solution.py:244
  155.8 1.8 fusion.11
  157.6 1.9 fusion.13
  160.6 1.5 fusion.9
  162.2 7.0 %all-to-all-start.3 = ((bf16[8,72,512]{2,1,0:T(8,128)(2,1)}), bf16[8,72,512]{2,1,0:T(8,128)(2,1)S(1)}, u32[]{:S(2)}, u32[]{:S(2)}) async-start(bf16[8,72,512]{2,1,0:T(8,128)(2,1)} %bitcast.20), calls=%async_computation.3 | async-start | bytes 1179648 | tf_op jit(solution)/shard_map/all_to_all | solution.py:124
  169.2 8.6 %collective-permute-done.10 = bf16[512,768]{1,0:T(8,128)(2,1)S(1)} collective-permute-done((bf16[512,768]{1,0:T(8,128)(2,1)}, bf16[512,768]{1,0:T(8,128)(2,1)S(1)}, u32[]{:S(2)}, u32[]{:S(2)}) %collective-permute-start.10) | collective-permute-done | bytes 786464 | tf_op jit(solution)/shard_map/ppermute | solution.py:244
  177.8 1.0 collective-permute-done.11
  178.8 16.4 %collective-permute-done.12 = bf16[512,768]{1,0:T(8,128)(2,1)} collective-permute-done((bf16[512,768]{1,0:T(8,128)(2,1)}, bf16[512,768]{1,0:T(8,128)(2,1)}, u32[]{:S(2)}, u32[]{:S(2)}) %collective-permute-start.12) | collective-permute-done | bytes 786464 | tf_op jit(solution)/shard_map/ppermute | solution.py:244
  195.2 1.6 multiply_convert_fusion
  196.8 1.0 fusion.28
  197.8 0.7 reduce_sum.25
  198.5 1.8 fusion.24
  (50 shorter events, 4.1 us)
Async XLA Ops:
  7.2 17.3 %copy-start.11 = (bf16[72,512]{1,0:T(8,128)(2,1)S(1)}, bf16[72,512]{1,0:T(8,128)(2,1)}, u32[]{:S(2)}) copy-start(bf16[72,512]{1,0:T(8,128)(2,1)} %param.8) | copy-start | bytes 221188
  7.2 106.3 %all-gather.3.cloned.1.call-start = ((), (), s32[]{:S(2)}) async-start(), calls=%async_computation.5 | async-start | bytes 3760128 | tf_op jit(solution)/shard_map/all_gather | solution.py:192
  8.3 10.9 %collective-permute-start.6 = (bf16[72,768]{1,0:T(8,128)(2,1)S(1)}, bf16[72,768]{1,0:T(8,128)(2,1)S(1)}, u32[]{:S(2)}, u32[]{:S(2)}) collective-permute-start(bf16[72,768]{1,0:T(8,128)(2,1)S(1)} %get-tuple-element.51), channel_id=1, source_target_pairs={{0,0},{1,1},{2,2},{3,3},{4,4},{5,5},{6,6},{7,7},{8,64},{9,65},{10,... | collective-permute-start | bytes 331784 | tf_op jit(solution)/shard_map/ppermute | solution.py:181
  11.1 12.5 %collective-permute-start.7 = (bf16[72,768]{1,0:T(8,128)(2,1)S(1)}, bf16[72,768]{1,0:T(8,128)(2,1)S(1)}, u32[]{:S(2)}, u32[]{:S(2)}) collective-permute-start(bf16[72,768]{1,0:T(8,128)(2,1)S(1)} %get-tuple-element.52), channel_id=1, source_target_pairs={{0,64},{1,65},{2,66},{3,67},{4,68},{5,69},{6,70},{7,71},{8,0},{9,1... | collective-permute-start | bytes 331784 | tf_op jit(solution)/shard_map/ppermute | solution.py:181
  23.7 12.0 %copy-start.9 = (bf16[384,512]{1,0:T(8,128)(2,1)S(1)}, bf16[384,512]{1,0:T(8,128)(2,1)}, u32[]{:S(2)}) copy-start(bf16[384,512]{1,0:T(8,128)(2,1)} %param.13) | copy-start | bytes 1179652
  23.7 20.0 %copy-start.10 = (bf16[512,384]{1,0:T(8,128)(2,1)S(1)}, bf16[512,384]{1,0:T(8,128)(2,1)}, u32[]{:S(2)}) copy-start(bf16[512,384]{1,0:T(8,128)(2,1)} %param.12) | copy-start | bytes 1179652
  25.3 35.0 %all-to-all-start = ((bf16[8,72,512]{2,1,0:T(8,128)(2,1)}), bf16[8,72,512]{2,1,0:T(8,128)(2,1)S(1)}, u32[]{:S(2)}, u32[]{:S(2)}) async-start(bf16[8,72,512]{2,1,0:T(8,128)(2,1)} %broadcast_in_dim.4), calls=%async_computation | async-start | bytes 1179648 | tf_op jit(solution)/shard_map/all_to_all | solution.py:124
  35.6 13.9 %collective-permute-start = (bf16[384,512]{1,0:T(8,128)(2,1)S(1)}, bf16[384,512]{1,0:T(8,128)(2,1)S(1)}, u32[]{:S(2)}, u32[]{:S(2)}) collective-permute-start(bf16[384,512]{1,0:T(8,128)(2,1)S(1)} %copy-done.9), channel_id=1, source_target_pairs={{0,8},{1,9},{2,10},{3,11},{4,12},{5,13},{6,14},{7,15},{8,16},{9,17... | collective-permute-start | bytes 1179656 | tf_op jit(solution)/shard_map/ppermute | solution.py:165
  37.6 22.4 %collective-permute-start.2 = (bf16[384,512]{1,0:T(8,128)(2,1)S(1)}, bf16[384,512]{1,0:T(8,128)(2,1)S(1)}, u32[]{:S(2)}, u32[]{:S(2)}) collective-permute-start(bf16[384,512]{1,0:T(8,128)(2,1)S(1)} %copy-done.9), channel_id=1, source_target_pairs={{0,24},{1,25},{2,26},{3,27},{4,28},{5,29},{6,30},{7,31},{8,0},{9,1... | collective-permute-start | bytes 1179656 | tf_op jit(solution)/shard_map/ppermute | solution.py:165
  41.5 18.5 %collective-permute-start.1 = (bf16[384,512]{1,0:T(8,128)(2,1)S(1)}, bf16[384,512]{1,0:T(8,128)(2,1)S(1)}, u32[]{:S(2)}, u32[]{:S(2)}) collective-permute-start(bf16[384,512]{1,0:T(8,128)(2,1)S(1)} %copy-done.9), channel_id=1, source_target_pairs={{0,16},{1,17},{2,18},{3,19},{4,20},{5,21},{6,22},{7,23},{8,24},{9,... | collective-permute-start | bytes 1179656 | tf_op jit(solution)/shard_map/ppermute | solution.py:165
  44.8 33.5 %copy-start.3 = (bf16[512,768]{1,0:T(8,128)(2,1)}, bf16[512,768]{1,0:T(8,128)(2,1)S(1)}, u32[]{:S(2)}) copy-start(bf16[512,768]{1,0:T(8,128)(2,1)S(1)} %pad_maximum_fusion.2) | copy-start | bytes 2359300
  60.3 6.6 %copy-start.7 = (bf16[8,72,512]{2,1,0:T(8,128)(2,1)}, bf16[8,72,512]{2,1,0:T(8,128)(2,1)S(1)}, u32[]{:S(2)}) copy-start(bf16[8,72,512]{2,1,0:T(8,128)(2,1)S(1)} %all-to-all-done) | copy-start | bytes 1769476
  61.0 4.3 %collective-permute-start.3 = (bf16[576,768]{1,0:T(8,128)(2,1)S(1)}, bf16[576,768]{1,0:T(8,128)(2,1)S(1)}, u32[]{:S(2)}, u32[]{:S(2)}) collective-permute-start(bf16[576,768]{1,0:T(8,128)(2,1)S(1)} %convolution_convert_fusion), channel_id=1, source_target_pairs={{0,32},{32,0},{64,96},{96,64},{128,160},{160,128},{192,224},{224,1... | collective-permute-start | bytes 2654216 | tf_op jit(solution)/shard_map/ppermute | solution.py:206
  66.9 16.5 %copy-start.12 = (bf16[72,512]{1,0:T(8,128)(2,1)S(1)}, bf16[72,512]{1,0:T(8,128)(2,1)}, u32[]{:S(2)}) copy-start(bf16[72,512]{1,0:T(8,128)(2,1)} %param.7) | copy-start | bytes 221188
  66.9 34.8 %all-to-all-start.1 = ((bf16[8,72,768]{2,1,0:T(8,128)(2,1)}), bf16[8,72,768]{2,1,0:T(8,128)(2,1)S(1)}, u32[]{:S(2)}, u32[]{:S(2)}) async-start(bf16[8,72,768]{2,1,0:T(8,128)(2,1)} %bitcast.11), calls=%async_computation.1 | async-start | bytes 1769472 | tf_op jit(solution)/shard_map/all_to_all | solution.py:124
  76.2 52.7 %all-gather.5.cloned.1.call-start = ((), (), s32[]{:S(2)}) async-start(), calls=%async_computation.6 | async-start | bytes 1327104 | tf_op jit(solution)/shard_map/all_gather | solution.py:198
  76.3 25.6 %collective-permute-start.5 = (bf16[512,768]{1,0:T(8,128)(2,1)S(1)}, bf16[512,768]{1,0:T(8,128)(2,1)S(1)}, u32[]{:S(2)}, u32[]{:S(2)}) collective-permute-start(bf16[512,768]{1,0:T(8,128)(2,1)S(1)} %pad_maximum_fusion.2), channel_id=1, source_target_pairs={{0,24},{1,25},{2,26},{3,27},{4,28},{5,29},{6,30},{7,31},{8,0},{9,1... | collective-permute-start | bytes 2359304 | tf_op jit(solution)/shard_map/ppermute | solution.py:203
  78.2 23.7 %collective-permute-start.4 = (bf16[512,768]{1,0:T(8,128)(2,1)S(1)}, bf16[512,768]{1,0:T(8,128)(2,1)}, u32[]{:S(2)}, u32[]{:S(2)}) collective-permute-start(bf16[512,768]{1,0:T(8,128)(2,1)S(1)} %pad_maximum_fusion.2), channel_id=1, source_target_pairs={{0,8},{1,9},{2,10},{3,11},{4,12},{5,13},{6,14},{7,15},{8,16},{9,17... | collective-permute-start | bytes 2359304 | tf_op jit(solution)/shard_map/ppermute | solution.py:202
  101.9 11.6 %copy-start.5 = (bf16[512,768]{1,0:T(8,128)(2,1)}, bf16[512,768]{1,0:T(8,128)(2,1)S(1)}, u32[]{:S(2)}) copy-start(bf16[512,768]{1,0:T(8,128)(2,1)S(1)} %collective-permute-done.5) | copy-start | bytes 2359300
  103.0 29.9 %all-to-all-start.2 = ((bf16[8,72,768]{2,1,0:T(8,128)(2,1)}), bf16[8,72,768]{2,1,0:T(8,128)(2,1)}, u32[]{:S(2)}, u32[]{:S(2)}) async-start(bf16[8,72,768]{2,1,0:T(8,128)(2,1)} %broadcast_in_dim.5), calls=%async_computation.2 | async-start | bytes 1769472 | tf_op jit(solution)/shard_map/all_to_all | solution.py:124
  107.7 90.7 %reduce-scatter.2.cloned.1.call-start = ((), (), s32[]{:S(2)}) async-start(), calls=%async_computation.7 | async-start | bytes 1966080 | tf_op jit(solution)/shard_map/reduce_scatter | solution.py:226
  107.8 21.2 %collective-permute-start.8 = (bf16[512,768]{1,0:T(8,128)(2,1)}, bf16[512,768]{1,0:T(8,128)(2,1)}, u32[]{:S(2)}, u32[]{:S(2)}) collective-permute-start(bf16[512,768]{1,0:T(8,128)(2,1)} %collective-permute-done.4), channel_id=1, source_target_pairs={{0,8},{1,9},{2,10},{3,11},{4,12},{5,13},{6,14},{7,15},{8,16},{9,17... | collective-permute-start | bytes 2359304 | tf_op jit(solution)/shard_map/ppermute | solution.py:213
  117.1 1.1 copy-start.8
  132.9 4.7 %collective-permute-start.9 = (bf16[576,768]{1,0:T(8,128)(2,1)}, bf16[576,768]{1,0:T(8,128)(2,1)}, u32[]{:S(2)}, u32[]{:S(2)}) collective-permute-start(bf16[576,768]{1,0:T(8,128)(2,1)} %bitcast.12.own_ref), channel_id=1, source_target_pairs={{0,32},{32,0},{64,96},{96,64},{128,160},{160,128},{192,224},{224,1... | collective-permute-start | bytes 2654216 | tf_op jit(solution)/shard_map/ppermute | solution.py:233
  137.5 1.3 copy-start.2
  146.7 12.8 %copy-start = (bf16[512,768]{1,0:T(8,128)(2,1)}, bf16[512,768]{1,0:T(8,128)(2,1)S(1)}, u32[]{:S(2)}) copy-start(bf16[512,768]{1,0:T(8,128)(2,1)S(1)} %get-tuple-element.34) | copy-start | bytes 2359300
  146.7 31.1 %collective-permute-start.10 = (bf16[512,768]{1,0:T(8,128)(2,1)}, bf16[512,768]{1,0:T(8,128)(2,1)S(1)}, u32[]{:S(2)}, u32[]{:S(2)}) collective-permute-start(bf16[512,768]{1,0:T(8,128)(2,1)} %get-tuple-element.35), channel_id=1, source_target_pairs={{0,8},{1,9},{2,10},{3,11},{4,12},{5,13},{6,14},{7,15},{8,16},{9,17... | collective-permute-start | bytes 2359304 | tf_op jit(solution)/shard_map/ppermute | solution.py:244
  151.1 27.7 %collective-permute-start.11 = (bf16[512,768]{1,0:T(8,128)(2,1)}, bf16[512,768]{1,0:T(8,128)(2,1)S(1)}, u32[]{:S(2)}, u32[]{:S(2)}) collective-permute-start(bf16[512,768]{1,0:T(8,128)(2,1)} %get-tuple-element.36), channel_id=1, source_target_pairs={{0,16},{1,17},{2,18},{3,19},{4,20},{5,21},{6,22},{7,23},{8,24},{9,... | collective-permute-start | bytes 2359304 | tf_op jit(solution)/shard_map/ppermute | solution.py:244
  153.0 42.2 %collective-permute-start.12 = (bf16[512,768]{1,0:T(8,128)(2,1)}, bf16[512,768]{1,0:T(8,128)(2,1)}, u32[]{:S(2)}, u32[]{:S(2)}) collective-permute-start(bf16[512,768]{1,0:T(8,128)(2,1)} %get-tuple-element.37), channel_id=1, source_target_pairs={{0,24},{1,25},{2,26},{3,27},{4,28},{5,29},{6,30},{7,31},{8,0},{9,1... | collective-permute-start | bytes 2359304 | tf_op jit(solution)/shard_map/ppermute | solution.py:244
  157.6 1.9 copy-start.6
  159.5 1.1 copy-start.4
  162.2 33.1 %copy-start.1 = (bf16[512,768]{1,0:T(8,128)(2,1)S(1)}, bf16[512,768]{1,0:T(8,128)(2,1)}, u32[]{:S(2)}) copy-start(bf16[512,768]{1,0:T(8,128)(2,1)} %copy-done) | copy-start | bytes 2359300
  162.2 35.6 %all-to-all-start.3 = ((bf16[8,72,512]{2,1,0:T(8,128)(2,1)}), bf16[8,72,512]{2,1,0:T(8,128)(2,1)S(1)}, u32[]{:S(2)}, u32[]{:S(2)}) async-start(bf16[8,72,512]{2,1,0:T(8,128)(2,1)} %bitcast.20), calls=%async_computation.3 | async-start | bytes 1179648 | tf_op jit(solution)/shard_map/all_to_all | solution.py:124
Sparse Core Ops, SparseCore 0:
  24.6 48.2 all-gather.2
  84.2 43.2 all-gather.4
  135.0 48.3 reduce-scatter.1

commit v14 on v12

--- a/solution.py
+++ b/solution.py
@@ -210,7 +210,12 @@
     terms = exchange(pair.reshape(n_y, block, half), "row", y_groups)
     share = jnp.sum(terms.astype(jnp.float32), axis=0).astype(jnp.bfloat16)
     share, w_left, w_right = lax.optimization_barrier((share, w_left, w_right))
-    w_far = lax.ppermute(w_left, "col", x_shift(1))
+    w_far = jnp.concatenate(
+        [
+            lax.ppermute(w_left[: features // 2], "col", x_shift(1)),
+            lax.ppermute(w_right[features // 2 :], "col", x_shift(n_x - 1)),
+        ]
+    )
     own = spread(share, n_y, "row", y_groups).reshape(group_rows, half)
 
     grad_scale = (rows * n_row) ** (-0.5)
@@ -224,8 +229,8 @@
     down_sum = lax.psum_scatter(
         down_part, "col", scatter_dimension=0, tiled=True, axis_index_groups=x_groups
     )[0]
-    own, gate_factor, up_factor, w_far, _ = lax.optimization_barrier(
-        (own, gate_factor, up_factor, w_far, down_part)
+    own, gate_factor, up_factor, w_left, w_right, w_far, _ = lax.optimization_barrier(
+        (own, gate_factor, up_factor, w_left, w_right, w_far, down_part)
     )
     weights = [w_both, w_right, w_far, w_left]
 
@@ -233,7 +238,6 @@
     *unit_parts, unit_grads = unit_blocks(
         jnp.stack([core, x_here]), own, other, gate_factor, up_factor, both_rows, n_x
     )
-    unit_grads, down_sum = lax.optimization_barrier((unit_grads, down_sum))
     part_in = 0.0
     for step, weight in enumerate(weights):
         columns = slice(2 * step * units, 2 * (step + 1) * units)
@@ -245,6 +249,7 @@
         unit_sum = unit_sum + moved_part.astype(jnp.float32)
     unit_wgrad = (unit_sum * grad_scale).astype(jnp.bfloat16)
     gate_wgrad, up_wgrad = unit_wgrad[:, :units], unit_wgrad[:, units:]
+    part_in, down_sum = lax.optimization_barrier((part_in, down_sum))
     down_wgrad = (down_sum.astype(jnp.float32) * grad_scale).astype(jnp.bfloat16)
     token_terms = exchange(
         part_in.reshape(N_Z, block, features), "col", z_groups

time: 217 us -> 205 us (0.945)
  waiting for transfers between devices: 87.9 us -> 77.3 us
  starting transfers between devices: 65.1 us -> 75.3 us
  local copies, waits for them, and re-layouts: 14.9 us -> 8.49 us
  matrix products: 12 us -> 7.32 us
    ppermute x1 -> x2, waiting for transfers between devices: 24.1 us -> 7.22 us  [the longest x1 6.04 us: local(): lax.ppermute(w_right[features // 2:], 'col', x_shift(n_x - 1))]
    unnamed x42 -> x34, local copies, waits for them, and re-layouts: 10.8 us -> 3.26 us
    ppermute x1 -> x2, starting transfers between devices: 2.2 us -> 7.52 us  [the longest x1 5.6 us: local(): lax.ppermute(w_left[:features // 2], 'col', x_shift(1))]
    dot_general x6, matrix products: 10.4 us -> 5.72 us  [contract_last(): lax.dot_general(left_side, right_side, (((1,), (1,)), ((), ())), preferre...]
    ppermute x3, starting transfers between devices: 7.75 us -> 10.6 us  [local(): moved_part = lax.ppermute(unit_parts[step], 'col', x_shift(step))]
    ppermute x1, waiting for transfers between devices: 0.01 us -> 2.39 us  [local(): got = lax.ppermute(give, 'row', core_swap)]
  transfers between devices with their start and end apart: 20 -> 21, of which waited for: 10 -> 12; matrix products, arithmetic and copies ran while one was open for 13% -> 11% of each run, Pallas kernels for 3% -> 4%
where the time goes in v14:
time: 205 us; the launch traced here: 203 us
  waiting for transfers between devices  77.3 us (38%)
  starting transfers between devices  75.3 us (37%)
  between operations  14.3 us (7%)
  other arithmetic  12.7 us (6%)
  local copies, waits for them, and re-layouts  8.49 us (4%)
  Pallas kernels  7.86 us (4%)
  matrix products  7.32 us (4%)
    all_to_all x4, starting transfers between devices, exchange(): lax.all_to_all(pieces, axis, 0, 0, tiled=True, axis_index_groups=groups)  31.7 us
    ppermute x3, waiting for transfers between devices, local(): moved_part = lax.ppermute(unit_parts[step], 'col', x_shift(step))  23.3 us
    all_to_all x4, waiting for transfers between devices, exchange(): lax.all_to_all(pieces, axis, 0, 0, tiled=True, axis_index_groups=groups)  17.7 us
    ppermute x3, waiting for transfers between devices, local(): lax.ppermute(w_down, 'col', x_shift(step))  15.2 us
    ppermute x3, starting transfers between devices, local(): moved_part = lax.ppermute(unit_parts[step], 'col', x_shift(step))  10.6 us
    ppermute x2, waiting for transfers between devices, local(): lax.ppermute(pick(saved_pieces, lax.rem(x_here + turn, 2)), ('row', 'col'...  8.74 us
    ppermute x3, starting transfers between devices, local(): lax.ppermute(w_down, 'col', x_shift(step))  7.95 us
    pallas_call x1, Pallas kernels, unit_blocks(): pl.pallas_call(unit_block_kernel, out_shape=(part,) * n_block + (grads,),...  7.86 us
  transfers between devices with their start and end apart: 21, of which 12 were waited for; matrix products, arithmetic and copies ran while one was open for 11% of the time, Pallas kernels for 4%

profile of v14, /device:TPU:6, one launch (start us, length us, event | category | flops | bytes accessed | tf_op | source)
XLA Modules:
  0.0 203.3 jit_solution(14556637391218557828)
XLA Ops:
  7.3 1.0 pad_maximum_fusion.4
  8.3 2.8 %collective-permute-start.6 = (bf16[72,768]{1,0:T(8,128)(2,1)S(1)}, bf16[72,768]{1,0:T(8,128)(2,1)S(1)}, u32[]{:S(2)}, u32[]{:S(2)}) collective-permute-start(bf16[72,768]{1,0:T(8,128)(2,1)S(1)} %get-tuple-element.55), channel_id=1, source_target_pairs={{0,0},{1,1},{2,2},{3,3},{4,4},{5,5},{6,6},{7,7},{8,64},{9,65},{10,... | collective-permute-start | bytes 331784 | tf_op jit(solution)/shard_map/ppermute | solution.py:181
  11.1 3.8 %collective-permute-start.7 = (bf16[72,768]{1,0:T(8,128)(2,1)S(1)}, bf16[72,768]{1,0:T(8,128)(2,1)S(1)}, u32[]{:S(2)}, u32[]{:S(2)}) collective-permute-start(bf16[72,768]{1,0:T(8,128)(2,1)S(1)} %get-tuple-element.56), channel_id=1, source_target_pairs={{0,64},{1,65},{2,66},{3,67},{4,68},{5,69},{6,70},{7,71},{8,0},{9,1... | collective-permute-start | bytes 331784 | tf_op jit(solution)/shard_map/ppermute | solution.py:181
  14.9 4.2 %collective-permute-done.6 = bf16[72,768]{1,0:T(8,128)(2,1)S(1)} collective-permute-done((bf16[72,768]{1,0:T(8,128)(2,1)S(1)}, bf16[72,768]{1,0:T(8,128)(2,1)S(1)}, u32[]{:S(2)}, u32[]{:S(2)}) %collective-permute-start.6) | collective-permute-done | bytes 110624 | tf_op jit(solution)/shard_map/ppermute | solution.py:181
  19.1 4.5 %collective-permute-done.7 = bf16[72,768]{1,0:T(8,128)(2,1)S(1)} collective-permute-done((bf16[72,768]{1,0:T(8,128)(2,1)S(1)}, bf16[72,768]{1,0:T(8,128)(2,1)S(1)}, u32[]{:S(2)}, u32[]{:S(2)}) %collective-permute-start.7) | collective-permute-done | bytes 110624 | tf_op jit(solution)/shard_map/ppermute | solution.py:181
  24.5 0.9 broadcast_in_dim.4
  25.3 10.3 %all-to-all-start = ((bf16[8,72,512]{2,1,0:T(8,128)(2,1)}), bf16[8,72,512]{2,1,0:T(8,128)(2,1)S(1)}, u32[]{:S(2)}, u32[]{:S(2)}) async-start(bf16[8,72,512]{2,1,0:T(8,128)(2,1)} %broadcast_in_dim.4), calls=%async_computation | async-start | bytes 1179648 | tf_op jit(solution)/shard_map/all_to_all | solution.py:124
  35.6 1.9 collective-permute-start
  37.6 3.9 %collective-permute-start.2 = (bf16[384,512]{1,0:T(8,128)(2,1)S(1)}, bf16[384,512]{1,0:T(8,128)(2,1)S(1)}, u32[]{:S(2)}, u32[]{:S(2)}) collective-permute-start(bf16[384,512]{1,0:T(8,128)(2,1)S(1)} %copy-done.12), channel_id=1, source_target_pairs={{0,24},{1,25},{2,26},{3,27},{4,28},{5,29},{6,30},{7,31},{8,0},{9,1... | collective-permute-start | bytes 1179656 | tf_op jit(solution)/shard_map/ppermute | solution.py:165
  41.5 2.1 %collective-permute-start.1 = (bf16[384,512]{1,0:T(8,128)(2,1)S(1)}, bf16[384,512]{1,0:T(8,128)(2,1)S(1)}, u32[]{:S(2)}, u32[]{:S(2)}) collective-permute-start(bf16[384,512]{1,0:T(8,128)(2,1)S(1)} %copy-done.12), channel_id=1, source_target_pairs={{0,16},{1,17},{2,18},{3,19},{4,20},{5,21},{6,22},{7,23},{8,24},{9,... | collective-permute-start | bytes 1179656 | tf_op jit(solution)/shard_map/ppermute | solution.py:165
  43.7 1.1 pad_maximum_fusion.2
  44.8 4.8 %collective-permute-done = bf16[384,512]{1,0:T(8,128)(2,1)S(1)} collective-permute-done((bf16[384,512]{1,0:T(8,128)(2,1)S(1)}, bf16[384,512]{1,0:T(8,128)(2,1)S(1)}, u32[]{:S(2)}, u32[]{:S(2)}) %collective-permute-start) | collective-permute-done | bytes 393248 | tf_op jit(solution)/shard_map/ppermute | solution.py:165
  49.5 10.4 %collective-permute-done.2 = bf16[384,512]{1,0:T(8,128)(2,1)S(1)} collective-permute-done((bf16[384,512]{1,0:T(8,128)(2,1)S(1)}, bf16[384,512]{1,0:T(8,128)(2,1)S(1)}, u32[]{:S(2)}, u32[]{:S(2)}) %collective-permute-start.2) | collective-permute-done | bytes 393248 | tf_op jit(solution)/shard_map/ppermute | solution.py:165
  61.0 1.9 collective-permute-start.3
  62.9 2.4 %collective-permute-done.3 = bf16[576,768]{1,0:T(8,128)(2,1)S(1)} collective-permute-done((bf16[576,768]{1,0:T(8,128)(2,1)S(1)}, bf16[576,768]{1,0:T(8,128)(2,1)S(1)}, u32[]{:S(2)}, u32[]{:S(2)}) %collective-permute-start.3) | collective-permute-done | bytes 884768 | tf_op jit(solution)/shard_map/ppermute | solution.py:206
  65.3 1.6 add_convert_fusion
  66.9 9.3 %all-to-all-start.1 = ((bf16[8,72,768]{2,1,0:T(8,128)(2,1)}), bf16[8,72,768]{2,1,0:T(8,128)(2,1)S(1)}, u32[]{:S(2)}, u32[]{:S(2)}) async-start(bf16[8,72,768]{2,1,0:T(8,128)(2,1)} %bitcast.11), calls=%async_computation.1 | async-start | bytes 1769472 | tf_op jit(solution)/shard_map/all_to_all | solution.py:124
  76.3 1.9 collective-permute-start.5
  78.2 5.1 %collective-permute-start.4 = (bf16[512,768]{1,0:T(8,128)(2,1)S(1)}, bf16[512,768]{1,0:T(8,128)(2,1)S(1)}, u32[]{:S(2)}, u32[]{:S(2)}) collective-permute-start(bf16[512,768]{1,0:T(8,128)(2,1)S(1)} %pad_maximum_fusion.2), channel_id=1, source_target_pairs={{0,8},{1,9},{2,10},{3,11},{4,12},{5,13},{6,14},{7,15},{8,16},{9,17... | collective-permute-start | bytes 2359304 | tf_op jit(solution)/shard_map/ppermute | solution.py:202
  84.1 17.7 %all-to-all-done.1 = bf16[8,72,768]{2,1,0:T(8,128)(2,1)S(1)} async-done(((bf16[8,72,768]{2,1,0:T(8,128)(2,1)}), bf16[8,72,768]{2,1,0:T(8,128)(2,1)S(1)}, u32[]{:S(2)}, u32[]{:S(2)}) %all-to-all-start.1) | async-done | bytes 884768 | tf_op jit(solution)/shard_map/all_to_all | solution.py:124
  101.9 1.1 broadcast_in_dim.5
  103.0 4.8 %all-to-all-start.2 = ((bf16[8,72,768]{2,1,0:T(8,128)(2,1)}), bf16[8,72,768]{2,1,0:T(8,128)(2,1)}, u32[]{:S(2)}, u32[]{:S(2)}) async-start(bf16[8,72,768]{2,1,0:T(8,128)(2,1)} %broadcast_in_dim.5), calls=%async_computation.2 | async-start | bytes 1769472 | tf_op jit(solution)/shard_map/all_to_all | solution.py:124
  107.9 3.5 %fusion.2 = (bf16[8,2,72,768]{3,2,1,0:T(8,128)(2,1)S(1)}, bf16[8,2,72,768]{3,2,1,0:T(8,128)(2,1)S(1)}, bf16[8,2,72,768]{3,2,1,0:T(8,128)(2,1)S(1)}) fusion(bf16[8,2,72,1536]{3,2,1,0:T(8,128)(2,1)} %bitcast.39), kind=kLoop, calls=%fused_computation.7 | loop fusion | flops 13271040 | bytes 8847360 | tf_op jit(solution)/shard_map/convert_element_type | solution.py:33
  111.6 0.9 copy-done.11
  113.3 0.8 convolution_convert_fusion.2
  114.1 1.3 pad_maximum_fusion.1
  115.4 1.0 slice.54
  116.5 1.0 slice.55
  117.5 1.9 collective-permute-start.9
  119.4 5.6 %collective-permute-start.8 = (bf16[256,768]{1,0:T(8,128)(2,1)S(1)}, bf16[256,768]{1,0:T(8,128)(2,1)S(1)}, u32[]{:S(2)}, u32[]{:S(2)}) collective-permute-start(bf16[256,768]{1,0:T(8,128)(2,1)S(1)} %slice.54), channel_id=1, source_target_pairs={{0,8},{1,9},{2,10},{3,11},{4,12},{5,13},{6,14},{7,15},{8,16},{9,17... | collective-permute-start | bytes 1179656 | tf_op jit(solution)/shard_map/ppermute | solution.py:215
  125.0 6.0 %collective-permute-done.9 = bf16[256,768]{1,0:T(8,128)(2,1)S(1)} collective-permute-done((bf16[256,768]{1,0:T(8,128)(2,1)S(1)}, bf16[256,768]{1,0:T(8,128)(2,1)S(1)}, u32[]{:S(2)}, u32[]{:S(2)}) %collective-permute-start.9) | collective-permute-done | bytes 393248 | tf_op jit(solution)/shard_map/ppermute | solution.py:216
  131.1 1.2 collective-permute-done.8
  132.2 0.9 pad_maximum_fusion.3
  133.2 1.9 collective-permute-start.10
  135.2 2.7 %collective-permute-done.10.other_ref = bf16[576,768]{1,0:T(8,128)(2,1)} collective-permute-done((bf16[576,768]{1,0:T(8,128)(2,1)}, bf16[576,768]{1,0:T(8,128)(2,1)}, u32[]{:S(2)}, u32[]{:S(2)}) %collective-permute-start.10) | collective-permute-done | bytes 884768 | tf_op jit(solution)/shard_map/ppermute | solution.py:237
  137.8 1.3 copy-done.2
  139.1 7.9 %shard_map.102 = (bf16[512,768]{1,0:T(8,128)(2,1)S(1)}, bf16[512,768]{1,0:T(8,128)(2,1)}, bf16[512,768]{1,0:T(8,128)(2,1)}, bf16[512,768]{1,0:T(8,128)(2,1)}, bf16[576,3072]{1,0:T(8,128)(2,1)S(1)}) custom-call(s32[2]{0:T(128)S(1)} %pad_add_fusion.place_ref, bf16[576,768]{1,0:T(8,128)(2,1)} %bitcast.12.own_ref, ...), custom_call_target="tpu_custom_call" | custom-call | flops 1811939328 | bytes 14000000 | tf_op jit(solution)/shard_map/pallas_call | solution.py:98
  147.0 5.9 %collective-permute-start.11 = (bf16[512,768]{1,0:T(8,128)(2,1)}, bf16[512,768]{1,0:T(8,128)(2,1)S(1)}, u32[]{:S(2)}, u32[]{:S(2)}) collective-permute-start(bf16[512,768]{1,0:T(8,128)(2,1)} %get-tuple-element.38), channel_id=1, source_target_pairs={{0,8},{1,9},{2,10},{3,11},{4,12},{5,13},{6,14},{7,15},{8,16},{9,17... | collective-permute-start | bytes 2359304 | tf_op jit(solution)/shard_map/ppermute | solution.py:248
  152.9 1.9 collective-permute-start.12
  154.8 2.8 %collective-permute-start.13 = (bf16[512,768]{1,0:T(8,128)(2,1)}, bf16[512,768]{1,0:T(8,128)(2,1)}, u32[]{:S(2)}, u32[]{:S(2)}) collective-permute-start(bf16[512,768]{1,0:T(8,128)(2,1)} %get-tuple-element.40), channel_id=1, source_target_pairs={{0,24},{1,25},{2,26},{3,27},{4,28},{5,29},{6,30},{7,31},{8,0},{9,1... | collective-permute-start | bytes 2359304 | tf_op jit(solution)/shard_map/ppermute | solution.py:248
  160.6 1.5 fusion.9
  162.1 7.2 %all-to-all-start.3 = ((bf16[8,72,512]{2,1,0:T(8,128)(2,1)}), bf16[8,72,512]{2,1,0:T(8,128)(2,1)S(1)}, u32[]{:S(2)}, u32[]{:S(2)}) async-start(bf16[8,72,512]{2,1,0:T(8,128)(2,1)} %bitcast.21), calls=%async_computation.4 | async-start | bytes 1179648 | tf_op jit(solution)/shard_map/all_to_all | solution.py:124
  169.3 4.0 %collective-permute-done.11 = bf16[512,768]{1,0:T(8,128)(2,1)S(1)} collective-permute-done((bf16[512,768]{1,0:T(8,128)(2,1)}, bf16[512,768]{1,0:T(8,128)(2,1)S(1)}, u32[]{:S(2)}, u32[]{:S(2)}) %collective-permute-start.11) | collective-permute-done | bytes 786464 | tf_op jit(solution)/shard_map/ppermute | solution.py:248
  173.3 3.7 %collective-permute-done.12 = bf16[512,768]{1,0:T(8,128)(2,1)S(1)} collective-permute-done((bf16[512,768]{1,0:T(8,128)(2,1)}, bf16[512,768]{1,0:T(8,128)(2,1)S(1)}, u32[]{:S(2)}, u32[]{:S(2)}) %collective-permute-start.12) | collective-permute-done | bytes 786464 | tf_op jit(solution)/shard_map/ppermute | solution.py:248
  177.0 15.6 %collective-permute-done.13 = bf16[512,768]{1,0:T(8,128)(2,1)} collective-permute-done((bf16[512,768]{1,0:T(8,128)(2,1)}, bf16[512,768]{1,0:T(8,128)(2,1)}, u32[]{:S(2)}, u32[]{:S(2)}) %collective-permute-start.13) | collective-permute-done | bytes 786464 | tf_op jit(solution)/shard_map/ppermute | solution.py:248
  192.6 1.6 multiply_convert_fusion
  194.2 1.0 fusion.27
  195.2 0.8 multiply_convert_fusion.1
  (63 shorter events, 7.5 us)
Async XLA Ops:
  7.2 17.3 %copy-start.15 = (bf16[72,512]{1,0:T(8,128)(2,1)S(1)}, bf16[72,512]{1,0:T(8,128)(2,1)}, u32[]{:S(2)}) copy-start(bf16[72,512]{1,0:T(8,128)(2,1)} %param.8) | copy-start | bytes 221188
  7.2 100.7 %all-gather.3.cloned.1.call-start = ((), (), s32[]{:S(2)}) async-start(), calls=%async_computation.5 | async-start | bytes 3760128 | tf_op jit(solution)/shard_map/all_gather | solution.py:192
  8.3 10.9 %collective-permute-start.6 = (bf16[72,768]{1,0:T(8,128)(2,1)S(1)}, bf16[72,768]{1,0:T(8,128)(2,1)S(1)}, u32[]{:S(2)}, u32[]{:S(2)}) collective-permute-start(bf16[72,768]{1,0:T(8,128)(2,1)S(1)} %get-tuple-element.55), channel_id=1, source_target_pairs={{0,0},{1,1},{2,2},{3,3},{4,4},{5,5},{6,6},{7,7},{8,64},{9,65},{10,... | collective-permute-start | bytes 331784 | tf_op jit(solution)/shard_map/ppermute | solution.py:181
  11.1 12.5 %collective-permute-start.7 = (bf16[72,768]{1,0:T(8,128)(2,1)S(1)}, bf16[72,768]{1,0:T(8,128)(2,1)S(1)}, u32[]{:S(2)}, u32[]{:S(2)}) collective-permute-start(bf16[72,768]{1,0:T(8,128)(2,1)S(1)} %get-tuple-element.56), channel_id=1, source_target_pairs={{0,64},{1,65},{2,66},{3,67},{4,68},{5,69},{6,70},{7,71},{8,0},{9,1... | collective-permute-start | bytes 331784 | tf_op jit(solution)/shard_map/ppermute | solution.py:181
  23.7 12.0 %copy-start.12 = (bf16[384,512]{1,0:T(8,128)(2,1)S(1)}, bf16[384,512]{1,0:T(8,128)(2,1)}, u32[]{:S(2)}) copy-start(bf16[384,512]{1,0:T(8,128)(2,1)} %param.13) | copy-start | bytes 1179652
  23.7 20.0 %copy-start.14 = (bf16[512,384]{1,0:T(8,128)(2,1)S(1)}, bf16[512,384]{1,0:T(8,128)(2,1)}, u32[]{:S(2)}) copy-start(bf16[512,384]{1,0:T(8,128)(2,1)} %param.12) | copy-start | bytes 1179652
  25.3 35.0 %all-to-all-start = ((bf16[8,72,512]{2,1,0:T(8,128)(2,1)}), bf16[8,72,512]{2,1,0:T(8,128)(2,1)S(1)}, u32[]{:S(2)}, u32[]{:S(2)}) async-start(bf16[8,72,512]{2,1,0:T(8,128)(2,1)} %broadcast_in_dim.4), calls=%async_computation | async-start | bytes 1179648 | tf_op jit(solution)/shard_map/all_to_all | solution.py:124
  35.6 13.9 %collective-permute-start = (bf16[384,512]{1,0:T(8,128)(2,1)S(1)}, bf16[384,512]{1,0:T(8,128)(2,1)S(1)}, u32[]{:S(2)}, u32[]{:S(2)}) collective-permute-start(bf16[384,512]{1,0:T(8,128)(2,1)S(1)} %copy-done.12), channel_id=1, source_target_pairs={{0,8},{1,9},{2,10},{3,11},{4,12},{5,13},{6,14},{7,15},{8,16},{9,17... | collective-permute-start | bytes 1179656 | tf_op jit(solution)/shard_map/ppermute | solution.py:165
  37.6 22.4 %collective-permute-start.2 = (bf16[384,512]{1,0:T(8,128)(2,1)S(1)}, bf16[384,512]{1,0:T(8,128)(2,1)S(1)}, u32[]{:S(2)}, u32[]{:S(2)}) collective-permute-start(bf16[384,512]{1,0:T(8,128)(2,1)S(1)} %copy-done.12), channel_id=1, source_target_pairs={{0,24},{1,25},{2,26},{3,27},{4,28},{5,29},{6,30},{7,31},{8,0},{9,1... | collective-permute-start | bytes 1179656 | tf_op jit(solution)/shard_map/ppermute | solution.py:165
  41.5 18.5 %collective-permute-start.1 = (bf16[384,512]{1,0:T(8,128)(2,1)S(1)}, bf16[384,512]{1,0:T(8,128)(2,1)S(1)}, u32[]{:S(2)}, u32[]{:S(2)}) collective-permute-start(bf16[384,512]{1,0:T(8,128)(2,1)S(1)} %copy-done.12), channel_id=1, source_target_pairs={{0,16},{1,17},{2,18},{3,19},{4,20},{5,21},{6,22},{7,23},{8,24},{9,... | collective-permute-start | bytes 1179656 | tf_op jit(solution)/shard_map/ppermute | solution.py:165
  44.8 33.5 %copy-start.4 = (bf16[512,768]{1,0:T(8,128)(2,1)}, bf16[512,768]{1,0:T(8,128)(2,1)S(1)}, u32[]{:S(2)}) copy-start(bf16[512,768]{1,0:T(8,128)(2,1)S(1)} %pad_maximum_fusion.2) | copy-start | bytes 2359300
  60.3 6.6 %copy-start.10 = (bf16[8,72,512]{2,1,0:T(8,128)(2,1)}, bf16[8,72,512]{2,1,0:T(8,128)(2,1)S(1)}, u32[]{:S(2)}) copy-start(bf16[8,72,512]{2,1,0:T(8,128)(2,1)S(1)} %all-to-all-done) | copy-start | bytes 1769476
  61.0 4.3 %collective-permute-start.3 = (bf16[576,768]{1,0:T(8,128)(2,1)S(1)}, bf16[576,768]{1,0:T(8,128)(2,1)S(1)}, u32[]{:S(2)}, u32[]{:S(2)}) collective-permute-start(bf16[576,768]{1,0:T(8,128)(2,1)S(1)} %convolution_convert_fusion), channel_id=1, source_target_pairs={{0,32},{32,0},{64,96},{96,64},{128,160},{160,128},{192,224},{224,1... | collective-permute-start | bytes 2654216 | tf_op jit(solution)/shard_map/ppermute | solution.py:206
  66.9 16.5 %copy-start.16 = (bf16[72,512]{1,0:T(8,128)(2,1)S(1)}, bf16[72,512]{1,0:T(8,128)(2,1)}, u32[]{:S(2)}) copy-start(bf16[72,512]{1,0:T(8,128)(2,1)} %param.7) | copy-start | bytes 221188
  66.9 34.8 %all-to-all-start.1 = ((bf16[8,72,768]{2,1,0:T(8,128)(2,1)}), bf16[8,72,768]{2,1,0:T(8,128)(2,1)S(1)}, u32[]{:S(2)}, u32[]{:S(2)}) async-start(bf16[8,72,768]{2,1,0:T(8,128)(2,1)} %bitcast.11), calls=%async_computation.1 | async-start | bytes 1769472 | tf_op jit(solution)/shard_map/all_to_all | solution.py:124
  76.2 58.9 %all-gather.5.cloned.1.call-start = ((), (), s32[]{:S(2)}) async-start(), calls=%async_computation.6 | async-start | bytes 1327104 | tf_op jit(solution)/shard_map/all_gather | solution.py:198
  76.3 25.6 %collective-permute-start.5 = (bf16[512,768]{1,0:T(8,128)(2,1)S(1)}, bf16[512,768]{1,0:T(8,128)(2,1)S(1)}, u32[]{:S(2)}, u32[]{:S(2)}) collective-permute-start(bf16[512,768]{1,0:T(8,128)(2,1)S(1)} %pad_maximum_fusion.2), channel_id=1, source_target_pairs={{0,24},{1,25},{2,26},{3,27},{4,28},{5,29},{6,30},{7,31},{8,0},{9,1... | collective-permute-start | bytes 2359304 | tf_op jit(solution)/shard_map/ppermute | solution.py:203
  78.2 23.7 %collective-permute-start.4 = (bf16[512,768]{1,0:T(8,128)(2,1)S(1)}, bf16[512,768]{1,0:T(8,128)(2,1)S(1)}, u32[]{:S(2)}, u32[]{:S(2)}) collective-permute-start(bf16[512,768]{1,0:T(8,128)(2,1)S(1)} %pad_maximum_fusion.2), channel_id=1, source_target_pairs={{0,8},{1,9},{2,10},{3,11},{4,12},{5,13},{6,14},{7,15},{8,16},{9,17... | collective-permute-start | bytes 2359304 | tf_op jit(solution)/shard_map/ppermute | solution.py:202
  101.9 6.0 %copy-start.6 = (bf16[512,768]{1,0:T(8,128)(2,1)}, bf16[512,768]{1,0:T(8,128)(2,1)S(1)}, u32[]{:S(2)}) copy-start(bf16[512,768]{1,0:T(8,128)(2,1)S(1)} %collective-permute-done.5) | copy-start | bytes 2359300
  101.9 6.0 %copy-start.8 = (bf16[512,768]{1,0:T(8,128)(2,1)}, bf16[512,768]{1,0:T(8,128)(2,1)S(1)}, u32[]{:S(2)}) copy-start(bf16[512,768]{1,0:T(8,128)(2,1)S(1)} %collective-permute-done.4) | copy-start | bytes 2359300
  103.0 30.2 %all-to-all-start.2 = ((bf16[8,72,768]{2,1,0:T(8,128)(2,1)}), bf16[8,72,768]{2,1,0:T(8,128)(2,1)}, u32[]{:S(2)}, u32[]{:S(2)}) async-start(bf16[8,72,768]{2,1,0:T(8,128)(2,1)} %broadcast_in_dim.5), calls=%async_computation.2 | async-start | bytes 1769472 | tf_op jit(solution)/shard_map/all_to_all | solution.py:124
  107.8 54.3 %reduce-scatter.2.cloned.1.call-start = ((), (), s32[]{:S(2)}) async-start(), calls=%async_computation.7 | async-start | bytes 1966080 | tf_op jit(solution)/shard_map/reduce_scatter | solution.py:229
  111.4 1.1 copy-start.11
  117.5 13.6 %collective-permute-start.9 = (bf16[256,768]{1,0:T(8,128)(2,1)S(1)}, bf16[256,768]{1,0:T(8,128)(2,1)S(1)}, u32[]{:S(2)}, u32[]{:S(2)}) collective-permute-start(bf16[256,768]{1,0:T(8,128)(2,1)S(1)} %slice.55), channel_id=1, source_target_pairs={{0,24},{1,25},{2,26},{3,27},{4,28},{5,29},{6,30},{7,31},{8,0},{9,1... | collective-permute-start | bytes 1179656 | tf_op jit(solution)/shard_map/ppermute | solution.py:216
  119.4 12.8 %collective-permute-start.8 = (bf16[256,768]{1,0:T(8,128)(2,1)S(1)}, bf16[256,768]{1,0:T(8,128)(2,1)S(1)}, u32[]{:S(2)}, u32[]{:S(2)}) collective-permute-start(bf16[256,768]{1,0:T(8,128)(2,1)S(1)} %slice.54), channel_id=1, source_target_pairs={{0,8},{1,9},{2,10},{3,11},{4,12},{5,13},{6,14},{7,15},{8,16},{9,17... | collective-permute-start | bytes 1179656 | tf_op jit(solution)/shard_map/ppermute | solution.py:215
  133.2 4.7 %collective-permute-start.10 = (bf16[576,768]{1,0:T(8,128)(2,1)}, bf16[576,768]{1,0:T(8,128)(2,1)}, u32[]{:S(2)}, u32[]{:S(2)}) collective-permute-start(bf16[576,768]{1,0:T(8,128)(2,1)} %bitcast.12.own_ref), channel_id=1, source_target_pairs={{0,32},{32,0},{64,96},{96,64},{128,160},{160,128},{192,224},{224,1... | collective-permute-start | bytes 2654216 | tf_op jit(solution)/shard_map/ppermute | solution.py:237
  137.8 1.3 copy-start.2
  139.1 18.5 %copy-start.9 = (bf16[512,768]{1,0:T(8,128)(2,1)S(1)}, bf16[512,768]{1,0:T(8,128)(2,1)}, u32[]{:S(2)}) copy-start(bf16[512,768]{1,0:T(8,128)(2,1)} %copy-done.8) | copy-start | bytes 2359300
  147.0 12.0 %copy-start = (bf16[512,768]{1,0:T(8,128)(2,1)}, bf16[512,768]{1,0:T(8,128)(2,1)S(1)}, u32[]{:S(2)}) copy-start(bf16[512,768]{1,0:T(8,128)(2,1)S(1)} %get-tuple-element.37) | copy-start | bytes 2359300
  147.0 11.3 %copy-start.3 = (bf16[512,768]{1,0:T(8,128)(2,1)S(1)}, bf16[512,768]{1,0:T(8,128)(2,1)}, u32[]{:S(2)}) copy-start(bf16[512,768]{1,0:T(8,128)(2,1)} %pad_maximum_fusion.3) | copy-start | bytes 2359300
  147.0 26.3 %collective-permute-start.11 = (bf16[512,768]{1,0:T(8,128)(2,1)}, bf16[512,768]{1,0:T(8,128)(2,1)S(1)}, u32[]{:S(2)}, u32[]{:S(2)}) collective-permute-start(bf16[512,768]{1,0:T(8,128)(2,1)} %get-tuple-element.38), channel_id=1, source_target_pairs={{0,8},{1,9},{2,10},{3,11},{4,12},{5,13},{6,14},{7,15},{8,16},{9,17... | collective-permute-start | bytes 2359304 | tf_op jit(solution)/shard_map/ppermute | solution.py:248
  152.9 24.1 %collective-permute-start.12 = (bf16[512,768]{1,0:T(8,128)(2,1)}, bf16[512,768]{1,0:T(8,128)(2,1)S(1)}, u32[]{:S(2)}, u32[]{:S(2)}) collective-permute-start(bf16[512,768]{1,0:T(8,128)(2,1)} %get-tuple-element.39), channel_id=1, source_target_pairs={{0,16},{1,17},{2,18},{3,19},{4,20},{5,21},{6,22},{7,23},{8,24},{9,... | collective-permute-start | bytes 2359304 | tf_op jit(solution)/shard_map/ppermute | solution.py:248
  154.8 37.8 %collective-permute-start.13 = (bf16[512,768]{1,0:T(8,128)(2,1)}, bf16[512,768]{1,0:T(8,128)(2,1)}, u32[]{:S(2)}, u32[]{:S(2)}) collective-permute-start(bf16[512,768]{1,0:T(8,128)(2,1)} %get-tuple-element.40), channel_id=1, source_target_pairs={{0,24},{1,25},{2,26},{3,27},{4,28},{5,29},{6,30},{7,31},{8,0},{9,1... | collective-permute-start | bytes 2359304 | tf_op jit(solution)/shard_map/ppermute | solution.py:248
  158.3 1.1 copy-start.7
  159.4 1.1 copy-start.5
  162.1 30.6 %copy-start.1 = (bf16[512,768]{1,0:T(8,128)(2,1)S(1)}, bf16[512,768]{1,0:T(8,128)(2,1)}, u32[]{:S(2)}) copy-start(bf16[512,768]{1,0:T(8,128)(2,1)} %copy-done) | copy-start | bytes 2359300
  162.1 34.0 %all-to-all-start.3 = ((bf16[8,72,512]{2,1,0:T(8,128)(2,1)}), bf16[8,72,512]{2,1,0:T(8,128)(2,1)S(1)}, u32[]{:S(2)}, u32[]{:S(2)}) async-start(bf16[8,72,512]{2,1,0:T(8,128)(2,1)} %bitcast.21), calls=%async_computation.4 | async-start | bytes 1179648 | tf_op jit(solution)/shard_map/all_to_all | solution.py:124
  194.2 1.0 copy-start.13
Sparse Core Ops, SparseCore 0:
  24.6 48.2 all-gather.2
  84.2 43.2 all-gather.4
  130.3 31.2 reduce-scatter.1

commit v15 on v12

--- a/solution.py
+++ b/solution.py
@@ -210,7 +210,8 @@
     terms = exchange(pair.reshape(n_y, block, half), "row", y_groups)
     share = jnp.sum(terms.astype(jnp.float32), axis=0).astype(jnp.bfloat16)
     share, w_left, w_right = lax.optimization_barrier((share, w_left, w_right))
-    w_far = lax.ppermute(w_left, "col", x_shift(1))
+    far_first = lax.ppermute(w_left[: features // 2], "col", x_shift(1))
+    far_second = lax.ppermute(w_right[features // 2 :], "col", x_shift(n_x - 1))
     own = spread(share, n_y, "row", y_groups).reshape(group_rows, half)
 
     grad_scale = (rows * n_row) ** (-0.5)
@@ -224,16 +225,18 @@
     down_sum = lax.psum_scatter(
         down_part, "col", scatter_dimension=0, tiled=True, axis_index_groups=x_groups
     )[0]
-    own, gate_factor, up_factor, w_far, _ = lax.optimization_barrier(
-        (own, gate_factor, up_factor, w_far, down_part)
-    )
+    own, gate_factor, up_factor, w_left, w_right, far_first, far_second, _ = (
+        lax.optimization_barrier(
+            (own, gate_factor, up_factor, w_left, w_right, far_first, far_second, down_part)
+        )
+    )
+    w_far = jnp.concatenate([far_first, far_second])
     weights = [w_both, w_right, w_far, w_left]
 
     other = lax.ppermute(own, "row", core_swap)
     *unit_parts, unit_grads = unit_blocks(
         jnp.stack([core, x_here]), own, other, gate_factor, up_factor, both_rows, n_x
     )
-    unit_grads, down_sum = lax.optimization_barrier((unit_grads, down_sum))
     part_in = 0.0
     for step, weight in enumerate(weights):
         columns = slice(2 * step * units, 2 * (step + 1) * units)
@@ -245,6 +248,7 @@
         unit_sum = unit_sum + moved_part.astype(jnp.float32)
     unit_wgrad = (unit_sum * grad_scale).astype(jnp.bfloat16)
     gate_wgrad, up_wgrad = unit_wgrad[:, :units], unit_wgrad[:, units:]
+    part_in, down_sum = lax.optimization_barrier((part_in, down_sum))
     down_wgrad = (down_sum.astype(jnp.float32) * grad_scale).astype(jnp.bfloat16)
     token_terms = exchange(
         part_in.reshape(N_Z, block, features), "col", z_groups

time: 217 us -> 205 us (0.945)
  waiting for transfers between devices: 87.9 us -> 76.4 us
  starting transfers between devices: 65.1 us -> 75.2 us
  local copies, waits for them, and re-layouts: 14.9 us -> 8.61 us
  matrix products: 12 us -> 8.4 us
    ppermute x1 -> x2, waiting for transfers between devices: 24.1 us -> 6.47 us  [the longest x1 6.04 us: local(): far_second = lax.ppermute(w_right[features // 2:], 'col', x_shift(n_x - 1))]
    unnamed x42 -> x36, local copies, waits for them, and re-layouts: 10.8 us -> 3.39 us
    ppermute x1 -> x2, starting transfers between devices: 2.2 us -> 7.51 us  [the longest x1 5.59 us: local(): far_first = lax.ppermute(w_left[:features // 2], 'col', x_shift(1))]
    dot_general x6, matrix products: 10.4 us -> 6.8 us  [contract_last(): lax.dot_general(left_side, right_side, (((1,), (1,)), ((), ())), preferre...]
    all_to_all x4, starting transfers between devices: 29.6 us -> 32.3 us  [exchange(): lax.all_to_all(pieces, axis, 0, 0, tiled=True, axis_index_groups=groups)]
    ppermute x1, waiting for transfers between devices: 0.01 us -> 2.39 us  [local(): got = lax.ppermute(give, 'row', core_swap)]
  transfers between devices with their start and end apart: 20 -> 21, of which waited for: 10 -> 14; matrix products, arithmetic and copies ran while one was open for 13% -> 11% of each run, Pallas kernels for 3% -> 4%
where the time goes in v15:
time: 205 us; the launch traced here: 202 us
  waiting for transfers between devices  76.4 us (37%)
  starting transfers between devices  75.2 us (37%)
  between operations  14.3 us (7%)
  other arithmetic  11.7 us (6%)
  local copies, waits for them, and re-layouts  8.61 us (4%)
  matrix products  8.4 us (4%)
  Pallas kernels  7.86 us (4%)
    all_to_all x4, starting transfers between devices, exchange(): lax.all_to_all(pieces, axis, 0, 0, tiled=True, axis_index_groups=groups)  32.3 us
    ppermute x3, waiting for transfers between devices, local(): moved_part = lax.ppermute(unit_parts[step], 'col', x_shift(step))  22.3 us
    all_to_all x4, waiting for transfers between devices, exchange(): lax.all_to_all(pieces, axis, 0, 0, tiled=True, axis_index_groups=groups)  18.4 us
    ppermute x3, waiting for transfers between devices, local(): lax.ppermute(w_down, 'col', x_shift(step))  15.2 us
    ppermute x3, starting transfers between devices, local(): moved_part = lax.ppermute(unit_parts[step], 'col', x_shift(step))  9.84 us
    ppermute x2, waiting for transfers between devices, local(): lax.ppermute(pick(saved_pieces, lax.rem(x_here + turn, 2)), ('row', 'col'...  8.74 us
    ppermute x3, starting transfers between devices, local(): lax.ppermute(w_down, 'col', x_shift(step))  7.95 us
    pallas_call x1, Pallas kernels, unit_blocks(): pl.pallas_call(unit_block_kernel, out_shape=(part,) * n_block + (grads,),...  7.86 us
  transfers between devices with their start and end apart: 21, of which 14 were waited for; matrix products, arithmetic and copies ran while one was open for 11% of the time, Pallas kernels for 4%

profile of v15, /device:TPU:6, one launch (start us, length us, event | category | flops | bytes accessed | tf_op | source)
XLA Modules:
  0.0 202.5 jit_solution(17043438070275185157)
XLA Ops:
  7.3 1.0 pad_maximum_fusion.3
  8.3 2.8 %collective-permute-start.6 = (bf16[72,768]{1,0:T(8,128)(2,1)S(1)}, bf16[72,768]{1,0:T(8,128)(2,1)S(1)}, u32[]{:S(2)}, u32[]{:S(2)}) collective-permute-start(bf16[72,768]{1,0:T(8,128)(2,1)S(1)} %get-tuple-element.57), channel_id=1, source_target_pairs={{0,0},{1,1},{2,2},{3,3},{4,4},{5,5},{6,6},{7,7},{8,64},{9,65},{10,... | collective-permute-start | bytes 331784 | tf_op jit(solution)/shard_map/ppermute | solution.py:181
  11.1 3.8 %collective-permute-start.7 = (bf16[72,768]{1,0:T(8,128)(2,1)S(1)}, bf16[72,768]{1,0:T(8,128)(2,1)S(1)}, u32[]{:S(2)}, u32[]{:S(2)}) collective-permute-start(bf16[72,768]{1,0:T(8,128)(2,1)S(1)} %get-tuple-element.58), channel_id=1, source_target_pairs={{0,64},{1,65},{2,66},{3,67},{4,68},{5,69},{6,70},{7,71},{8,0},{9,1... | collective-permute-start | bytes 331784 | tf_op jit(solution)/shard_map/ppermute | solution.py:181
  14.9 4.2 %collective-permute-done.6 = bf16[72,768]{1,0:T(8,128)(2,1)S(1)} collective-permute-done((bf16[72,768]{1,0:T(8,128)(2,1)S(1)}, bf16[72,768]{1,0:T(8,128)(2,1)S(1)}, u32[]{:S(2)}, u32[]{:S(2)}) %collective-permute-start.6) | collective-permute-done | bytes 110624 | tf_op jit(solution)/shard_map/ppermute | solution.py:181
  19.1 4.5 %collective-permute-done.7 = bf16[72,768]{1,0:T(8,128)(2,1)S(1)} collective-permute-done((bf16[72,768]{1,0:T(8,128)(2,1)S(1)}, bf16[72,768]{1,0:T(8,128)(2,1)S(1)}, u32[]{:S(2)}, u32[]{:S(2)}) %collective-permute-start.7) | collective-permute-done | bytes 110624 | tf_op jit(solution)/shard_map/ppermute | solution.py:181
  24.5 0.9 broadcast_in_dim.4
  25.3 10.3 %all-to-all-start = ((bf16[8,72,512]{2,1,0:T(8,128)(2,1)}), bf16[8,72,512]{2,1,0:T(8,128)(2,1)S(1)}, u32[]{:S(2)}, u32[]{:S(2)}) async-start(bf16[8,72,512]{2,1,0:T(8,128)(2,1)} %broadcast_in_dim.4), calls=%async_computation | async-start | bytes 1179648 | tf_op jit(solution)/shard_map/all_to_all | solution.py:124
  35.6 1.9 collective-permute-start
  37.6 3.9 %collective-permute-start.2 = (bf16[384,512]{1,0:T(8,128)(2,1)S(1)}, bf16[384,512]{1,0:T(8,128)(2,1)S(1)}, u32[]{:S(2)}, u32[]{:S(2)}) collective-permute-start(bf16[384,512]{1,0:T(8,128)(2,1)S(1)} %copy-done.11), channel_id=1, source_target_pairs={{0,24},{1,25},{2,26},{3,27},{4,28},{5,29},{6,30},{7,31},{8,0},{9,1... | collective-permute-start | bytes 1179656 | tf_op jit(solution)/shard_map/ppermute | solution.py:165
  41.5 2.1 %collective-permute-start.1 = (bf16[384,512]{1,0:T(8,128)(2,1)S(1)}, bf16[384,512]{1,0:T(8,128)(2,1)S(1)}, u32[]{:S(2)}, u32[]{:S(2)}) collective-permute-start(bf16[384,512]{1,0:T(8,128)(2,1)S(1)} %copy-done.11), channel_id=1, source_target_pairs={{0,16},{1,17},{2,18},{3,19},{4,20},{5,21},{6,22},{7,23},{8,24},{9,... | collective-permute-start | bytes 1179656 | tf_op jit(solution)/shard_map/ppermute | solution.py:165
  43.7 1.1 pad_maximum_fusion.2
  44.8 4.8 %collective-permute-done = bf16[384,512]{1,0:T(8,128)(2,1)S(1)} collective-permute-done((bf16[384,512]{1,0:T(8,128)(2,1)S(1)}, bf16[384,512]{1,0:T(8,128)(2,1)S(1)}, u32[]{:S(2)}, u32[]{:S(2)}) %collective-permute-start) | collective-permute-done | bytes 393248 | tf_op jit(solution)/shard_map/ppermute | solution.py:165
  49.5 10.4 %collective-permute-done.2 = bf16[384,512]{1,0:T(8,128)(2,1)S(1)} collective-permute-done((bf16[384,512]{1,0:T(8,128)(2,1)S(1)}, bf16[384,512]{1,0:T(8,128)(2,1)S(1)}, u32[]{:S(2)}, u32[]{:S(2)}) %collective-permute-start.2) | collective-permute-done | bytes 393248 | tf_op jit(solution)/shard_map/ppermute | solution.py:165
  61.0 1.9 collective-permute-start.3
  62.9 2.4 %collective-permute-done.3 = bf16[576,768]{1,0:T(8,128)(2,1)S(1)} collective-permute-done((bf16[576,768]{1,0:T(8,128)(2,1)S(1)}, bf16[576,768]{1,0:T(8,128)(2,1)S(1)}, u32[]{:S(2)}, u32[]{:S(2)}) %collective-permute-start.3) | collective-permute-done | bytes 884768 | tf_op jit(solution)/shard_map/ppermute | solution.py:206
  65.3 1.6 add_convert_fusion
  66.9 9.3 %all-to-all-start.1 = ((bf16[8,72,768]{2,1,0:T(8,128)(2,1)}), bf16[8,72,768]{2,1,0:T(8,128)(2,1)S(1)}, u32[]{:S(2)}, u32[]{:S(2)}) async-start(bf16[8,72,768]{2,1,0:T(8,128)(2,1)} %bitcast.11), calls=%async_computation.1 | async-start | bytes 1769472 | tf_op jit(solution)/shard_map/all_to_all | solution.py:124
  76.3 1.9 collective-permute-start.5
  78.2 5.1 %collective-permute-start.4 = (bf16[512,768]{1,0:T(8,128)(2,1)S(1)}, bf16[512,768]{1,0:T(8,128)(2,1)S(1)}, u32[]{:S(2)}, u32[]{:S(2)}) collective-permute-start(bf16[512,768]{1,0:T(8,128)(2,1)S(1)} %pad_maximum_fusion.2), channel_id=1, source_target_pairs={{0,8},{1,9},{2,10},{3,11},{4,12},{5,13},{6,14},{7,15},{8,16},{9,17... | collective-permute-start | bytes 2359304 | tf_op jit(solution)/shard_map/ppermute | solution.py:202
  84.0 17.7 %all-to-all-done.1 = bf16[8,72,768]{2,1,0:T(8,128)(2,1)S(1)} async-done(((bf16[8,72,768]{2,1,0:T(8,128)(2,1)}), bf16[8,72,768]{2,1,0:T(8,128)(2,1)S(1)}, u32[]{:S(2)}, u32[]{:S(2)}) %all-to-all-start.1) | async-done | bytes 884768 | tf_op jit(solution)/shard_map/all_to_all | solution.py:124
  101.9 1.1 broadcast_in_dim.5
  103.0 4.8 %all-to-all-start.2 = ((bf16[8,72,768]{2,1,0:T(8,128)(2,1)}), bf16[8,72,768]{2,1,0:T(8,128)(2,1)}, u32[]{:S(2)}, u32[]{:S(2)}) async-start(bf16[8,72,768]{2,1,0:T(8,128)(2,1)} %broadcast_in_dim.5), calls=%async_computation.2 | async-start | bytes 1769472 | tf_op jit(solution)/shard_map/all_to_all | solution.py:124
  107.9 3.5 %fusion.2 = (bf16[8,2,72,768]{3,2,1,0:T(8,128)(2,1)S(1)}, bf16[8,2,72,768]{3,2,1,0:T(8,128)(2,1)S(1)}, bf16[8,2,72,768]{3,2,1,0:T(8,128)(2,1)S(1)}) fusion(bf16[8,2,72,1536]{3,2,1,0:T(8,128)(2,1)} %bitcast.38), kind=kLoop, calls=%fused_computation.7 | loop fusion | flops 13271040 | bytes 8847360 | tf_op jit(solution)/shard_map/convert_element_type | solution.py:33
  111.6 0.9 copy-done.10
  112.5 0.8 convolution_convert_fusion.3
  113.3 0.8 convolution_convert_fusion.2
  114.1 1.3 pad_maximum_fusion.1
  115.4 1.0 slice.54
  116.5 1.0 slice.55
  117.5 1.9 collective-permute-start.9
  119.4 5.6 %collective-permute-start.8 = (bf16[256,768]{1,0:T(8,128)(2,1)S(1)}, bf16[256,768]{1,0:T(8,128)(2,1)}, u32[]{:S(2)}, u32[]{:S(2)}) collective-permute-start(bf16[256,768]{1,0:T(8,128)(2,1)S(1)} %slice.54), channel_id=1, source_target_pairs={{0,8},{1,9},{2,10},{3,11},{4,12},{5,13},{6,14},{7,15},{8,16},{9,17... | collective-permute-start | bytes 1179656 | tf_op jit(solution)/shard_map/ppermute | solution.py:213
  125.0 6.0 %collective-permute-done.9 = bf16[256,768]{1,0:T(8,128)(2,1)S(1)} collective-permute-done((bf16[256,768]{1,0:T(8,128)(2,1)S(1)}, bf16[256,768]{1,0:T(8,128)(2,1)S(1)}, u32[]{:S(2)}, u32[]{:S(2)}) %collective-permute-start.9) | collective-permute-done | bytes 393248 | tf_op jit(solution)/shard_map/ppermute | solution.py:214
  132.9 1.9 collective-permute-start.10
  134.9 2.6 %collective-permute-done.10.other_ref = bf16[576,768]{1,0:T(8,128)(2,1)} collective-permute-done((bf16[576,768]{1,0:T(8,128)(2,1)}, bf16[576,768]{1,0:T(8,128)(2,1)}, u32[]{:S(2)}, u32[]{:S(2)}) %collective-permute-start.10) | collective-permute-done | bytes 884768 | tf_op jit(solution)/shard_map/ppermute | solution.py:236
  137.6 1.3 copy-done.2
  138.8 7.9 %shard_map.102 = (bf16[512,768]{1,0:T(8,128)(2,1)S(1)}, bf16[512,768]{1,0:T(8,128)(2,1)}, bf16[512,768]{1,0:T(8,128)(2,1)}, bf16[512,768]{1,0:T(8,128)(2,1)}, bf16[576,3072]{1,0:T(8,128)(2,1)S(1)}) custom-call(s32[2]{0:T(128)S(1)} %pad_add_fusion.place_ref, bf16[576,768]{1,0:T(8,128)(2,1)} %bitcast.12.own_ref, ...), custom_call_target="tpu_custom_call" | custom-call | flops 1811939328 | bytes 14000000 | tf_op jit(solution)/shard_map/pallas_call | solution.py:98
  146.7 5.2 %collective-permute-start.11 = (bf16[512,768]{1,0:T(8,128)(2,1)}, bf16[512,768]{1,0:T(8,128)(2,1)S(1)}, u32[]{:S(2)}, u32[]{:S(2)}) collective-permute-start(bf16[512,768]{1,0:T(8,128)(2,1)} %get-tuple-element.40), channel_id=1, source_target_pairs={{0,8},{1,9},{2,10},{3,11},{4,12},{5,13},{6,14},{7,15},{8,16},{9,17... | collective-permute-start | bytes 2359304 | tf_op jit(solution)/shard_map/ppermute | solution.py:247
  151.9 1.9 collective-permute-start.12
  153.8 2.8 %collective-permute-start.13 = (bf16[512,768]{1,0:T(8,128)(2,1)}, bf16[512,768]{1,0:T(8,128)(2,1)}, u32[]{:S(2)}, u32[]{:S(2)}) collective-permute-start(bf16[512,768]{1,0:T(8,128)(2,1)} %get-tuple-element.42), channel_id=1, source_target_pairs={{0,24},{1,25},{2,26},{3,27},{4,28},{5,29},{6,30},{7,31},{8,0},{9,1... | collective-permute-start | bytes 2359304 | tf_op jit(solution)/shard_map/ppermute | solution.py:247
  158.3 1.7 fusion.13
  160.0 1.5 fusion.9
  161.7 7.8 %all-to-all-start.3 = ((bf16[8,72,512]{2,1,0:T(8,128)(2,1)}), bf16[8,72,512]{2,1,0:T(8,128)(2,1)S(1)}, u32[]{:S(2)}, u32[]{:S(2)}) async-start(bf16[8,72,512]{2,1,0:T(8,128)(2,1)} %bitcast.21), calls=%async_computation.4 | async-start | bytes 1179648 | tf_op jit(solution)/shard_map/all_to_all | solution.py:124
  169.5 3.8 %collective-permute-done.11 = bf16[512,768]{1,0:T(8,128)(2,1)S(1)} collective-permute-done((bf16[512,768]{1,0:T(8,128)(2,1)}, bf16[512,768]{1,0:T(8,128)(2,1)S(1)}, u32[]{:S(2)}, u32[]{:S(2)}) %collective-permute-start.11) | collective-permute-done | bytes 786464 | tf_op jit(solution)/shard_map/ppermute | solution.py:247
  173.3 2.6 %collective-permute-done.12 = bf16[512,768]{1,0:T(8,128)(2,1)S(1)} collective-permute-done((bf16[512,768]{1,0:T(8,128)(2,1)}, bf16[512,768]{1,0:T(8,128)(2,1)S(1)}, u32[]{:S(2)}, u32[]{:S(2)}) %collective-permute-start.12) | collective-permute-done | bytes 786464 | tf_op jit(solution)/shard_map/ppermute | solution.py:247
  175.9 15.9 %collective-permute-done.13 = bf16[512,768]{1,0:T(8,128)(2,1)} collective-permute-done((bf16[512,768]{1,0:T(8,128)(2,1)}, bf16[512,768]{1,0:T(8,128)(2,1)}, u32[]{:S(2)}, u32[]{:S(2)}) %collective-permute-start.13) | collective-permute-done | bytes 786464 | tf_op jit(solution)/shard_map/ppermute | solution.py:247
  191.8 1.6 multiply_convert_fusion
  193.4 1.0 fusion.31
  194.4 0.8 multiply_convert_fusion.1
  (64 shorter events, 7.5 us)
Async XLA Ops:
  7.2 17.3 %copy-start.14 = (bf16[72,512]{1,0:T(8,128)(2,1)S(1)}, bf16[72,512]{1,0:T(8,128)(2,1)}, u32[]{:S(2)}) copy-start(bf16[72,512]{1,0:T(8,128)(2,1)} %param.8) | copy-start | bytes 221188
  7.2 100.7 %all-gather.3.cloned.1.call-start = ((), (), s32[]{:S(2)}) async-start(), calls=%async_computation.5 | async-start | bytes 3760128 | tf_op jit(solution)/shard_map/all_gather | solution.py:192
  8.3 10.9 %collective-permute-start.6 = (bf16[72,768]{1,0:T(8,128)(2,1)S(1)}, bf16[72,768]{1,0:T(8,128)(2,1)S(1)}, u32[]{:S(2)}, u32[]{:S(2)}) collective-permute-start(bf16[72,768]{1,0:T(8,128)(2,1)S(1)} %get-tuple-element.57), channel_id=1, source_target_pairs={{0,0},{1,1},{2,2},{3,3},{4,4},{5,5},{6,6},{7,7},{8,64},{9,65},{10,... | collective-permute-start | bytes 331784 | tf_op jit(solution)/shard_map/ppermute | solution.py:181
  11.1 12.5 %collective-permute-start.7 = (bf16[72,768]{1,0:T(8,128)(2,1)S(1)}, bf16[72,768]{1,0:T(8,128)(2,1)S(1)}, u32[]{:S(2)}, u32[]{:S(2)}) collective-permute-start(bf16[72,768]{1,0:T(8,128)(2,1)S(1)} %get-tuple-element.58), channel_id=1, source_target_pairs={{0,64},{1,65},{2,66},{3,67},{4,68},{5,69},{6,70},{7,71},{8,0},{9,1... | collective-permute-start | bytes 331784 | tf_op jit(solution)/shard_map/ppermute | solution.py:181
  23.7 12.0 %copy-start.11 = (bf16[384,512]{1,0:T(8,128)(2,1)S(1)}, bf16[384,512]{1,0:T(8,128)(2,1)}, u32[]{:S(2)}) copy-start(bf16[384,512]{1,0:T(8,128)(2,1)} %param.13) | copy-start | bytes 1179652
  23.7 20.0 %copy-start.13 = (bf16[512,384]{1,0:T(8,128)(2,1)S(1)}, bf16[512,384]{1,0:T(8,128)(2,1)}, u32[]{:S(2)}) copy-start(bf16[512,384]{1,0:T(8,128)(2,1)} %param.12) | copy-start | bytes 1179652
  25.3 35.0 %all-to-all-start = ((bf16[8,72,512]{2,1,0:T(8,128)(2,1)}), bf16[8,72,512]{2,1,0:T(8,128)(2,1)S(1)}, u32[]{:S(2)}, u32[]{:S(2)}) async-start(bf16[8,72,512]{2,1,0:T(8,128)(2,1)} %broadcast_in_dim.4), calls=%async_computation | async-start | bytes 1179648 | tf_op jit(solution)/shard_map/all_to_all | solution.py:124
  35.6 13.9 %collective-permute-start = (bf16[384,512]{1,0:T(8,128)(2,1)S(1)}, bf16[384,512]{1,0:T(8,128)(2,1)S(1)}, u32[]{:S(2)}, u32[]{:S(2)}) collective-permute-start(bf16[384,512]{1,0:T(8,128)(2,1)S(1)} %copy-done.11), channel_id=1, source_target_pairs={{0,8},{1,9},{2,10},{3,11},{4,12},{5,13},{6,14},{7,15},{8,16},{9,17... | collective-permute-start | bytes 1179656 | tf_op jit(solution)/shard_map/ppermute | solution.py:165
  37.6 22.4 %collective-permute-start.2 = (bf16[384,512]{1,0:T(8,128)(2,1)S(1)}, bf16[384,512]{1,0:T(8,128)(2,1)S(1)}, u32[]{:S(2)}, u32[]{:S(2)}) collective-permute-start(bf16[384,512]{1,0:T(8,128)(2,1)S(1)} %copy-done.11), channel_id=1, source_target_pairs={{0,24},{1,25},{2,26},{3,27},{4,28},{5,29},{6,30},{7,31},{8,0},{9,1... | collective-permute-start | bytes 1179656 | tf_op jit(solution)/shard_map/ppermute | solution.py:165
  41.5 18.5 %collective-permute-start.1 = (bf16[384,512]{1,0:T(8,128)(2,1)S(1)}, bf16[384,512]{1,0:T(8,128)(2,1)S(1)}, u32[]{:S(2)}, u32[]{:S(2)}) collective-permute-start(bf16[384,512]{1,0:T(8,128)(2,1)S(1)} %copy-done.11), channel_id=1, source_target_pairs={{0,16},{1,17},{2,18},{3,19},{4,20},{5,21},{6,22},{7,23},{8,24},{9,... | collective-permute-start | bytes 1179656 | tf_op jit(solution)/shard_map/ppermute | solution.py:165
  44.7 33.4 %copy-start.3 = (bf16[512,768]{1,0:T(8,128)(2,1)}, bf16[512,768]{1,0:T(8,128)(2,1)S(1)}, u32[]{:S(2)}) copy-start(bf16[512,768]{1,0:T(8,128)(2,1)S(1)} %pad_maximum_fusion.2) | copy-start | bytes 2359300
  60.3 6.6 %copy-start.9 = (bf16[8,72,512]{2,1,0:T(8,128)(2,1)}, bf16[8,72,512]{2,1,0:T(8,128)(2,1)S(1)}, u32[]{:S(2)}) copy-start(bf16[8,72,512]{2,1,0:T(8,128)(2,1)S(1)} %all-to-all-done) | copy-start | bytes 1769476
  61.0 4.3 %collective-permute-start.3 = (bf16[576,768]{1,0:T(8,128)(2,1)S(1)}, bf16[576,768]{1,0:T(8,128)(2,1)S(1)}, u32[]{:S(2)}, u32[]{:S(2)}) collective-permute-start(bf16[576,768]{1,0:T(8,128)(2,1)S(1)} %convolution_convert_fusion), channel_id=1, source_target_pairs={{0,32},{32,0},{64,96},{96,64},{128,160},{160,128},{192,224},{224,1... | collective-permute-start | bytes 2654216 | tf_op jit(solution)/shard_map/ppermute | solution.py:206
  66.9 16.4 %copy-start.15 = (bf16[72,512]{1,0:T(8,128)(2,1)S(1)}, bf16[72,512]{1,0:T(8,128)(2,1)}, u32[]{:S(2)}) copy-start(bf16[72,512]{1,0:T(8,128)(2,1)} %param.7) | copy-start | bytes 221188
  66.9 34.8 %all-to-all-start.1 = ((bf16[8,72,768]{2,1,0:T(8,128)(2,1)}), bf16[8,72,768]{2,1,0:T(8,128)(2,1)S(1)}, u32[]{:S(2)}, u32[]{:S(2)}) async-start(bf16[8,72,768]{2,1,0:T(8,128)(2,1)} %bitcast.11), calls=%async_computation.1 | async-start | bytes 1769472 | tf_op jit(solution)/shard_map/all_to_all | solution.py:124
  76.2 58.7 %all-gather.5.cloned.1.call-start = ((), (), s32[]{:S(2)}) async-start(), calls=%async_computation.6 | async-start | bytes 1327104 | tf_op jit(solution)/shard_map/all_gather | solution.py:198
  76.3 25.6 %collective-permute-start.5 = (bf16[512,768]{1,0:T(8,128)(2,1)S(1)}, bf16[512,768]{1,0:T(8,128)(2,1)S(1)}, u32[]{:S(2)}, u32[]{:S(2)}) collective-permute-start(bf16[512,768]{1,0:T(8,128)(2,1)S(1)} %pad_maximum_fusion.2), channel_id=1, source_target_pairs={{0,24},{1,25},{2,26},{3,27},{4,28},{5,29},{6,30},{7,31},{8,0},{9,1... | collective-permute-start | bytes 2359304 | tf_op jit(solution)/shard_map/ppermute | solution.py:203
  78.2 23.7 %collective-permute-start.4 = (bf16[512,768]{1,0:T(8,128)(2,1)S(1)}, bf16[512,768]{1,0:T(8,128)(2,1)S(1)}, u32[]{:S(2)}, u32[]{:S(2)}) collective-permute-start(bf16[512,768]{1,0:T(8,128)(2,1)S(1)} %pad_maximum_fusion.2), channel_id=1, source_target_pairs={{0,8},{1,9},{2,10},{3,11},{4,12},{5,13},{6,14},{7,15},{8,16},{9,17... | collective-permute-start | bytes 2359304 | tf_op jit(solution)/shard_map/ppermute | solution.py:202
  101.9 6.0 %copy-start.5 = (bf16[512,768]{1,0:T(8,128)(2,1)}, bf16[512,768]{1,0:T(8,128)(2,1)S(1)}, u32[]{:S(2)}) copy-start(bf16[512,768]{1,0:T(8,128)(2,1)S(1)} %collective-permute-done.5) | copy-start | bytes 2359300
  101.9 6.0 %copy-start.7 = (bf16[512,768]{1,0:T(8,128)(2,1)}, bf16[512,768]{1,0:T(8,128)(2,1)S(1)}, u32[]{:S(2)}) copy-start(bf16[512,768]{1,0:T(8,128)(2,1)S(1)} %collective-permute-done.4) | copy-start | bytes 2359300
  103.0 29.9 %all-to-all-start.2 = ((bf16[8,72,768]{2,1,0:T(8,128)(2,1)}), bf16[8,72,768]{2,1,0:T(8,128)(2,1)}, u32[]{:S(2)}, u32[]{:S(2)}) async-start(bf16[8,72,768]{2,1,0:T(8,128)(2,1)} %broadcast_in_dim.5), calls=%async_computation.2 | async-start | bytes 1769472 | tf_op jit(solution)/shard_map/all_to_all | solution.py:124
  107.8 53.9 %reduce-scatter.2.cloned.1.call-start = ((), (), s32[]{:S(2)}) async-start(), calls=%async_computation.7 | async-start | bytes 1966080 | tf_op jit(solution)/shard_map/reduce_scatter | solution.py:225
  111.4 1.1 copy-start.10
  117.5 13.6 %collective-permute-start.9 = (bf16[256,768]{1,0:T(8,128)(2,1)S(1)}, bf16[256,768]{1,0:T(8,128)(2,1)S(1)}, u32[]{:S(2)}, u32[]{:S(2)}) collective-permute-start(bf16[256,768]{1,0:T(8,128)(2,1)S(1)} %slice.55), channel_id=1, source_target_pairs={{0,24},{1,25},{2,26},{3,27},{4,28},{5,29},{6,30},{7,31},{8,0},{9,1... | collective-permute-start | bytes 1179656 | tf_op jit(solution)/shard_map/ppermute | solution.py:214
  119.4 12.8 %collective-permute-start.8 = (bf16[256,768]{1,0:T(8,128)(2,1)S(1)}, bf16[256,768]{1,0:T(8,128)(2,1)}, u32[]{:S(2)}, u32[]{:S(2)}) collective-permute-start(bf16[256,768]{1,0:T(8,128)(2,1)S(1)} %slice.54), channel_id=1, source_target_pairs={{0,8},{1,9},{2,10},{3,11},{4,12},{5,13},{6,14},{7,15},{8,16},{9,17... | collective-permute-start | bytes 1179656 | tf_op jit(solution)/shard_map/ppermute | solution.py:213
  131.0 0.7 copy-start.16
  132.9 4.7 %collective-permute-start.10 = (bf16[576,768]{1,0:T(8,128)(2,1)}, bf16[576,768]{1,0:T(8,128)(2,1)}, u32[]{:S(2)}, u32[]{:S(2)}) collective-permute-start(bf16[576,768]{1,0:T(8,128)(2,1)} %bitcast.12.own_ref), channel_id=1, source_target_pairs={{0,32},{32,0},{64,96},{96,64},{128,160},{160,128},{192,224},{224,1... | collective-permute-start | bytes 2654216 | tf_op jit(solution)/shard_map/ppermute | solution.py:236
  137.6 1.3 copy-start.2
  138.8 17.8 %copy-start.8 = (bf16[512,768]{1,0:T(8,128)(2,1)S(1)}, bf16[512,768]{1,0:T(8,128)(2,1)}, u32[]{:S(2)}) copy-start(bf16[512,768]{1,0:T(8,128)(2,1)} %copy-done.7) | copy-start | bytes 2359300
  146.7 11.2 %copy-start = (bf16[512,768]{1,0:T(8,128)(2,1)}, bf16[512,768]{1,0:T(8,128)(2,1)S(1)}, u32[]{:S(2)}) copy-start(bf16[512,768]{1,0:T(8,128)(2,1)S(1)} %get-tuple-element.39) | copy-start | bytes 2359300
  146.7 10.6 %copy-start.6 = (bf16[512,768]{1,0:T(8,128)(2,1)S(1)}, bf16[512,768]{1,0:T(8,128)(2,1)}, u32[]{:S(2)}) copy-start(bf16[512,768]{1,0:T(8,128)(2,1)} %copy-done.5) | copy-start | bytes 2359300
  146.7 26.6 %collective-permute-start.11 = (bf16[512,768]{1,0:T(8,128)(2,1)}, bf16[512,768]{1,0:T(8,128)(2,1)S(1)}, u32[]{:S(2)}, u32[]{:S(2)}) collective-permute-start(bf16[512,768]{1,0:T(8,128)(2,1)} %get-tuple-element.40), channel_id=1, source_target_pairs={{0,8},{1,9},{2,10},{3,11},{4,12},{5,13},{6,14},{7,15},{8,16},{9,17... | collective-permute-start | bytes 2359304 | tf_op jit(solution)/shard_map/ppermute | solution.py:247
  151.9 24.1 %collective-permute-start.12 = (bf16[512,768]{1,0:T(8,128)(2,1)}, bf16[512,768]{1,0:T(8,128)(2,1)S(1)}, u32[]{:S(2)}, u32[]{:S(2)}) collective-permute-start(bf16[512,768]{1,0:T(8,128)(2,1)} %get-tuple-element.41), channel_id=1, source_target_pairs={{0,16},{1,17},{2,18},{3,19},{4,20},{5,21},{6,22},{7,23},{8,24},{9,... | collective-permute-start | bytes 2359304 | tf_op jit(solution)/shard_map/ppermute | solution.py:247
  153.8 38.0 %collective-permute-start.13 = (bf16[512,768]{1,0:T(8,128)(2,1)}, bf16[512,768]{1,0:T(8,128)(2,1)}, u32[]{:S(2)}, u32[]{:S(2)}) collective-permute-start(bf16[512,768]{1,0:T(8,128)(2,1)} %get-tuple-element.42), channel_id=1, source_target_pairs={{0,24},{1,25},{2,26},{3,27},{4,28},{5,29},{6,30},{7,31},{8,0},{9,1... | collective-permute-start | bytes 2359304 | tf_op jit(solution)/shard_map/ppermute | solution.py:247
  157.3 1.0 copy-start.17
  158.3 1.7 copy-start.4
  161.5 30.3 %copy-start.1 = (bf16[512,768]{1,0:T(8,128)(2,1)S(1)}, bf16[512,768]{1,0:T(8,128)(2,1)}, u32[]{:S(2)}) copy-start(bf16[512,768]{1,0:T(8,128)(2,1)} %copy-done) | copy-start | bytes 2359300
  161.7 33.5 %all-to-all-start.3 = ((bf16[8,72,512]{2,1,0:T(8,128)(2,1)}), bf16[8,72,512]{2,1,0:T(8,128)(2,1)S(1)}, u32[]{:S(2)}, u32[]{:S(2)}) async-start(bf16[8,72,512]{2,1,0:T(8,128)(2,1)} %bitcast.21), calls=%async_computation.4 | async-start | bytes 1179648 | tf_op jit(solution)/shard_map/all_to_all | solution.py:124
  193.4 1.0 copy-start.12
Sparse Core Ops, SparseCore 0:
  24.6 48.2 all-gather.2
  84.2 43.2 all-gather.4
  130.3 31.3 reduce-scatter.1
